TPU v7x, 32 devices: a whole 2x2x4 slice. The times are simulated.
32 devices in a mesh: loop: 16 (over z, y, core), grp: 2 (over x).
Axes of the slice: x: 2, y: 2, z: 4, core: 2. Of those that a mesh axis runs over, the one named last changes fastest.
Arguments:
- ratings: bfloat16 [2, 16384, 2048], P(None, ('loop', 'grp')), may hold values from -2.5 to 2.5, as said below
- user_factors: float32 [16384, 128], P(('loop', 'grp')), may hold values from -2 to 2
- user_accum: float32 [16384, 128], P(('loop', 'grp')), may hold values from 20 to 400
- item_factors: float32 [32768, 128], P('loop'), may hold values from -2 to 2
- item_accum: float32 [32768, 128], P('loop'), may hold values from 20 to 400
Outputs:
- users_out: float32 [16384, 128], P(('loop', 'grp'))
- items_out: float32 [32768, 128], P('loop')
Inputs may be any that keep to these rules, and one draw needn't show every extreme that they name: `ratings`: each entry is 0 (unobserved) or has magnitude 0.5 or more.
All inputs are finite; a program needn't handle non-finite values.
Results may differ from a plain program's by a relative error of at most 0.0085.
Values may be sent and summed in bfloat16 or wider, within the bound.
No kernel may reach another device: no remote copies, remote signals or barrier semaphores. Data moves between devices by JAX's collectives and lax.ppermute only.
A program may use at most 64 MiB of HBM per device.

v0:
```python
import jax
import jax.numpy as jnp
from jax import lax
from jax.sharding import PartitionSpec as P

SUB = 2
INNER = 2


shrink = 0.05
learn_rate = 0.2
tiny_eps = 1e-06


def shifted(shard, axis, by):
    devices = lax.axis_size(axis)
    return lax.ppermute(shard, axis, [(i, (i + by) % devices) for i in range(devices)])


def adagrad(param, accum, grad):
    accum = accum + grad * grad
    return (param - learn_rate * grad / jnp.sqrt(accum + tiny_eps), accum)


def residual_terms(rate_full, observed, users, item_half):
    user_half = users.astype(jnp.bfloat16)
    predicted = lax.dot_general(
        user_half, item_half, (((1,), (1,)), ((), ())), preferred_element_type=jnp.float32
    )
    resid = (observed * (rate_full - predicted)).astype(jnp.bfloat16)
    grad_user = -jnp.dot(resid, item_half, preferred_element_type=jnp.float32) + shrink * users
    return (user_half, resid, grad_user)


def local(ratings, user_factors, user_accum, item_factors, item_accum):
    users = user_factors
    user_acc = user_accum
    items = item_factors
    item_acc = item_accum
    for sub_epoch in range(SUB):
        if sub_epoch > 0:
            items, item_acc = shifted((items, item_acc), "loop", 1)
        rate_full = ratings[sub_epoch].astype(jnp.float32)
        observed = (jnp.abs(rate_full) > 0.25).astype(jnp.float32)
        for inner_step in range(INNER):
            item_half = items.astype(jnp.bfloat16)
            user_half, resid, grad_user = residual_terms(rate_full, observed, users, item_half)
            own_term = -lax.dot_general(
                resid, user_half, (((0,), (0,)), ((), ())), preferred_element_type=jnp.float32
            )
            grad_item = (
                lax.psum(own_term.astype(jnp.bfloat16), "grp").astype(jnp.float32) + shrink * items
            )
            users, user_acc = adagrad(users, user_acc, grad_user)
            items, item_acc = adagrad(items, item_acc, grad_item)
    return (users, items)


def solution(mesh):
    in_specs = (
        P(None, ("loop", "grp"), None),
        P(("loop", "grp"), None),
        P(("loop", "grp"), None),
        P("loop", None),
        P("loop", None),
    )
    out_specs = (P(("loop", "grp"), None), P("loop", None))
    return jax.shard_map(local, mesh=mesh, in_specs=in_specs, out_specs=out_specs, check_vma=False)
```

profile of v0, /device:TPU:0, one launch (start us, length us, event | category | flops | bytes accessed | tf_op | source)
XLA Modules:
  0.0 170.6 jit_solution(7967820486868653709)
XLA Ops:
  7.2 3.0 %fusion.2 = bf16[512,2048]{1,0:T(8,128)(2,1)S(1)} fusion(bf16[2,512,2048]{2,1,0:T(8,128)(2,1)} %param.5, f32[2048,128]{1,0:T(8,128)} %param.8, f32[512,128]{1,0:T(8,128)} %param.6), kind=kOutput, calls=%fused_computation.8 | convolution fusion | flops 275054592 | bytes 5505024 | tf_op jit(solution)/shard_map/dot_general | solution.py:27
  10.3 1.6 fusion.10
  11.9 0.0 all-reduce.7.cloned.1.call-start
  11.9 2.5 %multiply_subtract_fusion.7 = (f32[512,128]{1,0:T(8,128)}, f32[512,128]{1,0:T(8,128)}) fusion(f32[512,128]{1,0:T(8,128)} %param.6, f32[512,128]{1,0:T(8,128)S(1)} %copy-done.5, bf16[512,2048]{1,0:T(8,128)(2,1)S(1)} %fusion.2, f32[2048,128]{1,0:T(8,128)S(1)} %copy-done), kind=kOutput, calls=%fused_computation.52 | convolution fusion | flops 269287424 | bytes 4194304 | tf_op jit(solution)/shard_map/dot_general | solution.py:31
  14.4 28.9 %all-reduce.5.cloned.1.call-done = bf16[2048,128]{1,0:T(8,128)(2,1)} async-done(((bf16[2048,128]{1,0:T(8,128)(2,1)}), bf16[2048,128]{1,0:T(8,128)(2,1)}) %all-reduce.5.cloned.1.call-update) | async-done | bytes 524304 | tf_op jit(solution)/shard_map/psum | solution.py:52
  43.3 3.4 %fusion.4 = bf16[512,2048]{1,0:T(8,128)(2,1)S(1)} fusion(bf16[2,512,2048]{2,1,0:T(8,128)(2,1)} %param.5, f32[512,128]{1,0:T(8,128)} %get-tuple-element.6, f32[2048,128]{1,0:T(8,128)S(1)} %copy-done, bf16[2048,128]{1,0:T(8,128)(2,1)} %all-reduce.5.cloned.1.call-done, f32[2048,128]{1,0:T(8,128)} %param.9), kind=kOutput, calls=%fused_computation.10 | convolution fusion | flops 277413888 | bytes 7077888 | tf_op jit(solution)/shard_map/dot_general | solution.py:27
  46.7 1.6 fusion.11
  48.4 28.7 %all-reduce.7.cloned.1.call-done = bf16[2048,128]{1,0:T(8,128)(2,1)} async-done(((bf16[2048,128]{1,0:T(8,128)(2,1)}), bf16[2048,128]{1,0:T(8,128)(2,1)}) %all-reduce.7.cloned.1.call-update) | async-done | bytes 524304 | tf_op jit(solution)/shard_map/psum | solution.py:52
  77.1 3.3 %multiply_add_fusion.2 = (f32[2048,128]{1,0:T(8,128)}, f32[2048,128]{1,0:T(8,128)S(1)}) fusion(bf16[2048,128]{1,0:T(8,128)(2,1)} %all-reduce.7.cloned.1.call-done, f32[2048,128]{1,0:T(8,128)} %param.9, f32[2048,128]{1,0:T(8,128)S(1)} %copy-done, bf16[2048,128]{1,0:T(8,128)(2,1)} %all-reduce.5.cloned.1.call-done), kind=kLoop, calls=%fused_computation.37 | loop fusion | flops 4718592 | bytes 5242880 | tf_op jit(solution)/shard_map/add | solution.py:21
  80.4 2.8 %multiply_subtract_fusion.6 = (f32[512,128]{1,0:T(8,128)S(1)}, f32[512,128]{1,0:T(8,128)}) fusion(f32[512,128]{1,0:T(8,128)} %get-tuple-element.6, f32[512,128]{1,0:T(8,128)} %param.7, f32[512,128]{1,0:T(8,128)} %get-tuple-element.7, bf16[512,2048]{1,0:T(8,128)(2,1)S(1)} %fusion.4, f32[2048,128]{1,0:T(8,128)S(1)} %copy-done.1, ...), kind=kOutput, calls=%fused_computation.48 | convolution fusion | flops 271777792 | bytes 6029312 | tf_op jit(solution)/shard_map/dot_general | solution.py:31
  83.2 1.6 collective-permute-start.1
  84.8 12.5 %collective-permute-done = f32[2048,128]{1,0:T(8,128)S(1)} collective-permute-done((f32[2048,128]{1,0:T(8,128)S(1)}, f32[2048,128]{1,0:T(8,128)S(1)}, u32[]{:S(2)}, u32[]{:S(2)}) %collective-permute-start) | collective-permute-done | bytes 1048608 | tf_op jit(solution)/shard_map/ppermute | solution.py:17
  97.3 1.1 fusion.7
  98.4 1.6 fusion.12
  100.0 0.2 all-reduce.11.cloned.1.call-start
  100.2 2.4 %fusion.25 = (bf16[512,128]{1,0:T(8,128)(2,1)S(1)}, f32[512,128]{1,0:T(8,128)}) fusion(f32[512,128]{1,0:T(8,128)S(1)} %get-tuple-element.2, f32[512,128]{1,0:T(8,128)} %get-tuple-element.3, bf16[512,2048]{1,0:T(8,128)(2,1)S(1)} %fusion.7, f32[2048,128]{1,0:T(8,128)S(1)} %collective-permute-done), kind=kOutput, calls=%fused_computation.56 | convolution fusion | flops 269352960 | bytes 4063232 | tf_op jit(solution)/shard_map/dot_general | solution.py:31
  102.6 6.1 %collective-permute-done.1 = f32[2048,128]{1,0:T(8,128)} collective-permute-done((f32[2048,128]{1,0:T(8,128)}, f32[2048,128]{1,0:T(8,128)}, u32[]{:S(2)}, u32[]{:S(2)}) %collective-permute-start.1) | collective-permute-done | bytes 1048608 | tf_op jit(solution)/shard_map/ppermute | solution.py:17
  108.7 17.4 %all-reduce.9.cloned.1.call-done = bf16[2048,128]{1,0:T(8,128)(2,1)} async-done(((bf16[2048,128]{1,0:T(8,128)(2,1)}), bf16[2048,128]{1,0:T(8,128)(2,1)}) %all-reduce.9.cloned.1.call-update) | async-done | bytes 524304 | tf_op jit(solution)/shard_map/psum | solution.py:52
  126.1 1.7 %fusion.18 = bf16[2048,128]{1,0:T(8,128)(2,1)S(1)} fusion(f32[2048,128]{1,0:T(8,128)S(1)} %collective-permute-done, f32[2048,128]{1,0:T(8,128)} %collective-permute-done.1, bf16[2048,128]{1,0:T(8,128)(2,1)} %all-reduce.9.cloned.1.call-done), kind=kLoop, calls=%fused_computation.42 | loop fusion | flops 2621440 | bytes 3145728 | tf_op jit(solution)/shard_map/convert_element_type | solution.py:46
  127.8 2.7 %fusion.9 = bf16[512,2048]{1,0:T(8,128)(2,1)S(1)} fusion(bf16[512,128]{1,0:T(8,128)(2,1)S(1)} %get-tuple-element.8, bf16[2048,128]{1,0:T(8,128)(2,1)S(1)} %fusion.18, bf16[2,512,2048]{2,1,0:T(8,128)(2,1)} %param.5), kind=kOutput, calls=%fused_computation.15 | convolution fusion | flops 274726912 | bytes 4849664 | tf_op jit(solution)/shard_map/dot_general | solution.py:27
  130.5 1.6 fusion.13
  132.1 2.6 %multiply_subtract_fusion.4 = f32[512,128]{1,0:T(8,128)} fusion(bf16[512,2048]{1,0:T(8,128)(2,1)S(1)} %fusion.9, bf16[2048,128]{1,0:T(8,128)(2,1)} %copy-done.7, f32[512,128]{1,0:T(8,128)} %get-tuple-element.3, f32[512,128]{1,0:T(8,128)} %get-tuple-element.9, f32[512,128]{1,0:T(8,128)S(1)} %get-tuple-element.2), kind=kOutput, calls=%fused_computation.43 | convolution fusion | flops 269418496 | bytes 3670016 | tf_op jit(solution)/shard_map/dot_general | solution.py:31
  134.8 26.1 %all-reduce.11.cloned.1.call-done = bf16[2048,128]{1,0:T(8,128)(2,1)} async-done(((bf16[2048,128]{1,0:T(8,128)(2,1)}), bf16[2048,128]{1,0:T(8,128)(2,1)}) %all-reduce.11.cloned.1.call-update) | async-done | bytes 524304 | tf_op jit(solution)/shard_map/psum | solution.py:52
  160.9 3.2 %multiply_subtract_fusion = f32[2048,128]{1,0:T(8,128)} fusion(bf16[2048,128]{1,0:T(8,128)(2,1)} %all-reduce.11.cloned.1.call-done, f32[2048,128]{1,0:T(8,128)} %collective-permute-done.1, f32[2048,128]{1,0:T(8,128)S(1)} %collective-permute-done, bf16[2048,128]{1,0:T(8,128)(2,1)} %all-reduce.9.cloned.1.call-done), kind=kLoop, calls=%fused_computation.32 | loop fusion | flops 4718592 | bytes 4194304 | tf_op jit(solution)/shard_map/sub | solution.py:22
  (25 shorter events, 0.2 us)
Async XLA Ops:
  7.2 36.2 %all-reduce.5.cloned.1.call-start = ((), (), s32[]{:S(2)}) async-start(), calls=%async_computation | async-start | bytes 1048576 | tf_op jit(solution)/shard_map/psum | solution.py:52
  7.2 3.0 %copy-start.6 = (f32[512,128]{1,0:T(8,128)S(1)}, f32[512,128]{1,0:T(8,128)}, u32[]{:S(2)}) copy-start(f32[512,128]{1,0:T(8,128)} %param.6) | copy-start | bytes 786436
  10.3 1.7 copy-start
  10.3 1.7 copy-start.5
  11.9 65.2 %all-reduce.7.cloned.1.call-start = ((), (), s32[]{:S(2)}) async-start(), calls=%async_computation.1 | async-start | bytes 1048576 | tf_op jit(solution)/shard_map/psum | solution.py:52
  43.3 3.4 %copy-start.3 = (f32[512,128]{1,0:T(8,128)S(1)}, f32[512,128]{1,0:T(8,128)}, u32[]{:S(2)}) copy-start(f32[512,128]{1,0:T(8,128)} %get-tuple-element.6) | copy-start | bytes 786436
  48.3 77.7 %all-reduce.9.cloned.1.call-start = ((), (), s32[]{:S(2)}) async-start(), calls=%async_computation.2 | async-start | bytes 1048576 | tf_op jit(solution)/shard_map/psum | solution.py:52
  77.1 3.3 %copy-start.1 = (f32[2048,128]{1,0:T(8,128)S(1)}, f32[2048,128]{1,0:T(8,128)}, u32[]{:S(2)}) copy-start(f32[2048,128]{1,0:T(8,128)} %param.8) | copy-start | bytes 3145732
  77.1 3.3 %copy-start.2 = (f32[2048,128]{1,0:T(8,128)S(1)}, f32[2048,128]{1,0:T(8,128)}, u32[]{:S(2)}) copy-start(f32[2048,128]{1,0:T(8,128)} %param.9) | copy-start | bytes 3145732
  77.1 3.3 %copy-start.4 = (bf16[2048,128]{1,0:T(8,128)(2,1)S(1)}, bf16[2048,128]{1,0:T(8,128)(2,1)}, u32[]{:S(2)}) copy-start(bf16[2048,128]{1,0:T(8,128)(2,1)} %all-reduce.5.cloned.1.call-done) | copy-start | bytes 1572868
  80.4 16.9 %collective-permute-start = (f32[2048,128]{1,0:T(8,128)S(1)}, f32[2048,128]{1,0:T(8,128)S(1)}, u32[]{:S(2)}, u32[]{:S(2)}) collective-permute-start(f32[2048,128]{1,0:T(8,128)S(1)} %get-tuple-element.5), channel_id=1, source_target_pairs={{0,2},{2,4},{4,6},{6,8},{8,10},{10,12},{12,14},{14,16},{16,18},{18... | collective-permute-start | bytes 3145736 | tf_op jit(solution)/shard_map/ppermute | solution.py:17
  80.4 16.9 %copy-start.8 = (bf16[2,512,2048]{2,1,0:T(8,128)(2,1)S(1)}, bf16[2,512,2048]{2,1,0:T(8,128)(2,1)}, u32[]{:S(2)}) copy-start(bf16[2,512,2048]{2,1,0:T(8,128)(2,1)} %param.5) | copy-start | bytes 12582916
  83.2 25.4 %collective-permute-start.1 = (f32[2048,128]{1,0:T(8,128)}, f32[2048,128]{1,0:T(8,128)}, u32[]{:S(2)}, u32[]{:S(2)}) collective-permute-start(f32[2048,128]{1,0:T(8,128)} %get-tuple-element.4), channel_id=1, source_target_pairs={{0,2},{2,4},{4,6},{6,8},{8,10},{10,12},{12,14},{14,16},{16,18},{18... | collective-permute-start | bytes 3145736 | tf_op jit(solution)/shard_map/ppermute | solution.py:17
  100.0 60.9 %all-reduce.11.cloned.1.call-start = ((), (), s32[]{:S(2)}) async-start(), calls=%async_computation.3 | async-start | bytes 1048576 | tf_op jit(solution)/shard_map/psum | solution.py:52
  127.8 2.7 %copy-start.7 = (bf16[2048,128]{1,0:T(8,128)(2,1)}, bf16[2048,128]{1,0:T(8,128)(2,1)S(1)}, u32[]{:S(2)}) copy-start(bf16[2048,128]{1,0:T(8,128)(2,1)S(1)} %fusion.18) | copy-start | bytes 1572868
Sparse Core Ops, SparseCore 0:
  12.0 31.2 all-reduce.4
  48.4 28.5 all-reduce.6
  100.1 25.8 all-reduce.8
  132.3 28.5 all-reduce.10
where the time goes:
time: 171 us
  waiting for transfers between devices  120 us (70%)
  matrix products  26.7 us (16%)
  between operations  13.9 us (8%)
  other arithmetic  8.22 us (5%)
  starting transfers between devices  1.92 us (1%)
    psum x4, waiting for transfers between devices, local(): lax.psum(own_term.astype(jnp.bfloat16), 'grp').astype(jnp.float32)  101 us
    ppermute x2, waiting for transfers between devices, shifted(): lax.ppermute(shard, axis, [(i, (i + by) % devices) for i in range(devices)])  18.6 us
    dot_general x4, matrix products, residual_terms(): jnp.dot(resid, item_half, preferred_element_type=jnp.float32)  10.3 us
    dot_general x4, matrix products, residual_terms(): lax.dot_general(user_half, item_half, (((1,), (1,)), ((), ())), preferred...  10.2 us
    dot_general x4, matrix products, local(): lax.dot_general(resid, user_half, (((0,), (0,)), ((), ())), preferred_ele...  6.29 us
  transfers between devices with their start and end apart: 6, of which 6 were waited for; matrix products, arithmetic and copies ran while one was open for 8% of the time, Pallas kernels for 0%

commit v1 on v0

v1 whole, which is shorter than its diff:
```python
import jax
import jax.numpy as jnp
from jax import lax
from jax.sharding import PartitionSpec as P

SUB = 2
INNER = 2
CHUNKS = 4


shrink = 0.05
learn_rate = 0.2
tiny_eps = 1e-06


def shifted(shard, axis, by):
    devices = lax.axis_size(axis)
    return lax.ppermute(shard, axis, [(i, (i + by) % devices) for i in range(devices)])


def adagrad(param, accum, grad):
    accum = accum + grad * grad
    return (param - learn_rate * grad * lax.rsqrt(accum + tiny_eps), accum)


def group_sum(term):
    if lax.axis_size("grp") == 2:
        return term.astype(jnp.float32) + shifted(term, "grp", 1).astype(jnp.float32)
    return lax.psum(term, "grp").astype(jnp.float32)


def local(ratings, user_factors, user_accum, item_factors, item_accum):
    users = user_factors
    user_acc = user_accum
    size = item_factors.shape[0] // CHUNKS
    items = [item_factors[c * size : (c + 1) * size] for c in range(CHUNKS)]
    item_acc = [item_accum[c * size : (c + 1) * size] for c in range(CHUNKS)]
    for sub_epoch in range(SUB):
        if sub_epoch > 0:
            for c in range(CHUNKS):
                items[c] = shifted(items[c].astype(jnp.bfloat16), "loop", 1).astype(jnp.float32)
                item_acc[c] = shifted(item_acc[c].astype(jnp.bfloat16), "loop", 1).astype(jnp.float32)
        for inner_step in range(INNER):
            user_half = users.astype(jnp.bfloat16)
            grad_user = shrink * users
            sums = []
            for c in range(CHUNKS):
                rate = ratings[sub_epoch, :, c * size : (c + 1) * size]
                item_half = items[c].astype(jnp.bfloat16)
                predicted = lax.dot_general(
                    user_half, item_half, (((1,), (1,)), ((), ())), preferred_element_type=jnp.float32
                )
                rate = rate.astype(jnp.float32)
                resid = jnp.where(jnp.abs(rate) > 0.25, rate - predicted, 0.0).astype(jnp.bfloat16)
                term = -lax.dot_general(
                    resid, user_half, (((0,), (0,)), ((), ())), preferred_element_type=jnp.float32
                )
                sums.append(group_sum(term.astype(jnp.bfloat16)))
                grad_user = grad_user - jnp.dot(resid, item_half, preferred_element_type=jnp.float32)
            users, user_acc = adagrad(users, user_acc, grad_user)
            for c in range(CHUNKS):
                grad_item = sums[c] + shrink * items[c]
                items[c], item_acc[c] = adagrad(items[c], item_acc[c], grad_item)
    return (users, jnp.concatenate(items, axis=0))


def solution(mesh):
    in_specs = (
        P(None, ("loop", "grp"), None),
        P(("loop", "grp"), None),
        P(("loop", "grp"), None),
        P("loop", None),
        P("loop", None),
    )
    out_specs = (P(("loop", "grp"), None), P("loop", None))
    return jax.shard_map(local, mesh=mesh, in_specs=in_specs, out_specs=out_specs, check_vma=False)
```

time: 171 us -> 78.5 us (0.46)
  waiting for transfers between devices: 120 us -> 31.6 us
  starting transfers between devices: 1.92 us -> 21.5 us
  between operations: 13.9 us -> 1.1 us
  matrix products: 26.7 us -> 19.6 us
  other arithmetic: 8.22 us -> 4.6 us
    psum x4 -> x0, waiting for transfers between devices: 101 us -> none  [local(): lax.psum(own_term.astype(jnp.bfloat16), 'grp').astype(jnp.float32)]
    ppermute x2 -> x24, starting transfers between devices: 1.57 us -> 21.5 us  [shifted(): lax.ppermute(shard, axis, [(i, (i + by) % devices) for i in range(devices)])]
    ppermute x2 -> x24, waiting for transfers between devices: 18.6 us -> 31.6 us  [shifted(): lax.ppermute(shard, axis, [(i, (i + by) % devices) for i in range(devices)])]
    dot_general x8 -> x32, matrix products: 20.4 us -> 14 us  [the longest x16 8.49 us: local(): lax.dot_general(user_half, item_half, (((1,), (1,)), ((), ())), preferred...]
    add x1 -> x0, other arithmetic: 3.31 us -> none  [adagrad(): accum = accum + grad * grad]
    sub x1 -> x5, other arithmetic: 3.17 us -> 1.36 us  [adagrad(): return (param - learn_rate * grad * lax.rsqrt(accum + tiny_eps), accum)]
    dot_general x4 -> x16, matrix products: 6.29 us -> 5.57 us  [local(): lax.dot_general(resid, user_half, (((0,), (0,)), ((), ())), preferred_ele...]
  transfers between devices with their start and end apart: 6 -> 24, of which waited for: 6 -> 12; matrix products, arithmetic and copies ran while one was open for 8% -> 22% of each run, Pallas kernels for 0% -> 0%
where the time goes in v1:
time: 78.5 us; the launch traced here: 78.3 us
  waiting for transfers between devices  31.6 us (40%)
  starting transfers between devices  21.5 us (27%)
  matrix products  19.6 us (25%)
  other arithmetic  4.6 us (6%)
  between operations  1.1 us (1%)
    ppermute x24, waiting for transfers between devices, shifted(): lax.ppermute(shard, axis, [(i, (i + by) % devices) for i in range(devices)])  31.6 us
    ppermute x24, starting transfers between devices, shifted(): lax.ppermute(shard, axis, [(i, (i + by) % devices) for i in range(devices)])  21.5 us
    dot_general x16, matrix products, local(): lax.dot_general(user_half, item_half, (((1,), (1,)), ((), ())), preferred...  8.49 us
    dot_general x16, matrix products, local(): lax.dot_general(resid, user_half, (((0,), (0,)), ((), ())), preferred_ele...  5.57 us
    dot_general x16, matrix products, local(): jnp.dot(resid, item_half, preferred_element_type=jnp.float32)  5.5 us
  transfers between devices with their start and end apart: 24, of which 12 were waited for; matrix products, arithmetic and copies ran while one was open for 22% of the time, Pallas kernels for 0%

profile of v1, /device:TPU:0, one launch (start us, length us, event | category | flops | bytes accessed | tf_op | source)
XLA Modules:
  0.0 78.3 jit_solution(16791368088825892382)
XLA Ops:
  0.7 1.1 %convert_element_type.350 = bf16[512,128]{1,0:T(8,128)(2,1)S(1)} convert(f32[512,128]{1,0:T(8,128)} %param.6) | non-fusion elementwise | flops 65536 | bytes 393216 | tf_op jit(solution)/shard_map/convert_element_type | solution.py:44
  1.8 2.0 %fusion.19 = bf16[512,512]{1,0:T(8,128)(2,1)S(1)} fusion(bf16[512,128]{1,0:T(8,128)(2,1)S(1)} %convert_element_type.350, bf16[2,512,2048]{2,1,0:T(8,128)(2,1)} %param.5, f32[2048,128]{1,0:T(8,128)} %param.8), kind=kOutput, calls=%fused_computation.43 | convolution fusion | flops 68681728 | bytes 1310720 | tf_op jit(solution)/shard_map/dot_general | solution.py:50
  4.1 3.0 %collective-permute-start.3 = (bf16[512,128]{1,0:T(8,128)(2,1)S(1)}, bf16[512,128]{1,0:T(8,128)(2,1)S(1)}, u32[]{:S(2)}, u32[]{:S(2)}) collective-permute-start(bf16[512,128]{1,0:T(8,128)(2,1)S(1)} %fusion.41), channel_id=1, source_target_pairs={{0,1},{1,0},{2,3},{3,2},{4,5},{5,4},{6,7},{7,6},{8,9},{9,8},{10,11... | collective-permute-start | bytes 393224 | tf_op jit(solution)/shard_map/ppermute | solution.py:18
  7.1 1.5 %fusion.18 = bf16[512,512]{1,0:T(8,128)(2,1)S(1)} fusion(bf16[512,128]{1,0:T(8,128)(2,1)S(1)} %convert_element_type.350, bf16[2,512,2048]{2,1,0:T(8,128)(2,1)} %param.5, f32[2048,128]{1,0:T(8,128)} %param.8), kind=kOutput, calls=%fused_computation.42 | convolution fusion | flops 68681728 | bytes 1310720 | tf_op jit(solution)/shard_map/dot_general | solution.py:50
  9.8 2.1 %collective-permute-start.1 = (bf16[512,128]{1,0:T(8,128)(2,1)S(1)}, bf16[512,128]{1,0:T(8,128)(2,1)S(1)}, u32[]{:S(2)}, u32[]{:S(2)}) collective-permute-start(bf16[512,128]{1,0:T(8,128)(2,1)S(1)} %fusion.39), channel_id=1, source_target_pairs={{0,1},{1,0},{2,3},{3,2},{4,5},{5,4},{6,7},{7,6},{8,9},{9,8},{10,11... | collective-permute-start | bytes 393224 | tf_op jit(solution)/shard_map/ppermute | solution.py:18
  13.9 1.5 %collective-permute-done.2 = bf16[512,128]{1,0:T(8,128)(2,1)S(1)} collective-permute-done((bf16[512,128]{1,0:T(8,128)(2,1)S(1)}, bf16[512,128]{1,0:T(8,128)(2,1)S(1)}, u32[]{:S(2)}, u32[]{:S(2)}) %collective-permute-start.2) | collective-permute-done | bytes 131104 | tf_op jit(solution)/shard_map/ppermute | solution.py:18
  15.5 2.8 %collective-permute-done.1 = bf16[512,128]{1,0:T(8,128)(2,1)S(1)} collective-permute-done((bf16[512,128]{1,0:T(8,128)(2,1)S(1)}, bf16[512,128]{1,0:T(8,128)(2,1)S(1)}, u32[]{:S(2)}, u32[]{:S(2)}) %collective-permute-start.1) | collective-permute-done | bytes 131104 | tf_op jit(solution)/shard_map/ppermute | solution.py:18
  18.2 1.4 %collective-permute-done = bf16[512,128]{1,0:T(8,128)(2,1)S(1)} collective-permute-done((bf16[512,128]{1,0:T(8,128)(2,1)S(1)}, bf16[512,128]{1,0:T(8,128)(2,1)S(1)}, u32[]{:S(2)}, u32[]{:S(2)}) %collective-permute-start) | collective-permute-done | bytes 131104 | tf_op jit(solution)/shard_map/ppermute | solution.py:18
  20.8 1.3 %collective-permute-start.10 = (bf16[512,128]{1,0:T(8,128)(2,1)S(1)}, bf16[512,128]{1,0:T(8,128)(2,1)S(1)}, u32[]{:S(2)}, u32[]{:S(2)}) collective-permute-start(bf16[512,128]{1,0:T(8,128)(2,1)S(1)} %fusion.45), channel_id=1, source_target_pairs={{0,1},{1,0},{2,3},{3,2},{4,5},{5,4},{6,7},{7,6},{8,9},{9,8},{10,11... | collective-permute-start | bytes 393224 | tf_op jit(solution)/shard_map/ppermute | solution.py:18
  25.0 1.2 %collective-permute-start.6 = (bf16[512,128]{1,0:T(8,128)(2,1)S(1)}, bf16[512,128]{1,0:T(8,128)(2,1)S(1)}, u32[]{:S(2)}, u32[]{:S(2)}) collective-permute-start(bf16[512,128]{1,0:T(8,128)(2,1)S(1)} %fusion.43), channel_id=1, source_target_pairs={{0,1},{1,0},{2,3},{3,2},{4,5},{5,4},{6,7},{7,6},{8,9},{9,8},{10,11... | collective-permute-start | bytes 393224 | tf_op jit(solution)/shard_map/ppermute | solution.py:18
  28.7 1.6 %collective-permute-start.11 = (bf16[512,128]{1,0:T(8,128)(2,1)S(1)}, bf16[512,128]{1,0:T(8,128)(2,1)S(1)}, u32[]{:S(2)}, u32[]{:S(2)}) collective-permute-start(bf16[512,128]{1,0:T(8,128)(2,1)S(1)} %get-tuple-element.28), channel_id=1, source_target_pairs={{0,2},{2,4},{4,6},{6,8},{8,10},{10,12},{12,14},{14,16},{16,18},{18... | collective-permute-start | bytes 393224 | tf_op jit(solution)/shard_map/ppermute | solution.py:18
  30.6 3.7 %collective-permute-done.8 = bf16[512,128]{1,0:T(8,128)(2,1)S(1)} collective-permute-done((bf16[512,128]{1,0:T(8,128)(2,1)S(1)}, bf16[512,128]{1,0:T(8,128)(2,1)S(1)}, u32[]{:S(2)}, u32[]{:S(2)}) %collective-permute-start.8) | collective-permute-done | bytes 131104 | tf_op jit(solution)/shard_map/ppermute | solution.py:18
  34.4 1.7 %collective-permute-start.9 = (bf16[512,128]{1,0:T(8,128)(2,1)S(1)}, bf16[512,128]{1,0:T(8,128)(2,1)S(1)}, u32[]{:S(2)}, u32[]{:S(2)}) collective-permute-start(bf16[512,128]{1,0:T(8,128)(2,1)S(1)} %get-tuple-element.26), channel_id=1, source_target_pairs={{0,2},{2,4},{4,6},{6,8},{8,10},{10,12},{12,14},{14,16},{16,18},{18... | collective-permute-start | bytes 393224 | tf_op jit(solution)/shard_map/ppermute | solution.py:18
  36.2 6.5 %collective-permute-done.9 = bf16[512,128]{1,0:T(8,128)(2,1)S(1)} collective-permute-done((bf16[512,128]{1,0:T(8,128)(2,1)S(1)}, bf16[512,128]{1,0:T(8,128)(2,1)S(1)}, u32[]{:S(2)}, u32[]{:S(2)}) %collective-permute-start.9) | collective-permute-done | bytes 131104 | tf_op jit(solution)/shard_map/ppermute | solution.py:18
  44.8 6.4 %collective-permute-done.7 = bf16[512,128]{1,0:T(8,128)(2,1)S(1)} collective-permute-done((bf16[512,128]{1,0:T(8,128)(2,1)S(1)}, bf16[512,128]{1,0:T(8,128)(2,1)S(1)}, u32[]{:S(2)}, u32[]{:S(2)}) %collective-permute-start.7) | collective-permute-done | bytes 131104 | tf_op jit(solution)/shard_map/ppermute | solution.py:18
  54.2 1.3 %collective-permute-start.16 = (bf16[512,128]{1,0:T(8,128)(2,1)S(1)}, bf16[512,128]{1,0:T(8,128)(2,1)S(1)}, u32[]{:S(2)}, u32[]{:S(2)}) collective-permute-start(bf16[512,128]{1,0:T(8,128)(2,1)S(1)} %fusion.48), channel_id=1, source_target_pairs={{0,1},{1,0},{2,3},{3,2},{4,5},{5,4},{6,7},{7,6},{8,9},{9,8},{10,11... | collective-permute-start | bytes 393224 | tf_op jit(solution)/shard_map/ppermute | solution.py:18
  55.4 3.2 %collective-permute-done.18 = bf16[512,128]{1,0:T(8,128)(2,1)S(1)} collective-permute-done((bf16[512,128]{1,0:T(8,128)(2,1)S(1)}, bf16[512,128]{1,0:T(8,128)(2,1)S(1)}, u32[]{:S(2)}, u32[]{:S(2)}) %collective-permute-start.18) | collective-permute-done | bytes 131104 | tf_op jit(solution)/shard_map/ppermute | solution.py:18
  60.5 1.4 %collective-permute-start.12 = (bf16[512,128]{1,0:T(8,128)(2,1)S(1)}, bf16[512,128]{1,0:T(8,128)(2,1)S(1)}, u32[]{:S(2)}, u32[]{:S(2)}) collective-permute-start(bf16[512,128]{1,0:T(8,128)(2,1)S(1)} %fusion.46), channel_id=1, source_target_pairs={{0,1},{1,0},{2,3},{3,2},{4,5},{5,4},{6,7},{7,6},{8,9},{9,8},{10,11... | collective-permute-start | bytes 393224 | tf_op jit(solution)/shard_map/ppermute | solution.py:18
  65.1 1.9 %collective-permute-done.12 = bf16[512,128]{1,0:T(8,128)(2,1)S(1)} collective-permute-done((bf16[512,128]{1,0:T(8,128)(2,1)S(1)}, bf16[512,128]{1,0:T(8,128)(2,1)S(1)}, u32[]{:S(2)}, u32[]{:S(2)}) %collective-permute-start.12) | collective-permute-done | bytes 131104 | tf_op jit(solution)/shard_map/ppermute | solution.py:18
  67.8 1.4 %collective-permute-start.20 = (bf16[512,128]{1,0:T(8,128)(2,1)S(1)}, bf16[512,128]{1,0:T(8,128)(2,1)S(1)}, u32[]{:S(2)}, u32[]{:S(2)}) collective-permute-start(bf16[512,128]{1,0:T(8,128)(2,1)S(1)} %fusion.50), channel_id=1, source_target_pairs={{0,1},{1,0},{2,3},{3,2},{4,5},{5,4},{6,7},{7,6},{8,9},{9,8},{10,11... | collective-permute-start | bytes 393224 | tf_op jit(solution)/shard_map/ppermute | solution.py:18
  69.9 1.3 %collective-permute-start.22 = (bf16[512,128]{1,0:T(8,128)(2,1)S(1)}, bf16[512,128]{1,0:T(8,128)(2,1)S(1)}, u32[]{:S(2)}, u32[]{:S(2)}) collective-permute-start(bf16[512,128]{1,0:T(8,128)(2,1)S(1)} %fusion.52), channel_id=1, source_target_pairs={{0,1},{1,0},{2,3},{3,2},{4,5},{5,4},{6,7},{7,6},{8,9},{9,8},{10,11... | collective-permute-start | bytes 393224 | tf_op jit(solution)/shard_map/ppermute | solution.py:18
  73.2 1.1 %collective-permute-done.23 = bf16[512,128]{1,0:T(8,128)(2,1)S(1)} collective-permute-done((bf16[512,128]{1,0:T(8,128)(2,1)S(1)}, bf16[512,128]{1,0:T(8,128)(2,1)S(1)}, u32[]{:S(2)}, u32[]{:S(2)}) %collective-permute-start.23) | collective-permute-done | bytes 131104 | tf_op jit(solution)/shard_map/ppermute | solution.py:18
  74.5 1.2 %collective-permute-done.22 = bf16[512,128]{1,0:T(8,128)(2,1)S(1)} collective-permute-done((bf16[512,128]{1,0:T(8,128)(2,1)S(1)}, bf16[512,128]{1,0:T(8,128)(2,1)S(1)}, u32[]{:S(2)}, u32[]{:S(2)}) %collective-permute-start.22) | collective-permute-done | bytes 131104 | tf_op jit(solution)/shard_map/ppermute | solution.py:18
  75.9 1.2 %collective-permute-done.21 = bf16[512,128]{1,0:T(8,128)(2,1)S(1)} collective-permute-done((bf16[512,128]{1,0:T(8,128)(2,1)S(1)}, bf16[512,128]{1,0:T(8,128)(2,1)S(1)}, u32[]{:S(2)}, u32[]{:S(2)}) %collective-permute-start.21) | collective-permute-done | bytes 131104 | tf_op jit(solution)/shard_map/ppermute | solution.py:18
  (97 shorter events, 25.7 us)
Async XLA Ops:
  4.1 9.8 %collective-permute-start.3 = (bf16[512,128]{1,0:T(8,128)(2,1)S(1)}, bf16[512,128]{1,0:T(8,128)(2,1)S(1)}, u32[]{:S(2)}, u32[]{:S(2)}) collective-permute-start(bf16[512,128]{1,0:T(8,128)(2,1)S(1)} %fusion.41), channel_id=1, source_target_pairs={{0,1},{1,0},{2,3},{3,2},{4,5},{5,4},{6,7},{7,6},{8,9},{9,8},{10,11... | collective-permute-start | bytes 393224 | tf_op jit(solution)/shard_map/ppermute | solution.py:18
  9.0 6.5 %collective-permute-start.2 = (bf16[512,128]{1,0:T(8,128)(2,1)S(1)}, bf16[512,128]{1,0:T(8,128)(2,1)S(1)}, u32[]{:S(2)}, u32[]{:S(2)}) collective-permute-start(bf16[512,128]{1,0:T(8,128)(2,1)S(1)} %fusion.40), channel_id=1, source_target_pairs={{0,1},{1,0},{2,3},{3,2},{4,5},{5,4},{6,7},{7,6},{8,9},{9,8},{10,11... | collective-permute-start | bytes 393224 | tf_op jit(solution)/shard_map/ppermute | solution.py:18
  9.8 8.4 %collective-permute-start.1 = (bf16[512,128]{1,0:T(8,128)(2,1)S(1)}, bf16[512,128]{1,0:T(8,128)(2,1)S(1)}, u32[]{:S(2)}, u32[]{:S(2)}) collective-permute-start(bf16[512,128]{1,0:T(8,128)(2,1)S(1)} %fusion.39), channel_id=1, source_target_pairs={{0,1},{1,0},{2,3},{3,2},{4,5},{5,4},{6,7},{7,6},{8,9},{9,8},{10,11... | collective-permute-start | bytes 393224 | tf_op jit(solution)/shard_map/ppermute | solution.py:18
  12.6 7.0 %collective-permute-start = (bf16[512,128]{1,0:T(8,128)(2,1)S(1)}, bf16[512,128]{1,0:T(8,128)(2,1)S(1)}, u32[]{:S(2)}, u32[]{:S(2)}) collective-permute-start(bf16[512,128]{1,0:T(8,128)(2,1)S(1)} %fusion.38), channel_id=1, source_target_pairs={{0,1},{1,0},{2,3},{3,2},{4,5},{5,4},{6,7},{7,6},{8,9},{9,8},{10,11... | collective-permute-start | bytes 393224 | tf_op jit(solution)/shard_map/ppermute | solution.py:18
  20.8 7.7 %collective-permute-start.10 = (bf16[512,128]{1,0:T(8,128)(2,1)S(1)}, bf16[512,128]{1,0:T(8,128)(2,1)S(1)}, u32[]{:S(2)}, u32[]{:S(2)}) collective-permute-start(bf16[512,128]{1,0:T(8,128)(2,1)S(1)} %fusion.45), channel_id=1, source_target_pairs={{0,1},{1,0},{2,3},{3,2},{4,5},{5,4},{6,7},{7,6},{8,9},{9,8},{10,11... | collective-permute-start | bytes 393224 | tf_op jit(solution)/shard_map/ppermute | solution.py:18
  23.0 7.3 %collective-permute-start.4 = (bf16[512,128]{1,0:T(8,128)(2,1)S(1)}, bf16[512,128]{1,0:T(8,128)(2,1)S(1)}, u32[]{:S(2)}, u32[]{:S(2)}) collective-permute-start(bf16[512,128]{1,0:T(8,128)(2,1)S(1)} %fusion.42), channel_id=1, source_target_pairs={{0,1},{1,0},{2,3},{3,2},{4,5},{5,4},{6,7},{7,6},{8,9},{9,8},{10,11... | collective-permute-start | bytes 393224 | tf_op jit(solution)/shard_map/ppermute | solution.py:18
  25.0 9.4 %collective-permute-start.6 = (bf16[512,128]{1,0:T(8,128)(2,1)S(1)}, bf16[512,128]{1,0:T(8,128)(2,1)S(1)}, u32[]{:S(2)}, u32[]{:S(2)}) collective-permute-start(bf16[512,128]{1,0:T(8,128)(2,1)S(1)} %fusion.43), channel_id=1, source_target_pairs={{0,1},{1,0},{2,3},{3,2},{4,5},{5,4},{6,7},{7,6},{8,9},{9,8},{10,11... | collective-permute-start | bytes 393224 | tf_op jit(solution)/shard_map/ppermute | solution.py:18
  27.3 7.0 %collective-permute-start.8 = (bf16[512,128]{1,0:T(8,128)(2,1)S(1)}, bf16[512,128]{1,0:T(8,128)(2,1)S(1)}, u32[]{:S(2)}, u32[]{:S(2)}) collective-permute-start(bf16[512,128]{1,0:T(8,128)(2,1)S(1)} %fusion.44), channel_id=1, source_target_pairs={{0,1},{1,0},{2,3},{3,2},{4,5},{5,4},{6,7},{7,6},{8,9},{9,8},{10,11... | collective-permute-start | bytes 393224 | tf_op jit(solution)/shard_map/ppermute | solution.py:18
  28.6 25.5 %collective-permute-start.19 = (bf16[512,128]{1,0:T(8,128)(2,1)S(1)}, bf16[512,128]{1,0:T(8,128)(2,1)S(1)}, u32[]{:S(2)}, u32[]{:S(2)}) collective-permute-start(bf16[512,128]{1,0:T(8,128)(2,1)S(1)} %get-tuple-element.27), channel_id=1, source_target_pairs={{0,2},{2,4},{4,6},{6,8},{8,10},{10,12},{12,14},{14,16},{16,18},{18... | collective-permute-start | bytes 393224 | tf_op jit(solution)/shard_map/ppermute | solution.py:18
  28.7 15.0 %collective-permute-start.11 = (bf16[512,128]{1,0:T(8,128)(2,1)S(1)}, bf16[512,128]{1,0:T(8,128)(2,1)S(1)}, u32[]{:S(2)}, u32[]{:S(2)}) collective-permute-start(bf16[512,128]{1,0:T(8,128)(2,1)S(1)} %get-tuple-element.28), channel_id=1, source_target_pairs={{0,2},{2,4},{4,6},{6,8},{8,10},{10,12},{12,14},{14,16},{16,18},{18... | collective-permute-start | bytes 393224 | tf_op jit(solution)/shard_map/ppermute | solution.py:18
  30.4 34.6 %collective-permute-start.13 = (bf16[512,128]{1,0:T(8,128)(2,1)S(1)}, bf16[512,128]{1,0:T(8,128)(2,1)S(1)}, u32[]{:S(2)}, u32[]{:S(2)}) collective-permute-start(bf16[512,128]{1,0:T(8,128)(2,1)S(1)} %get-tuple-element.21), channel_id=1, source_target_pairs={{0,2},{2,4},{4,6},{6,8},{8,10},{10,12},{12,14},{14,16},{16,18},{18... | collective-permute-start | bytes 393224 | tf_op jit(solution)/shard_map/ppermute | solution.py:18
  34.2 18.0 %collective-permute-start.5 = (bf16[512,128]{1,0:T(8,128)(2,1)S(1)}, bf16[512,128]{1,0:T(8,128)(2,1)S(1)}, u32[]{:S(2)}, u32[]{:S(2)}) collective-permute-start(bf16[512,128]{1,0:T(8,128)(2,1)S(1)} %get-tuple-element.22), channel_id=1, source_target_pairs={{0,2},{2,4},{4,6},{6,8},{8,10},{10,12},{12,14},{14,16},{16,18},{18... | collective-permute-start | bytes 393224 | tf_op jit(solution)/shard_map/ppermute | solution.py:18
  34.4 8.3 %collective-permute-start.9 = (bf16[512,128]{1,0:T(8,128)(2,1)S(1)}, bf16[512,128]{1,0:T(8,128)(2,1)S(1)}, u32[]{:S(2)}, u32[]{:S(2)}) collective-permute-start(bf16[512,128]{1,0:T(8,128)(2,1)S(1)} %get-tuple-element.26), channel_id=1, source_target_pairs={{0,2},{2,4},{4,6},{6,8},{8,10},{10,12},{12,14},{14,16},{16,18},{18... | collective-permute-start | bytes 393224 | tf_op jit(solution)/shard_map/ppermute | solution.py:18
  42.7 20.4 %collective-permute-start.15 = (bf16[512,128]{1,0:T(8,128)(2,1)S(1)}, bf16[512,128]{1,0:T(8,128)(2,1)S(1)}, u32[]{:S(2)}, u32[]{:S(2)}) collective-permute-start(bf16[512,128]{1,0:T(8,128)(2,1)S(1)} %get-tuple-element.23), channel_id=1, source_target_pairs={{0,2},{2,4},{4,6},{6,8},{8,10},{10,12},{12,14},{14,16},{16,18},{18... | collective-permute-start | bytes 393224 | tf_op jit(solution)/shard_map/ppermute | solution.py:18
  43.7 7.5 %collective-permute-start.7 = (bf16[512,128]{1,0:T(8,128)(2,1)S(1)}, bf16[512,128]{1,0:T(8,128)(2,1)S(1)}, u32[]{:S(2)}, u32[]{:S(2)}) collective-permute-start(bf16[512,128]{1,0:T(8,128)(2,1)S(1)} %get-tuple-element.24), channel_id=1, source_target_pairs={{0,2},{2,4},{4,6},{6,8},{8,10},{10,12},{12,14},{14,16},{16,18},{18... | collective-permute-start | bytes 393224 | tf_op jit(solution)/shard_map/ppermute | solution.py:18
  51.2 9.3 %collective-permute-start.17 = (bf16[512,128]{1,0:T(8,128)(2,1)S(1)}, bf16[512,128]{1,0:T(8,128)(2,1)S(1)}, u32[]{:S(2)}, u32[]{:S(2)}) collective-permute-start(bf16[512,128]{1,0:T(8,128)(2,1)S(1)} %get-tuple-element.25), channel_id=1, source_target_pairs={{0,2},{2,4},{4,6},{6,8},{8,10},{10,12},{12,14},{14,16},{16,18},{18... | collective-permute-start | bytes 393224 | tf_op jit(solution)/shard_map/ppermute | solution.py:18
  52.2 6.4 %collective-permute-start.18 = (bf16[512,128]{1,0:T(8,128)(2,1)S(1)}, bf16[512,128]{1,0:T(8,128)(2,1)S(1)}, u32[]{:S(2)}, u32[]{:S(2)}) collective-permute-start(bf16[512,128]{1,0:T(8,128)(2,1)S(1)} %fusion.49), channel_id=1, source_target_pairs={{0,1},{1,0},{2,3},{3,2},{4,5},{5,4},{6,7},{7,6},{8,9},{9,8},{10,11... | collective-permute-start | bytes 393224 | tf_op jit(solution)/shard_map/ppermute | solution.py:18
  54.2 7.8 %collective-permute-start.16 = (bf16[512,128]{1,0:T(8,128)(2,1)S(1)}, bf16[512,128]{1,0:T(8,128)(2,1)S(1)}, u32[]{:S(2)}, u32[]{:S(2)}) collective-permute-start(bf16[512,128]{1,0:T(8,128)(2,1)S(1)} %fusion.48), channel_id=1, source_target_pairs={{0,1},{1,0},{2,3},{3,2},{4,5},{5,4},{6,7},{7,6},{8,9},{9,8},{10,11... | collective-permute-start | bytes 393224 | tf_op jit(solution)/shard_map/ppermute | solution.py:18
  58.7 5.3 %collective-permute-start.14 = (bf16[512,128]{1,0:T(8,128)(2,1)S(1)}, bf16[512,128]{1,0:T(8,128)(2,1)S(1)}, u32[]{:S(2)}, u32[]{:S(2)}) collective-permute-start(bf16[512,128]{1,0:T(8,128)(2,1)S(1)} %fusion.47), channel_id=1, source_target_pairs={{0,1},{1,0},{2,3},{3,2},{4,5},{5,4},{6,7},{7,6},{8,9},{9,8},{10,11... | collective-permute-start | bytes 393224 | tf_op jit(solution)/shard_map/ppermute | solution.py:18
  60.5 6.4 %collective-permute-start.12 = (bf16[512,128]{1,0:T(8,128)(2,1)S(1)}, bf16[512,128]{1,0:T(8,128)(2,1)S(1)}, u32[]{:S(2)}, u32[]{:S(2)}) collective-permute-start(bf16[512,128]{1,0:T(8,128)(2,1)S(1)} %fusion.46), channel_id=1, source_target_pairs={{0,1},{1,0},{2,3},{3,2},{4,5},{5,4},{6,7},{7,6},{8,9},{9,8},{10,11... | collective-permute-start | bytes 393224 | tf_op jit(solution)/shard_map/ppermute | solution.py:18
  67.8 5.1 %collective-permute-start.20 = (bf16[512,128]{1,0:T(8,128)(2,1)S(1)}, bf16[512,128]{1,0:T(8,128)(2,1)S(1)}, u32[]{:S(2)}, u32[]{:S(2)}) collective-permute-start(bf16[512,128]{1,0:T(8,128)(2,1)S(1)} %fusion.50), channel_id=1, source_target_pairs={{0,1},{1,0},{2,3},{3,2},{4,5},{5,4},{6,7},{7,6},{8,9},{9,8},{10,11... | collective-permute-start | bytes 393224 | tf_op jit(solution)/shard_map/ppermute | solution.py:18
  69.2 5.1 %collective-permute-start.23 = (bf16[512,128]{1,0:T(8,128)(2,1)S(1)}, bf16[512,128]{1,0:T(8,128)(2,1)S(1)}, u32[]{:S(2)}, u32[]{:S(2)}) collective-permute-start(bf16[512,128]{1,0:T(8,128)(2,1)S(1)} %fusion.53), channel_id=1, source_target_pairs={{0,1},{1,0},{2,3},{3,2},{4,5},{5,4},{6,7},{7,6},{8,9},{9,8},{10,11... | collective-permute-start | bytes 393224 | tf_op jit(solution)/shard_map/ppermute | solution.py:18
  69.9 5.8 %collective-permute-start.22 = (bf16[512,128]{1,0:T(8,128)(2,1)S(1)}, bf16[512,128]{1,0:T(8,128)(2,1)S(1)}, u32[]{:S(2)}, u32[]{:S(2)}) collective-permute-start(bf16[512,128]{1,0:T(8,128)(2,1)S(1)} %fusion.52), channel_id=1, source_target_pairs={{0,1},{1,0},{2,3},{3,2},{4,5},{5,4},{6,7},{7,6},{8,9},{9,8},{10,11... | collective-permute-start | bytes 393224 | tf_op jit(solution)/shard_map/ppermute | solution.py:18
  71.2 5.8 %collective-permute-start.21 = (bf16[512,128]{1,0:T(8,128)(2,1)S(1)}, bf16[512,128]{1,0:T(8,128)(2,1)S(1)}, u32[]{:S(2)}, u32[]{:S(2)}) collective-permute-start(bf16[512,128]{1,0:T(8,128)(2,1)S(1)} %fusion.51), channel_id=1, source_target_pairs={{0,1},{1,0},{2,3},{3,2},{4,5},{5,4},{6,7},{7,6},{8,9},{9,8},{10,11... | collective-permute-start | bytes 393224 | tf_op jit(solution)/shard_map/ppermute | solution.py:18
  (5 other events, 39.4 us)

commit v2 on v0

v2 whole, which is shorter than its diff:
```python
import jax
import jax.numpy as jnp
from jax import lax
from jax.sharding import PartitionSpec as P

SUB = 2
INNER = 2
CHUNKS = 2


shrink = 0.05
learn_rate = 0.2
tiny_eps = 1e-06


def moved(shard, loop_by, grp_by):
    loops, groups = lax.axis_size("loop"), lax.axis_size("grp")
    pairs = [
        (w * groups + g, (w + loop_by) % loops * groups + (g + grp_by) % groups)
        for w in range(loops)
        for g in range(groups)
    ]
    return lax.ppermute(shard, ("loop", "grp"), pairs)


def adagrad(param, accum, grad):
    accum = accum + grad * grad
    return (param - learn_rate * grad * lax.rsqrt(accum + tiny_eps), accum)


def group_terms(term, loop_by):
    if lax.axis_size("grp") == 2:
        own = moved(term, loop_by, 0) if loop_by else term
        return (own, moved(term, loop_by, 1))
    total = lax.psum(term, "grp")
    return (moved(total, loop_by, 0) if loop_by else total,)


def item_step(items, item_acc, terms):
    items, item_acc, terms = lax.optimization_barrier((items, item_acc, terms))
    grad = sum(term.astype(jnp.float32) for term in terms) + shrink * items.astype(jnp.float32)
    return adagrad(items.astype(jnp.float32), item_acc.astype(jnp.float32), grad)


def local(ratings, user_factors, user_accum, item_factors, item_accum):
    users = user_factors
    user_acc = user_accum
    size = item_factors.shape[0] // CHUNKS
    rows = [slice(c * size, (c + 1) * size) for c in range(CHUNKS)]
    items = [item_factors[r] for r in rows]
    item_acc = [item_accum[r] for r in rows]
    terms = [None] * CHUNKS
    for step in range(SUB * INNER):
        sub_epoch = step // INNER
        last_inner = step % INNER == INNER - 1
        rotates = sub_epoch < SUB - 1
        user_half = users.astype(jnp.bfloat16)
        grad_user = shrink * users
        sent = [None] * CHUNKS
        for c in range(CHUNKS):
            if terms[c] is not None:
                items[c], item_acc[c] = item_step(items[c], item_acc[c], terms[c])
            if rotates and last_inner:
                both = jnp.concatenate((items[c], item_acc[c]), axis=0).astype(jnp.bfloat16)
                sent[c] = moved(both, 1, 0)
            rate = ratings[sub_epoch, :, rows[c]].astype(jnp.float32)
            item_half = items[c].astype(jnp.bfloat16)
            predicted = lax.dot_general(
                user_half, item_half, (((1,), (1,)), ((), ())), preferred_element_type=jnp.float32
            )
            resid = jnp.where(jnp.abs(rate) > 0.25, rate - predicted, 0.0).astype(jnp.bfloat16)
            term = -lax.dot_general(
                resid, user_half, (((0,), (0,)), ((), ())), preferred_element_type=jnp.float32
            )
            terms[c] = group_terms(term.astype(jnp.bfloat16), 1 if rotates and last_inner else 0)
            grad_user = grad_user - jnp.dot(resid, item_half, preferred_element_type=jnp.float32)
        users, user_acc = adagrad(users, user_acc, grad_user)
        if rotates and last_inner:
            items = [both[:size] for both in sent]
            item_acc = [both[size:] for both in sent]
    for c in range(CHUNKS):
        items[c], _ = item_step(items[c], item_acc[c], terms[c])
    return (users, jnp.concatenate(items, axis=0))


def solution(mesh):
    in_specs = (
        P(None, ("loop", "grp"), None),
        P(("loop", "grp"), None),
        P(("loop", "grp"), None),
        P("loop", None),
        P("loop", None),
    )
    out_specs = (P(("loop", "grp"), None), P("loop", None))
    return jax.shard_map(local, mesh=mesh, in_specs=in_specs, out_specs=out_specs, check_vma=False)
```

time: 171 us -> 79.6 us (0.47)
  the two profiles are of different devices: /device:TPU:0 before, /device:TPU:8 now
where the time goes in v2:
time: 79.6 us; the launch traced here: 79.4 us
  waiting for transfers between devices  47.2 us (59%)
  matrix products  14.3 us (18%)
  starting transfers between devices  12 us (15%)
  other arithmetic  3.92 us (5%)
  local copies, waits for them, and re-layouts  1.03 us (1%)
  between operations  0.92 us (1%)
    ppermute x12, waiting for transfers between devices, moved(): return lax.ppermute(shard, ('loop', 'grp'), pairs)  47.2 us
    ppermute x12, starting transfers between devices, moved(): return lax.ppermute(shard, ('loop', 'grp'), pairs)  12 us
    dot_general x8, matrix products, local(): lax.dot_general(user_half, item_half, (((1,), (1,)), ((), ())), preferred...  6.12 us
    dot_general x8, matrix products, local(): jnp.dot(resid, item_half, preferred_element_type=jnp.float32)  4.28 us
    dot_general x8, matrix products, local(): lax.dot_general(resid, user_half, (((0,), (0,)), ((), ())), preferred_ele...  3.92 us
  transfers between devices with their start and end apart: 12, of which 8 were waited for; matrix products, arithmetic and copies ran while one was open for 13% of the time, Pallas kernels for 0%

profile of v2, /device:TPU:8, one launch (start us, length us, event | category | flops | bytes accessed | tf_op | source)
XLA Modules:
  0.0 79.4 jit_solution(5690539449906703134)
XLA Ops:
  0.6 1.0 %convert_element_type.178 = bf16[512,128]{1,0:T(8,128)(2,1)S(1)} convert(f32[512,128]{1,0:T(8,128)} %param.6) | non-fusion elementwise | flops 65536 | bytes 393216 | tf_op jit(solution)/shard_map/convert_element_type | solution.py:57
  1.6 2.1 %fusion.7 = bf16[512,1024]{1,0:T(8,128)(2,1)S(1)} fusion(bf16[512,128]{1,0:T(8,128)(2,1)S(1)} %convert_element_type.178, bf16[2,512,2048]{2,1,0:T(8,128)(2,1)} %param.5, f32[2048,128]{1,0:T(8,128)} %param.8), kind=kOutput, calls=%fused_computation.19 | convolution fusion | flops 137363456 | bytes 2490368 | tf_op jit(solution)/shard_map/dot_general | solution.py:68
  4.2 1.6 %collective-permute-start.1 = (bf16[1024,128]{1,0:T(8,128)(2,1)S(1)}, bf16[1024,128]{1,0:T(8,128)(2,1)S(1)}, u32[]{:S(2)}, u32[]{:S(2)}) collective-permute-start(bf16[1024,128]{1,0:T(8,128)(2,1)S(1)} %fusion.21), channel_id=1, source_target_pairs={{0,1},{1,0},{2,3},{3,2},{4,5},{5,4},{6,7},{7,6},{8,9},{9,8},{10,11... | collective-permute-start | bytes 786440 | tf_op jit(solution)/shard_map/ppermute | solution.py:23
  5.8 0.6 fusion.2
  6.9 0.6 collective-permute-start
  8.1 0.8 %copy-done.2 = f32[512,128]{1,0:T(8,128)S(1)} copy-done((f32[512,128]{1,0:T(8,128)S(1)}, f32[512,128]{1,0:T(8,128)}, u32[]{:S(2)}) %copy-start.2) | copy-done | bytes 262168
  9.4 8.6 %collective-permute-done = bf16[1024,128]{1,0:T(8,128)(2,1)S(1)} collective-permute-done((bf16[1024,128]{1,0:T(8,128)(2,1)S(1)}, bf16[1024,128]{1,0:T(8,128)(2,1)S(1)}, u32[]{:S(2)}, u32[]{:S(2)}) %collective-permute-start) | collective-permute-done | bytes 262176 | tf_op jit(solution)/shard_map/ppermute | solution.py:23
  19.4 2.5 %collective-permute-start.3 = (bf16[1024,128]{1,0:T(8,128)(2,1)S(1)}, bf16[1024,128]{1,0:T(8,128)(2,1)S(1)}, u32[]{:S(2)}, u32[]{:S(2)}) collective-permute-start(bf16[1024,128]{1,0:T(8,128)(2,1)S(1)} %fusion.22), channel_id=1, source_target_pairs={{0,2},{1,3},{2,4},{3,5},{4,6},{5,7},{6,8},{7,9},{8,10},{9,11},{10,... | collective-permute-start | bytes 786440 | tf_op jit(solution)/shard_map/ppermute | solution.py:23
  22.9 1.6 %collective-permute-start.2 = (bf16[2048,128]{1,0:T(8,128)(2,1)S(1)}, bf16[2048,128]{1,0:T(8,128)(2,1)S(1)}, u32[]{:S(2)}, u32[]{:S(2)}) collective-permute-start(bf16[2048,128]{1,0:T(8,128)(2,1)S(1)} %pad_maximum_fusion.1), channel_id=1, source_target_pairs={{0,2},{1,3},{2,4},{3,5},{4,6},{5,7},{6,8},{7,9},{8,10},{9,11},{10,... | collective-permute-start | bytes 1572872 | tf_op jit(solution)/shard_map/ppermute | solution.py:23
  26.2 14.9 %collective-permute-done.2 = bf16[2048,128]{1,0:T(8,128)(2,1)S(1)} collective-permute-done((bf16[2048,128]{1,0:T(8,128)(2,1)S(1)}, bf16[2048,128]{1,0:T(8,128)(2,1)S(1)}, u32[]{:S(2)}, u32[]{:S(2)}) %collective-permute-start.2) | collective-permute-done | bytes 524320 | tf_op jit(solution)/shard_map/ppermute | solution.py:23
  41.1 1.0 %collective-permute-start.6 = (bf16[1024,128]{1,0:T(8,128)(2,1)S(1)}, bf16[1024,128]{1,0:T(8,128)(2,1)S(1)}, u32[]{:S(2)}, u32[]{:S(2)}) collective-permute-start(bf16[1024,128]{1,0:T(8,128)(2,1)S(1)} %fusion.23), channel_id=1, source_target_pairs={{0,2},{1,3},{2,4},{3,5},{4,6},{5,7},{6,8},{7,9},{8,10},{9,11},{10,... | collective-permute-start | bytes 786440 | tf_op jit(solution)/shard_map/ppermute | solution.py:23
  42.2 2.6 %collective-permute-done.7 = bf16[1024,128]{1,0:T(8,128)(2,1)S(1)} collective-permute-done((bf16[1024,128]{1,0:T(8,128)(2,1)S(1)}, bf16[1024,128]{1,0:T(8,128)(2,1)S(1)}, u32[]{:S(2)}, u32[]{:S(2)}) %collective-permute-start.7) | collective-permute-done | bytes 262176 | tf_op jit(solution)/shard_map/ppermute | solution.py:23
  44.8 3.0 %collective-permute-done.6 = bf16[1024,128]{1,0:T(8,128)(2,1)S(1)} collective-permute-done((bf16[1024,128]{1,0:T(8,128)(2,1)S(1)}, bf16[1024,128]{1,0:T(8,128)(2,1)S(1)}, u32[]{:S(2)}, u32[]{:S(2)}) %collective-permute-start.6) | collective-permute-done | bytes 262176 | tf_op jit(solution)/shard_map/ppermute | solution.py:23
  49.1 1.6 %collective-permute-start.9 = (bf16[1024,128]{1,0:T(8,128)(2,1)S(1)}, bf16[1024,128]{1,0:T(8,128)(2,1)S(1)}, u32[]{:S(2)}, u32[]{:S(2)}) collective-permute-start(bf16[1024,128]{1,0:T(8,128)(2,1)S(1)} %fusion.25), channel_id=1, source_target_pairs={{0,1},{1,0},{2,3},{3,2},{4,5},{5,4},{6,7},{7,6},{8,9},{9,8},{10,11... | collective-permute-start | bytes 786440 | tf_op jit(solution)/shard_map/ppermute | solution.py:23
  52.4 0.6 collective-permute-start.8
  53.5 4.8 %collective-permute-done.9 = bf16[1024,128]{1,0:T(8,128)(2,1)S(1)} collective-permute-done((bf16[1024,128]{1,0:T(8,128)(2,1)S(1)}, bf16[1024,128]{1,0:T(8,128)(2,1)S(1)}, u32[]{:S(2)}, u32[]{:S(2)}) %collective-permute-start.9) | collective-permute-done | bytes 262176 | tf_op jit(solution)/shard_map/ppermute | solution.py:23
  58.3 4.7 %collective-permute-done.8 = bf16[1024,128]{1,0:T(8,128)(2,1)S(1)} collective-permute-done((bf16[1024,128]{1,0:T(8,128)(2,1)S(1)}, bf16[1024,128]{1,0:T(8,128)(2,1)S(1)}, u32[]{:S(2)}, u32[]{:S(2)}) %collective-permute-start.8) | collective-permute-done | bytes 262176 | tf_op jit(solution)/shard_map/ppermute | solution.py:23
  63.3 0.6 fusion.14
  64.8 0.7 collective-permute-start.10
  66.8 1.4 %collective-permute-start.11 = (bf16[1024,128]{1,0:T(8,128)(2,1)S(1)}, bf16[1024,128]{1,0:T(8,128)(2,1)S(1)}, u32[]{:S(2)}, u32[]{:S(2)}) collective-permute-start(bf16[1024,128]{1,0:T(8,128)(2,1)S(1)} %fusion.27), channel_id=1, source_target_pairs={{0,1},{1,0},{2,3},{3,2},{4,5},{5,4},{6,7},{7,6},{8,9},{9,8},{10,11... | collective-permute-start | bytes 786440 | tf_op jit(solution)/shard_map/ppermute | solution.py:23
  68.3 1.2 %multiply_subtract_fusion.4 = f32[512,128]{1,0:T(8,128)} fusion(f32[512,128]{1,0:T(8,128)S(1)} %convolution_subtract_fusion.1, bf16[512,1024]{1,0:T(8,128)(2,1)S(1)} %fusion.19, f32[1024,128]{1,0:T(8,128)S(1)} %get-tuple-element.62, f32[512,128]{1,0:T(8,128)S(1)} %get-tuple-element.68, f32[512,128]{1,0:T(8,128)S(1)} %get-tuple-element.93, ...), kind=kOutput, calls=%fused_computation.83 | convolution fusion | flops 135200768 | bytes 2883584 | tf_op jit(solution)/shard_map/dot_general | solution.py:76
  69.4 4.7 %collective-permute-done.10 = bf16[1024,128]{1,0:T(8,128)(2,1)S(1)} collective-permute-done((bf16[1024,128]{1,0:T(8,128)(2,1)S(1)}, bf16[1024,128]{1,0:T(8,128)(2,1)S(1)}, u32[]{:S(2)}, u32[]{:S(2)}) %collective-permute-start.10) | collective-permute-done | bytes 262176 | tf_op jit(solution)/shard_map/ppermute | solution.py:23
  74.1 3.8 %collective-permute-done.11 = bf16[1024,128]{1,0:T(8,128)(2,1)S(1)} collective-permute-done((bf16[1024,128]{1,0:T(8,128)(2,1)S(1)}, bf16[1024,128]{1,0:T(8,128)(2,1)S(1)}, u32[]{:S(2)}, u32[]{:S(2)}) %collective-permute-start.11) | collective-permute-done | bytes 262176 | tf_op jit(solution)/shard_map/ppermute | solution.py:23
  78.4 1.0 %pad_maximum_fusion = f32[2048,128]{1,0:T(8,128)} fusion(f32[1024,128]{1,0:T(8,128)S(1)} %multiply_subtract_fusion, f32[1024,128]{1,0:T(8,128)S(1)} %multiply_subtract_fusion.1), kind=kLoop, calls=%fused_computation.56 | loop fusion | flops 262144 | bytes 2097152 | tf_op jit(solution)/shard_map/concatenate | solution.py:83
  (49 shorter events, 12.5 us)
Async XLA Ops:
  1.6 4.2 %copy-start = (f32[2048,128]{1,0:T(8,128)S(1)}, f32[2048,128]{1,0:T(8,128)}, u32[]{:S(2)}) copy-start(f32[2048,128]{1,0:T(8,128)} %param.8) | copy-start | bytes 3145732
  1.6 4.2 %copy-start.4 = (bf16[2,512,2048]{2,1,0:T(8,128)(2,1)S(1)}, bf16[2,512,2048]{2,1,0:T(8,128)(2,1)}, u32[]{:S(2)}) copy-start(bf16[2,512,2048]{2,1,0:T(8,128)(2,1)} %param.5) | copy-start | bytes 12582916
  4.2 3.3 %copy-start.1 = (f32[512,128]{1,0:T(8,128)S(1)}, f32[512,128]{1,0:T(8,128)}, u32[]{:S(2)}) copy-start(f32[512,128]{1,0:T(8,128)} %param.6) | copy-start | bytes 786436
  4.2 17.7 %collective-permute-start.1 = (bf16[1024,128]{1,0:T(8,128)(2,1)S(1)}, bf16[1024,128]{1,0:T(8,128)(2,1)S(1)}, u32[]{:S(2)}, u32[]{:S(2)}) collective-permute-start(bf16[1024,128]{1,0:T(8,128)(2,1)S(1)} %fusion.21), channel_id=1, source_target_pairs={{0,1},{1,0},{2,3},{3,2},{4,5},{5,4},{6,7},{7,6},{8,9},{9,8},{10,11... | collective-permute-start | bytes 786440 | tf_op jit(solution)/shard_map/ppermute | solution.py:23
  6.4 1.6 %copy-start.3 = (f32[2048,128]{1,0:T(8,128)S(1)}, f32[2048,128]{1,0:T(8,128)}, u32[]{:S(2)}) copy-start(f32[2048,128]{1,0:T(8,128)} %param.9) | copy-start | bytes 3145732
  6.9 11.1 %collective-permute-start = (bf16[1024,128]{1,0:T(8,128)(2,1)S(1)}, bf16[1024,128]{1,0:T(8,128)(2,1)S(1)}, u32[]{:S(2)}, u32[]{:S(2)}) collective-permute-start(bf16[1024,128]{1,0:T(8,128)(2,1)S(1)} %fusion.20), channel_id=1, source_target_pairs={{0,1},{1,0},{2,3},{3,2},{4,5},{5,4},{6,7},{7,6},{8,9},{9,8},{10,11... | collective-permute-start | bytes 786440 | tf_op jit(solution)/shard_map/ppermute | solution.py:23
  7.9 1.0 %copy-start.2 = (f32[512,128]{1,0:T(8,128)S(1)}, f32[512,128]{1,0:T(8,128)}, u32[]{:S(2)}) copy-start(f32[512,128]{1,0:T(8,128)} %param.7) | copy-start | bytes 786436
  19.3 22.8 %collective-permute-start.4 = (bf16[1024,128]{1,0:T(8,128)(2,1)S(1)}, bf16[1024,128]{1,0:T(8,128)(2,1)S(1)}, u32[]{:S(2)}, u32[]{:S(2)}) collective-permute-start(bf16[1024,128]{1,0:T(8,128)(2,1)S(1)} %fusion.22), channel_id=1, source_target_pairs={{0,3},{1,2},{2,5},{3,4},{4,7},{5,6},{6,9},{7,8},{8,11},{9,10},{10,... | collective-permute-start | bytes 786440 | tf_op jit(solution)/shard_map/ppermute | solution.py:23
  19.4 22.7 %collective-permute-start.3 = (bf16[1024,128]{1,0:T(8,128)(2,1)S(1)}, bf16[1024,128]{1,0:T(8,128)(2,1)S(1)}, u32[]{:S(2)}, u32[]{:S(2)}) collective-permute-start(bf16[1024,128]{1,0:T(8,128)(2,1)S(1)} %fusion.22), channel_id=1, source_target_pairs={{0,2},{1,3},{2,4},{3,5},{4,6},{5,7},{6,8},{7,9},{8,10},{9,11},{10,... | collective-permute-start | bytes 786440 | tf_op jit(solution)/shard_map/ppermute | solution.py:23
  22.8 19.3 %collective-permute-start.5 = (bf16[2048,128]{1,0:T(8,128)(2,1)S(1)}, bf16[2048,128]{1,0:T(8,128)(2,1)S(1)}, u32[]{:S(2)}, u32[]{:S(2)}) collective-permute-start(bf16[2048,128]{1,0:T(8,128)(2,1)S(1)} %pad_maximum_fusion.2), channel_id=1, source_target_pairs={{0,2},{1,3},{2,4},{3,5},{4,6},{5,7},{6,8},{7,9},{8,10},{9,11},{10,... | collective-permute-start | bytes 1572872 | tf_op jit(solution)/shard_map/ppermute | solution.py:23
  22.9 18.2 %collective-permute-start.2 = (bf16[2048,128]{1,0:T(8,128)(2,1)S(1)}, bf16[2048,128]{1,0:T(8,128)(2,1)S(1)}, u32[]{:S(2)}, u32[]{:S(2)}) collective-permute-start(bf16[2048,128]{1,0:T(8,128)(2,1)S(1)} %pad_maximum_fusion.1), channel_id=1, source_target_pairs={{0,2},{1,3},{2,4},{3,5},{4,6},{5,7},{6,8},{7,9},{8,10},{9,11},{10,... | collective-permute-start | bytes 1572872 | tf_op jit(solution)/shard_map/ppermute | solution.py:23
  25.0 19.8 %collective-permute-start.7 = (bf16[1024,128]{1,0:T(8,128)(2,1)S(1)}, bf16[1024,128]{1,0:T(8,128)(2,1)S(1)}, u32[]{:S(2)}, u32[]{:S(2)}) collective-permute-start(bf16[1024,128]{1,0:T(8,128)(2,1)S(1)} %fusion.23), channel_id=1, source_target_pairs={{0,3},{1,2},{2,5},{3,4},{4,7},{5,6},{6,9},{7,8},{8,11},{9,10},{10,... | collective-permute-start | bytes 786440 | tf_op jit(solution)/shard_map/ppermute | solution.py:23
  41.1 6.7 %collective-permute-start.6 = (bf16[1024,128]{1,0:T(8,128)(2,1)S(1)}, bf16[1024,128]{1,0:T(8,128)(2,1)S(1)}, u32[]{:S(2)}, u32[]{:S(2)}) collective-permute-start(bf16[1024,128]{1,0:T(8,128)(2,1)S(1)} %fusion.23), channel_id=1, source_target_pairs={{0,2},{1,3},{2,4},{3,5},{4,6},{5,7},{6,8},{7,9},{8,10},{9,11},{10,... | collective-permute-start | bytes 786440 | tf_op jit(solution)/shard_map/ppermute | solution.py:23
  49.1 9.2 %collective-permute-start.9 = (bf16[1024,128]{1,0:T(8,128)(2,1)S(1)}, bf16[1024,128]{1,0:T(8,128)(2,1)S(1)}, u32[]{:S(2)}, u32[]{:S(2)}) collective-permute-start(bf16[1024,128]{1,0:T(8,128)(2,1)S(1)} %fusion.25), channel_id=1, source_target_pairs={{0,1},{1,0},{2,3},{3,2},{4,5},{5,4},{6,7},{7,6},{8,9},{9,8},{10,11... | collective-permute-start | bytes 786440 | tf_op jit(solution)/shard_map/ppermute | solution.py:23
  52.4 10.6 %collective-permute-start.8 = (bf16[1024,128]{1,0:T(8,128)(2,1)S(1)}, bf16[1024,128]{1,0:T(8,128)(2,1)S(1)}, u32[]{:S(2)}, u32[]{:S(2)}) collective-permute-start(bf16[1024,128]{1,0:T(8,128)(2,1)S(1)} %fusion.24), channel_id=1, source_target_pairs={{0,1},{1,0},{2,3},{3,2},{4,5},{5,4},{6,7},{7,6},{8,9},{9,8},{10,11... | collective-permute-start | bytes 786440 | tf_op jit(solution)/shard_map/ppermute | solution.py:23
  64.8 9.3 %collective-permute-start.10 = (bf16[1024,128]{1,0:T(8,128)(2,1)S(1)}, bf16[1024,128]{1,0:T(8,128)(2,1)S(1)}, u32[]{:S(2)}, u32[]{:S(2)}) collective-permute-start(bf16[1024,128]{1,0:T(8,128)(2,1)S(1)} %fusion.26), channel_id=1, source_target_pairs={{0,1},{1,0},{2,3},{3,2},{4,5},{5,4},{6,7},{7,6},{8,9},{9,8},{10,11... | collective-permute-start | bytes 786440 | tf_op jit(solution)/shard_map/ppermute | solution.py:23
  66.8 11.1 %collective-permute-start.11 = (bf16[1024,128]{1,0:T(8,128)(2,1)S(1)}, bf16[1024,128]{1,0:T(8,128)(2,1)S(1)}, u32[]{:S(2)}, u32[]{:S(2)}) collective-permute-start(bf16[1024,128]{1,0:T(8,128)(2,1)S(1)} %fusion.27), channel_id=1, source_target_pairs={{0,1},{1,0},{2,3},{3,2},{4,5},{5,4},{6,7},{7,6},{8,9},{9,8},{10,11... | collective-permute-start | bytes 786440 | tf_op jit(solution)/shard_map/ppermute | solution.py:23

commit v3 on v2

v3 whole, which is shorter than its diff:
```python
import functools

import jax
import jax.numpy as jnp
from jax import lax
from jax.experimental import pallas as pl
from jax.experimental.pallas import tpu as pltpu
from jax.sharding import PartitionSpec as P

SUB = 2
INNER = 2
CHUNKS = 2
TILE = 256


shrink = 0.05
learn_rate = 0.2
tiny_eps = 1e-06


def moved(shard, loop_by, grp_by):
    loops, groups = lax.axis_size("loop"), lax.axis_size("grp")
    pairs = [
        (w * groups + g, (w + loop_by) % loops * groups + (g + grp_by) % groups)
        for w in range(loops)
        for g in range(groups)
    ]
    return lax.ppermute(shard, ("loop", "grp"), pairs)


def adagrad(param, accum, grad):
    accum = accum + grad * grad
    return (param - learn_rate * grad * lax.rsqrt(accum + tiny_eps), accum)


def group_terms(term):
    if lax.axis_size("grp") == 2:
        return (term, moved(term, 0, 1))
    return (lax.psum(term, "grp"),)


def item_step(items, accum, terms):
    items = items.astype(jnp.float32)
    grad = sum(term.astype(jnp.float32) for term in terms) + shrink * items
    return adagrad(items, accum.astype(jnp.float32), grad)


def chunk_kernel(n_terms, sub_epoch, column, offset, rate_ref, half_ref, grad_ref, items_ref, *refs):
    if n_terms:
        accum_ref, *refs = refs
    term_refs, (term_out, grad_out, *updated) = refs[:n_terms], refs[n_terms:]
    half = half_ref[...]
    grad = grad_ref[...]
    for start in range(0, term_out.shape[0], TILE):
        at = pl.ds(start, TILE)
        held = pl.ds(offset + start, TILE)
        items = items_ref[held, :]
        if n_terms:
            items, accum = item_step(items, accum_ref[held, :], [ref[at, :] for ref in term_refs])
            updated[0][at, :] = items
            updated[1][at, :] = accum
        item_half = items.astype(jnp.bfloat16)
        predicted = lax.dot_general(
            half, item_half, (((1,), (1,)), ((), ())), preferred_element_type=jnp.float32
        )
        rate = rate_ref[sub_epoch, :, pl.ds(column + start, TILE)].astype(jnp.float32)
        resid = jnp.where(jnp.abs(rate) > 0.25, rate - predicted, 0.0).astype(jnp.bfloat16)
        term = lax.dot_general(
            resid, half, (((0,), (0,)), ((), ())), preferred_element_type=jnp.float32
        )
        term_out[at, :] = (-term).astype(jnp.bfloat16)
        grad = grad - jnp.dot(resid, item_half, preferred_element_type=jnp.float32)
    grad_out[...] = grad


def chunk_pass(ratings, sub_epoch, rows, half, grad, items, accum, terms):
    size, rank = rows.stop - rows.start, items.shape[1]
    offset = 0 if items.shape[0] == size else rows.start
    whole = pl.BlockSpec(memory_space=pltpu.VMEM)
    out_shape = [
        jax.ShapeDtypeStruct((size, rank), jnp.bfloat16),
        jax.ShapeDtypeStruct(grad.shape, jnp.float32),
    ]
    operands = [ratings, half, grad, items]
    if terms:
        out_shape += [jax.ShapeDtypeStruct((size, rank), jnp.float32)] * 2
        operands += [accum, *terms]
    return pl.pallas_call(
        functools.partial(chunk_kernel, len(terms), sub_epoch, rows.start, offset),
        out_shape=out_shape,
        in_specs=[whole] * len(operands),
        out_specs=[whole] * len(out_shape),
        compiler_params=pltpu.CompilerParams(vmem_limit_bytes=16 * 2**20),
        cost_estimate=pl.CostEstimate(
            flops=6 * half.shape[0] * size * rank, bytes_accessed=2 * half.shape[0] * size, transcendentals=0
        ),
    )(*operands)


def last_kernel(n_terms, items_ref, accum_ref, *refs):
    items, _ = item_step(items_ref[...], accum_ref[...], [ref[...] for ref in refs[:n_terms]])
    refs[-1][...] = items


def last_item_step(rows, n_items, items, accum, terms, filled):
    size, rank = items.shape
    block = pl.BlockSpec((TILE, rank), lambda i: (i, 0))
    first = rows.start // TILE
    held = [] if filled is None else [filled]
    return pl.pallas_call(
        functools.partial(last_kernel, len(terms)),
        grid=(size // TILE,),
        out_shape=jax.ShapeDtypeStruct((n_items, rank), jnp.float32),
        in_specs=[block] * (2 + len(terms)) + [pl.BlockSpec(memory_space=pl.ANY)] * len(held),
        out_specs=pl.BlockSpec((TILE, rank), lambda i: (first + i, 0)),
        input_output_aliases={2 + len(terms): 0} if held else {},
        compiler_params=pltpu.CompilerParams(vmem_limit_bytes=16 * 2**20),
        cost_estimate=pl.CostEstimate(flops=10 * size * rank, bytes_accessed=16 * size * rank, transcendentals=0),
    )(items, accum, *terms, *held)


def local(ratings, user_factors, user_accum, item_factors, item_accum):
    users = user_factors
    user_acc = user_accum
    size = item_factors.shape[0] // CHUNKS
    rows = [slice(c * size, (c + 1) * size) for c in range(CHUNKS)]
    items = [item_factors] * CHUNKS
    item_acc = [item_accum] * CHUNKS
    terms = [()] * CHUNKS
    for step in range(SUB * INNER):
        sub_epoch = step // INNER
        if step > 0 and step % INNER == 0:
            for c in range(CHUNKS):
                stepped, accum = item_step(items[c], item_acc[c], terms[c])
                items[c] = moved(stepped.astype(jnp.bfloat16), 1, 0)
                item_acc[c] = moved(accum.astype(jnp.bfloat16), 1, 0)
                terms[c] = ()
        user_half = users.astype(jnp.bfloat16)
        grad_user = shrink * users
        for c in range(CHUNKS):
            term, grad_user, *updated = chunk_pass(
                ratings, sub_epoch, rows[c], user_half, grad_user, items[c], item_acc[c], terms[c]
            )
            if updated:
                items[c], item_acc[c] = updated
            terms[c] = group_terms(term)
        users, user_acc = adagrad(users, user_acc, grad_user)
    filled = None
    for c in range(CHUNKS):
        filled = last_item_step(rows[c], item_factors.shape[0], items[c], item_acc[c], terms[c], filled)
    return (users, filled)


def solution(mesh):
    in_specs = (
        P(None, ("loop", "grp"), None),
        P(("loop", "grp"), None),
        P(("loop", "grp"), None),
        P("loop", None),
        P("loop", None),
    )
    out_specs = (P(("loop", "grp"), None), P("loop", None))
    return jax.shard_map(local, mesh=mesh, in_specs=in_specs, out_specs=out_specs, check_vma=False)
```

time: 79.6 us -> 70.7 us (0.89)
  the two profiles are of different devices: /device:TPU:8 before, /device:TPU:0 now
where the time goes in v3:
time: 70.7 us; the launch traced here: 70.5 us
  waiting for transfers between devices  35.7 us (50%)
  Pallas kernels  15.5 us (22%)
  starting transfers between devices  12.4 us (18%)
  local copies, waits for them, and re-layouts  3.43 us (5%)
  other arithmetic  2.68 us (4%)
  between operations  0.76 us (1%)
    ppermute x12, waiting for transfers between devices, moved(): return lax.ppermute(shard, ('loop', 'grp'), pairs)  35.7 us
    pallas_call x8, Pallas kernels, chunk_pass(): pl.pallas_call(functools.partial(chunk_kernel, len(terms), sub_epoch, row...  12.5 us
    ppermute x12, starting transfers between devices, moved(): return lax.ppermute(shard, ('loop', 'grp'), pairs)  12.4 us
    unnamed x12, local copies, waits for them, and re-layouts  3.43 us
    pallas_call x2, Pallas kernels, last_item_step(): pl.pallas_call(functools.partial(last_kernel, len(terms)), grid=(size //...  3 us
  transfers between devices with their start and end apart: 12, of which 9 were waited for; matrix products, arithmetic and copies ran while one was open for 2% of the time, Pallas kernels for 15%

profile of v3, /device:TPU:0, one launch (start us, length us, event | category | flops | bytes accessed | tf_op | source)
XLA Modules:
  0.0 70.5 jit_solution(17805057495701046092)
XLA Ops:
  1.7 2.2 %copy-done = bf16[2,512,2048]{2,1,0:T(8,128)(2,1)S(1)} copy-done((bf16[2,512,2048]{2,1,0:T(8,128)(2,1)S(1)}, bf16[2,512,2048]{2,1,0:T(8,128)(2,1)}, u32[]{:S(2)}) %copy-start) | copy-done | bytes 4194328
  5.1 1.5 %shard_map.68 = (bf16[1024,128]{1,0:T(8,128)(2,1)S(1)}, f32[512,128]{1,0:T(8,128)S(1)}) custom-call(bf16[2,512,2048]{2,1,0:T(8,128)(2,1)S(1)} %copy-done, bf16[512,128]{1,0:T(8,128)(2,1)S(1)} %get-tuple-element.62.half_ref, f32[512,128]{1,0:T(8,128)S(1)} %get-tuple-element.61.grad_ref, f32[2048,128]{1,0:T(8,128)S(1)} %copy-done.1), custom_call_target="tpu_custom_call" | custom-call | flops 402653184 | bytes 1048576 | tf_op jit(solution)/shard_map/pallas_call | solution.py:88
  6.7 3.0 %collective-permute-start = (bf16[1024,128]{1,0:T(8,128)(2,1)S(1)}, bf16[1024,128]{1,0:T(8,128)(2,1)S(1)}, u32[]{:S(2)}, u32[]{:S(2)}) collective-permute-start(bf16[1024,128]{1,0:T(8,128)(2,1)S(1)} %get-tuple-element.28.refs_1_), channel_id=1, source_target_pairs={{0,1},{1,0},{2,3},{3,2},{4,5},{5,4},{6,7},{7,6},{8,9},{9,8},{10,11... | collective-permute-start | bytes 786440 | tf_op jit(solution)/shard_map/ppermute | solution.py:28
  9.7 1.5 %shard_map.69 = (bf16[1024,128]{1,0:T(8,128)(2,1)S(1)}, f32[512,128]{1,0:T(8,128)S(1)}) custom-call(bf16[2,512,2048]{2,1,0:T(8,128)(2,1)S(1)} %copy-done, bf16[512,128]{1,0:T(8,128)(2,1)S(1)} %get-tuple-element.62.half_ref, f32[512,128]{1,0:T(8,128)S(1)} %get-tuple-element.26.grad_ref, f32[2048,128]{1,0:T(8,128)S(1)} %copy-done.2), custom_call_target="tpu_custom_call" | custom-call | flops 402653184 | bytes 1048576 | tf_op jit(solution)/shard_map/pallas_call | solution.py:88
  11.4 5.4 %collective-permute-done.refs_2_ = bf16[1024,128]{1,0:T(8,128)(2,1)S(1)} collective-permute-done((bf16[1024,128]{1,0:T(8,128)(2,1)S(1)}, bf16[1024,128]{1,0:T(8,128)(2,1)S(1)}, u32[]{:S(2)}, u32[]{:S(2)}) %collective-permute-start) | collective-permute-done | bytes 262176 | tf_op jit(solution)/shard_map/ppermute | solution.py:28
  16.8 1.6 %shard_map.70 = (bf16[1024,128]{1,0:T(8,128)(2,1)S(1)}, f32[512,128]{1,0:T(8,128)S(1)}, f32[1024,128]{1,0:T(8,128)S(1)}, f32[1024,128]{1,0:T(8,128)S(1)}) custom-call(bf16[2,512,2048]{2,1,0:T(8,128)(2,1)S(1)} %copy-done, bf16[512,128]{1,0:T(8,128)(2,1)S(1)} %convert_element_type.37.half_ref, f32[512,128]{1,0:T(8,128)S(1)} %get-tuple-element.53.grad_ref, ...), custom_call_target="tpu_custom_call" | custom-call | flops 402653184 | bytes 1048576 | tf_op jit(solution)/shard_map/pallas_call | solution.py:88
  18.4 3.2 %collective-permute-done.1.refs_2_ = bf16[1024,128]{1,0:T(8,128)(2,1)S(1)} collective-permute-done((bf16[1024,128]{1,0:T(8,128)(2,1)S(1)}, bf16[1024,128]{1,0:T(8,128)(2,1)S(1)}, u32[]{:S(2)}, u32[]{:S(2)}) %collective-permute-start.1) | collective-permute-done | bytes 262176 | tf_op jit(solution)/shard_map/ppermute | solution.py:28
  21.6 1.6 %shard_map.71 = (bf16[1024,128]{1,0:T(8,128)(2,1)S(1)}, f32[512,128]{1,0:T(8,128)S(1)}, f32[1024,128]{1,0:T(8,128)S(1)}, f32[1024,128]{1,0:T(8,128)S(1)}) custom-call(bf16[2,512,2048]{2,1,0:T(8,128)(2,1)S(1)} %copy-done, bf16[512,128]{1,0:T(8,128)(2,1)S(1)} %convert_element_type.37.half_ref, f32[512,128]{1,0:T(8,128)S(1)} %get-tuple-element.29.grad_ref, ...), custom_call_target="tpu_custom_call" | custom-call | flops 402653184 | bytes 1048576 | tf_op jit(solution)/shard_map/pallas_call | solution.py:88
  23.2 1.8 %collective-permute-start.4 = (bf16[1024,128]{1,0:T(8,128)(2,1)S(1)}, bf16[1024,128]{1,0:T(8,128)(2,1)S(1)}, u32[]{:S(2)}, u32[]{:S(2)}) collective-permute-start(bf16[1024,128]{1,0:T(8,128)(2,1)S(1)} %get-tuple-element.37), channel_id=1, source_target_pairs={{0,1},{1,0},{2,3},{3,2},{4,5},{5,4},{6,7},{7,6},{8,9},{9,8},{10,11... | collective-permute-start | bytes 786440 | tf_op jit(solution)/shard_map/ppermute | solution.py:28
  25.3 7.2 %collective-permute-done.4 = bf16[1024,128]{1,0:T(8,128)(2,1)S(1)} collective-permute-done((bf16[1024,128]{1,0:T(8,128)(2,1)S(1)}, bf16[1024,128]{1,0:T(8,128)(2,1)S(1)}, u32[]{:S(2)}, u32[]{:S(2)}) %collective-permute-start.4) | collective-permute-done | bytes 262176 | tf_op jit(solution)/shard_map/ppermute | solution.py:28
  32.8 3.6 %collective-permute-done.2 = bf16[1024,128]{1,0:T(8,128)(2,1)S(1)} collective-permute-done((bf16[1024,128]{1,0:T(8,128)(2,1)S(1)}, bf16[1024,128]{1,0:T(8,128)(2,1)S(1)}, u32[]{:S(2)}, u32[]{:S(2)}) %collective-permute-start.2) | collective-permute-done | bytes 262176 | tf_op jit(solution)/shard_map/ppermute | solution.py:28
  36.8 1.6 %collective-permute-start.6 = (bf16[1024,128]{1,0:T(8,128)(2,1)S(1)}, bf16[1024,128]{1,0:T(8,128)(2,1)S(1)}, u32[]{:S(2)}, u32[]{:S(2)}) collective-permute-start(bf16[1024,128]{1,0:T(8,128)(2,1)S(1)} %get-tuple-element.57), channel_id=1, source_target_pairs={{0,2},{1,3},{2,4},{3,5},{4,6},{5,7},{6,8},{7,9},{8,10},{9,11},{10,... | collective-permute-start | bytes 786440 | tf_op jit(solution)/shard_map/ppermute | solution.py:28
  38.7 6.5 %collective-permute-done.3.items_ref = bf16[1024,128]{1,0:T(8,128)(2,1)S(1)} collective-permute-done((bf16[1024,128]{1,0:T(8,128)(2,1)S(1)}, bf16[1024,128]{1,0:T(8,128)(2,1)S(1)}, u32[]{:S(2)}, u32[]{:S(2)}) %collective-permute-start.3) | collective-permute-done | bytes 262176 | tf_op jit(solution)/shard_map/ppermute | solution.py:28
  45.2 1.5 %shard_map.72 = (bf16[1024,128]{1,0:T(8,128)(2,1)S(1)}, f32[512,128]{1,0:T(8,128)S(1)}) custom-call(bf16[2,512,2048]{2,1,0:T(8,128)(2,1)S(1)} %copy-done, bf16[512,128]{1,0:T(8,128)(2,1)S(1)} %convert_element_type.38.half_ref, f32[512,128]{1,0:T(8,128)S(1)} %get-tuple-element.50.grad_ref, bf16[1024,128]{1,0:T(8,128)(2,1)S(1)} %collective-permute-done.3.items_ref), custom_call_target="tpu_custom_call" | custom-call | flops 402653184 | bytes 1048576 | tf_op jit(solution)/shard_map/pallas_call | solution.py:88
  48.2 1.5 %shard_map.73 = (bf16[1024,128]{1,0:T(8,128)(2,1)S(1)}, f32[512,128]{1,0:T(8,128)S(1)}) custom-call(bf16[2,512,2048]{2,1,0:T(8,128)(2,1)S(1)} %copy-done, bf16[512,128]{1,0:T(8,128)(2,1)S(1)} %convert_element_type.38.half_ref, f32[512,128]{1,0:T(8,128)S(1)} %get-tuple-element.35.grad_ref, bf16[1024,128]{1,0:T(8,128)(2,1)S(1)} %collective-permute-done.5.items_ref), custom_call_target="tpu_custom_call" | custom-call | flops 402653184 | bytes 1048576 | tf_op jit(solution)/shard_map/pallas_call | solution.py:88
  50.5 4.9 %collective-permute-done.7.refs_2_ = bf16[1024,128]{1,0:T(8,128)(2,1)S(1)} collective-permute-done((bf16[1024,128]{1,0:T(8,128)(2,1)S(1)}, bf16[1024,128]{1,0:T(8,128)(2,1)S(1)}, u32[]{:S(2)}, u32[]{:S(2)}) %collective-permute-start.7) | collective-permute-done | bytes 262176 | tf_op jit(solution)/shard_map/ppermute | solution.py:28
  55.3 1.6 %shard_map.74 = (bf16[1024,128]{1,0:T(8,128)(2,1)S(1)}, f32[512,128]{1,0:T(8,128)S(1)}, f32[1024,128]{1,0:T(8,128)S(1)}, f32[1024,128]{1,0:T(8,128)S(1)}) custom-call(bf16[2,512,2048]{2,1,0:T(8,128)(2,1)S(1)} %copy-done, bf16[512,128]{1,0:T(8,128)(2,1)S(1)} %get-tuple-element.60.half_ref, f32[512,128]{1,0:T(8,128)S(1)} %get-tuple-element.59.grad_ref, ...), custom_call_target="tpu_custom_call" | custom-call | flops 402653184 | bytes 1048576 | tf_op jit(solution)/shard_map/pallas_call | solution.py:88
  56.9 1.6 %collective-permute-start.11 = (bf16[1024,128]{1,0:T(8,128)(2,1)S(1)}, bf16[1024,128]{1,0:T(8,128)(2,1)S(1)}, u32[]{:S(2)}, u32[]{:S(2)}) collective-permute-start(bf16[1024,128]{1,0:T(8,128)(2,1)S(1)} %get-tuple-element.49.refs_0_), channel_id=1, source_target_pairs={{0,1},{1,0},{2,3},{3,2},{4,5},{5,4},{6,7},{7,6},{8,9},{9,8},{10,11... | collective-permute-start | bytes 786440 | tf_op jit(solution)/shard_map/ppermute | solution.py:28
  58.5 2.4 %collective-permute-done.9.refs_2_ = bf16[1024,128]{1,0:T(8,128)(2,1)S(1)} collective-permute-done((bf16[1024,128]{1,0:T(8,128)(2,1)S(1)}, bf16[1024,128]{1,0:T(8,128)(2,1)S(1)}, u32[]{:S(2)}, u32[]{:S(2)}) %collective-permute-start.9) | collective-permute-done | bytes 262176 | tf_op jit(solution)/shard_map/ppermute | solution.py:28
  60.9 1.6 %shard_map.75 = (bf16[1024,128]{1,0:T(8,128)(2,1)S(1)}, f32[512,128]{1,0:T(8,128)S(1)}, f32[1024,128]{1,0:T(8,128)S(1)}, f32[1024,128]{1,0:T(8,128)S(1)}) custom-call(bf16[2,512,2048]{2,1,0:T(8,128)(2,1)S(1)} %copy-done, bf16[512,128]{1,0:T(8,128)(2,1)S(1)} %get-tuple-element.60.half_ref, f32[512,128]{1,0:T(8,128)S(1)} %get-tuple-element.41.grad_ref, ...), custom_call_target="tpu_custom_call" | custom-call | flops 402653184 | bytes 1048576 | tf_op jit(solution)/shard_map/pallas_call | solution.py:88
  62.6 1.6 %collective-permute-start.10 = (bf16[1024,128]{1,0:T(8,128)(2,1)S(1)}, bf16[1024,128]{1,0:T(8,128)(2,1)S(1)}, u32[]{:S(2)}, u32[]{:S(2)}) collective-permute-start(bf16[1024,128]{1,0:T(8,128)(2,1)S(1)} %get-tuple-element.46.refs_0_), channel_id=1, source_target_pairs={{0,1},{1,0},{2,3},{3,2},{4,5},{5,4},{6,7},{7,6},{8,9},{9,8},{10,11... | collective-permute-start | bytes 786440 | tf_op jit(solution)/shard_map/ppermute | solution.py:28
  65.4 1.5 %shard_map.76.refs_2_ = f32[2048,128]{1,0:T(8,128)} custom-call(f32[1024,128]{1,0:T(8,128)S(1)} %get-tuple-element.47.items_ref, f32[1024,128]{1,0:T(8,128)S(1)} %get-tuple-element.48.accum_ref, bf16[1024,128]{1,0:T(8,128)(2,1)S(1)} %get-tuple-element.49.refs_0_, bf16[1024,128]{1,0:T(8,128)(2,1)S(1)} %collective-permute-done.11.refs_1_), custom_call_target="tpu_custom_call" | custom-call | flops 1310720 | bytes 2097152 | tf_op jit(solution)/shard_map/pallas_call | solution.py:110
  66.9 2.1 %collective-permute-done.10.refs_1_ = bf16[1024,128]{1,0:T(8,128)(2,1)S(1)} collective-permute-done((bf16[1024,128]{1,0:T(8,128)(2,1)S(1)}, bf16[1024,128]{1,0:T(8,128)(2,1)S(1)}, u32[]{:S(2)}, u32[]{:S(2)}) %collective-permute-start.10) | collective-permute-done | bytes 262176 | tf_op jit(solution)/shard_map/ppermute | solution.py:28
  69.0 1.5 %shard_map.77 = f32[2048,128]{1,0:T(8,128)} custom-call(f32[1024,128]{1,0:T(8,128)S(1)} %get-tuple-element.44.items_ref, f32[1024,128]{1,0:T(8,128)S(1)} %get-tuple-element.45.accum_ref, bf16[1024,128]{1,0:T(8,128)(2,1)S(1)} %get-tuple-element.46.refs_0_, bf16[1024,128]{1,0:T(8,128)(2,1)S(1)} %collective-permute-done.10.refs_1_, ...), custom_call_target="tpu_custom_call", output_to_operand_aliasing={{}: (4, {})} | custom-call | flops 1310720 | bytes 2097152 | tf_op jit(solution)/shard_map/pallas_call | solution.py:110
  (31 shorter events, 7.3 us)
Async XLA Ops:
  1.7 2.2 %copy-start = (bf16[2,512,2048]{2,1,0:T(8,128)(2,1)S(1)}, bf16[2,512,2048]{2,1,0:T(8,128)(2,1)}, u32[]{:S(2)}) copy-start(bf16[2,512,2048]{2,1,0:T(8,128)(2,1)} %rate_ref.15) | copy-start | bytes 12582916
  3.9 1.2 %copy-start.1 = (f32[2048,128]{1,0:T(8,128)S(1)}, f32[2048,128]{1,0:T(8,128)}, u32[]{:S(2)}) copy-start(f32[2048,128]{1,0:T(8,128)} %items_ref.7) | copy-start | bytes 3145732
  5.1 4.6 %copy-start.2 = (f32[2048,128]{1,0:T(8,128)S(1)}, f32[2048,128]{1,0:T(8,128)}, u32[]{:S(2)}) copy-start(f32[2048,128]{1,0:T(8,128)} %items_ref.7) | copy-start | bytes 3145732
  6.6 4.7 %copy-start.4 = (f32[512,128]{1,0:T(8,128)S(1)}, f32[512,128]{1,0:T(8,128)}, u32[]{:S(2)}) copy-start(f32[512,128]{1,0:T(8,128)} %param.7) | copy-start | bytes 786436
  6.7 4.7 %copy-start.5 = (f32[512,128]{1,0:T(8,128)S(1)}, f32[512,128]{1,0:T(8,128)}, u32[]{:S(2)}) copy-start(f32[512,128]{1,0:T(8,128)} %param.6) | copy-start | bytes 786436
  6.7 10.2 %copy-start.3 = (f32[2048,128]{1,0:T(8,128)S(1)}, f32[2048,128]{1,0:T(8,128)}, u32[]{:S(2)}) copy-start(f32[2048,128]{1,0:T(8,128)} %refs_0_.3) | copy-start | bytes 3145732
  6.7 10.1 %collective-permute-start = (bf16[1024,128]{1,0:T(8,128)(2,1)S(1)}, bf16[1024,128]{1,0:T(8,128)(2,1)S(1)}, u32[]{:S(2)}, u32[]{:S(2)}) collective-permute-start(bf16[1024,128]{1,0:T(8,128)(2,1)S(1)} %get-tuple-element.28.refs_1_), channel_id=1, source_target_pairs={{0,1},{1,0},{2,3},{3,2},{4,5},{5,4},{6,7},{7,6},{8,9},{9,8},{10,11... | collective-permute-start | bytes 786440 | tf_op jit(solution)/shard_map/ppermute | solution.py:28
  11.2 10.4 %collective-permute-start.1 = (bf16[1024,128]{1,0:T(8,128)(2,1)S(1)}, bf16[1024,128]{1,0:T(8,128)(2,1)S(1)}, u32[]{:S(2)}, u32[]{:S(2)}) collective-permute-start(bf16[1024,128]{1,0:T(8,128)(2,1)S(1)} %get-tuple-element.30.refs_1_), channel_id=1, source_target_pairs={{0,1},{1,0},{2,3},{3,2},{4,5},{5,4},{6,7},{7,6},{8,9},{9,8},{10,11... | collective-permute-start | bytes 786440 | tf_op jit(solution)/shard_map/ppermute | solution.py:28
  23.2 9.3 %collective-permute-start.4 = (bf16[1024,128]{1,0:T(8,128)(2,1)S(1)}, bf16[1024,128]{1,0:T(8,128)(2,1)S(1)}, u32[]{:S(2)}, u32[]{:S(2)}) collective-permute-start(bf16[1024,128]{1,0:T(8,128)(2,1)S(1)} %get-tuple-element.37), channel_id=1, source_target_pairs={{0,1},{1,0},{2,3},{3,2},{4,5},{5,4},{6,7},{7,6},{8,9},{9,8},{10,11... | collective-permute-start | bytes 786440 | tf_op jit(solution)/shard_map/ppermute | solution.py:28
  25.0 11.4 %collective-permute-start.2 = (bf16[1024,128]{1,0:T(8,128)(2,1)S(1)}, bf16[1024,128]{1,0:T(8,128)(2,1)S(1)}, u32[]{:S(2)}, u32[]{:S(2)}) collective-permute-start(bf16[1024,128]{1,0:T(8,128)(2,1)S(1)} %get-tuple-element.33), channel_id=1, source_target_pairs={{0,1},{1,0},{2,3},{3,2},{4,5},{5,4},{6,7},{7,6},{8,9},{9,8},{10,11... | collective-permute-start | bytes 786440 | tf_op jit(solution)/shard_map/ppermute | solution.py:28
  32.8 15.4 %collective-permute-start.5 = (bf16[1024,128]{1,0:T(8,128)(2,1)S(1)}, bf16[1024,128]{1,0:T(8,128)(2,1)S(1)}, u32[]{:S(2)}, u32[]{:S(2)}) collective-permute-start(bf16[1024,128]{1,0:T(8,128)(2,1)S(1)} %get-tuple-element.56), channel_id=1, source_target_pairs={{0,2},{1,3},{2,4},{3,5},{4,6},{5,7},{6,8},{7,9},{8,10},{9,11},{10,... | collective-permute-start | bytes 786440 | tf_op jit(solution)/shard_map/ppermute | solution.py:28
  36.6 8.5 %collective-permute-start.3 = (bf16[1024,128]{1,0:T(8,128)(2,1)S(1)}, bf16[1024,128]{1,0:T(8,128)(2,1)S(1)}, u32[]{:S(2)}, u32[]{:S(2)}) collective-permute-start(bf16[1024,128]{1,0:T(8,128)(2,1)S(1)} %get-tuple-element.58), channel_id=1, source_target_pairs={{0,2},{1,3},{2,4},{3,5},{4,6},{5,7},{6,8},{7,9},{8,10},{9,11},{10,... | collective-permute-start | bytes 786440 | tf_op jit(solution)/shard_map/ppermute | solution.py:28
  36.8 13.6 %collective-permute-start.6 = (bf16[1024,128]{1,0:T(8,128)(2,1)S(1)}, bf16[1024,128]{1,0:T(8,128)(2,1)S(1)}, u32[]{:S(2)}, u32[]{:S(2)}) collective-permute-start(bf16[1024,128]{1,0:T(8,128)(2,1)S(1)} %get-tuple-element.57), channel_id=1, source_target_pairs={{0,2},{1,3},{2,4},{3,5},{4,6},{5,7},{6,8},{7,9},{8,10},{9,11},{10,... | collective-permute-start | bytes 786440 | tf_op jit(solution)/shard_map/ppermute | solution.py:28
  38.4 20.1 %collective-permute-start.8 = (bf16[1024,128]{1,0:T(8,128)(2,1)S(1)}, bf16[1024,128]{1,0:T(8,128)(2,1)S(1)}, u32[]{:S(2)}, u32[]{:S(2)}) collective-permute-start(bf16[1024,128]{1,0:T(8,128)(2,1)S(1)} %get-tuple-element.55), channel_id=1, source_target_pairs={{0,2},{1,3},{2,4},{3,5},{4,6},{5,7},{6,8},{7,9},{8,10},{9,11},{10,... | collective-permute-start | bytes 786440 | tf_op jit(solution)/shard_map/ppermute | solution.py:28
  46.7 8.6 %collective-permute-start.7 = (bf16[1024,128]{1,0:T(8,128)(2,1)S(1)}, bf16[1024,128]{1,0:T(8,128)(2,1)S(1)}, u32[]{:S(2)}, u32[]{:S(2)}) collective-permute-start(bf16[1024,128]{1,0:T(8,128)(2,1)S(1)} %get-tuple-element.40.refs_1_), channel_id=1, source_target_pairs={{0,1},{1,0},{2,3},{3,2},{4,5},{5,4},{6,7},{7,6},{8,9},{9,8},{10,11... | collective-permute-start | bytes 786440 | tf_op jit(solution)/shard_map/ppermute | solution.py:28
  49.7 11.2 %collective-permute-start.9 = (bf16[1024,128]{1,0:T(8,128)(2,1)S(1)}, bf16[1024,128]{1,0:T(8,128)(2,1)S(1)}, u32[]{:S(2)}, u32[]{:S(2)}) collective-permute-start(bf16[1024,128]{1,0:T(8,128)(2,1)S(1)} %get-tuple-element.42.refs_1_), channel_id=1, source_target_pairs={{0,1},{1,0},{2,3},{3,2},{4,5},{5,4},{6,7},{7,6},{8,9},{9,8},{10,11... | collective-permute-start | bytes 786440 | tf_op jit(solution)/shard_map/ppermute | solution.py:28
  56.9 8.5 %collective-permute-start.11 = (bf16[1024,128]{1,0:T(8,128)(2,1)S(1)}, bf16[1024,128]{1,0:T(8,128)(2,1)S(1)}, u32[]{:S(2)}, u32[]{:S(2)}) collective-permute-start(bf16[1024,128]{1,0:T(8,128)(2,1)S(1)} %get-tuple-element.49.refs_0_), channel_id=1, source_target_pairs={{0,1},{1,0},{2,3},{3,2},{4,5},{5,4},{6,7},{7,6},{8,9},{9,8},{10,11... | collective-permute-start | bytes 786440 | tf_op jit(solution)/shard_map/ppermute | solution.py:28
  62.6 6.4 %collective-permute-start.10 = (bf16[1024,128]{1,0:T(8,128)(2,1)S(1)}, bf16[1024,128]{1,0:T(8,128)(2,1)S(1)}, u32[]{:S(2)}, u32[]{:S(2)}) collective-permute-start(bf16[1024,128]{1,0:T(8,128)(2,1)S(1)} %get-tuple-element.46.refs_0_), channel_id=1, source_target_pairs={{0,1},{1,0},{2,3},{3,2},{4,5},{5,4},{6,7},{7,6},{8,9},{9,8},{10,11... | collective-permute-start | bytes 786440 | tf_op jit(solution)/shard_map/ppermute | solution.py:28

commit v4 on v3

v4 whole, which is shorter than its diff:
```python
import functools

import jax
import jax.numpy as jnp
from jax import lax
from jax.experimental import pallas as pl
from jax.experimental.pallas import tpu as pltpu
from jax.sharding import PartitionSpec as P

SUB = 2
INNER = 2
CHUNKS = 2
TILE = 256


shrink = 0.05
learn_rate = 0.2
tiny_eps = 1e-06


def moved(shard, loop_by, grp_by):
    loops, groups = lax.axis_size("loop"), lax.axis_size("grp")
    pairs = [
        (w * groups + g, (w + loop_by) % loops * groups + (g + grp_by) % groups)
        for w in range(loops)
        for g in range(groups)
    ]
    return lax.ppermute(shard, ("loop", "grp"), pairs)


def adagrad(param, accum, grad):
    accum = accum + grad * grad
    return (param - learn_rate * grad * lax.rsqrt(accum + tiny_eps), accum)


def group_terms(term):
    if lax.axis_size("grp") == 2:
        return (term, moved(term, 0, 1))
    return (lax.psum(term, "grp"),)


def item_step(items, accum, terms):
    items = items.astype(jnp.float32)
    grad = sum(term.astype(jnp.float32) for term in terms) + shrink * items
    return adagrad(items, accum.astype(jnp.float32), grad)


def chunk_tile(half, items, rate):
    item_half = items.astype(jnp.bfloat16)
    predicted = lax.dot_general(
        half, item_half, (((1,), (1,)), ((), ())), preferred_element_type=jnp.float32
    )
    rate = rate.astype(jnp.float32)
    resid = jnp.where(jnp.abs(rate) > 0.25, rate - predicted, 0.0).astype(jnp.bfloat16)
    term = lax.dot_general(resid, half, (((0,), (0,)), ((), ())), preferred_element_type=jnp.float32)
    return (-term).astype(jnp.bfloat16), jnp.dot(resid, item_half, preferred_element_type=jnp.float32)


def params(mib=16):
    return pltpu.CompilerParams(vmem_limit_bytes=mib * 2**20)


def cost(users, items, rank):
    return pl.CostEstimate(
        flops=6 * users * items * rank, bytes_accessed=2 * users * items, transcendentals=0
    )


WHOLE = pl.BlockSpec(memory_space=pltpu.VMEM)
AWAY = pl.BlockSpec(memory_space=pltpu.HBM)


def first_kernel(column, first, rate_hbm, items_hbm, *refs):
    if first:
        users_hbm, term_out, grad_out, users_ref, rate_ref, items_ref, sems = refs
        load_users = pltpu.make_async_copy(users_hbm, users_ref, sems.at[2, 0])
        load_users.start()
    else:
        users_ref, grad_ref, term_out, grad_out, rate_ref, items_ref, sems = refs
    tiles = range(term_out.shape[0] // TILE)
    loads = []
    for t in tiles:
        at = pl.ds(column + t * TILE, TILE)
        loads.append(
            (
                pltpu.make_async_copy(items_hbm.at[at, :], items_ref.at[t], sems.at[0, t]),
                pltpu.make_async_copy(rate_hbm.at[0, :, at], rate_ref.at[t], sems.at[1, t]),
            )
        )
        for load in loads[-1]:
            load.start()
    if first:
        load_users.wait()
        grad = shrink * users_ref[...]
    else:
        grad = grad_ref[...]
    half = users_ref[...].astype(jnp.bfloat16)
    for t in tiles:
        for load in loads[t]:
            load.wait()
        term, part = chunk_tile(half, items_ref[t], rate_ref[t])
        term_out[pl.ds(t * TILE, TILE), :] = term
        grad = grad - part
    grad_out[...] = grad


def first_pass(ratings, rows, users, grad, items):
    size, (n_users, rank) = rows.stop - rows.start, users.shape
    first = grad is None
    return pl.pallas_call(
        functools.partial(first_kernel, rows.start, first),
        out_shape=[
            jax.ShapeDtypeStruct((size, rank), jnp.bfloat16),
            jax.ShapeDtypeStruct(users.shape, jnp.float32),
        ],
        in_specs=[AWAY, AWAY, AWAY] if first else [AWAY, AWAY, WHOLE, WHOLE],
        out_specs=[WHOLE] * 2,
        scratch_shapes=([pltpu.VMEM(users.shape, jnp.float32)] if first else [])
        + [
            pltpu.VMEM((size // TILE, n_users, TILE), jnp.bfloat16),
            pltpu.VMEM((size // TILE, TILE, rank), jnp.float32),
            pltpu.SemaphoreType.DMA((3, size // TILE)),
        ],
        compiler_params=params(62 if first else 16),
        cost_estimate=cost(n_users, size, rank),
    )(ratings, items, users, *([] if first else [grad]))


def chunk_kernel(n_terms, sub_epoch, column, offset, rate_ref, half_ref, grad_ref, items_ref, *refs):
    if n_terms:
        accum_ref, *refs = refs
    term_refs, (term_out, grad_out, *updated) = refs[:n_terms], refs[n_terms:]
    half = half_ref[...]
    grad = grad_ref[...]
    for start in range(0, term_out.shape[0], TILE):
        at = pl.ds(start, TILE)
        held = pl.ds(offset + start, TILE)
        items = items_ref[held, :]
        if n_terms:
            items, accum = item_step(items, accum_ref[held, :], [ref[at, :] for ref in term_refs])
            updated[0][at, :] = items
            updated[1][at, :] = accum
        term_out[at, :], part = chunk_tile(half, items, rate_ref[sub_epoch, :, pl.ds(column + start, TILE)])
        grad = grad - part
    grad_out[...] = grad


def chunk_pass(ratings, sub_epoch, rows, half, grad, items, accum, terms):
    size, rank = rows.stop - rows.start, items.shape[1]
    offset = 0 if items.shape[0] == size else rows.start
    out_shape = [
        jax.ShapeDtypeStruct((size, rank), jnp.bfloat16),
        jax.ShapeDtypeStruct(grad.shape, jnp.float32),
    ]
    operands = [ratings, half, grad, items]
    if terms:
        out_shape += [jax.ShapeDtypeStruct((size, rank), jnp.float32)] * 2
        operands += [accum, *terms]
    return pl.pallas_call(
        functools.partial(chunk_kernel, len(terms), sub_epoch, rows.start, offset),
        out_shape=out_shape,
        in_specs=[WHOLE] * len(operands),
        out_specs=[WHOLE] * len(out_shape),
        compiler_params=params(),
        cost_estimate=cost(half.shape[0], size, rank),
    )(*operands)


def parting_kernel(n_terms, items_ref, accum_ref, *refs):
    items, accum = item_step(items_ref[...], accum_ref[...], [ref[...] for ref in refs[:n_terms]])
    items_out, accum_out = refs[-2:]
    items_out[...] = items.astype(jnp.bfloat16)
    accum_out[...] = accum.astype(jnp.bfloat16)


def parting_step(items, accum, terms, before):
    return pl.pallas_call(
        functools.partial(parting_kernel, len(terms)),
        out_shape=[jax.ShapeDtypeStruct(items.shape, jnp.bfloat16)] * 2,
        in_specs=[WHOLE] * (2 + len(terms)) + [pl.BlockSpec(memory_space=pl.ANY)] * len(before),
        out_specs=[WHOLE] * 2,
        compiler_params=params(),
        cost_estimate=cost(1, *items.shape),
    )(items, accum, *terms, *before)


def last_kernel(n_terms, row, items_ref, accum_ref, *refs):
    out_hbm, out_ref, sems = refs[-3:]
    stores = []
    for t in range(items_ref.shape[0] // TILE):
        at = pl.ds(t * TILE, TILE)
        out_ref[at, :], _ = item_step(items_ref[at, :], accum_ref[at, :], [ref[at, :] for ref in refs[:n_terms]])
        stores.append(
            pltpu.make_async_copy(out_ref.at[at, :], out_hbm.at[pl.ds(row + t * TILE, TILE), :], sems.at[t])
        )
        stores[-1].start()
    for store in stores:
        store.wait()


def last_item_step(rows, n_items, items, accum, terms, filled):
    size, rank = items.shape
    return pl.pallas_call(
        functools.partial(last_kernel, len(terms), rows.start),
        out_shape=jax.ShapeDtypeStruct((n_items, rank), jnp.float32),
        in_specs=[WHOLE] * (2 + len(terms)) + [AWAY] * len(filled),
        out_specs=AWAY,
        scratch_shapes=[
            pltpu.VMEM((size, rank), jnp.float32),
            pltpu.SemaphoreType.DMA((size // TILE,)),
        ],
        input_output_aliases={2 + len(terms): 0} if filled else {},
        compiler_params=params(),
        cost_estimate=cost(1, size, rank),
    )(items, accum, *terms, *filled)


def local(ratings, user_factors, user_accum, item_factors, item_accum):
    users = user_factors
    user_acc = user_accum
    size = item_factors.shape[0] // CHUNKS
    rows = [slice(c * size, (c + 1) * size) for c in range(CHUNKS)]
    items = [item_factors] * CHUNKS
    item_acc = [item_accum] * CHUNKS
    terms = [()] * CHUNKS
    for step in range(SUB * INNER):
        sub_epoch = step // INNER
        if step > 0 and step % INNER == 0:
            before = []
            for c in range(CHUNKS):
                stepped, accum = parting_step(items[c], item_acc[c], terms[c], before)
                items[c] = moved(stepped, 1, 0)
                item_acc[c] = moved(accum, 1, 0)
                terms[c] = ()
                before = [stepped]
        if step == 0:
            grad_user = None
        else:
            user_half = users.astype(jnp.bfloat16)
            grad_user = shrink * users
        for c in range(CHUNKS):
            if step == 0:
                term, grad_user = first_pass(ratings, rows[c], users, grad_user, items[c])
            else:
                term, grad_user, *updated = chunk_pass(
                    ratings, sub_epoch, rows[c], user_half, grad_user, items[c], item_acc[c], terms[c]
                )
                if updated:
                    items[c], item_acc[c] = updated
            terms[c] = group_terms(term)
        users, user_acc = adagrad(users, user_acc, grad_user)
    filled = []
    for c in range(CHUNKS):
        filled = [last_item_step(rows[c], item_factors.shape[0], items[c], item_acc[c], terms[c], filled)]
    return (users, filled[0])


def solution(mesh):
    in_specs = (
        P(None, ("loop", "grp"), None),
        P(("loop", "grp"), None),
        P(("loop", "grp"), None),
        P("loop", None),
        P("loop", None),
    )
    out_specs = (P(("loop", "grp"), None), P("loop", None))
    return jax.shard_map(local, mesh=mesh, in_specs=in_specs, out_specs=out_specs, check_vma=False)
```

time: 70.7 us -> 65.2 us (0.922)
  starting transfers between devices: 12.4 us -> 7.84 us
  Pallas kernels: 15.5 us -> 19.3 us
  waiting for transfers between devices: 35.7 us -> 32.5 us
  other arithmetic: 2.68 us -> 1.12 us
    pallas_call x2 -> x6, Pallas kernels: 3 us -> 9.92 us  [the longest x2 7.65 us: first_pass(): pl.pallas_call(functools.partial(first_kernel, rows.start, first), out_sh...]
    ppermute x12, starting transfers between devices: 12.4 us -> 7.84 us  [moved(): return lax.ppermute(shard, ('loop', 'grp'), pairs)]
    ppermute x12, waiting for transfers between devices: 35.7 us -> 32.5 us  [moved(): return lax.ppermute(shard, ('loop', 'grp'), pairs)]
    pallas_call x8 -> x6, Pallas kernels: 12.5 us -> 9.43 us  [chunk_pass(): pl.pallas_call(functools.partial(chunk_kernel, len(terms), sub_epoch, row...]
    mul x4 -> x3, other arithmetic: 1.33 us -> 0.25 us  [local(): grad_user = shrink * users]
    unnamed x12 -> x16, local copies, waits for them, and re-layouts: 3.43 us -> 3.16 us
  transfers between devices with their start and end apart: 12 -> 12, of which waited for: 9 -> 10; matrix products, arithmetic and copies ran while one was open for 2% -> 2% of each run, Pallas kernels for 15% -> 22%
where the time goes in v4:
time: 65.2 us; the launch traced here: 65 us
  waiting for transfers between devices  32.5 us (50%)
  Pallas kernels  19.3 us (30%)
  starting transfers between devices  7.84 us (12%)
  local copies, waits for them, and re-layouts  3.16 us (5%)
  other arithmetic  1.12 us (2%)
  between operations  0.99 us (2%)
    ppermute x12, waiting for transfers between devices, moved(): return lax.ppermute(shard, ('loop', 'grp'), pairs)  32.5 us
    pallas_call x6, Pallas kernels, chunk_pass(): pl.pallas_call(functools.partial(chunk_kernel, len(terms), sub_epoch, row...  9.43 us
    ppermute x12, starting transfers between devices, moved(): return lax.ppermute(shard, ('loop', 'grp'), pairs)  7.84 us
    pallas_call x2, Pallas kernels, first_pass(): pl.pallas_call(functools.partial(first_kernel, rows.start, first), out_sh...  7.65 us
    unnamed x16, local copies, waits for them, and re-layouts  3.16 us
    pallas_call x2, Pallas kernels, last_item_step(): pl.pallas_call(functools.partial(last_kernel, len(terms), rows.start), ou...  1.8 us
  transfers between devices with their start and end apart: 12, of which 10 were waited for; matrix products, arithmetic and copies ran while one was open for 2% of the time, Pallas kernels for 22%

profile of v4, /device:TPU:0, one launch (start us, length us, event | category | flops | bytes accessed | tf_op | source)
XLA Modules:
  0.0 65.0 jit_solution(15518638869519362934)
XLA Ops:
  0.7 4.4 %shard_map.68 = (bf16[1024,128]{1,0:T(8,128)(2,1)}, f32[512,128]{1,0:T(8,128)}) custom-call(bf16[2,512,2048]{2,1,0:T(8,128)(2,1)} %rate_ref.11, f32[2048,128]{1,0:T(8,128)} %items_ref.3, f32[512,128]{1,0:T(8,128)} %refs_0_.5), custom_call_target="tpu_custom_call" | custom-call | flops 402653184 | bytes 1048576 | tf_op jit(solution)/shard_map/pallas_call | solution.py:110
  5.0 3.0 %collective-permute-start = (bf16[1024,128]{1,0:T(8,128)(2,1)}, bf16[1024,128]{1,0:T(8,128)(2,1)S(1)}, u32[]{:S(2)}, u32[]{:S(2)}) collective-permute-start(bf16[1024,128]{1,0:T(8,128)(2,1)} %get-tuple-element.32.refs_1_), channel_id=1, source_target_pairs={{0,1},{1,0},{2,3},{3,2},{4,5},{5,4},{6,7},{7,6},{8,9},{9,8},{10,11... | collective-permute-start | bytes 786440 | tf_op jit(solution)/shard_map/ppermute | solution.py:28
  8.1 2.2 %copy-done = bf16[2,512,2048]{2,1,0:T(8,128)(2,1)S(1)} copy-done((bf16[2,512,2048]{2,1,0:T(8,128)(2,1)S(1)}, bf16[2,512,2048]{2,1,0:T(8,128)(2,1)}, u32[]{:S(2)}) %copy-start) | copy-done | bytes 4194328
  10.2 0.9 %copy-done.6 = f32[512,128]{1,0:T(8,128)S(1)} copy-done((f32[512,128]{1,0:T(8,128)S(1)}, f32[512,128]{1,0:T(8,128)}, u32[]{:S(2)}) %copy-start.6) | copy-done | bytes 262168
  11.2 3.3 %shard_map.69 = (bf16[1024,128]{1,0:T(8,128)(2,1)S(1)}, f32[512,128]{1,0:T(8,128)S(1)}) custom-call(bf16[2,512,2048]{2,1,0:T(8,128)(2,1)S(1)} %copy-done, f32[2048,128]{1,0:T(8,128)S(1)} %copy-done.2, f32[512,128]{1,0:T(8,128)S(1)} %copy-done.4, f32[512,128]{1,0:T(8,128)S(1)} %copy-done.6), custom_call_target="tpu_custom_call" | custom-call | flops 402653184 | bytes 1048576 | tf_op jit(solution)/shard_map/pallas_call | solution.py:110
  14.7 1.6 %shard_map.70 = (bf16[1024,128]{1,0:T(8,128)(2,1)S(1)}, f32[512,128]{1,0:T(8,128)S(1)}, f32[1024,128]{1,0:T(8,128)S(1)}, f32[1024,128]{1,0:T(8,128)S(1)}) custom-call(bf16[2,512,2048]{2,1,0:T(8,128)(2,1)S(1)} %copy-done, bf16[512,128]{1,0:T(8,128)(2,1)S(1)} %convert_element_type.9.half_ref, f32[512,128]{1,0:T(8,128)S(1)} %get-tuple-element.61.grad_ref, ...), custom_call_target="tpu_custom_call" | custom-call | flops 402653184 | bytes 1048576 | tf_op jit(solution)/shard_map/pallas_call | solution.py:159
  16.3 2.1 %collective-permute-start.2 = (bf16[1024,128]{1,0:T(8,128)(2,1)S(1)}, bf16[1024,128]{1,0:T(8,128)(2,1)S(1)}, u32[]{:S(2)}, u32[]{:S(2)}) collective-permute-start(bf16[1024,128]{1,0:T(8,128)(2,1)S(1)} %get-tuple-element.38.refs_0_), channel_id=1, source_target_pairs={{0,1},{1,0},{2,3},{3,2},{4,5},{5,4},{6,7},{7,6},{8,9},{9,8},{10,11... | collective-permute-start | bytes 786440 | tf_op jit(solution)/shard_map/ppermute | solution.py:28
  18.4 5.4 %collective-permute-done.1.refs_2_ = bf16[1024,128]{1,0:T(8,128)(2,1)S(1)} collective-permute-done((bf16[1024,128]{1,0:T(8,128)(2,1)S(1)}, bf16[1024,128]{1,0:T(8,128)(2,1)S(1)}, u32[]{:S(2)}, u32[]{:S(2)}) %collective-permute-start.1) | collective-permute-done | bytes 262176 | tf_op jit(solution)/shard_map/ppermute | solution.py:28
  23.8 1.6 %shard_map.71 = (bf16[1024,128]{1,0:T(8,128)(2,1)S(1)}, f32[512,128]{1,0:T(8,128)S(1)}, f32[1024,128]{1,0:T(8,128)S(1)}, f32[1024,128]{1,0:T(8,128)S(1)}) custom-call(bf16[2,512,2048]{2,1,0:T(8,128)(2,1)S(1)} %copy-done, bf16[512,128]{1,0:T(8,128)(2,1)S(1)} %convert_element_type.9.half_ref, f32[512,128]{1,0:T(8,128)S(1)} %get-tuple-element.33.grad_ref, ...), custom_call_target="tpu_custom_call" | custom-call | flops 402653184 | bytes 1048576 | tf_op jit(solution)/shard_map/pallas_call | solution.py:159
  25.5 3.9 %collective-permute-done.2.refs_1_ = bf16[1024,128]{1,0:T(8,128)(2,1)S(1)} collective-permute-done((bf16[1024,128]{1,0:T(8,128)(2,1)S(1)}, bf16[1024,128]{1,0:T(8,128)(2,1)S(1)}, u32[]{:S(2)}, u32[]{:S(2)}) %collective-permute-start.2) | collective-permute-done | bytes 262176 | tf_op jit(solution)/shard_map/ppermute | solution.py:28
  29.7 3.8 %collective-permute-done.4.refs_1_ = bf16[1024,128]{1,0:T(8,128)(2,1)S(1)} collective-permute-done((bf16[1024,128]{1,0:T(8,128)(2,1)S(1)}, bf16[1024,128]{1,0:T(8,128)(2,1)S(1)}, u32[]{:S(2)}, u32[]{:S(2)}) %collective-permute-start.4) | collective-permute-done | bytes 262176 | tf_op jit(solution)/shard_map/ppermute | solution.py:28
  34.0 1.7 %collective-permute-start.6 = (bf16[1024,128]{1,0:T(8,128)(2,1)S(1)}, bf16[1024,128]{1,0:T(8,128)(2,1)S(1)}, u32[]{:S(2)}, u32[]{:S(2)}) collective-permute-start(bf16[1024,128]{1,0:T(8,128)(2,1)S(1)} %get-tuple-element.46), channel_id=1, source_target_pairs={{0,2},{1,3},{2,4},{3,5},{4,6},{5,7},{6,8},{7,9},{8,10},{9,11},{10,... | collective-permute-start | bytes 786440 | tf_op jit(solution)/shard_map/ppermute | solution.py:28
  35.9 2.3 %collective-permute-done.3.items_ref = bf16[1024,128]{1,0:T(8,128)(2,1)S(1)} collective-permute-done((bf16[1024,128]{1,0:T(8,128)(2,1)S(1)}, bf16[1024,128]{1,0:T(8,128)(2,1)S(1)}, u32[]{:S(2)}, u32[]{:S(2)}) %collective-permute-start.3) | collective-permute-done | bytes 262176 | tf_op jit(solution)/shard_map/ppermute | solution.py:28
  38.2 1.5 %shard_map.73 = (bf16[1024,128]{1,0:T(8,128)(2,1)S(1)}, f32[512,128]{1,0:T(8,128)S(1)}) custom-call(bf16[2,512,2048]{2,1,0:T(8,128)(2,1)S(1)} %copy-done.1, bf16[512,128]{1,0:T(8,128)(2,1)S(1)} %convert_element_type.10.half_ref, f32[512,128]{1,0:T(8,128)S(1)} %get-tuple-element.58.grad_ref, bf16[1024,128]{1,0:T(8,128)(2,1)S(1)} %collective-permute-done.3.items_ref), custom_call_target="tpu_custom_call" | custom-call | flops 402653184 | bytes 1048576 | tf_op jit(solution)/shard_map/pallas_call | solution.py:159
  39.8 2.5 %collective-permute-done.5.items_ref = bf16[1024,128]{1,0:T(8,128)(2,1)S(1)} collective-permute-done((bf16[1024,128]{1,0:T(8,128)(2,1)S(1)}, bf16[1024,128]{1,0:T(8,128)(2,1)S(1)}, u32[]{:S(2)}, u32[]{:S(2)}) %collective-permute-start.5) | collective-permute-done | bytes 262176 | tf_op jit(solution)/shard_map/ppermute | solution.py:28
  42.3 1.5 %shard_map.75 = (bf16[1024,128]{1,0:T(8,128)(2,1)S(1)}, f32[512,128]{1,0:T(8,128)S(1)}) custom-call(bf16[2,512,2048]{2,1,0:T(8,128)(2,1)S(1)} %copy-done.1, bf16[512,128]{1,0:T(8,128)(2,1)S(1)} %convert_element_type.10.half_ref, f32[512,128]{1,0:T(8,128)S(1)} %get-tuple-element.40.grad_ref, bf16[1024,128]{1,0:T(8,128)(2,1)S(1)} %collective-permute-done.5.items_ref), custom_call_target="tpu_custom_call" | custom-call | flops 402653184 | bytes 1048576 | tf_op jit(solution)/shard_map/pallas_call | solution.py:159
  45.1 3.9 %collective-permute-done.7.refs_2_ = bf16[1024,128]{1,0:T(8,128)(2,1)S(1)} collective-permute-done((bf16[1024,128]{1,0:T(8,128)(2,1)S(1)}, bf16[1024,128]{1,0:T(8,128)(2,1)S(1)}, u32[]{:S(2)}, u32[]{:S(2)}) %collective-permute-start.7) | collective-permute-done | bytes 262176 | tf_op jit(solution)/shard_map/ppermute | solution.py:28
  49.0 1.6 %shard_map.76 = (bf16[1024,128]{1,0:T(8,128)(2,1)S(1)}, f32[512,128]{1,0:T(8,128)S(1)}, f32[1024,128]{1,0:T(8,128)S(1)}, f32[1024,128]{1,0:T(8,128)S(1)}) custom-call(bf16[2,512,2048]{2,1,0:T(8,128)(2,1)S(1)} %copy-done.1, bf16[512,128]{1,0:T(8,128)(2,1)S(1)} %get-tuple-element.64.half_ref, f32[512,128]{1,0:T(8,128)S(1)} %get-tuple-element.63.grad_ref, ...), custom_call_target="tpu_custom_call" | custom-call | flops 402653184 | bytes 1048576 | tf_op jit(solution)/shard_map/pallas_call | solution.py:159
  50.7 3.9 %collective-permute-done.9.refs_2_ = bf16[1024,128]{1,0:T(8,128)(2,1)S(1)} collective-permute-done((bf16[1024,128]{1,0:T(8,128)(2,1)S(1)}, bf16[1024,128]{1,0:T(8,128)(2,1)S(1)}, u32[]{:S(2)}, u32[]{:S(2)}) %collective-permute-start.9) | collective-permute-done | bytes 262176 | tf_op jit(solution)/shard_map/ppermute | solution.py:28
  54.6 1.6 %shard_map.77 = (bf16[1024,128]{1,0:T(8,128)(2,1)S(1)}, f32[512,128]{1,0:T(8,128)S(1)}, f32[1024,128]{1,0:T(8,128)S(1)}, f32[1024,128]{1,0:T(8,128)S(1)}) custom-call(bf16[2,512,2048]{2,1,0:T(8,128)(2,1)S(1)} %copy-done.1, bf16[512,128]{1,0:T(8,128)(2,1)S(1)} %get-tuple-element.64.half_ref, f32[512,128]{1,0:T(8,128)S(1)} %get-tuple-element.48.grad_ref, ...), custom_call_target="tpu_custom_call" | custom-call | flops 402653184 | bytes 1048576 | tf_op jit(solution)/shard_map/pallas_call | solution.py:159
  57.1 3.1 %collective-permute-done.11.refs_1_ = bf16[1024,128]{1,0:T(8,128)(2,1)S(1)} collective-permute-done((bf16[1024,128]{1,0:T(8,128)(2,1)S(1)}, bf16[1024,128]{1,0:T(8,128)(2,1)S(1)}, u32[]{:S(2)}, u32[]{:S(2)}) %collective-permute-start.11) | collective-permute-done | bytes 262176 | tf_op jit(solution)/shard_map/ppermute | solution.py:28
  60.3 0.9 %shard_map.78.refs_2_ = f32[2048,128]{1,0:T(8,128)} custom-call(f32[1024,128]{1,0:T(8,128)S(1)} %get-tuple-element.55.items_ref, f32[1024,128]{1,0:T(8,128)S(1)} %get-tuple-element.56.accum_ref, bf16[1024,128]{1,0:T(8,128)(2,1)S(1)} %get-tuple-element.57.refs_0_, bf16[1024,128]{1,0:T(8,128)(2,1)S(1)} %collective-permute-done.11.refs_1_), custom_call_target="tpu_custom_call" | custom-call | flops 786432 | bytes 2048 | tf_op jit(solution)/shard_map/pallas_call | solution.py:203
  61.2 2.8 %collective-permute-done.10.refs_1_ = bf16[1024,128]{1,0:T(8,128)(2,1)S(1)} collective-permute-done((bf16[1024,128]{1,0:T(8,128)(2,1)S(1)}, bf16[1024,128]{1,0:T(8,128)(2,1)S(1)}, u32[]{:S(2)}, u32[]{:S(2)}) %collective-permute-start.10) | collective-permute-done | bytes 262176 | tf_op jit(solution)/shard_map/ppermute | solution.py:28
  63.9 0.9 %shard_map.79 = f32[2048,128]{1,0:T(8,128)} custom-call(f32[1024,128]{1,0:T(8,128)S(1)} %get-tuple-element.52.items_ref, f32[1024,128]{1,0:T(8,128)S(1)} %get-tuple-element.53.accum_ref, bf16[1024,128]{1,0:T(8,128)(2,1)S(1)} %get-tuple-element.54.refs_0_, bf16[1024,128]{1,0:T(8,128)(2,1)S(1)} %collective-permute-done.10.refs_1_, ...), custom_call_target="tpu_custom_call", output_to_operand_aliasing={{}: (4, {})} | custom-call | flops 786432 | bytes 2048 | tf_op jit(solution)/shard_map/pallas_call | solution.py:203
  (34 shorter events, 3.6 us)
Async XLA Ops:
  0.6 7.4 %copy-start.4 = (f32[512,128]{1,0:T(8,128)S(1)}, f32[512,128]{1,0:T(8,128)}, u32[]{:S(2)}) copy-start(f32[512,128]{1,0:T(8,128)} %refs_0_.5) | copy-start | bytes 786436
  0.6 7.4 %copy-start.2 = (f32[2048,128]{1,0:T(8,128)S(1)}, f32[2048,128]{1,0:T(8,128)}, u32[]{:S(2)}) copy-start(f32[2048,128]{1,0:T(8,128)} %items_ref.3) | copy-start | bytes 3145732
  0.7 13.9 %copy-start.7 = (f32[512,128]{1,0:T(8,128)S(1)}, f32[512,128]{1,0:T(8,128)}, u32[]{:S(2)}) copy-start(f32[512,128]{1,0:T(8,128)} %param.7) | copy-start | bytes 786436
  5.0 9.6 %collective-permute-start = (bf16[1024,128]{1,0:T(8,128)(2,1)}, bf16[1024,128]{1,0:T(8,128)(2,1)S(1)}, u32[]{:S(2)}, u32[]{:S(2)}) collective-permute-start(bf16[1024,128]{1,0:T(8,128)(2,1)} %get-tuple-element.32.refs_1_), channel_id=1, source_target_pairs={{0,1},{1,0},{2,3},{3,2},{4,5},{5,4},{6,7},{7,6},{8,9},{9,8},{10,11... | collective-permute-start | bytes 786440 | tf_op jit(solution)/shard_map/ppermute | solution.py:28
  8.0 2.2 %copy-start = (bf16[2,512,2048]{2,1,0:T(8,128)(2,1)S(1)}, bf16[2,512,2048]{2,1,0:T(8,128)(2,1)}, u32[]{:S(2)}) copy-start(bf16[2,512,2048]{2,1,0:T(8,128)(2,1)} %rate_ref.11) | copy-start | bytes 12582916
  10.2 0.9 %copy-start.6 = (f32[512,128]{1,0:T(8,128)S(1)}, f32[512,128]{1,0:T(8,128)}, u32[]{:S(2)}) copy-start(f32[512,128]{1,0:T(8,128)} %get-tuple-element.30.refs_1_) | copy-start | bytes 786436
  11.2 3.5 %copy-start.3 = (f32[2048,128]{1,0:T(8,128)S(1)}, f32[2048,128]{1,0:T(8,128)}, u32[]{:S(2)}) copy-start(f32[2048,128]{1,0:T(8,128)} %refs_0_.7) | copy-start | bytes 3145732
  11.2 3.5 %copy-start.5 = (bf16[1024,128]{1,0:T(8,128)(2,1)S(1)}, bf16[1024,128]{1,0:T(8,128)(2,1)}, u32[]{:S(2)}) copy-start(bf16[1024,128]{1,0:T(8,128)(2,1)} %get-tuple-element.32.refs_1_) | copy-start | bytes 786436
  14.5 9.3 %collective-permute-start.1 = (bf16[1024,128]{1,0:T(8,128)(2,1)S(1)}, bf16[1024,128]{1,0:T(8,128)(2,1)S(1)}, u32[]{:S(2)}, u32[]{:S(2)}) collective-permute-start(bf16[1024,128]{1,0:T(8,128)(2,1)S(1)} %get-tuple-element.34.refs_1_), channel_id=1, source_target_pairs={{0,1},{1,0},{2,3},{3,2},{4,5},{5,4},{6,7},{7,6},{8,9},{9,8},{10,11... | collective-permute-start | bytes 786440 | tf_op jit(solution)/shard_map/ppermute | solution.py:28
  16.3 13.1 %collective-permute-start.2 = (bf16[1024,128]{1,0:T(8,128)(2,1)S(1)}, bf16[1024,128]{1,0:T(8,128)(2,1)S(1)}, u32[]{:S(2)}, u32[]{:S(2)}) collective-permute-start(bf16[1024,128]{1,0:T(8,128)(2,1)S(1)} %get-tuple-element.38.refs_0_), channel_id=1, source_target_pairs={{0,1},{1,0},{2,3},{3,2},{4,5},{5,4},{6,7},{7,6},{8,9},{9,8},{10,11... | collective-permute-start | bytes 786440 | tf_op jit(solution)/shard_map/ppermute | solution.py:28
  25.4 12.8 %copy-start.1 = (bf16[2,512,2048]{2,1,0:T(8,128)(2,1)S(1)}, bf16[2,512,2048]{2,1,0:T(8,128)(2,1)}, u32[]{:S(2)}) copy-start(bf16[2,512,2048]{2,1,0:T(8,128)(2,1)} %rate_ref.11) | copy-start | bytes 12582916
  25.4 8.2 %collective-permute-start.4 = (bf16[1024,128]{1,0:T(8,128)(2,1)S(1)}, bf16[1024,128]{1,0:T(8,128)(2,1)S(1)}, u32[]{:S(2)}, u32[]{:S(2)}) collective-permute-start(bf16[1024,128]{1,0:T(8,128)(2,1)S(1)} %get-tuple-element.43.refs_0_), channel_id=1, source_target_pairs={{0,1},{1,0},{2,3},{3,2},{4,5},{5,4},{6,7},{7,6},{8,9},{9,8},{10,11... | collective-permute-start | bytes 786440 | tf_op jit(solution)/shard_map/ppermute | solution.py:28
  29.6 8.5 %collective-permute-start.3 = (bf16[1024,128]{1,0:T(8,128)(2,1)S(1)}, bf16[1024,128]{1,0:T(8,128)(2,1)S(1)}, u32[]{:S(2)}, u32[]{:S(2)}) collective-permute-start(bf16[1024,128]{1,0:T(8,128)(2,1)S(1)} %get-tuple-element.39.refs_2_), channel_id=1, source_target_pairs={{0,2},{1,3},{2,4},{3,5},{4,6},{5,7},{6,8},{7,9},{8,10},{9,11},{10,... | collective-permute-start | bytes 786440 | tf_op jit(solution)/shard_map/ppermute | solution.py:28
  33.8 8.5 %collective-permute-start.5 = (bf16[1024,128]{1,0:T(8,128)(2,1)S(1)}, bf16[1024,128]{1,0:T(8,128)(2,1)S(1)}, u32[]{:S(2)}, u32[]{:S(2)}) collective-permute-start(bf16[1024,128]{1,0:T(8,128)(2,1)S(1)} %get-tuple-element.44), channel_id=1, source_target_pairs={{0,2},{1,3},{2,4},{3,5},{4,6},{5,7},{6,8},{7,9},{8,10},{9,11},{10,... | collective-permute-start | bytes 786440 | tf_op jit(solution)/shard_map/ppermute | solution.py:28
  34.0 11.2 %collective-permute-start.6 = (bf16[1024,128]{1,0:T(8,128)(2,1)S(1)}, bf16[1024,128]{1,0:T(8,128)(2,1)S(1)}, u32[]{:S(2)}, u32[]{:S(2)}) collective-permute-start(bf16[1024,128]{1,0:T(8,128)(2,1)S(1)} %get-tuple-element.46), channel_id=1, source_target_pairs={{0,2},{1,3},{2,4},{3,5},{4,6},{5,7},{6,8},{7,9},{8,10},{9,11},{10,... | collective-permute-start | bytes 786440 | tf_op jit(solution)/shard_map/ppermute | solution.py:28
  35.6 15.1 %collective-permute-start.8 = (bf16[1024,128]{1,0:T(8,128)(2,1)S(1)}, bf16[1024,128]{1,0:T(8,128)(2,1)S(1)}, u32[]{:S(2)}, u32[]{:S(2)}) collective-permute-start(bf16[1024,128]{1,0:T(8,128)(2,1)S(1)} %get-tuple-element.49), channel_id=1, source_target_pairs={{0,2},{1,3},{2,4},{3,5},{4,6},{5,7},{6,8},{7,9},{8,10},{9,11},{10,... | collective-permute-start | bytes 786440 | tf_op jit(solution)/shard_map/ppermute | solution.py:28
  39.7 9.3 %collective-permute-start.7 = (bf16[1024,128]{1,0:T(8,128)(2,1)S(1)}, bf16[1024,128]{1,0:T(8,128)(2,1)S(1)}, u32[]{:S(2)}, u32[]{:S(2)}) collective-permute-start(bf16[1024,128]{1,0:T(8,128)(2,1)S(1)} %get-tuple-element.47.refs_1_), channel_id=1, source_target_pairs={{0,1},{1,0},{2,3},{3,2},{4,5},{5,4},{6,7},{7,6},{8,9},{9,8},{10,11... | collective-permute-start | bytes 786440 | tf_op jit(solution)/shard_map/ppermute | solution.py:28
  43.8 10.8 %collective-permute-start.9 = (bf16[1024,128]{1,0:T(8,128)(2,1)S(1)}, bf16[1024,128]{1,0:T(8,128)(2,1)S(1)}, u32[]{:S(2)}, u32[]{:S(2)}) collective-permute-start(bf16[1024,128]{1,0:T(8,128)(2,1)S(1)} %get-tuple-element.50.refs_1_), channel_id=1, source_target_pairs={{0,1},{1,0},{2,3},{3,2},{4,5},{5,4},{6,7},{7,6},{8,9},{9,8},{10,11... | collective-permute-start | bytes 786440 | tf_op jit(solution)/shard_map/ppermute | solution.py:28
  50.6 9.6 %collective-permute-start.11 = (bf16[1024,128]{1,0:T(8,128)(2,1)S(1)}, bf16[1024,128]{1,0:T(8,128)(2,1)S(1)}, u32[]{:S(2)}, u32[]{:S(2)}) collective-permute-start(bf16[1024,128]{1,0:T(8,128)(2,1)S(1)} %get-tuple-element.57.refs_0_), channel_id=1, source_target_pairs={{0,1},{1,0},{2,3},{3,2},{4,5},{5,4},{6,7},{7,6},{8,9},{9,8},{10,11... | collective-permute-start | bytes 786440 | tf_op jit(solution)/shard_map/ppermute | solution.py:28
  56.2 7.7 %collective-permute-start.10 = (bf16[1024,128]{1,0:T(8,128)(2,1)S(1)}, bf16[1024,128]{1,0:T(8,128)(2,1)S(1)}, u32[]{:S(2)}, u32[]{:S(2)}) collective-permute-start(bf16[1024,128]{1,0:T(8,128)(2,1)S(1)} %get-tuple-element.54.refs_0_), channel_id=1, source_target_pairs={{0,1},{1,0},{2,3},{3,2},{4,5},{5,4},{6,7},{7,6},{8,9},{9,8},{10,11... | collective-permute-start | bytes 786440 | tf_op jit(solution)/shard_map/ppermute | solution.py:28

commit v5 on v4

--- a/solution.py
+++ b/solution.py
@@ -10,6 +10,7 @@
 SUB = 2
 INNER = 2
 CHUNKS = 2
+EARLY = 1
 TILE = 256
 
 
@@ -33,10 +34,12 @@
     return (param - learn_rate * grad * lax.rsqrt(accum + tiny_eps), accum)
 
 
-def group_terms(term):
+def group_terms(term, loop_by=0):
     if lax.axis_size("grp") == 2:
-        return (term, moved(term, 0, 1))
-    return (lax.psum(term, "grp"),)
+        own = moved(term, loop_by, 0) if loop_by else term
+        return (own, moved(term, loop_by, 1))
+    total = lax.psum(term, "grp")
+    return (moved(total, loop_by, 0) if loop_by else total,)
 
 
 def item_step(items, accum, terms):
@@ -45,15 +48,15 @@
     return adagrad(items, accum.astype(jnp.float32), grad)
 
 
-def chunk_tile(half, items, rate):
+def chunk_tile(half, half_t, items, rate):
     item_half = items.astype(jnp.bfloat16)
     predicted = lax.dot_general(
         half, item_half, (((1,), (1,)), ((), ())), preferred_element_type=jnp.float32
     )
     rate = rate.astype(jnp.float32)
     resid = jnp.where(jnp.abs(rate) > 0.25, rate - predicted, 0.0).astype(jnp.bfloat16)
-    term = lax.dot_general(resid, half, (((0,), (0,)), ((), ())), preferred_element_type=jnp.float32)
-    return (-term).astype(jnp.bfloat16), jnp.dot(resid, item_half, preferred_element_type=jnp.float32)
+    term = jnp.dot(half_t, resid, preferred_element_type=jnp.float32)
+    return (-term).T.astype(jnp.bfloat16), jnp.dot(resid, item_half, preferred_element_type=jnp.float32)
 
 
 def params(mib=16):
@@ -70,13 +73,10 @@
 AWAY = pl.BlockSpec(memory_space=pltpu.HBM)
 
 
-def first_kernel(column, first, rate_hbm, items_hbm, *refs):
-    if first:
-        users_hbm, term_out, grad_out, users_ref, rate_ref, items_ref, sems = refs
-        load_users = pltpu.make_async_copy(users_hbm, users_ref, sems.at[2, 0])
-        load_users.start()
-    else:
-        users_ref, grad_ref, term_out, grad_out, rate_ref, items_ref, sems = refs
+def first_kernel(column, rate_hbm, items_hbm, users_hbm, term_out, grad_out, half_out, *scratch):
+    users_ref, rate_ref, items_ref, sems = scratch
+    load_users = pltpu.make_async_copy(users_hbm, users_ref, sems.at[2, 0])
+    load_users.start()
     tiles = range(term_out.shape[0] // TILE)
     loads = []
     for t in tiles:
@@ -89,41 +89,40 @@
         )
         for load in loads[-1]:
             load.start()
-    if first:
-        load_users.wait()
-        grad = shrink * users_ref[...]
-    else:
-        grad = grad_ref[...]
+    load_users.wait()
+    grad = shrink * users_ref[...]
     half = users_ref[...].astype(jnp.bfloat16)
+    half_t = half.T
+    half_out[...] = half
     for t in tiles:
         for load in loads[t]:
             load.wait()
-        term, part = chunk_tile(half, items_ref[t], rate_ref[t])
+        term, part = chunk_tile(half, half_t, items_ref[t], rate_ref[t])
         term_out[pl.ds(t * TILE, TILE), :] = term
         grad = grad - part
     grad_out[...] = grad
 
 
-def first_pass(ratings, rows, users, grad, items):
+def first_pass(ratings, rows, users, items):
     size, (n_users, rank) = rows.stop - rows.start, users.shape
-    first = grad is None
-    return pl.pallas_call(
-        functools.partial(first_kernel, rows.start, first),
+    return pl.pallas_call(
+        functools.partial(first_kernel, rows.start),
         out_shape=[
             jax.ShapeDtypeStruct((size, rank), jnp.bfloat16),
             jax.ShapeDtypeStruct(users.shape, jnp.float32),
+            jax.ShapeDtypeStruct(users.shape, jnp.bfloat16),
         ],
-        in_specs=[AWAY, AWAY, AWAY] if first else [AWAY, AWAY, WHOLE, WHOLE],
-        out_specs=[WHOLE] * 2,
-        scratch_shapes=([pltpu.VMEM(users.shape, jnp.float32)] if first else [])
-        + [
+        in_specs=[AWAY] * 3,
+        out_specs=[WHOLE] * 3,
+        scratch_shapes=[
+            pltpu.VMEM(users.shape, jnp.float32),
             pltpu.VMEM((size // TILE, n_users, TILE), jnp.bfloat16),
             pltpu.VMEM((size // TILE, TILE, rank), jnp.float32),
             pltpu.SemaphoreType.DMA((3, size // TILE)),
         ],
-        compiler_params=params(62 if first else 16),
+        compiler_params=params(62),
         cost_estimate=cost(n_users, size, rank),
-    )(ratings, items, users, *([] if first else [grad]))
+    )(ratings, items, users)
 
 
 def chunk_kernel(n_terms, sub_epoch, column, offset, rate_ref, half_ref, grad_ref, items_ref, *refs):
@@ -131,6 +130,7 @@
         accum_ref, *refs = refs
     term_refs, (term_out, grad_out, *updated) = refs[:n_terms], refs[n_terms:]
     half = half_ref[...]
+    half_t = half.T
     grad = grad_ref[...]
     for start in range(0, term_out.shape[0], TILE):
         at = pl.ds(start, TILE)
@@ -138,14 +138,14 @@
         items = items_ref[held, :]
         if n_terms:
             items, accum = item_step(items, accum_ref[held, :], [ref[at, :] for ref in term_refs])
-            updated[0][at, :] = items
-            updated[1][at, :] = accum
-        term_out[at, :], part = chunk_tile(half, items, rate_ref[sub_epoch, :, pl.ds(column + start, TILE)])
+            updated[0][at, :] = items.astype(updated[0].dtype)
+            updated[1][at, :] = accum.astype(updated[1].dtype)
+        term_out[at, :], part = chunk_tile(half, half_t, items, rate_ref[sub_epoch, :, pl.ds(column + start, TILE)])
         grad = grad - part
     grad_out[...] = grad
 
 
-def chunk_pass(ratings, sub_epoch, rows, half, grad, items, accum, terms):
+def chunk_pass(ratings, sub_epoch, rows, half, grad, items, accum, terms, kept):
     size, rank = rows.stop - rows.start, items.shape[1]
     offset = 0 if items.shape[0] == size else rows.start
     out_shape = [
@@ -154,7 +154,7 @@
     ]
     operands = [ratings, half, grad, items]
     if terms:
-        out_shape += [jax.ShapeDtypeStruct((size, rank), jnp.float32)] * 2
+        out_shape += [jax.ShapeDtypeStruct((size, rank), kept)] * 2
         operands += [accum, *terms]
     return pl.pallas_call(
         functools.partial(chunk_kernel, len(terms), sub_epoch, rows.start, offset),
@@ -169,8 +169,8 @@
 def parting_kernel(n_terms, items_ref, accum_ref, *refs):
     items, accum = item_step(items_ref[...], accum_ref[...], [ref[...] for ref in refs[:n_terms]])
     items_out, accum_out = refs[-2:]
-    items_out[...] = items.astype(jnp.bfloat16)
-    accum_out[...] = accum.astype(jnp.bfloat16)
+    items_out[...] = items.astype(items_out.dtype)
+    accum_out[...] = accum.astype(accum_out.dtype)
 
 
 def parting_step(items, accum, terms, before):
@@ -225,29 +225,32 @@
     terms = [()] * CHUNKS
     for step in range(SUB * INNER):
         sub_epoch = step // INNER
-        if step > 0 and step % INNER == 0:
-            before = []
-            for c in range(CHUNKS):
-                stepped, accum = parting_step(items[c], item_acc[c], terms[c], before)
-                items[c] = moved(stepped, 1, 0)
-                item_acc[c] = moved(accum, 1, 0)
-                terms[c] = ()
-                before = [stepped]
-        if step == 0:
-            grad_user = None
-        else:
+        early = EARLY if step % INNER == INNER - 1 and sub_epoch < SUB - 1 else 0
+        if step > 0:
             user_half = users.astype(jnp.bfloat16)
             grad_user = shrink * users
         for c in range(CHUNKS):
-            if step == 0:
-                term, grad_user = first_pass(ratings, rows[c], users, grad_user, items[c])
+            if step > 0 and step % INNER == 0 and c == EARLY:
+                before = [term] if c else []
+                for d in range(c, CHUNKS):
+                    items[d], item_acc[d] = parting_step(items[d], item_acc[d], terms[d], before)
+                    before = [items[d]]
+                    items[d] = moved(items[d], 1, 0)
+                    item_acc[d] = moved(item_acc[d], 1, 0)
+                    terms[d] = ()
+            if step == 0 and c == 0:
+                term, grad_user, user_half = first_pass(ratings, rows[c], users, items[c])
             else:
+                kept = jnp.bfloat16 if c < early else jnp.float32
                 term, grad_user, *updated = chunk_pass(
-                    ratings, sub_epoch, rows[c], user_half, grad_user, items[c], item_acc[c], terms[c]
+                    ratings, sub_epoch, rows[c], user_half, grad_user, items[c], item_acc[c], terms[c], kept
                 )
                 if updated:
                     items[c], item_acc[c] = updated
-            terms[c] = group_terms(term)
+            terms[c] = group_terms(term, 1 if c < early else 0)
+            if c < early:
+                items[c] = moved(items[c], 1, 0)
+                item_acc[c] = moved(item_acc[c], 1, 0)
         users, user_acc = adagrad(users, user_acc, grad_user)
     filled = []
     for c in range(CHUNKS):

time: 65.2 us -> 63.5 us (0.974)
  Pallas kernels: 19.3 us -> 15.6 us
  starting transfers between devices: 7.84 us -> 11.1 us
  waiting for transfers between devices: 32.5 us -> 30.4 us
  local copies, waits for them, and re-layouts: 3.16 us -> 4.07 us
    pallas_call x2 -> x1, Pallas kernels: 7.65 us -> 4.16 us  [first_pass(): pl.pallas_call(functools.partial(first_kernel, rows.start), out_shape=[ja...]
    ppermute x12 -> x13, starting transfers between devices: 7.84 us -> 11.1 us  [moved(): return lax.ppermute(shard, ('loop', 'grp'), pairs)]
    ppermute x12 -> x13, waiting for transfers between devices: 32.5 us -> 30.4 us  [moved(): return lax.ppermute(shard, ('loop', 'grp'), pairs)]
    unnamed x16 -> x18, local copies, waits for them, and re-layouts: 3.16 us -> 4.07 us
    pallas_call x6 -> x7, Pallas kernels: 9.43 us -> 9.4 us  [chunk_pass(): pl.pallas_call(functools.partial(chunk_kernel, len(terms), sub_epoch, row...]
  transfers between devices with their start and end apart: 12 -> 13, of which waited for: 10 -> 10; matrix products, arithmetic and copies ran while one was open for 2% -> 2% of each run, Pallas kernels for 22% -> 16%
where the time goes in v5:
time: 63.5 us; the launch traced here: 63.3 us
  waiting for transfers between devices  30.4 us (48%)
  Pallas kernels  15.6 us (25%)
  starting transfers between devices  11.1 us (17%)
  local copies, waits for them, and re-layouts  4.07 us (6%)
  other arithmetic  1.12 us (2%)
  between operations  0.96 us (2%)
    ppermute x13, waiting for transfers between devices, moved(): return lax.ppermute(shard, ('loop', 'grp'), pairs)  30.4 us
    ppermute x13, starting transfers between devices, moved(): return lax.ppermute(shard, ('loop', 'grp'), pairs)  11.1 us
    pallas_call x7, Pallas kernels, chunk_pass(): pl.pallas_call(functools.partial(chunk_kernel, len(terms), sub_epoch, row...  9.4 us
    pallas_call x1, Pallas kernels, first_pass(): pl.pallas_call(functools.partial(first_kernel, rows.start), out_shape=[ja...  4.16 us
    unnamed x18, local copies, waits for them, and re-layouts  4.07 us
    pallas_call x2, Pallas kernels, last_item_step(): pl.pallas_call(functools.partial(last_kernel, len(terms), rows.start), ou...  1.8 us
  transfers between devices with their start and end apart: 13, of which 10 were waited for; matrix products, arithmetic and copies ran while one was open for 2% of the time, Pallas kernels for 16%

profile of v5, /device:TPU:0, one launch (start us, length us, event | category | flops | bytes accessed | tf_op | source)
XLA Modules:
  0.0 63.3 jit_solution(6177504416681879071)
XLA Ops:
  0.7 4.2 %shard_map.68 = (bf16[1024,128]{1,0:T(8,128)(2,1)}, f32[512,128]{1,0:T(8,128)}, bf16[512,128]{1,0:T(8,128)(2,1)}) custom-call(bf16[2,512,2048]{2,1,0:T(8,128)(2,1)} %rate_ref.13, f32[2048,128]{1,0:T(8,128)} %items_ref.5, f32[512,128]{1,0:T(8,128)} %users_hbm.1), custom_call_target="tpu_custom_call" | custom-call | flops 402653184 | bytes 1048576 | tf_op jit(solution)/shard_map/pallas_call | solution.py:108
  4.8 3.0 %collective-permute-start = (bf16[1024,128]{1,0:T(8,128)(2,1)}, bf16[1024,128]{1,0:T(8,128)(2,1)S(1)}, u32[]{:S(2)}, u32[]{:S(2)}) collective-permute-start(bf16[1024,128]{1,0:T(8,128)(2,1)} %get-tuple-element.34.refs_1_), channel_id=1, source_target_pairs={{0,1},{1,0},{2,3},{3,2},{4,5},{5,4},{6,7},{7,6},{8,9},{9,8},{10,11... | collective-permute-start | bytes 786440 | tf_op jit(solution)/shard_map/ppermute | solution.py:29
  7.8 2.2 %copy-done = bf16[2,512,2048]{2,1,0:T(8,128)(2,1)S(1)} copy-done((bf16[2,512,2048]{2,1,0:T(8,128)(2,1)S(1)}, bf16[2,512,2048]{2,1,0:T(8,128)(2,1)}, u32[]{:S(2)}) %copy-start) | copy-done | bytes 4194328
  10.0 0.9 %copy-done.5 = f32[512,128]{1,0:T(8,128)S(1)} copy-done((f32[512,128]{1,0:T(8,128)S(1)}, f32[512,128]{1,0:T(8,128)}, u32[]{:S(2)}) %copy-start.5) | copy-done | bytes 262168
  11.0 0.9 %copy-done.6 = bf16[512,128]{1,0:T(8,128)(2,1)S(1)} copy-done((bf16[512,128]{1,0:T(8,128)(2,1)S(1)}, bf16[512,128]{1,0:T(8,128)(2,1)}, u32[]{:S(2)}) %copy-start.6) | copy-done | bytes 131096
  11.9 1.3 %shard_map.69 = (bf16[1024,128]{1,0:T(8,128)(2,1)S(1)}, f32[512,128]{1,0:T(8,128)S(1)}) custom-call(bf16[2,512,2048]{2,1,0:T(8,128)(2,1)S(1)} %copy-done, bf16[512,128]{1,0:T(8,128)(2,1)S(1)} %copy-done.6, f32[512,128]{1,0:T(8,128)S(1)} %copy-done.5, f32[2048,128]{1,0:T(8,128)S(1)} %copy-done.2), custom_call_target="tpu_custom_call" | custom-call | flops 402653184 | bytes 1048576 | tf_op jit(solution)/shard_map/pallas_call | solution.py:159
  13.4 1.0 %collective-permute-done.refs_2_ = bf16[1024,128]{1,0:T(8,128)(2,1)S(1)} collective-permute-done((bf16[1024,128]{1,0:T(8,128)(2,1)}, bf16[1024,128]{1,0:T(8,128)(2,1)S(1)}, u32[]{:S(2)}, u32[]{:S(2)}) %collective-permute-start) | collective-permute-done | bytes 262176 | tf_op jit(solution)/shard_map/ppermute | solution.py:29
  14.4 1.4 %shard_map.70 = (bf16[1024,128]{1,0:T(8,128)(2,1)S(1)}, f32[512,128]{1,0:T(8,128)S(1)}, bf16[1024,128]{1,0:T(8,128)(2,1)S(1)}, bf16[1024,128]{1,0:T(8,128)(2,1)S(1)}) custom-call(bf16[2,512,2048]{2,1,0:T(8,128)(2,1)S(1)} %copy-done, bf16[512,128]{1,0:T(8,128)(2,1)S(1)} %convert_element_type.9.half_ref, f32[512,128]{1,0:T(8,128)S(1)} %get-tuple-element.63.grad_ref, ...), custom_call_target="tpu_custom_call" | custom-call | flops 402653184 | bytes 1048576 | tf_op jit(solution)/shard_map/pallas_call | solution.py:159
  15.8 3.1 %collective-permute-start.5 = (bf16[1024,128]{1,0:T(8,128)(2,1)S(1)}, bf16[1024,128]{1,0:T(8,128)(2,1)S(1)}, u32[]{:S(2)}, u32[]{:S(2)}) collective-permute-start(bf16[1024,128]{1,0:T(8,128)(2,1)S(1)} %get-tuple-element.40), channel_id=1, source_target_pairs={{0,3},{1,2},{2,5},{3,4},{4,7},{5,6},{6,9},{7,8},{8,11},{9,10},{10,... | collective-permute-start | bytes 786440 | tf_op jit(solution)/shard_map/ppermute | solution.py:29
  18.9 1.6 %collective-permute-start.3 = (bf16[1024,128]{1,0:T(8,128)(2,1)S(1)}, bf16[1024,128]{1,0:T(8,128)(2,1)S(1)}, u32[]{:S(2)}, u32[]{:S(2)}) collective-permute-start(bf16[1024,128]{1,0:T(8,128)(2,1)S(1)} %get-tuple-element.39), channel_id=1, source_target_pairs={{0,2},{1,3},{2,4},{3,5},{4,6},{5,7},{6,8},{7,9},{8,10},{9,11},{10,... | collective-permute-start | bytes 786440 | tf_op jit(solution)/shard_map/ppermute | solution.py:29
  20.5 1.4 %collective-permute-done.1.refs_2_ = bf16[1024,128]{1,0:T(8,128)(2,1)S(1)} collective-permute-done((bf16[1024,128]{1,0:T(8,128)(2,1)S(1)}, bf16[1024,128]{1,0:T(8,128)(2,1)S(1)}, u32[]{:S(2)}, u32[]{:S(2)}) %collective-permute-start.1) | collective-permute-done | bytes 262176 | tf_op jit(solution)/shard_map/ppermute | solution.py:29
  21.9 1.4 %shard_map.71 = (bf16[1024,128]{1,0:T(8,128)(2,1)S(1)}, f32[512,128]{1,0:T(8,128)S(1)}, f32[1024,128]{1,0:T(8,128)S(1)}, f32[1024,128]{1,0:T(8,128)S(1)}) custom-call(bf16[2,512,2048]{2,1,0:T(8,128)(2,1)S(1)} %copy-done, bf16[512,128]{1,0:T(8,128)(2,1)S(1)} %convert_element_type.9.half_ref, f32[512,128]{1,0:T(8,128)S(1)} %get-tuple-element.35.grad_ref, ...), custom_call_target="tpu_custom_call" | custom-call | flops 402653184 | bytes 1048576 | tf_op jit(solution)/shard_map/pallas_call | solution.py:159
  24.3 5.7 %collective-permute-done.5.refs_2_ = bf16[1024,128]{1,0:T(8,128)(2,1)S(1)} collective-permute-done((bf16[1024,128]{1,0:T(8,128)(2,1)S(1)}, bf16[1024,128]{1,0:T(8,128)(2,1)S(1)}, u32[]{:S(2)}, u32[]{:S(2)}) %collective-permute-start.5) | collective-permute-done | bytes 262176 | tf_op jit(solution)/shard_map/ppermute | solution.py:29
  30.0 1.5 %collective-permute-done.2.items_ref = bf16[1024,128]{1,0:T(8,128)(2,1)S(1)} collective-permute-done((bf16[1024,128]{1,0:T(8,128)(2,1)S(1)}, bf16[1024,128]{1,0:T(8,128)(2,1)S(1)}, u32[]{:S(2)}, u32[]{:S(2)}) %collective-permute-start.2) | collective-permute-done | bytes 262176 | tf_op jit(solution)/shard_map/ppermute | solution.py:29
  31.5 2.8 %collective-permute-done.3.refs_0_ = bf16[1024,128]{1,0:T(8,128)(2,1)S(1)} collective-permute-done((bf16[1024,128]{1,0:T(8,128)(2,1)S(1)}, bf16[1024,128]{1,0:T(8,128)(2,1)S(1)}, u32[]{:S(2)}, u32[]{:S(2)}) %collective-permute-start.3) | collective-permute-done | bytes 262176 | tf_op jit(solution)/shard_map/ppermute | solution.py:29
  34.3 1.4 %shard_map.72 = (bf16[1024,128]{1,0:T(8,128)(2,1)S(1)}, f32[512,128]{1,0:T(8,128)S(1)}, f32[1024,128]{1,0:T(8,128)S(1)}, f32[1024,128]{1,0:T(8,128)S(1)}) custom-call(bf16[2,512,2048]{2,1,0:T(8,128)(2,1)S(1)} %copy-done, bf16[512,128]{1,0:T(8,128)(2,1)S(1)} %convert_element_type.10.half_ref, f32[512,128]{1,0:T(8,128)S(1)} %get-tuple-element.60.grad_ref, ...), custom_call_target="tpu_custom_call" | custom-call | flops 402653184 | bytes 1048576 | tf_op jit(solution)/shard_map/pallas_call | solution.py:159
  36.6 7.9 %collective-permute-done.7.items_ref = bf16[1024,128]{1,0:T(8,128)(2,1)S(1)} collective-permute-done((bf16[1024,128]{1,0:T(8,128)(2,1)S(1)}, bf16[1024,128]{1,0:T(8,128)(2,1)S(1)}, u32[]{:S(2)}, u32[]{:S(2)}) %collective-permute-start.7) | collective-permute-done | bytes 262176 | tf_op jit(solution)/shard_map/ppermute | solution.py:29
  44.5 1.3 %shard_map.74 = (bf16[1024,128]{1,0:T(8,128)(2,1)S(1)}, f32[512,128]{1,0:T(8,128)S(1)}) custom-call(bf16[2,512,2048]{2,1,0:T(8,128)(2,1)S(1)} %copy-done.1, bf16[512,128]{1,0:T(8,128)(2,1)S(1)} %convert_element_type.10.half_ref, f32[512,128]{1,0:T(8,128)S(1)} %get-tuple-element.41.grad_ref, bf16[1024,128]{1,0:T(8,128)(2,1)S(1)} %collective-permute-done.7.items_ref), custom_call_target="tpu_custom_call" | custom-call | flops 402653184 | bytes 1048576 | tf_op jit(solution)/shard_map/pallas_call | solution.py:159
  46.4 1.4 %shard_map.75 = (bf16[1024,128]{1,0:T(8,128)(2,1)S(1)}, f32[512,128]{1,0:T(8,128)S(1)}, f32[1024,128]{1,0:T(8,128)S(1)}, f32[1024,128]{1,0:T(8,128)S(1)}) custom-call(bf16[2,512,2048]{2,1,0:T(8,128)(2,1)S(1)} %copy-done.1, bf16[512,128]{1,0:T(8,128)(2,1)S(1)} %get-tuple-element.66.half_ref, f32[512,128]{1,0:T(8,128)S(1)} %get-tuple-element.65.grad_ref, ...), custom_call_target="tpu_custom_call" | custom-call | flops 402653184 | bytes 1048576 | tf_op jit(solution)/shard_map/pallas_call | solution.py:159
  47.8 1.6 %collective-permute-start.12 = (bf16[1024,128]{1,0:T(8,128)(2,1)S(1)}, bf16[1024,128]{1,0:T(8,128)(2,1)S(1)}, u32[]{:S(2)}, u32[]{:S(2)}) collective-permute-start(bf16[1024,128]{1,0:T(8,128)(2,1)S(1)} %get-tuple-element.59.refs_0_), channel_id=1, source_target_pairs={{0,1},{1,0},{2,3},{3,2},{4,5},{5,4},{6,7},{7,6},{8,9},{9,8},{10,11... | collective-permute-start | bytes 786440 | tf_op jit(solution)/shard_map/ppermute | solution.py:29
  49.4 5.0 %collective-permute-done.10.refs_2_ = bf16[1024,128]{1,0:T(8,128)(2,1)S(1)} collective-permute-done((bf16[1024,128]{1,0:T(8,128)(2,1)S(1)}, bf16[1024,128]{1,0:T(8,128)(2,1)S(1)}, u32[]{:S(2)}, u32[]{:S(2)}) %collective-permute-start.10) | collective-permute-done | bytes 262176 | tf_op jit(solution)/shard_map/ppermute | solution.py:29
  54.4 1.4 %shard_map.76 = (bf16[1024,128]{1,0:T(8,128)(2,1)S(1)}, f32[512,128]{1,0:T(8,128)S(1)}, f32[1024,128]{1,0:T(8,128)S(1)}, f32[1024,128]{1,0:T(8,128)S(1)}) custom-call(bf16[2,512,2048]{2,1,0:T(8,128)(2,1)S(1)} %copy-done.1, bf16[512,128]{1,0:T(8,128)(2,1)S(1)} %get-tuple-element.66.half_ref, f32[512,128]{1,0:T(8,128)S(1)} %get-tuple-element.50.grad_ref, ...), custom_call_target="tpu_custom_call" | custom-call | flops 402653184 | bytes 1048576 | tf_op jit(solution)/shard_map/pallas_call | solution.py:159
  56.2 1.6 %collective-permute-done.12.refs_1_ = bf16[1024,128]{1,0:T(8,128)(2,1)S(1)} collective-permute-done((bf16[1024,128]{1,0:T(8,128)(2,1)S(1)}, bf16[1024,128]{1,0:T(8,128)(2,1)S(1)}, u32[]{:S(2)}, u32[]{:S(2)}) %collective-permute-start.12) | collective-permute-done | bytes 262176 | tf_op jit(solution)/shard_map/ppermute | solution.py:29
  59.6 2.7 %collective-permute-done.11.refs_1_ = bf16[1024,128]{1,0:T(8,128)(2,1)S(1)} collective-permute-done((bf16[1024,128]{1,0:T(8,128)(2,1)S(1)}, bf16[1024,128]{1,0:T(8,128)(2,1)S(1)}, u32[]{:S(2)}, u32[]{:S(2)}) %collective-permute-start.11) | collective-permute-done | bytes 262176 | tf_op jit(solution)/shard_map/ppermute | solution.py:29
  (37 shorter events, 5.9 us)
Async XLA Ops:
  0.6 7.2 %copy-start.2 = (f32[2048,128]{1,0:T(8,128)S(1)}, f32[2048,128]{1,0:T(8,128)}, u32[]{:S(2)}) copy-start(f32[2048,128]{1,0:T(8,128)} %items_ref.5) | copy-start | bytes 3145732
  0.6 12.6 %copy-start.7 = (f32[512,128]{1,0:T(8,128)S(1)}, f32[512,128]{1,0:T(8,128)}, u32[]{:S(2)}) copy-start(f32[512,128]{1,0:T(8,128)} %param.7) | copy-start | bytes 786436
  0.7 12.6 %copy-start.8 = (f32[512,128]{1,0:T(8,128)S(1)}, f32[512,128]{1,0:T(8,128)}, u32[]{:S(2)}) copy-start(f32[512,128]{1,0:T(8,128)} %users_hbm.1) | copy-start | bytes 786436
  4.8 9.5 %collective-permute-start = (bf16[1024,128]{1,0:T(8,128)(2,1)}, bf16[1024,128]{1,0:T(8,128)(2,1)S(1)}, u32[]{:S(2)}, u32[]{:S(2)}) collective-permute-start(bf16[1024,128]{1,0:T(8,128)(2,1)} %get-tuple-element.34.refs_1_), channel_id=1, source_target_pairs={{0,1},{1,0},{2,3},{3,2},{4,5},{5,4},{6,7},{7,6},{8,9},{9,8},{10,11... | collective-permute-start | bytes 786440 | tf_op jit(solution)/shard_map/ppermute | solution.py:29
  7.8 2.2 %copy-start = (bf16[2,512,2048]{2,1,0:T(8,128)(2,1)S(1)}, bf16[2,512,2048]{2,1,0:T(8,128)(2,1)}, u32[]{:S(2)}) copy-start(bf16[2,512,2048]{2,1,0:T(8,128)(2,1)} %rate_ref.13) | copy-start | bytes 12582916
  10.0 0.9 %copy-start.5 = (f32[512,128]{1,0:T(8,128)S(1)}, f32[512,128]{1,0:T(8,128)}, u32[]{:S(2)}) copy-start(f32[512,128]{1,0:T(8,128)} %get-tuple-element.32.grad_ref) | copy-start | bytes 786436
  11.0 0.9 %copy-start.6 = (bf16[512,128]{1,0:T(8,128)(2,1)S(1)}, bf16[512,128]{1,0:T(8,128)(2,1)}, u32[]{:S(2)}) copy-start(bf16[512,128]{1,0:T(8,128)(2,1)} %get-tuple-element.31.half_ref) | copy-start | bytes 393220
  11.9 2.5 %copy-start.3 = (f32[2048,128]{1,0:T(8,128)S(1)}, f32[2048,128]{1,0:T(8,128)}, u32[]{:S(2)}) copy-start(f32[2048,128]{1,0:T(8,128)} %refs_0_.3) | copy-start | bytes 3145732
  11.9 2.5 %copy-start.4 = (bf16[1024,128]{1,0:T(8,128)(2,1)S(1)}, bf16[1024,128]{1,0:T(8,128)(2,1)}, u32[]{:S(2)}) copy-start(bf16[1024,128]{1,0:T(8,128)(2,1)} %get-tuple-element.34.refs_1_) | copy-start | bytes 786436
  13.2 8.7 %collective-permute-start.1 = (bf16[1024,128]{1,0:T(8,128)(2,1)S(1)}, bf16[1024,128]{1,0:T(8,128)(2,1)S(1)}, u32[]{:S(2)}, u32[]{:S(2)}) collective-permute-start(bf16[1024,128]{1,0:T(8,128)(2,1)S(1)} %get-tuple-element.36.refs_1_), channel_id=1, source_target_pairs={{0,1},{1,0},{2,3},{3,2},{4,5},{5,4},{6,7},{7,6},{8,9},{9,8},{10,11... | collective-permute-start | bytes 786440 | tf_op jit(solution)/shard_map/ppermute | solution.py:29
  15.7 8.5 %collective-permute-start.4 = (bf16[1024,128]{1,0:T(8,128)(2,1)S(1)}, bf16[1024,128]{1,0:T(8,128)(2,1)S(1)}, u32[]{:S(2)}, u32[]{:S(2)}) collective-permute-start(bf16[1024,128]{1,0:T(8,128)(2,1)S(1)} %get-tuple-element.40), channel_id=1, source_target_pairs={{0,2},{1,3},{2,4},{3,5},{4,6},{5,7},{6,8},{7,9},{8,10},{9,11},{10,... | collective-permute-start | bytes 786440 | tf_op jit(solution)/shard_map/ppermute | solution.py:29
  15.8 14.2 %collective-permute-start.5 = (bf16[1024,128]{1,0:T(8,128)(2,1)S(1)}, bf16[1024,128]{1,0:T(8,128)(2,1)S(1)}, u32[]{:S(2)}, u32[]{:S(2)}) collective-permute-start(bf16[1024,128]{1,0:T(8,128)(2,1)S(1)} %get-tuple-element.40), channel_id=1, source_target_pairs={{0,3},{1,2},{2,5},{3,4},{4,7},{5,6},{6,9},{7,8},{8,11},{9,10},{10,... | collective-permute-start | bytes 786440 | tf_op jit(solution)/shard_map/ppermute | solution.py:29
  18.8 12.6 %collective-permute-start.2 = (bf16[1024,128]{1,0:T(8,128)(2,1)S(1)}, bf16[1024,128]{1,0:T(8,128)(2,1)S(1)}, u32[]{:S(2)}, u32[]{:S(2)}) collective-permute-start(bf16[1024,128]{1,0:T(8,128)(2,1)S(1)} %get-tuple-element.38), channel_id=1, source_target_pairs={{0,2},{1,3},{2,4},{3,5},{4,6},{5,7},{6,8},{7,9},{8,10},{9,11},{10,... | collective-permute-start | bytes 786440 | tf_op jit(solution)/shard_map/ppermute | solution.py:29
  18.9 15.4 %collective-permute-start.3 = (bf16[1024,128]{1,0:T(8,128)(2,1)S(1)}, bf16[1024,128]{1,0:T(8,128)(2,1)S(1)}, u32[]{:S(2)}, u32[]{:S(2)}) collective-permute-start(bf16[1024,128]{1,0:T(8,128)(2,1)S(1)} %get-tuple-element.39), channel_id=1, source_target_pairs={{0,2},{1,3},{2,4},{3,5},{4,6},{5,7},{6,8},{7,9},{8,10},{9,11},{10,... | collective-permute-start | bytes 786440 | tf_op jit(solution)/shard_map/ppermute | solution.py:29
  23.2 12.4 %collective-permute-start.6 = (bf16[1024,128]{1,0:T(8,128)(2,1)S(1)}, bf16[1024,128]{1,0:T(8,128)(2,1)S(1)}, u32[]{:S(2)}, u32[]{:S(2)}) collective-permute-start(bf16[1024,128]{1,0:T(8,128)(2,1)S(1)} %get-tuple-element.44.refs_0_), channel_id=1, source_target_pairs={{0,1},{1,0},{2,3},{3,2},{4,5},{5,4},{6,7},{7,6},{8,9},{9,8},{10,11... | collective-permute-start | bytes 786440 | tf_op jit(solution)/shard_map/ppermute | solution.py:29
  23.4 21.1 %copy-start.1 = (bf16[2,512,2048]{2,1,0:T(8,128)(2,1)S(1)}, bf16[2,512,2048]{2,1,0:T(8,128)(2,1)}, u32[]{:S(2)}) copy-start(bf16[2,512,2048]{2,1,0:T(8,128)(2,1)} %rate_ref.13) | copy-start | bytes 12582916
  35.9 8.5 %collective-permute-start.7 = (bf16[1024,128]{1,0:T(8,128)(2,1)S(1)}, bf16[1024,128]{1,0:T(8,128)(2,1)S(1)}, u32[]{:S(2)}, u32[]{:S(2)}) collective-permute-start(bf16[1024,128]{1,0:T(8,128)(2,1)S(1)} %get-tuple-element.46), channel_id=1, source_target_pairs={{0,2},{1,3},{2,4},{3,5},{4,6},{5,7},{6,8},{7,9},{8,10},{9,11},{10,... | collective-permute-start | bytes 786440 | tf_op jit(solution)/shard_map/ppermute | solution.py:29
  36.0 10.4 %collective-permute-start.8 = (bf16[1024,128]{1,0:T(8,128)(2,1)S(1)}, bf16[1024,128]{1,0:T(8,128)(2,1)S(1)}, u32[]{:S(2)}, u32[]{:S(2)}) collective-permute-start(bf16[1024,128]{1,0:T(8,128)(2,1)S(1)} %get-tuple-element.45.refs_2_.refs_1_), channel_id=1, source_target_pairs={{0,1},{1,0},{2,3},{3,2},{4,5},{5,4},{6,7},{7,6},{8,9},{9,8},{10,11... | collective-permute-start | bytes 786440 | tf_op jit(solution)/shard_map/ppermute | solution.py:29
  36.6 12.8 %collective-permute-start.9 = (bf16[1024,128]{1,0:T(8,128)(2,1)S(1)}, bf16[1024,128]{1,0:T(8,128)(2,1)S(1)}, u32[]{:S(2)}, u32[]{:S(2)}) collective-permute-start(bf16[1024,128]{1,0:T(8,128)(2,1)S(1)} %get-tuple-element.51), channel_id=1, source_target_pairs={{0,2},{1,3},{2,4},{3,5},{4,6},{5,7},{6,8},{7,9},{8,10},{9,11},{10,... | collective-permute-start | bytes 786440 | tf_op jit(solution)/shard_map/ppermute | solution.py:29
  45.8 8.6 %collective-permute-start.10 = (bf16[1024,128]{1,0:T(8,128)(2,1)S(1)}, bf16[1024,128]{1,0:T(8,128)(2,1)S(1)}, u32[]{:S(2)}, u32[]{:S(2)}) collective-permute-start(bf16[1024,128]{1,0:T(8,128)(2,1)S(1)} %get-tuple-element.52.refs_1_), channel_id=1, source_target_pairs={{0,1},{1,0},{2,3},{3,2},{4,5},{5,4},{6,7},{7,6},{8,9},{9,8},{10,11... | collective-permute-start | bytes 786440 | tf_op jit(solution)/shard_map/ppermute | solution.py:29
  47.8 10.0 %collective-permute-start.12 = (bf16[1024,128]{1,0:T(8,128)(2,1)S(1)}, bf16[1024,128]{1,0:T(8,128)(2,1)S(1)}, u32[]{:S(2)}, u32[]{:S(2)}) collective-permute-start(bf16[1024,128]{1,0:T(8,128)(2,1)S(1)} %get-tuple-element.59.refs_0_), channel_id=1, source_target_pairs={{0,1},{1,0},{2,3},{3,2},{4,5},{5,4},{6,7},{7,6},{8,9},{9,8},{10,11... | collective-permute-start | bytes 786440 | tf_op jit(solution)/shard_map/ppermute | solution.py:29
  55.8 6.4 %collective-permute-start.11 = (bf16[1024,128]{1,0:T(8,128)(2,1)S(1)}, bf16[1024,128]{1,0:T(8,128)(2,1)S(1)}, u32[]{:S(2)}, u32[]{:S(2)}) collective-permute-start(bf16[1024,128]{1,0:T(8,128)(2,1)S(1)} %get-tuple-element.56.refs_0_), channel_id=1, source_target_pairs={{0,1},{1,0},{2,3},{3,2},{4,5},{5,4},{6,7},{7,6},{8,9},{9,8},{10,11... | collective-permute-start | bytes 786440 | tf_op jit(solution)/shard_map/ppermute | solution.py:29

commit v6 on v5

--- a/solution.py
+++ b/solution.py
@@ -10,7 +10,6 @@
 SUB = 2
 INNER = 2
 CHUNKS = 2
-EARLY = 1
 TILE = 256
 
 
@@ -34,12 +33,10 @@
     return (param - learn_rate * grad * lax.rsqrt(accum + tiny_eps), accum)
 
 
-def group_terms(term, loop_by=0):
+def group_terms(term):
     if lax.axis_size("grp") == 2:
-        own = moved(term, loop_by, 0) if loop_by else term
-        return (own, moved(term, loop_by, 1))
-    total = lax.psum(term, "grp")
-    return (moved(total, loop_by, 0) if loop_by else total,)
+        return (term, moved(term, 0, 1))
+    return (lax.psum(term, "grp"),)
 
 
 def item_step(items, accum, terms):
@@ -125,9 +122,12 @@
     )(ratings, items, users)
 
 
-def chunk_kernel(n_terms, sub_epoch, column, offset, rate_ref, half_ref, grad_ref, items_ref, *refs):
+def chunk_kernel(n_terms, leaves, sub_epoch, column, offset, rate_ref, half_ref, grad_ref, items_ref, *refs):
     if n_terms:
         accum_ref, *refs = refs
+    if leaves:
+        leaving_ref, *refs, leaving_out = refs
+        leaving_out[...] = leaving_ref[...]
     term_refs, (term_out, grad_out, *updated) = refs[:n_terms], refs[n_terms:]
     half = half_ref[...]
     half_t = half.T
@@ -138,14 +138,14 @@
         items = items_ref[held, :]
         if n_terms:
             items, accum = item_step(items, accum_ref[held, :], [ref[at, :] for ref in term_refs])
-            updated[0][at, :] = items.astype(updated[0].dtype)
-            updated[1][at, :] = accum.astype(updated[1].dtype)
+            updated[0][at, :] = items
+            updated[1][at, :] = accum
         term_out[at, :], part = chunk_tile(half, half_t, items, rate_ref[sub_epoch, :, pl.ds(column + start, TILE)])
         grad = grad - part
     grad_out[...] = grad
 
 
-def chunk_pass(ratings, sub_epoch, rows, half, grad, items, accum, terms, kept):
+def chunk_pass(ratings, sub_epoch, rows, half, grad, items, accum, terms, leaving=()):
     size, rank = rows.stop - rows.start, items.shape[1]
     offset = 0 if items.shape[0] == size else rows.start
     out_shape = [
@@ -154,10 +154,12 @@
     ]
     operands = [ratings, half, grad, items]
     if terms:
-        out_shape += [jax.ShapeDtypeStruct((size, rank), kept)] * 2
+        out_shape += [jax.ShapeDtypeStruct((size, rank), jnp.float32)] * 2
         operands += [accum, *terms]
-    return pl.pallas_call(
-        functools.partial(chunk_kernel, len(terms), sub_epoch, rows.start, offset),
+    operands += leaving
+    out_shape += [jax.ShapeDtypeStruct(array.shape, array.dtype) for array in leaving]
+    return pl.pallas_call(
+        functools.partial(chunk_kernel, len(terms), len(leaving), sub_epoch, rows.start, offset),
         out_shape=out_shape,
         in_specs=[WHOLE] * len(operands),
         out_specs=[WHOLE] * len(out_shape),
@@ -225,32 +227,30 @@
     terms = [()] * CHUNKS
     for step in range(SUB * INNER):
         sub_epoch = step // INNER
-        early = EARLY if step % INNER == INNER - 1 and sub_epoch < SUB - 1 else 0
+        rotates = step > 0 and step % INNER == 0
+        if rotates:
+            before = []
+            for c in range(CHUNKS):
+                items[c], item_acc[c] = parting_step(items[c], item_acc[c], terms[c], before)
+                before = [items[c]]
+                items[c] = moved(items[c], 1, 0)
+                terms[c] = ()
         if step > 0:
             user_half = users.astype(jnp.bfloat16)
             grad_user = shrink * users
         for c in range(CHUNKS):
-            if step > 0 and step % INNER == 0 and c == EARLY:
-                before = [term] if c else []
-                for d in range(c, CHUNKS):
-                    items[d], item_acc[d] = parting_step(items[d], item_acc[d], terms[d], before)
-                    before = [items[d]]
-                    items[d] = moved(items[d], 1, 0)
-                    item_acc[d] = moved(item_acc[d], 1, 0)
-                    terms[d] = ()
             if step == 0 and c == 0:
                 term, grad_user, user_half = first_pass(ratings, rows[c], users, items[c])
             else:
-                kept = jnp.bfloat16 if c < early else jnp.float32
                 term, grad_user, *updated = chunk_pass(
-                    ratings, sub_epoch, rows[c], user_half, grad_user, items[c], item_acc[c], terms[c], kept
+                    ratings, sub_epoch, rows[c], user_half, grad_user, items[c], item_acc[c], terms[c],
+                    [item_acc[c]] if rotates else [],
                 )
-                if updated:
+                if rotates:
+                    item_acc[c] = moved(updated[0], 1, 0)
+                elif updated:
                     items[c], item_acc[c] = updated
-            terms[c] = group_terms(term, 1 if c < early else 0)
-            if c < early:
-                items[c] = moved(items[c], 1, 0)
-                item_acc[c] = moved(item_acc[c], 1, 0)
+            terms[c] = group_terms(term)
         users, user_acc = adagrad(users, user_acc, grad_user)
     filled = []
     for c in range(CHUNKS):

time: 63.5 us -> 63.5 us (level)
  starting transfers between devices: 11.1 us -> 7.28 us
  waiting for transfers between devices: 30.4 us -> 34.1 us
    ppermute x13 -> x12, starting transfers between devices: 11.1 us -> 7.28 us  [moved(): return lax.ppermute(shard, ('loop', 'grp'), pairs)]
    ppermute x13 -> x12, waiting for transfers between devices: 30.4 us -> 34.1 us  [moved(): return lax.ppermute(shard, ('loop', 'grp'), pairs)]
  transfers between devices with their start and end apart: 13 -> 12, of which waited for: 10 -> 11; matrix products, arithmetic and copies ran while one was open for 2% -> 2% of each run, Pallas kernels for 16% -> 17%
where the time goes in v6:
time: 63.5 us; the launch traced here: 63.3 us
  waiting for transfers between devices  34.1 us (54%)
  Pallas kernels  15.8 us (25%)
  starting transfers between devices  7.28 us (11%)
  local copies, waits for them, and re-layouts  4.07 us (6%)
  other arithmetic  1.12 us (2%)
  between operations  0.96 us (2%)
    ppermute x12, waiting for transfers between devices, moved(): return lax.ppermute(shard, ('loop', 'grp'), pairs)  34.1 us
    pallas_call x7, Pallas kernels, chunk_pass(): pl.pallas_call(functools.partial(chunk_kernel, len(terms), len(leaving),...  9.38 us
    ppermute x12, starting transfers between devices, moved(): return lax.ppermute(shard, ('loop', 'grp'), pairs)  7.28 us
    pallas_call x1, Pallas kernels, first_pass(): pl.pallas_call(functools.partial(first_kernel, rows.start), out_shape=[ja...  4.16 us
    unnamed x18, local copies, waits for them, and re-layouts  4.07 us
    pallas_call x2, Pallas kernels, last_item_step(): pl.pallas_call(functools.partial(last_kernel, len(terms), rows.start), ou...  1.8 us
  transfers between devices with their start and end apart: 12, of which 11 were waited for; matrix products, arithmetic and copies ran while one was open for 2% of the time, Pallas kernels for 17%

profile of v6, /device:TPU:0, one launch (start us, length us, event | category | flops | bytes accessed | tf_op | source)
XLA Modules:
  0.0 63.3 jit_solution(6325892227542657065)
XLA Ops:
  0.7 4.2 %shard_map.68 = (bf16[1024,128]{1,0:T(8,128)(2,1)}, f32[512,128]{1,0:T(8,128)}, bf16[512,128]{1,0:T(8,128)(2,1)}) custom-call(bf16[2,512,2048]{2,1,0:T(8,128)(2,1)} %rate_ref.13, f32[2048,128]{1,0:T(8,128)} %items_ref.5, f32[512,128]{1,0:T(8,128)} %users_hbm.1), custom_call_target="tpu_custom_call" | custom-call | flops 402653184 | bytes 1048576 | tf_op jit(solution)/shard_map/pallas_call | solution.py:105
  4.8 3.0 %collective-permute-start = (bf16[1024,128]{1,0:T(8,128)(2,1)}, bf16[1024,128]{1,0:T(8,128)(2,1)S(1)}, u32[]{:S(2)}, u32[]{:S(2)}) collective-permute-start(bf16[1024,128]{1,0:T(8,128)(2,1)} %get-tuple-element.36.refs_1_), channel_id=1, source_target_pairs={{0,1},{1,0},{2,3},{3,2},{4,5},{5,4},{6,7},{7,6},{8,9},{9,8},{10,11... | collective-permute-start | bytes 786440 | tf_op jit(solution)/shard_map/ppermute | solution.py:28
  7.8 2.2 %copy-done = bf16[2,512,2048]{2,1,0:T(8,128)(2,1)S(1)} copy-done((bf16[2,512,2048]{2,1,0:T(8,128)(2,1)S(1)}, bf16[2,512,2048]{2,1,0:T(8,128)(2,1)}, u32[]{:S(2)}) %copy-start) | copy-done | bytes 4194328
  10.0 0.9 %copy-done.5 = f32[512,128]{1,0:T(8,128)S(1)} copy-done((f32[512,128]{1,0:T(8,128)S(1)}, f32[512,128]{1,0:T(8,128)}, u32[]{:S(2)}) %copy-start.5) | copy-done | bytes 262168
  11.0 0.9 %copy-done.6 = bf16[512,128]{1,0:T(8,128)(2,1)S(1)} copy-done((bf16[512,128]{1,0:T(8,128)(2,1)S(1)}, bf16[512,128]{1,0:T(8,128)(2,1)}, u32[]{:S(2)}) %copy-start.6) | copy-done | bytes 131096
  11.9 1.3 %shard_map.69 = (bf16[1024,128]{1,0:T(8,128)(2,1)S(1)}, f32[512,128]{1,0:T(8,128)S(1)}) custom-call(bf16[2,512,2048]{2,1,0:T(8,128)(2,1)S(1)} %copy-done, bf16[512,128]{1,0:T(8,128)(2,1)S(1)} %copy-done.6, f32[512,128]{1,0:T(8,128)S(1)} %copy-done.5, f32[2048,128]{1,0:T(8,128)S(1)} %copy-done.2), custom_call_target="tpu_custom_call" | custom-call | flops 402653184 | bytes 1048576 | tf_op jit(solution)/shard_map/pallas_call | solution.py:161
  13.4 1.0 %collective-permute-done.refs_2_ = bf16[1024,128]{1,0:T(8,128)(2,1)S(1)} collective-permute-done((bf16[1024,128]{1,0:T(8,128)(2,1)}, bf16[1024,128]{1,0:T(8,128)(2,1)S(1)}, u32[]{:S(2)}, u32[]{:S(2)}) %collective-permute-start) | collective-permute-done | bytes 262176 | tf_op jit(solution)/shard_map/ppermute | solution.py:28
  14.4 1.4 %shard_map.70 = (bf16[1024,128]{1,0:T(8,128)(2,1)S(1)}, f32[512,128]{1,0:T(8,128)S(1)}, f32[1024,128]{1,0:T(8,128)S(1)}, f32[1024,128]{1,0:T(8,128)S(1)}) custom-call(bf16[2,512,2048]{2,1,0:T(8,128)(2,1)S(1)} %copy-done, bf16[512,128]{1,0:T(8,128)(2,1)S(1)} %convert_element_type.9.half_ref, f32[512,128]{1,0:T(8,128)S(1)} %get-tuple-element.67.grad_ref, ...), custom_call_target="tpu_custom_call" | custom-call | flops 402653184 | bytes 1048576 | tf_op jit(solution)/shard_map/pallas_call | solution.py:161
  15.7 2.1 %collective-permute-start.2 = (bf16[1024,128]{1,0:T(8,128)(2,1)S(1)}, bf16[1024,128]{1,0:T(8,128)(2,1)S(1)}, u32[]{:S(2)}, u32[]{:S(2)}) collective-permute-start(bf16[1024,128]{1,0:T(8,128)(2,1)S(1)} %get-tuple-element.42.refs_0_), channel_id=1, source_target_pairs={{0,1},{1,0},{2,3},{3,2},{4,5},{5,4},{6,7},{7,6},{8,9},{9,8},{10,11... | collective-permute-start | bytes 786440 | tf_op jit(solution)/shard_map/ppermute | solution.py:28
  17.8 4.6 %collective-permute-done.1.refs_2_ = bf16[1024,128]{1,0:T(8,128)(2,1)S(1)} collective-permute-done((bf16[1024,128]{1,0:T(8,128)(2,1)S(1)}, bf16[1024,128]{1,0:T(8,128)(2,1)S(1)}, u32[]{:S(2)}, u32[]{:S(2)}) %collective-permute-start.1) | collective-permute-done | bytes 262176 | tf_op jit(solution)/shard_map/ppermute | solution.py:28
  22.5 1.4 %shard_map.71 = (bf16[1024,128]{1,0:T(8,128)(2,1)S(1)}, f32[512,128]{1,0:T(8,128)S(1)}, f32[1024,128]{1,0:T(8,128)S(1)}, f32[1024,128]{1,0:T(8,128)S(1)}) custom-call(bf16[2,512,2048]{2,1,0:T(8,128)(2,1)S(1)} %copy-done, bf16[512,128]{1,0:T(8,128)(2,1)S(1)} %convert_element_type.9.half_ref, f32[512,128]{1,0:T(8,128)S(1)} %get-tuple-element.37.grad_ref, ...), custom_call_target="tpu_custom_call" | custom-call | flops 402653184 | bytes 1048576 | tf_op jit(solution)/shard_map/pallas_call | solution.py:161
  23.9 4.2 %collective-permute-done.2.refs_1_ = bf16[1024,128]{1,0:T(8,128)(2,1)S(1)} collective-permute-done((bf16[1024,128]{1,0:T(8,128)(2,1)S(1)}, bf16[1024,128]{1,0:T(8,128)(2,1)S(1)}, u32[]{:S(2)}, u32[]{:S(2)}) %collective-permute-start.2) | collective-permute-done | bytes 262176 | tf_op jit(solution)/shard_map/ppermute | solution.py:28
  28.4 3.8 %collective-permute-done.4.refs_1_ = bf16[1024,128]{1,0:T(8,128)(2,1)S(1)} collective-permute-done((bf16[1024,128]{1,0:T(8,128)(2,1)S(1)}, bf16[1024,128]{1,0:T(8,128)(2,1)S(1)}, u32[]{:S(2)}, u32[]{:S(2)}) %collective-permute-start.4) | collective-permute-done | bytes 262176 | tf_op jit(solution)/shard_map/ppermute | solution.py:28
  32.7 4.2 %collective-permute-done.3.items_ref = bf16[1024,128]{1,0:T(8,128)(2,1)S(1)} collective-permute-done((bf16[1024,128]{1,0:T(8,128)(2,1)S(1)}, bf16[1024,128]{1,0:T(8,128)(2,1)S(1)}, u32[]{:S(2)}, u32[]{:S(2)}) %collective-permute-start.3) | collective-permute-done | bytes 262176 | tf_op jit(solution)/shard_map/ppermute | solution.py:28
  36.9 1.3 %shard_map.73 = (bf16[1024,128]{1,0:T(8,128)(2,1)S(1)}, f32[512,128]{1,0:T(8,128)S(1)}, bf16[1024,128]{1,0:T(8,128)(2,1)S(1)}) custom-call(bf16[2,512,2048]{2,1,0:T(8,128)(2,1)S(1)} %copy-done.1, bf16[512,128]{1,0:T(8,128)(2,1)S(1)} %convert_element_type.10.half_ref, f32[512,128]{1,0:T(8,128)S(1)} %get-tuple-element.64.grad_ref, ...), custom_call_target="tpu_custom_call" | custom-call | flops 402653184 | bytes 1048576 | tf_op jit(solution)/shard_map/pallas_call | solution.py:161
  38.3 2.7 %collective-permute-done.5.items_ref = bf16[1024,128]{1,0:T(8,128)(2,1)S(1)} collective-permute-done((bf16[1024,128]{1,0:T(8,128)(2,1)S(1)}, bf16[1024,128]{1,0:T(8,128)(2,1)S(1)}, u32[]{:S(2)}, u32[]{:S(2)}) %collective-permute-start.5) | collective-permute-done | bytes 262176 | tf_op jit(solution)/shard_map/ppermute | solution.py:28
  41.0 1.3 %shard_map.75 = (bf16[1024,128]{1,0:T(8,128)(2,1)S(1)}, f32[512,128]{1,0:T(8,128)S(1)}, bf16[1024,128]{1,0:T(8,128)(2,1)S(1)}) custom-call(bf16[2,512,2048]{2,1,0:T(8,128)(2,1)S(1)} %copy-done.1, bf16[512,128]{1,0:T(8,128)(2,1)S(1)} %convert_element_type.10.half_ref, f32[512,128]{1,0:T(8,128)S(1)} %get-tuple-element.45.grad_ref, ...), custom_call_target="tpu_custom_call" | custom-call | flops 402653184 | bytes 1048576 | tf_op jit(solution)/shard_map/pallas_call | solution.py:161
  43.4 3.3 %collective-permute-done.6.refs_0_ = bf16[1024,128]{1,0:T(8,128)(2,1)S(1)} collective-permute-done((bf16[1024,128]{1,0:T(8,128)(2,1)S(1)}, bf16[1024,128]{1,0:T(8,128)(2,1)S(1)}, u32[]{:S(2)}, u32[]{:S(2)}) %collective-permute-start.6) | collective-permute-done | bytes 262176 | tf_op jit(solution)/shard_map/ppermute | solution.py:28
  46.8 1.4 %shard_map.76 = (bf16[1024,128]{1,0:T(8,128)(2,1)S(1)}, f32[512,128]{1,0:T(8,128)S(1)}, f32[1024,128]{1,0:T(8,128)S(1)}, f32[1024,128]{1,0:T(8,128)S(1)}) custom-call(bf16[2,512,2048]{2,1,0:T(8,128)(2,1)S(1)} %copy-done.1, bf16[512,128]{1,0:T(8,128)(2,1)S(1)} %get-tuple-element.70.half_ref, f32[512,128]{1,0:T(8,128)S(1)} %get-tuple-element.69.grad_ref, ...), custom_call_target="tpu_custom_call" | custom-call | flops 402653184 | bytes 1048576 | tf_op jit(solution)/shard_map/pallas_call | solution.py:161
  48.4 2.6 %collective-permute-done.8.refs_0_ = bf16[1024,128]{1,0:T(8,128)(2,1)S(1)} collective-permute-done((bf16[1024,128]{1,0:T(8,128)(2,1)S(1)}, bf16[1024,128]{1,0:T(8,128)(2,1)S(1)}, u32[]{:S(2)}, u32[]{:S(2)}) %collective-permute-start.8) | collective-permute-done | bytes 262176 | tf_op jit(solution)/shard_map/ppermute | solution.py:28
  51.1 1.2 %collective-permute-done.9.refs_2_ = bf16[1024,128]{1,0:T(8,128)(2,1)S(1)} collective-permute-done((bf16[1024,128]{1,0:T(8,128)(2,1)S(1)}, bf16[1024,128]{1,0:T(8,128)(2,1)S(1)}, u32[]{:S(2)}, u32[]{:S(2)}) %collective-permute-start.9) | collective-permute-done | bytes 262176 | tf_op jit(solution)/shard_map/ppermute | solution.py:28
  52.2 1.4 %shard_map.77 = (bf16[1024,128]{1,0:T(8,128)(2,1)S(1)}, f32[512,128]{1,0:T(8,128)S(1)}, f32[1024,128]{1,0:T(8,128)S(1)}, f32[1024,128]{1,0:T(8,128)S(1)}) custom-call(bf16[2,512,2048]{2,1,0:T(8,128)(2,1)S(1)} %copy-done.1, bf16[512,128]{1,0:T(8,128)(2,1)S(1)} %get-tuple-element.70.half_ref, f32[512,128]{1,0:T(8,128)S(1)} %get-tuple-element.54.grad_ref, ...), custom_call_target="tpu_custom_call" | custom-call | flops 402653184 | bytes 1048576 | tf_op jit(solution)/shard_map/pallas_call | solution.py:161
  54.9 3.0 %collective-permute-done.11.refs_1_ = bf16[1024,128]{1,0:T(8,128)(2,1)S(1)} collective-permute-done((bf16[1024,128]{1,0:T(8,128)(2,1)S(1)}, bf16[1024,128]{1,0:T(8,128)(2,1)S(1)}, u32[]{:S(2)}, u32[]{:S(2)}) %collective-permute-start.11) | collective-permute-done | bytes 262176 | tf_op jit(solution)/shard_map/ppermute | solution.py:28
  58.8 3.5 %collective-permute-done.10.refs_1_ = bf16[1024,128]{1,0:T(8,128)(2,1)S(1)} collective-permute-done((bf16[1024,128]{1,0:T(8,128)(2,1)S(1)}, bf16[1024,128]{1,0:T(8,128)(2,1)S(1)}, u32[]{:S(2)}, u32[]{:S(2)}) %collective-permute-start.10) | collective-permute-done | bytes 262176 | tf_op jit(solution)/shard_map/ppermute | solution.py:28
  (36 shorter events, 5.6 us)
Async XLA Ops:
  0.6 7.2 %copy-start.2 = (f32[2048,128]{1,0:T(8,128)S(1)}, f32[2048,128]{1,0:T(8,128)}, u32[]{:S(2)}) copy-start(f32[2048,128]{1,0:T(8,128)} %items_ref.5) | copy-start | bytes 3145732
  0.6 12.6 %copy-start.7 = (f32[512,128]{1,0:T(8,128)S(1)}, f32[512,128]{1,0:T(8,128)}, u32[]{:S(2)}) copy-start(f32[512,128]{1,0:T(8,128)} %param.7) | copy-start | bytes 786436
  0.7 12.6 %copy-start.8 = (f32[512,128]{1,0:T(8,128)S(1)}, f32[512,128]{1,0:T(8,128)}, u32[]{:S(2)}) copy-start(f32[512,128]{1,0:T(8,128)} %users_hbm.1) | copy-start | bytes 786436
  4.8 9.5 %collective-permute-start = (bf16[1024,128]{1,0:T(8,128)(2,1)}, bf16[1024,128]{1,0:T(8,128)(2,1)S(1)}, u32[]{:S(2)}, u32[]{:S(2)}) collective-permute-start(bf16[1024,128]{1,0:T(8,128)(2,1)} %get-tuple-element.36.refs_1_), channel_id=1, source_target_pairs={{0,1},{1,0},{2,3},{3,2},{4,5},{5,4},{6,7},{7,6},{8,9},{9,8},{10,11... | collective-permute-start | bytes 786440 | tf_op jit(solution)/shard_map/ppermute | solution.py:28
  7.8 2.2 %copy-start = (bf16[2,512,2048]{2,1,0:T(8,128)(2,1)S(1)}, bf16[2,512,2048]{2,1,0:T(8,128)(2,1)}, u32[]{:S(2)}) copy-start(bf16[2,512,2048]{2,1,0:T(8,128)(2,1)} %rate_ref.13) | copy-start | bytes 12582916
  10.0 0.9 %copy-start.5 = (f32[512,128]{1,0:T(8,128)S(1)}, f32[512,128]{1,0:T(8,128)}, u32[]{:S(2)}) copy-start(f32[512,128]{1,0:T(8,128)} %get-tuple-element.34.grad_ref) | copy-start | bytes 786436
  11.0 0.9 %copy-start.6 = (bf16[512,128]{1,0:T(8,128)(2,1)S(1)}, bf16[512,128]{1,0:T(8,128)(2,1)}, u32[]{:S(2)}) copy-start(bf16[512,128]{1,0:T(8,128)(2,1)} %get-tuple-element.33.half_ref) | copy-start | bytes 393220
  11.9 2.5 %copy-start.3 = (f32[2048,128]{1,0:T(8,128)S(1)}, f32[2048,128]{1,0:T(8,128)}, u32[]{:S(2)}) copy-start(f32[2048,128]{1,0:T(8,128)} %refs_0_.3) | copy-start | bytes 3145732
  11.9 2.5 %copy-start.4 = (bf16[1024,128]{1,0:T(8,128)(2,1)S(1)}, bf16[1024,128]{1,0:T(8,128)(2,1)}, u32[]{:S(2)}) copy-start(bf16[1024,128]{1,0:T(8,128)(2,1)} %get-tuple-element.36.refs_1_) | copy-start | bytes 786436
  13.2 9.3 %collective-permute-start.1 = (bf16[1024,128]{1,0:T(8,128)(2,1)S(1)}, bf16[1024,128]{1,0:T(8,128)(2,1)S(1)}, u32[]{:S(2)}, u32[]{:S(2)}) collective-permute-start(bf16[1024,128]{1,0:T(8,128)(2,1)S(1)} %get-tuple-element.38.refs_1_), channel_id=1, source_target_pairs={{0,1},{1,0},{2,3},{3,2},{4,5},{5,4},{6,7},{7,6},{8,9},{9,8},{10,11... | collective-permute-start | bytes 786440 | tf_op jit(solution)/shard_map/ppermute | solution.py:28
  15.7 12.4 %collective-permute-start.2 = (bf16[1024,128]{1,0:T(8,128)(2,1)S(1)}, bf16[1024,128]{1,0:T(8,128)(2,1)S(1)}, u32[]{:S(2)}, u32[]{:S(2)}) collective-permute-start(bf16[1024,128]{1,0:T(8,128)(2,1)S(1)} %get-tuple-element.42.refs_0_), channel_id=1, source_target_pairs={{0,1},{1,0},{2,3},{3,2},{4,5},{5,4},{6,7},{7,6},{8,9},{9,8},{10,11... | collective-permute-start | bytes 786440 | tf_op jit(solution)/shard_map/ppermute | solution.py:28
  23.8 13.0 %copy-start.1 = (bf16[2,512,2048]{2,1,0:T(8,128)(2,1)S(1)}, bf16[2,512,2048]{2,1,0:T(8,128)(2,1)}, u32[]{:S(2)}) copy-start(bf16[2,512,2048]{2,1,0:T(8,128)(2,1)} %rate_ref.13) | copy-start | bytes 12582916
  23.8 8.4 %collective-permute-start.4 = (bf16[1024,128]{1,0:T(8,128)(2,1)S(1)}, bf16[1024,128]{1,0:T(8,128)(2,1)S(1)}, u32[]{:S(2)}, u32[]{:S(2)}) collective-permute-start(bf16[1024,128]{1,0:T(8,128)(2,1)S(1)} %get-tuple-element.48.refs_0_), channel_id=1, source_target_pairs={{0,1},{1,0},{2,3},{3,2},{4,5},{5,4},{6,7},{7,6},{8,9},{9,8},{10,11... | collective-permute-start | bytes 786440 | tf_op jit(solution)/shard_map/ppermute | solution.py:28
  28.3 8.5 %collective-permute-start.3 = (bf16[1024,128]{1,0:T(8,128)(2,1)S(1)}, bf16[1024,128]{1,0:T(8,128)(2,1)S(1)}, u32[]{:S(2)}, u32[]{:S(2)}) collective-permute-start(bf16[1024,128]{1,0:T(8,128)(2,1)S(1)} %get-tuple-element.43.refs_2_), channel_id=1, source_target_pairs={{0,2},{1,3},{2,4},{3,5},{4,6},{5,7},{6,8},{7,9},{8,10},{9,11},{10,... | collective-permute-start | bytes 786440 | tf_op jit(solution)/shard_map/ppermute | solution.py:28
  32.5 8.5 %collective-permute-start.5 = (bf16[1024,128]{1,0:T(8,128)(2,1)S(1)}, bf16[1024,128]{1,0:T(8,128)(2,1)S(1)}, u32[]{:S(2)}, u32[]{:S(2)}) collective-permute-start(bf16[1024,128]{1,0:T(8,128)(2,1)S(1)} %get-tuple-element.49), channel_id=1, source_target_pairs={{0,2},{1,3},{2,4},{3,5},{4,6},{5,7},{6,8},{7,9},{8,10},{9,11},{10,... | collective-permute-start | bytes 786440 | tf_op jit(solution)/shard_map/ppermute | solution.py:28
  38.2 8.5 %collective-permute-start.6 = (bf16[1024,128]{1,0:T(8,128)(2,1)S(1)}, bf16[1024,128]{1,0:T(8,128)(2,1)S(1)}, u32[]{:S(2)}, u32[]{:S(2)}) collective-permute-start(bf16[1024,128]{1,0:T(8,128)(2,1)S(1)} %get-tuple-element.52), channel_id=1, source_target_pairs={{0,2},{1,3},{2,4},{3,5},{4,6},{5,7},{6,8},{7,9},{8,10},{9,11},{10,... | collective-permute-start | bytes 786440 | tf_op jit(solution)/shard_map/ppermute | solution.py:28
  38.3 8.5 %collective-permute-start.7 = (bf16[1024,128]{1,0:T(8,128)(2,1)S(1)}, bf16[1024,128]{1,0:T(8,128)(2,1)S(1)}, u32[]{:S(2)}, u32[]{:S(2)}) collective-permute-start(bf16[1024,128]{1,0:T(8,128)(2,1)S(1)} %get-tuple-element.53.refs_1_), channel_id=1, source_target_pairs={{0,1},{1,0},{2,3},{3,2},{4,5},{5,4},{6,7},{7,6},{8,9},{9,8},{10,11... | collective-permute-start | bytes 786440 | tf_op jit(solution)/shard_map/ppermute | solution.py:28
  42.3 8.7 %collective-permute-start.8 = (bf16[1024,128]{1,0:T(8,128)(2,1)S(1)}, bf16[1024,128]{1,0:T(8,128)(2,1)S(1)}, u32[]{:S(2)}, u32[]{:S(2)}) collective-permute-start(bf16[1024,128]{1,0:T(8,128)(2,1)S(1)} %get-tuple-element.55), channel_id=1, source_target_pairs={{0,2},{1,3},{2,4},{3,5},{4,6},{5,7},{6,8},{7,9},{8,10},{9,11},{10,... | collective-permute-start | bytes 786440 | tf_op jit(solution)/shard_map/ppermute | solution.py:28
  42.6 9.7 %collective-permute-start.9 = (bf16[1024,128]{1,0:T(8,128)(2,1)S(1)}, bf16[1024,128]{1,0:T(8,128)(2,1)S(1)}, u32[]{:S(2)}, u32[]{:S(2)}) collective-permute-start(bf16[1024,128]{1,0:T(8,128)(2,1)S(1)} %get-tuple-element.56.refs_1_), channel_id=1, source_target_pairs={{0,1},{1,0},{2,3},{3,2},{4,5},{5,4},{6,7},{7,6},{8,9},{9,8},{10,11... | collective-permute-start | bytes 786440 | tf_op jit(solution)/shard_map/ppermute | solution.py:28
  48.1 9.7 %collective-permute-start.11 = (bf16[1024,128]{1,0:T(8,128)(2,1)S(1)}, bf16[1024,128]{1,0:T(8,128)(2,1)S(1)}, u32[]{:S(2)}, u32[]{:S(2)}) collective-permute-start(bf16[1024,128]{1,0:T(8,128)(2,1)S(1)} %get-tuple-element.63.refs_0_), channel_id=1, source_target_pairs={{0,1},{1,0},{2,3},{3,2},{4,5},{5,4},{6,7},{7,6},{8,9},{9,8},{10,11... | collective-permute-start | bytes 786440 | tf_op jit(solution)/shard_map/ppermute | solution.py:28
  53.6 8.6 %collective-permute-start.10 = (bf16[1024,128]{1,0:T(8,128)(2,1)S(1)}, bf16[1024,128]{1,0:T(8,128)(2,1)S(1)}, u32[]{:S(2)}, u32[]{:S(2)}) collective-permute-start(bf16[1024,128]{1,0:T(8,128)(2,1)S(1)} %get-tuple-element.60.refs_0_), channel_id=1, source_target_pairs={{0,1},{1,0},{2,3},{3,2},{4,5},{5,4},{6,7},{7,6},{8,9},{9,8},{10,11... | collective-permute-start | bytes 786440 | tf_op jit(solution)/shard_map/ppermute | solution.py:28

commit v7 on v6

--- a/solution.py
+++ b/solution.py
@@ -123,12 +123,13 @@
 
 
 def chunk_kernel(n_terms, leaves, sub_epoch, column, offset, rate_ref, half_ref, grad_ref, items_ref, *refs):
-    if n_terms:
-        accum_ref, *refs = refs
     if leaves:
         leaving_ref, *refs, leaving_out = refs
         leaving_out[...] = leaving_ref[...]
-    term_refs, (term_out, grad_out, *updated) = refs[:n_terms], refs[n_terms:]
+    term_refs, refs = refs[:n_terms], refs[n_terms:]
+    if n_terms:
+        accum_ref, *refs = refs
+    term_out, grad_out, *updated = refs
     half = half_ref[...]
     half_t = half.T
     grad = grad_ref[...]
@@ -155,7 +156,7 @@
     operands = [ratings, half, grad, items]
     if terms:
         out_shape += [jax.ShapeDtypeStruct((size, rank), jnp.float32)] * 2
-        operands += [accum, *terms]
+        operands += [*terms, accum]
     operands += leaving
     out_shape += [jax.ShapeDtypeStruct(array.shape, array.dtype) for array in leaving]
     return pl.pallas_call(

time: 63.5 us -> 62.6 us (0.986)
  waiting for transfers between devices: 34.1 us -> 32.7 us
    ppermute x12, waiting for transfers between devices: 34.1 us -> 32.7 us  [moved(): return lax.ppermute(shard, ('loop', 'grp'), pairs)]
  transfers between devices with their start and end apart: 12 -> 12, of which waited for: 11 -> 10; matrix products, arithmetic and copies ran while one was open for 2% -> 2% of each run, Pallas kernels for 17% -> 17%
where the time goes in v7:
time: 62.6 us; the launch traced here: 62.4 us
  waiting for transfers between devices  32.7 us (52%)
  Pallas kernels  15.8 us (25%)
  starting transfers between devices  7.78 us (12%)
  local copies, waits for them, and re-layouts  4.07 us (7%)
  other arithmetic  1.12 us (2%)
  between operations  0.96 us (2%)
    ppermute x12, waiting for transfers between devices, moved(): return lax.ppermute(shard, ('loop', 'grp'), pairs)  32.7 us
    pallas_call x7, Pallas kernels, chunk_pass(): pl.pallas_call(functools.partial(chunk_kernel, len(terms), len(leaving),...  9.38 us
    ppermute x12, starting transfers between devices, moved(): return lax.ppermute(shard, ('loop', 'grp'), pairs)  7.78 us
    pallas_call x1, Pallas kernels, first_pass(): pl.pallas_call(functools.partial(first_kernel, rows.start), out_shape=[ja...  4.16 us
    unnamed x18, local copies, waits for them, and re-layouts  4.07 us
    pallas_call x2, Pallas kernels, last_item_step(): pl.pallas_call(functools.partial(last_kernel, len(terms), rows.start), ou...  1.8 us
  transfers between devices with their start and end apart: 12, of which 10 were waited for; matrix products, arithmetic and copies ran while one was open for 2% of the time, Pallas kernels for 17%

profile of v7, /device:TPU:0, one launch (start us, length us, event | category | flops | bytes accessed | tf_op | source)
XLA Modules:
  0.0 62.4 jit_solution(2066324451918381704)
XLA Ops:
  0.7 4.2 %shard_map.68 = (bf16[1024,128]{1,0:T(8,128)(2,1)}, f32[512,128]{1,0:T(8,128)}, bf16[512,128]{1,0:T(8,128)(2,1)}) custom-call(bf16[2,512,2048]{2,1,0:T(8,128)(2,1)} %rate_ref.13, f32[2048,128]{1,0:T(8,128)} %items_ref.5, f32[512,128]{1,0:T(8,128)} %users_hbm.1), custom_call_target="tpu_custom_call" | custom-call | flops 402653184 | bytes 1048576 | tf_op jit(solution)/shard_map/pallas_call | solution.py:105
  4.8 3.0 %collective-permute-start = (bf16[1024,128]{1,0:T(8,128)(2,1)}, bf16[1024,128]{1,0:T(8,128)(2,1)S(1)}, u32[]{:S(2)}, u32[]{:S(2)}) collective-permute-start(bf16[1024,128]{1,0:T(8,128)(2,1)} %get-tuple-element.36.refs_0_), channel_id=1, source_target_pairs={{0,1},{1,0},{2,3},{3,2},{4,5},{5,4},{6,7},{7,6},{8,9},{9,8},{10,11... | collective-permute-start | bytes 786440 | tf_op jit(solution)/shard_map/ppermute | solution.py:28
  7.8 2.2 %copy-done = bf16[2,512,2048]{2,1,0:T(8,128)(2,1)S(1)} copy-done((bf16[2,512,2048]{2,1,0:T(8,128)(2,1)S(1)}, bf16[2,512,2048]{2,1,0:T(8,128)(2,1)}, u32[]{:S(2)}) %copy-start) | copy-done | bytes 4194328
  10.0 0.9 %copy-done.5 = f32[512,128]{1,0:T(8,128)S(1)} copy-done((f32[512,128]{1,0:T(8,128)S(1)}, f32[512,128]{1,0:T(8,128)}, u32[]{:S(2)}) %copy-start.5) | copy-done | bytes 262168
  11.0 0.9 %copy-done.6 = bf16[512,128]{1,0:T(8,128)(2,1)S(1)} copy-done((bf16[512,128]{1,0:T(8,128)(2,1)S(1)}, bf16[512,128]{1,0:T(8,128)(2,1)}, u32[]{:S(2)}) %copy-start.6) | copy-done | bytes 131096
  11.9 1.3 %shard_map.69 = (bf16[1024,128]{1,0:T(8,128)(2,1)S(1)}, f32[512,128]{1,0:T(8,128)S(1)}) custom-call(bf16[2,512,2048]{2,1,0:T(8,128)(2,1)S(1)} %copy-done, bf16[512,128]{1,0:T(8,128)(2,1)S(1)} %copy-done.6, f32[512,128]{1,0:T(8,128)S(1)} %copy-done.5, f32[2048,128]{1,0:T(8,128)S(1)} %copy-done.2), custom_call_target="tpu_custom_call" | custom-call | flops 402653184 | bytes 1048576 | tf_op jit(solution)/shard_map/pallas_call | solution.py:162
  13.4 1.0 %collective-permute-done.refs_1_ = bf16[1024,128]{1,0:T(8,128)(2,1)S(1)} collective-permute-done((bf16[1024,128]{1,0:T(8,128)(2,1)}, bf16[1024,128]{1,0:T(8,128)(2,1)S(1)}, u32[]{:S(2)}, u32[]{:S(2)}) %collective-permute-start) | collective-permute-done | bytes 262176 | tf_op jit(solution)/shard_map/ppermute | solution.py:28
  14.4 1.4 %shard_map.70 = (bf16[1024,128]{1,0:T(8,128)(2,1)S(1)}, f32[512,128]{1,0:T(8,128)S(1)}, f32[1024,128]{1,0:T(8,128)S(1)}, f32[1024,128]{1,0:T(8,128)S(1)}) custom-call(bf16[2,512,2048]{2,1,0:T(8,128)(2,1)S(1)} %copy-done, bf16[512,128]{1,0:T(8,128)(2,1)S(1)} %convert_element_type.9.half_ref, f32[512,128]{1,0:T(8,128)S(1)} %get-tuple-element.67.grad_ref, ...), custom_call_target="tpu_custom_call" | custom-call | flops 402653184 | bytes 1048576 | tf_op jit(solution)/shard_map/pallas_call | solution.py:162
  15.7 2.1 %collective-permute-start.2 = (bf16[1024,128]{1,0:T(8,128)(2,1)S(1)}, bf16[1024,128]{1,0:T(8,128)(2,1)S(1)}, u32[]{:S(2)}, u32[]{:S(2)}) collective-permute-start(bf16[1024,128]{1,0:T(8,128)(2,1)S(1)} %get-tuple-element.42.refs_0_), channel_id=1, source_target_pairs={{0,1},{1,0},{2,3},{3,2},{4,5},{5,4},{6,7},{7,6},{8,9},{9,8},{10,11... | collective-permute-start | bytes 786440 | tf_op jit(solution)/shard_map/ppermute | solution.py:28
  17.8 4.6 %collective-permute-done.1.refs_1_ = bf16[1024,128]{1,0:T(8,128)(2,1)S(1)} collective-permute-done((bf16[1024,128]{1,0:T(8,128)(2,1)S(1)}, bf16[1024,128]{1,0:T(8,128)(2,1)S(1)}, u32[]{:S(2)}, u32[]{:S(2)}) %collective-permute-start.1) | collective-permute-done | bytes 262176 | tf_op jit(solution)/shard_map/ppermute | solution.py:28
  22.5 1.4 %shard_map.71 = (bf16[1024,128]{1,0:T(8,128)(2,1)S(1)}, f32[512,128]{1,0:T(8,128)S(1)}, f32[1024,128]{1,0:T(8,128)S(1)}, f32[1024,128]{1,0:T(8,128)S(1)}) custom-call(bf16[2,512,2048]{2,1,0:T(8,128)(2,1)S(1)} %copy-done, bf16[512,128]{1,0:T(8,128)(2,1)S(1)} %convert_element_type.9.half_ref, f32[512,128]{1,0:T(8,128)S(1)} %get-tuple-element.37.grad_ref, ...), custom_call_target="tpu_custom_call" | custom-call | flops 402653184 | bytes 1048576 | tf_op jit(solution)/shard_map/pallas_call | solution.py:162
  23.9 4.2 %collective-permute-done.2.refs_1_ = bf16[1024,128]{1,0:T(8,128)(2,1)S(1)} collective-permute-done((bf16[1024,128]{1,0:T(8,128)(2,1)S(1)}, bf16[1024,128]{1,0:T(8,128)(2,1)S(1)}, u32[]{:S(2)}, u32[]{:S(2)}) %collective-permute-start.2) | collective-permute-done | bytes 262176 | tf_op jit(solution)/shard_map/ppermute | solution.py:28
  28.4 3.8 %collective-permute-done.4.refs_1_ = bf16[1024,128]{1,0:T(8,128)(2,1)S(1)} collective-permute-done((bf16[1024,128]{1,0:T(8,128)(2,1)S(1)}, bf16[1024,128]{1,0:T(8,128)(2,1)S(1)}, u32[]{:S(2)}, u32[]{:S(2)}) %collective-permute-start.4) | collective-permute-done | bytes 262176 | tf_op jit(solution)/shard_map/ppermute | solution.py:28
  32.7 4.2 %collective-permute-done.3.items_ref = bf16[1024,128]{1,0:T(8,128)(2,1)S(1)} collective-permute-done((bf16[1024,128]{1,0:T(8,128)(2,1)S(1)}, bf16[1024,128]{1,0:T(8,128)(2,1)S(1)}, u32[]{:S(2)}, u32[]{:S(2)}) %collective-permute-start.3) | collective-permute-done | bytes 262176 | tf_op jit(solution)/shard_map/ppermute | solution.py:28
  36.9 1.3 %shard_map.73 = (bf16[1024,128]{1,0:T(8,128)(2,1)S(1)}, f32[512,128]{1,0:T(8,128)S(1)}, bf16[1024,128]{1,0:T(8,128)(2,1)S(1)}) custom-call(bf16[2,512,2048]{2,1,0:T(8,128)(2,1)S(1)} %copy-done.1, bf16[512,128]{1,0:T(8,128)(2,1)S(1)} %convert_element_type.10.half_ref, f32[512,128]{1,0:T(8,128)S(1)} %get-tuple-element.64.grad_ref, ...), custom_call_target="tpu_custom_call" | custom-call | flops 402653184 | bytes 1048576 | tf_op jit(solution)/shard_map/pallas_call | solution.py:162
  38.3 2.7 %collective-permute-done.5.items_ref = bf16[1024,128]{1,0:T(8,128)(2,1)S(1)} collective-permute-done((bf16[1024,128]{1,0:T(8,128)(2,1)S(1)}, bf16[1024,128]{1,0:T(8,128)(2,1)S(1)}, u32[]{:S(2)}, u32[]{:S(2)}) %collective-permute-start.5) | collective-permute-done | bytes 262176 | tf_op jit(solution)/shard_map/ppermute | solution.py:28
  41.0 1.3 %shard_map.75 = (bf16[1024,128]{1,0:T(8,128)(2,1)S(1)}, f32[512,128]{1,0:T(8,128)S(1)}, bf16[1024,128]{1,0:T(8,128)(2,1)S(1)}) custom-call(bf16[2,512,2048]{2,1,0:T(8,128)(2,1)S(1)} %copy-done.1, bf16[512,128]{1,0:T(8,128)(2,1)S(1)} %convert_element_type.10.half_ref, f32[512,128]{1,0:T(8,128)S(1)} %get-tuple-element.45.grad_ref, ...), custom_call_target="tpu_custom_call" | custom-call | flops 402653184 | bytes 1048576 | tf_op jit(solution)/shard_map/pallas_call | solution.py:162
  43.2 4.3 %collective-permute-done.6.refs_1_ = bf16[1024,128]{1,0:T(8,128)(2,1)S(1)} collective-permute-done((bf16[1024,128]{1,0:T(8,128)(2,1)S(1)}, bf16[1024,128]{1,0:T(8,128)(2,1)S(1)}, u32[]{:S(2)}, u32[]{:S(2)}) %collective-permute-start.6) | collective-permute-done | bytes 262176 | tf_op jit(solution)/shard_map/ppermute | solution.py:28
  47.4 1.4 %shard_map.76 = (bf16[1024,128]{1,0:T(8,128)(2,1)S(1)}, f32[512,128]{1,0:T(8,128)S(1)}, f32[1024,128]{1,0:T(8,128)S(1)}, f32[1024,128]{1,0:T(8,128)S(1)}) custom-call(bf16[2,512,2048]{2,1,0:T(8,128)(2,1)S(1)} %copy-done.1, bf16[512,128]{1,0:T(8,128)(2,1)S(1)} %get-tuple-element.70.half_ref, f32[512,128]{1,0:T(8,128)S(1)} %get-tuple-element.69.grad_ref, ...), custom_call_target="tpu_custom_call" | custom-call | flops 402653184 | bytes 1048576 | tf_op jit(solution)/shard_map/pallas_call | solution.py:162
  48.8 1.4 %collective-permute-start.11 = (bf16[1024,128]{1,0:T(8,128)(2,1)S(1)}, bf16[1024,128]{1,0:T(8,128)(2,1)S(1)}, u32[]{:S(2)}, u32[]{:S(2)}) collective-permute-start(bf16[1024,128]{1,0:T(8,128)(2,1)S(1)} %get-tuple-element.63.refs_0_), channel_id=1, source_target_pairs={{0,1},{1,0},{2,3},{3,2},{4,5},{5,4},{6,7},{7,6},{8,9},{9,8},{10,11... | collective-permute-start | bytes 786440 | tf_op jit(solution)/shard_map/ppermute | solution.py:28
  50.2 2.8 %collective-permute-done.8.refs_1_ = bf16[1024,128]{1,0:T(8,128)(2,1)S(1)} collective-permute-done((bf16[1024,128]{1,0:T(8,128)(2,1)S(1)}, bf16[1024,128]{1,0:T(8,128)(2,1)S(1)}, u32[]{:S(2)}, u32[]{:S(2)}) %collective-permute-start.8) | collective-permute-done | bytes 262176 | tf_op jit(solution)/shard_map/ppermute | solution.py:28
  53.1 1.4 %shard_map.77 = (bf16[1024,128]{1,0:T(8,128)(2,1)S(1)}, f32[512,128]{1,0:T(8,128)S(1)}, f32[1024,128]{1,0:T(8,128)S(1)}, f32[1024,128]{1,0:T(8,128)S(1)}) custom-call(bf16[2,512,2048]{2,1,0:T(8,128)(2,1)S(1)} %copy-done.1, bf16[512,128]{1,0:T(8,128)(2,1)S(1)} %get-tuple-element.70.half_ref, f32[512,128]{1,0:T(8,128)S(1)} %get-tuple-element.54.grad_ref, ...), custom_call_target="tpu_custom_call" | custom-call | flops 402653184 | bytes 1048576 | tf_op jit(solution)/shard_map/pallas_call | solution.py:162
  55.4 3.2 %collective-permute-done.11.refs_1_ = bf16[1024,128]{1,0:T(8,128)(2,1)S(1)} collective-permute-done((bf16[1024,128]{1,0:T(8,128)(2,1)S(1)}, bf16[1024,128]{1,0:T(8,128)(2,1)S(1)}, u32[]{:S(2)}, u32[]{:S(2)}) %collective-permute-start.11) | collective-permute-done | bytes 262176 | tf_op jit(solution)/shard_map/ppermute | solution.py:28
  59.5 1.9 %collective-permute-done.10.refs_1_ = bf16[1024,128]{1,0:T(8,128)(2,1)S(1)} collective-permute-done((bf16[1024,128]{1,0:T(8,128)(2,1)S(1)}, bf16[1024,128]{1,0:T(8,128)(2,1)S(1)}, u32[]{:S(2)}, u32[]{:S(2)}) %collective-permute-start.10) | collective-permute-done | bytes 262176 | tf_op jit(solution)/shard_map/ppermute | solution.py:28
  (36 shorter events, 4.7 us)
Async XLA Ops:
  0.6 7.2 %copy-start.2 = (f32[2048,128]{1,0:T(8,128)S(1)}, f32[2048,128]{1,0:T(8,128)}, u32[]{:S(2)}) copy-start(f32[2048,128]{1,0:T(8,128)} %items_ref.5) | copy-start | bytes 3145732
  0.6 12.6 %copy-start.7 = (f32[512,128]{1,0:T(8,128)S(1)}, f32[512,128]{1,0:T(8,128)}, u32[]{:S(2)}) copy-start(f32[512,128]{1,0:T(8,128)} %param.7) | copy-start | bytes 786436
  0.7 12.6 %copy-start.8 = (f32[512,128]{1,0:T(8,128)S(1)}, f32[512,128]{1,0:T(8,128)}, u32[]{:S(2)}) copy-start(f32[512,128]{1,0:T(8,128)} %users_hbm.1) | copy-start | bytes 786436
  4.8 9.5 %collective-permute-start = (bf16[1024,128]{1,0:T(8,128)(2,1)}, bf16[1024,128]{1,0:T(8,128)(2,1)S(1)}, u32[]{:S(2)}, u32[]{:S(2)}) collective-permute-start(bf16[1024,128]{1,0:T(8,128)(2,1)} %get-tuple-element.36.refs_0_), channel_id=1, source_target_pairs={{0,1},{1,0},{2,3},{3,2},{4,5},{5,4},{6,7},{7,6},{8,9},{9,8},{10,11... | collective-permute-start | bytes 786440 | tf_op jit(solution)/shard_map/ppermute | solution.py:28
  7.8 2.2 %copy-start = (bf16[2,512,2048]{2,1,0:T(8,128)(2,1)S(1)}, bf16[2,512,2048]{2,1,0:T(8,128)(2,1)}, u32[]{:S(2)}) copy-start(bf16[2,512,2048]{2,1,0:T(8,128)(2,1)} %rate_ref.13) | copy-start | bytes 12582916
  10.0 0.9 %copy-start.5 = (f32[512,128]{1,0:T(8,128)S(1)}, f32[512,128]{1,0:T(8,128)}, u32[]{:S(2)}) copy-start(f32[512,128]{1,0:T(8,128)} %get-tuple-element.34.grad_ref) | copy-start | bytes 786436
  11.0 0.9 %copy-start.6 = (bf16[512,128]{1,0:T(8,128)(2,1)S(1)}, bf16[512,128]{1,0:T(8,128)(2,1)}, u32[]{:S(2)}) copy-start(bf16[512,128]{1,0:T(8,128)(2,1)} %get-tuple-element.33.half_ref) | copy-start | bytes 393220
  11.9 2.5 %copy-start.3 = (f32[2048,128]{1,0:T(8,128)S(1)}, f32[2048,128]{1,0:T(8,128)}, u32[]{:S(2)}) copy-start(f32[2048,128]{1,0:T(8,128)} %refs_2_.3) | copy-start | bytes 3145732
  11.9 2.5 %copy-start.4 = (bf16[1024,128]{1,0:T(8,128)(2,1)S(1)}, bf16[1024,128]{1,0:T(8,128)(2,1)}, u32[]{:S(2)}) copy-start(bf16[1024,128]{1,0:T(8,128)(2,1)} %get-tuple-element.36.refs_0_) | copy-start | bytes 786436
  13.2 9.3 %collective-permute-start.1 = (bf16[1024,128]{1,0:T(8,128)(2,1)S(1)}, bf16[1024,128]{1,0:T(8,128)(2,1)S(1)}, u32[]{:S(2)}, u32[]{:S(2)}) collective-permute-start(bf16[1024,128]{1,0:T(8,128)(2,1)S(1)} %get-tuple-element.38.refs_0_), channel_id=1, source_target_pairs={{0,1},{1,0},{2,3},{3,2},{4,5},{5,4},{6,7},{7,6},{8,9},{9,8},{10,11... | collective-permute-start | bytes 786440 | tf_op jit(solution)/shard_map/ppermute | solution.py:28
  15.7 12.4 %collective-permute-start.2 = (bf16[1024,128]{1,0:T(8,128)(2,1)S(1)}, bf16[1024,128]{1,0:T(8,128)(2,1)S(1)}, u32[]{:S(2)}, u32[]{:S(2)}) collective-permute-start(bf16[1024,128]{1,0:T(8,128)(2,1)S(1)} %get-tuple-element.42.refs_0_), channel_id=1, source_target_pairs={{0,1},{1,0},{2,3},{3,2},{4,5},{5,4},{6,7},{7,6},{8,9},{9,8},{10,11... | collective-permute-start | bytes 786440 | tf_op jit(solution)/shard_map/ppermute | solution.py:28
  23.8 13.0 %copy-start.1 = (bf16[2,512,2048]{2,1,0:T(8,128)(2,1)S(1)}, bf16[2,512,2048]{2,1,0:T(8,128)(2,1)}, u32[]{:S(2)}) copy-start(bf16[2,512,2048]{2,1,0:T(8,128)(2,1)} %rate_ref.13) | copy-start | bytes 12582916
  23.8 8.4 %collective-permute-start.4 = (bf16[1024,128]{1,0:T(8,128)(2,1)S(1)}, bf16[1024,128]{1,0:T(8,128)(2,1)S(1)}, u32[]{:S(2)}, u32[]{:S(2)}) collective-permute-start(bf16[1024,128]{1,0:T(8,128)(2,1)S(1)} %get-tuple-element.48.refs_0_), channel_id=1, source_target_pairs={{0,1},{1,0},{2,3},{3,2},{4,5},{5,4},{6,7},{7,6},{8,9},{9,8},{10,11... | collective-permute-start | bytes 786440 | tf_op jit(solution)/shard_map/ppermute | solution.py:28
  28.3 8.5 %collective-permute-start.3 = (bf16[1024,128]{1,0:T(8,128)(2,1)S(1)}, bf16[1024,128]{1,0:T(8,128)(2,1)S(1)}, u32[]{:S(2)}, u32[]{:S(2)}) collective-permute-start(bf16[1024,128]{1,0:T(8,128)(2,1)S(1)} %get-tuple-element.43.refs_2_), channel_id=1, source_target_pairs={{0,2},{1,3},{2,4},{3,5},{4,6},{5,7},{6,8},{7,9},{8,10},{9,11},{10,... | collective-permute-start | bytes 786440 | tf_op jit(solution)/shard_map/ppermute | solution.py:28
  32.5 8.5 %collective-permute-start.5 = (bf16[1024,128]{1,0:T(8,128)(2,1)S(1)}, bf16[1024,128]{1,0:T(8,128)(2,1)S(1)}, u32[]{:S(2)}, u32[]{:S(2)}) collective-permute-start(bf16[1024,128]{1,0:T(8,128)(2,1)S(1)} %get-tuple-element.49), channel_id=1, source_target_pairs={{0,2},{1,3},{2,4},{3,5},{4,6},{5,7},{6,8},{7,9},{8,10},{9,11},{10,... | collective-permute-start | bytes 786440 | tf_op jit(solution)/shard_map/ppermute | solution.py:28
  38.2 9.2 %collective-permute-start.6 = (bf16[1024,128]{1,0:T(8,128)(2,1)S(1)}, bf16[1024,128]{1,0:T(8,128)(2,1)S(1)}, u32[]{:S(2)}, u32[]{:S(2)}) collective-permute-start(bf16[1024,128]{1,0:T(8,128)(2,1)S(1)} %get-tuple-element.52.refs_0_), channel_id=1, source_target_pairs={{0,1},{1,0},{2,3},{3,2},{4,5},{5,4},{6,7},{7,6},{8,9},{9,8},{10,11... | collective-permute-start | bytes 786440 | tf_op jit(solution)/shard_map/ppermute | solution.py:28
  38.3 9.2 %collective-permute-start.7 = (bf16[1024,128]{1,0:T(8,128)(2,1)S(1)}, bf16[1024,128]{1,0:T(8,128)(2,1)S(1)}, u32[]{:S(2)}, u32[]{:S(2)}) collective-permute-start(bf16[1024,128]{1,0:T(8,128)(2,1)S(1)} %get-tuple-element.53), channel_id=1, source_target_pairs={{0,2},{1,3},{2,4},{3,5},{4,6},{5,7},{6,8},{7,9},{8,10},{9,11},{10,... | collective-permute-start | bytes 786440 | tf_op jit(solution)/shard_map/ppermute | solution.py:28
  42.3 10.7 %collective-permute-start.8 = (bf16[1024,128]{1,0:T(8,128)(2,1)S(1)}, bf16[1024,128]{1,0:T(8,128)(2,1)S(1)}, u32[]{:S(2)}, u32[]{:S(2)}) collective-permute-start(bf16[1024,128]{1,0:T(8,128)(2,1)S(1)} %get-tuple-element.55.refs_0_), channel_id=1, source_target_pairs={{0,1},{1,0},{2,3},{3,2},{4,5},{5,4},{6,7},{7,6},{8,9},{9,8},{10,11... | collective-permute-start | bytes 786440 | tf_op jit(solution)/shard_map/ppermute | solution.py:28
  43.1 10.0 %collective-permute-start.9 = (bf16[1024,128]{1,0:T(8,128)(2,1)S(1)}, bf16[1024,128]{1,0:T(8,128)(2,1)S(1)}, u32[]{:S(2)}, u32[]{:S(2)}) collective-permute-start(bf16[1024,128]{1,0:T(8,128)(2,1)S(1)} %get-tuple-element.56), channel_id=1, source_target_pairs={{0,2},{1,3},{2,4},{3,5},{4,6},{5,7},{6,8},{7,9},{8,10},{9,11},{10,... | collective-permute-start | bytes 786440 | tf_op jit(solution)/shard_map/ppermute | solution.py:28
  48.8 9.7 %collective-permute-start.11 = (bf16[1024,128]{1,0:T(8,128)(2,1)S(1)}, bf16[1024,128]{1,0:T(8,128)(2,1)S(1)}, u32[]{:S(2)}, u32[]{:S(2)}) collective-permute-start(bf16[1024,128]{1,0:T(8,128)(2,1)S(1)} %get-tuple-element.63.refs_0_), channel_id=1, source_target_pairs={{0,1},{1,0},{2,3},{3,2},{4,5},{5,4},{6,7},{7,6},{8,9},{9,8},{10,11... | collective-permute-start | bytes 786440 | tf_op jit(solution)/shard_map/ppermute | solution.py:28
  54.4 6.9 %collective-permute-start.10 = (bf16[1024,128]{1,0:T(8,128)(2,1)S(1)}, bf16[1024,128]{1,0:T(8,128)(2,1)S(1)}, u32[]{:S(2)}, u32[]{:S(2)}) collective-permute-start(bf16[1024,128]{1,0:T(8,128)(2,1)S(1)} %get-tuple-element.60.refs_0_), channel_id=1, source_target_pairs={{0,1},{1,0},{2,3},{3,2},{4,5},{5,4},{6,7},{7,6},{8,9},{9,8},{10,11... | collective-permute-start | bytes 786440 | tf_op jit(solution)/shard_map/ppermute | solution.py:28

commit v8 on v7

--- a/solution.py
+++ b/solution.py
@@ -9,7 +9,8 @@
 
 SUB = 2
 INNER = 2
-CHUNKS = 2
+CHUNKS = 4
+FIRST = 2
 TILE = 256
 
 
@@ -122,10 +123,7 @@
     )(ratings, items, users)
 
 
-def chunk_kernel(n_terms, leaves, sub_epoch, column, offset, rate_ref, half_ref, grad_ref, items_ref, *refs):
-    if leaves:
-        leaving_ref, *refs, leaving_out = refs
-        leaving_out[...] = leaving_ref[...]
+def chunk_kernel(n_terms, sub_epoch, column, items_at, accum_at, terms_at, rate_ref, half_ref, grad_ref, items_ref, *refs):
     term_refs, refs = refs[:n_terms], refs[n_terms:]
     if n_terms:
         accum_ref, *refs = refs
@@ -135,32 +133,31 @@
     grad = grad_ref[...]
     for start in range(0, term_out.shape[0], TILE):
         at = pl.ds(start, TILE)
-        held = pl.ds(offset + start, TILE)
-        items = items_ref[held, :]
+        items = items_ref[pl.ds(items_at + start, TILE), :]
         if n_terms:
-            items, accum = item_step(items, accum_ref[held, :], [ref[at, :] for ref in term_refs])
+            accum = accum_ref[pl.ds(accum_at + start, TILE), :]
+            items, accum = item_step(items, accum, [ref[pl.ds(terms_at + start, TILE), :] for ref in term_refs])
             updated[0][at, :] = items
             updated[1][at, :] = accum
-        term_out[at, :], part = chunk_tile(half, half_t, items, rate_ref[sub_epoch, :, pl.ds(column + start, TILE)])
+        term_out[at, :], part = chunk_tile(
+            half, half_t, items, rate_ref[sub_epoch, :, pl.ds(column + start, TILE)]
+        )
         grad = grad - part
     grad_out[...] = grad
 
 
-def chunk_pass(ratings, sub_epoch, rows, half, grad, items, accum, terms, leaving=()):
-    size, rank = rows.stop - rows.start, items.shape[1]
-    offset = 0 if items.shape[0] == size else rows.start
+def chunk_pass(ratings, sub_epoch, rows, half, grad, items, accum, terms, terms_at):
+    size, rank = rows.stop - rows.start, half.shape[1]
     out_shape = [
         jax.ShapeDtypeStruct((size, rank), jnp.bfloat16),
         jax.ShapeDtypeStruct(grad.shape, jnp.float32),
     ]
-    operands = [ratings, half, grad, items]
+    operands = [ratings, half, grad, items[0]]
     if terms:
         out_shape += [jax.ShapeDtypeStruct((size, rank), jnp.float32)] * 2
-        operands += [*terms, accum]
-    operands += leaving
-    out_shape += [jax.ShapeDtypeStruct(array.shape, array.dtype) for array in leaving]
-    return pl.pallas_call(
-        functools.partial(chunk_kernel, len(terms), len(leaving), sub_epoch, rows.start, offset),
+        operands += [*terms, accum[0]]
+    return pl.pallas_call(
+        functools.partial(chunk_kernel, len(terms), sub_epoch, rows.start, items[1], accum[1], terms_at),
         out_shape=out_shape,
         in_specs=[WHOLE] * len(operands),
         out_specs=[WHOLE] * len(out_shape),
@@ -169,22 +166,29 @@
     )(*operands)
 
 
-def parting_kernel(n_terms, items_ref, accum_ref, *refs):
+def parting_kernel(n_terms, n_behind, items_ref, accum_ref, *refs):
+    size = items_ref.shape[0]
     items, accum = item_step(items_ref[...], accum_ref[...], [ref[...] for ref in refs[:n_terms]])
-    items_out, accum_out = refs[-2:]
-    items_out[...] = items.astype(items_out.dtype)
-    accum_out[...] = accum.astype(accum_out.dtype)
-
-
-def parting_step(items, accum, terms, before):
-    return pl.pallas_call(
-        functools.partial(parting_kernel, len(terms)),
-        out_shape=[jax.ShapeDtypeStruct(items.shape, jnp.bfloat16)] * 2,
-        in_specs=[WHOLE] * (2 + len(terms)) + [pl.BlockSpec(memory_space=pl.ANY)] * len(before),
+    sent, accum_out = refs[-2:]
+    sent[pl.ds(0, size), :] = items.astype(jnp.bfloat16)
+    if n_behind:
+        sent[pl.ds(size, size), :] = refs[n_terms][...]
+    accum_out[...] = accum.astype(jnp.bfloat16)
+
+
+def parting_step(items, accum, terms, behind, after):
+    size, rank = items.shape
+    return pl.pallas_call(
+        functools.partial(parting_kernel, len(terms), len(behind)),
+        out_shape=[
+            jax.ShapeDtypeStruct((size * (1 + len(behind)), rank), jnp.bfloat16),
+            jax.ShapeDtypeStruct((size, rank), jnp.bfloat16),
+        ],
+        in_specs=[WHOLE] * (2 + len(terms) + len(behind)) + [pl.BlockSpec(memory_space=pl.ANY)] * len(after),
         out_specs=[WHOLE] * 2,
         compiler_params=params(),
-        cost_estimate=cost(1, *items.shape),
-    )(items, accum, *terms, *before)
+        cost_estimate=cost(1, size, rank),
+    )(items, accum, *terms, *behind, *after)
 
 
 def last_kernel(n_terms, row, items_ref, accum_ref, *refs):
@@ -223,39 +227,54 @@
     user_acc = user_accum
     size = item_factors.shape[0] // CHUNKS
     rows = [slice(c * size, (c + 1) * size) for c in range(CHUNKS)]
-    items = [item_factors] * CHUNKS
-    item_acc = [item_accum] * CHUNKS
+    items = [(item_factors, r.start) for r in rows]
+    item_acc = [(item_accum, r.start) for r in rows]
     terms = [()] * CHUNKS
+    behind = []
+
+    def part(c, after):
+        nonlocal behind
+        sent, accum = parting_step(items[c][0], item_acc[c][0], terms[c], behind, after)
+        items[c] = (moved(sent, 1, 0), 0)
+        if c > 0:
+            item_acc[c - 1] = (items[c][0], size)
+        behind, terms[c] = [accum], ()
+
     for step in range(SUB * INNER):
         sub_epoch = step // INNER
         rotates = step > 0 and step % INNER == 0
         if rotates:
-            before = []
-            for c in range(CHUNKS):
-                items[c], item_acc[c] = parting_step(items[c], item_acc[c], terms[c], before)
-                before = [items[c]]
-                items[c] = moved(items[c], 1, 0)
-                terms[c] = ()
+            behind = []
+            for c in range(CHUNKS - 1):
+                part(c, [])
         if step > 0:
             user_half = users.astype(jnp.bfloat16)
             grad_user = shrink * users
         for c in range(CHUNKS):
-            if step == 0 and c == 0:
-                term, grad_user, user_half = first_pass(ratings, rows[c], users, items[c])
+            if rotates and c == 1:
+                part(CHUNKS - 1, [term])
+                item_acc[CHUNKS - 1] = (moved(behind[0], 1, 0), 0)
+            if step == 0:
+                if c % FIRST:
+                    terms[c] = terms[c - 1]
+                    continue
+                both = slice(rows[c].start, rows[c + FIRST - 1].stop)
+                if c == 0:
+                    term, grad_user, user_half = first_pass(ratings, both, users, item_factors)
+                else:
+                    term, grad_user = chunk_pass(ratings, 0, both, user_half, grad_user, items[c], item_acc[c], (), 0)
             else:
                 term, grad_user, *updated = chunk_pass(
                     ratings, sub_epoch, rows[c], user_half, grad_user, items[c], item_acc[c], terms[c],
-                    [item_acc[c]] if rotates else [],
+                    c % FIRST * size if step == 1 else 0,
                 )
-                if rotates:
-                    item_acc[c] = moved(updated[0], 1, 0)
-                elif updated:
-                    items[c], item_acc[c] = updated
+                if updated:
+                    items[c], item_acc[c] = ((array, 0) for array in updated)
             terms[c] = group_terms(term)
         users, user_acc = adagrad(users, user_acc, grad_user)
     filled = []
     for c in range(CHUNKS):
-        filled = [last_item_step(rows[c], item_factors.shape[0], items[c], item_acc[c], terms[c], filled)]
+        filled = [last_item_step(rows[c], item_factors.shape[0], items[c][0], item_acc[c][0], terms[c], filled)]
     return (users, filled[0])
 
 

time: 62.6 us -> 61.7 us (0.986)
  waiting for transfers between devices: 32.7 us -> 22.3 us
  starting transfers between devices: 7.78 us -> 15.1 us
  Pallas kernels: 15.8 us -> 17.9 us
    ppermute x12 -> x19, waiting for transfers between devices: 32.7 us -> 22.3 us  [moved(): return lax.ppermute(shard, ('loop', 'grp'), pairs)]
    ppermute x12 -> x19, starting transfers between devices: 7.78 us -> 15.1 us  [moved(): return lax.ppermute(shard, ('loop', 'grp'), pairs)]
    pallas_call x2 -> x4, Pallas kernels: 1.8 us -> 3.14 us  [last_item_step(): pl.pallas_call(functools.partial(last_kernel, len(terms), rows.start), ou...]
    pallas_call x9 -> x17, Pallas kernels: 9.84 us -> 10.6 us  [the longest x13 10.1 us: chunk_pass(): pl.pallas_call(functools.partial(chunk_kernel, len(terms), sub_epoch, row...]
  transfers between devices with their start and end apart: 12 -> 19, of which waited for: 10 -> 10; matrix products, arithmetic and copies ran while one was open for 2% -> 2% of each run, Pallas kernels for 17% -> 21%
where the time goes in v8:
time: 61.7 us; the launch traced here: 61.5 us
  waiting for transfers between devices  22.3 us (36%)
  Pallas kernels  17.9 us (29%)
  starting transfers between devices  15.1 us (24%)
  local copies, waits for them, and re-layouts  4.07 us (7%)
  other arithmetic  1.12 us (2%)
  between operations  1.05 us (2%)
    ppermute x19, waiting for transfers between devices, moved(): return lax.ppermute(shard, ('loop', 'grp'), pairs)  22.3 us
    ppermute x19, starting transfers between devices, moved(): return lax.ppermute(shard, ('loop', 'grp'), pairs)  15.1 us
    pallas_call x13, Pallas kernels, chunk_pass(): pl.pallas_call(functools.partial(chunk_kernel, len(terms), sub_epoch, row...  10.1 us
    pallas_call x1, Pallas kernels, first_pass(): pl.pallas_call(functools.partial(first_kernel, rows.start), out_shape=[ja...  4.16 us
    unnamed x18, local copies, waits for them, and re-layouts  4.07 us
    pallas_call x4, Pallas kernels, last_item_step(): pl.pallas_call(functools.partial(last_kernel, len(terms), rows.start), ou...  3.14 us
  transfers between devices with their start and end apart: 19, of which 10 were waited for; matrix products, arithmetic and copies ran while one was open for 2% of the time, Pallas kernels for 21%

profile of v8, /device:TPU:0, one launch (start us, length us, event | category | flops | bytes accessed | tf_op | source)
XLA Modules:
  0.0 61.5 jit_solution(18351489492844344144)
XLA Ops:
  0.7 4.2 %shard_map.68 = (bf16[1024,128]{1,0:T(8,128)(2,1)}, f32[512,128]{1,0:T(8,128)}, bf16[512,128]{1,0:T(8,128)(2,1)}) custom-call(bf16[2,512,2048]{2,1,0:T(8,128)(2,1)} %rate_ref.25, f32[2048,128]{1,0:T(8,128)} %items_ref.9, f32[512,128]{1,0:T(8,128)} %users_hbm.1), custom_call_target="tpu_custom_call" | custom-call | flops 402653184 | bytes 1048576 | tf_op jit(solution)/shard_map/pallas_call | solution.py:106
  4.8 3.0 %collective-permute-start = (bf16[1024,128]{1,0:T(8,128)(2,1)}, bf16[1024,128]{1,0:T(8,128)(2,1)S(1)}, u32[]{:S(2)}, u32[]{:S(2)}) collective-permute-start(bf16[1024,128]{1,0:T(8,128)(2,1)} %get-tuple-element.58.refs_0_), channel_id=1, source_target_pairs={{0,1},{1,0},{2,3},{3,2},{4,5},{5,4},{6,7},{7,6},{8,9},{9,8},{10,11... | collective-permute-start | bytes 786440 | tf_op jit(solution)/shard_map/ppermute | solution.py:29
  7.8 2.2 %copy-done = bf16[2,512,2048]{2,1,0:T(8,128)(2,1)S(1)} copy-done((bf16[2,512,2048]{2,1,0:T(8,128)(2,1)S(1)}, bf16[2,512,2048]{2,1,0:T(8,128)(2,1)}, u32[]{:S(2)}) %copy-start) | copy-done | bytes 4194328
  10.0 0.9 %copy-done.5 = f32[512,128]{1,0:T(8,128)S(1)} copy-done((f32[512,128]{1,0:T(8,128)S(1)}, f32[512,128]{1,0:T(8,128)}, u32[]{:S(2)}) %copy-start.5) | copy-done | bytes 262168
  11.0 0.9 %copy-done.6 = bf16[512,128]{1,0:T(8,128)(2,1)S(1)} copy-done((bf16[512,128]{1,0:T(8,128)(2,1)S(1)}, bf16[512,128]{1,0:T(8,128)(2,1)}, u32[]{:S(2)}) %copy-start.6) | copy-done | bytes 131096
  11.9 1.3 %shard_map.69 = (bf16[1024,128]{1,0:T(8,128)(2,1)S(1)}, f32[512,128]{1,0:T(8,128)S(1)}) custom-call(bf16[2,512,2048]{2,1,0:T(8,128)(2,1)S(1)} %copy-done, bf16[512,128]{1,0:T(8,128)(2,1)S(1)} %copy-done.6, f32[512,128]{1,0:T(8,128)S(1)} %copy-done.5, f32[2048,128]{1,0:T(8,128)S(1)} %copy-done.2), custom_call_target="tpu_custom_call" | custom-call | flops 402653184 | bytes 1048576 | tf_op jit(solution)/shard_map/pallas_call | solution.py:159
  13.4 1.0 %collective-permute-done.refs_1_ = bf16[1024,128]{1,0:T(8,128)(2,1)S(1)} collective-permute-done((bf16[1024,128]{1,0:T(8,128)(2,1)}, bf16[1024,128]{1,0:T(8,128)(2,1)S(1)}, u32[]{:S(2)}, u32[]{:S(2)}) %collective-permute-start) | collective-permute-done | bytes 262176 | tf_op jit(solution)/shard_map/ppermute | solution.py:29
  15.1 2.1 %collective-permute-start.2 = (bf16[512,128]{1,0:T(8,128)(2,1)S(1)}, bf16[512,128]{1,0:T(8,128)(2,1)S(1)}, u32[]{:S(2)}, u32[]{:S(2)}) collective-permute-start(bf16[512,128]{1,0:T(8,128)(2,1)S(1)} %get-tuple-element.66.refs_0_), channel_id=1, source_target_pairs={{0,1},{1,0},{2,3},{3,2},{4,5},{5,4},{6,7},{7,6},{8,9},{9,8},{10,11... | collective-permute-start | bytes 393224 | tf_op jit(solution)/shard_map/ppermute | solution.py:29
  18.1 4.4 %collective-permute-done.1.refs_1_ = bf16[1024,128]{1,0:T(8,128)(2,1)S(1)} collective-permute-done((bf16[1024,128]{1,0:T(8,128)(2,1)S(1)}, bf16[1024,128]{1,0:T(8,128)(2,1)S(1)}, u32[]{:S(2)}, u32[]{:S(2)}) %collective-permute-start.1) | collective-permute-done | bytes 262176 | tf_op jit(solution)/shard_map/ppermute | solution.py:29
  24.1 2.0 %collective-permute-start.6 = (bf16[512,128]{1,0:T(8,128)(2,1)S(1)}, bf16[512,128]{1,0:T(8,128)(2,1)S(1)}, u32[]{:S(2)}, u32[]{:S(2)}) collective-permute-start(bf16[512,128]{1,0:T(8,128)(2,1)S(1)} %get-tuple-element.77.refs_0_), channel_id=1, source_target_pairs={{0,1},{1,0},{2,3},{3,2},{4,5},{5,4},{6,7},{7,6},{8,9},{9,8},{10,11... | collective-permute-start | bytes 393224 | tf_op jit(solution)/shard_map/ppermute | solution.py:29
  26.3 1.8 %collective-permute-done.4.refs_1_ = bf16[512,128]{1,0:T(8,128)(2,1)S(1)} collective-permute-done((bf16[512,128]{1,0:T(8,128)(2,1)S(1)}, bf16[512,128]{1,0:T(8,128)(2,1)S(1)}, u32[]{:S(2)}, u32[]{:S(2)}) %collective-permute-start.4) | collective-permute-done | bytes 131104 | tf_op jit(solution)/shard_map/ppermute | solution.py:29
  28.4 3.8 %collective-permute-done.6.refs_1_ = bf16[512,128]{1,0:T(8,128)(2,1)S(1)} collective-permute-done((bf16[512,128]{1,0:T(8,128)(2,1)S(1)}, bf16[512,128]{1,0:T(8,128)(2,1)S(1)}, u32[]{:S(2)}, u32[]{:S(2)}) %collective-permute-start.6) | collective-permute-done | bytes 131104 | tf_op jit(solution)/shard_map/ppermute | solution.py:29
  32.4 0.9 %collective-permute-done.3.items_ref = bf16[512,128]{1,0:T(8,128)(2,1)S(1)} collective-permute-done((bf16[512,128]{1,0:T(8,128)(2,1)S(1)}, bf16[512,128]{1,0:T(8,128)(2,1)S(1)}, u32[]{:S(2)}, u32[]{:S(2)}) %collective-permute-start.3) | collective-permute-done | bytes 131104 | tf_op jit(solution)/shard_map/ppermute | solution.py:29
  35.7 1.1 %collective-permute-done.5.items_ref.refs_2_ = bf16[1024,128]{1,0:T(8,128)(2,1)S(1)} collective-permute-done((bf16[1024,128]{1,0:T(8,128)(2,1)S(1)}, bf16[1024,128]{1,0:T(8,128)(2,1)S(1)}, u32[]{:S(2)}, u32[]{:S(2)}) %collective-permute-start.5) | collective-permute-done | bytes 262176 | tf_op jit(solution)/shard_map/ppermute | solution.py:29
  37.8 3.1 %collective-permute-done.7.items_ref.refs_2_ = bf16[1024,128]{1,0:T(8,128)(2,1)S(1)} collective-permute-done((bf16[1024,128]{1,0:T(8,128)(2,1)S(1)}, bf16[1024,128]{1,0:T(8,128)(2,1)S(1)}, u32[]{:S(2)}, u32[]{:S(2)}) %collective-permute-start.7) | collective-permute-done | bytes 262176 | tf_op jit(solution)/shard_map/ppermute | solution.py:29
  42.4 1.3 %collective-permute-done.9.items_ref.refs_2_ = bf16[1024,128]{1,0:T(8,128)(2,1)S(1)} collective-permute-done((bf16[1024,128]{1,0:T(8,128)(2,1)S(1)}, bf16[1024,128]{1,0:T(8,128)(2,1)S(1)}, u32[]{:S(2)}, u32[]{:S(2)}) %collective-permute-start.9) | collective-permute-done | bytes 262176 | tf_op jit(solution)/shard_map/ppermute | solution.py:29
  46.0 1.4 %collective-permute-start.18 = (bf16[512,128]{1,0:T(8,128)(2,1)S(1)}, bf16[512,128]{1,0:T(8,128)(2,1)S(1)}, u32[]{:S(2)}, u32[]{:S(2)}) collective-permute-start(bf16[512,128]{1,0:T(8,128)(2,1)S(1)} %get-tuple-element.107.refs_0_), channel_id=1, source_target_pairs={{0,1},{1,0},{2,3},{3,2},{4,5},{5,4},{6,7},{7,6},{8,9},{9,8},{10,11... | collective-permute-start | bytes 393224 | tf_op jit(solution)/shard_map/ppermute | solution.py:29
  49.7 1.3 %collective-permute-start.17 = (bf16[512,128]{1,0:T(8,128)(2,1)S(1)}, bf16[512,128]{1,0:T(8,128)(2,1)S(1)}, u32[]{:S(2)}, u32[]{:S(2)}) collective-permute-start(bf16[512,128]{1,0:T(8,128)(2,1)S(1)} %get-tuple-element.104.refs_0_), channel_id=1, source_target_pairs={{0,1},{1,0},{2,3},{3,2},{4,5},{5,4},{6,7},{7,6},{8,9},{9,8},{10,11... | collective-permute-start | bytes 393224 | tf_op jit(solution)/shard_map/ppermute | solution.py:29
  52.6 1.1 %collective-permute-done.18.refs_1_ = bf16[512,128]{1,0:T(8,128)(2,1)S(1)} collective-permute-done((bf16[512,128]{1,0:T(8,128)(2,1)S(1)}, bf16[512,128]{1,0:T(8,128)(2,1)S(1)}, u32[]{:S(2)}, u32[]{:S(2)}) %collective-permute-start.18) | collective-permute-done | bytes 131104 | tf_op jit(solution)/shard_map/ppermute | solution.py:29
  54.5 0.8 %multiply_subtract_fusion = f32[512,128]{1,0:T(8,128)} fusion(f32[512,128]{1,0:T(8,128)S(1)} %get-tuple-element.95, f32[512,128]{1,0:T(8,128)S(1)} %get-tuple-element.110, f32[512,128]{1,0:T(8,128)S(1)} %get-tuple-element.87, f32[512,128]{1,0:T(8,128)S(1)} %get-tuple-element.109), kind=kLoop, calls=%fused_computation | loop fusion | flops 786432 | bytes 1310720 | tf_op jit(solution)/shard_map/sub | solution.py:34
  55.4 3.6 %collective-permute-done.17.refs_1_ = bf16[512,128]{1,0:T(8,128)(2,1)S(1)} collective-permute-done((bf16[512,128]{1,0:T(8,128)(2,1)S(1)}, bf16[512,128]{1,0:T(8,128)(2,1)S(1)}, u32[]{:S(2)}, u32[]{:S(2)}) %collective-permute-start.17) | collective-permute-done | bytes 131104 | tf_op jit(solution)/shard_map/ppermute | solution.py:29
  58.9 0.8 %shard_map.87.refs_2_ = f32[2048,128]{1,0:T(8,128)} custom-call(f32[512,128]{1,0:T(8,128)S(1)} %get-tuple-element.102.items_ref, f32[512,128]{1,0:T(8,128)S(1)} %get-tuple-element.103.accum_ref, bf16[512,128]{1,0:T(8,128)(2,1)S(1)} %get-tuple-element.104.refs_0_, ...), custom_call_target="tpu_custom_call", output_to_operand_aliasing={{}: (4, {})} | custom-call | flops 393216 | bytes 1024 | tf_op jit(solution)/shard_map/pallas_call | solution.py:210
  59.7 0.8 %shard_map.88.refs_2_ = f32[2048,128]{1,0:T(8,128)} custom-call(f32[512,128]{1,0:T(8,128)S(1)} %get-tuple-element.99.items_ref, f32[512,128]{1,0:T(8,128)S(1)} %get-tuple-element.100.accum_ref, bf16[512,128]{1,0:T(8,128)(2,1)S(1)} %get-tuple-element.101.refs_0_, ...), custom_call_target="tpu_custom_call", output_to_operand_aliasing={{}: (4, {})} | custom-call | flops 393216 | bytes 1024 | tf_op jit(solution)/shard_map/pallas_call | solution.py:210
  60.5 0.8 %shard_map.89 = f32[2048,128]{1,0:T(8,128)} custom-call(f32[512,128]{1,0:T(8,128)S(1)} %get-tuple-element.96.items_ref, f32[512,128]{1,0:T(8,128)S(1)} %get-tuple-element.97.accum_ref, bf16[512,128]{1,0:T(8,128)(2,1)S(1)} %get-tuple-element.98.refs_0_, bf16[512,128]{1,0:T(8,128)(2,1)S(1)} %collective-permute-done.15.refs_1_, ...), custom_call_target="tpu_custom_call", output_to_operand_aliasing={{}: (4, {})} | custom-call | flops 393216 | bytes 1024 | tf_op jit(solution)/shard_map/pallas_call | solution.py:210
  (60 shorter events, 15.6 us)
Async XLA Ops:
  0.6 7.2 %copy-start.2 = (f32[2048,128]{1,0:T(8,128)S(1)}, f32[2048,128]{1,0:T(8,128)}, u32[]{:S(2)}) copy-start(f32[2048,128]{1,0:T(8,128)} %items_ref.9) | copy-start | bytes 3145732
  0.6 12.6 %copy-start.7 = (f32[512,128]{1,0:T(8,128)S(1)}, f32[512,128]{1,0:T(8,128)}, u32[]{:S(2)}) copy-start(f32[512,128]{1,0:T(8,128)} %param.7) | copy-start | bytes 786436
  0.7 12.6 %copy-start.8 = (f32[512,128]{1,0:T(8,128)S(1)}, f32[512,128]{1,0:T(8,128)}, u32[]{:S(2)}) copy-start(f32[512,128]{1,0:T(8,128)} %users_hbm.1) | copy-start | bytes 786436
  4.8 9.5 %collective-permute-start = (bf16[1024,128]{1,0:T(8,128)(2,1)}, bf16[1024,128]{1,0:T(8,128)(2,1)S(1)}, u32[]{:S(2)}, u32[]{:S(2)}) collective-permute-start(bf16[1024,128]{1,0:T(8,128)(2,1)} %get-tuple-element.58.refs_0_), channel_id=1, source_target_pairs={{0,1},{1,0},{2,3},{3,2},{4,5},{5,4},{6,7},{7,6},{8,9},{9,8},{10,11... | collective-permute-start | bytes 786440 | tf_op jit(solution)/shard_map/ppermute | solution.py:29
  11.9 2.5 %copy-start.4 = (bf16[1024,128]{1,0:T(8,128)(2,1)S(1)}, bf16[1024,128]{1,0:T(8,128)(2,1)}, u32[]{:S(2)}) copy-start(bf16[1024,128]{1,0:T(8,128)(2,1)} %get-tuple-element.58.refs_0_) | copy-start | bytes 786436
  13.2 9.3 %collective-permute-start.1 = (bf16[1024,128]{1,0:T(8,128)(2,1)S(1)}, bf16[1024,128]{1,0:T(8,128)(2,1)S(1)}, u32[]{:S(2)}, u32[]{:S(2)}) collective-permute-start(bf16[1024,128]{1,0:T(8,128)(2,1)S(1)} %get-tuple-element.61.refs_0_), channel_id=1, source_target_pairs={{0,1},{1,0},{2,3},{3,2},{4,5},{5,4},{6,7},{7,6},{8,9},{9,8},{10,11... | collective-permute-start | bytes 786440 | tf_op jit(solution)/shard_map/ppermute | solution.py:29
  15.1 11.0 %collective-permute-start.2 = (bf16[512,128]{1,0:T(8,128)(2,1)S(1)}, bf16[512,128]{1,0:T(8,128)(2,1)S(1)}, u32[]{:S(2)}, u32[]{:S(2)}) collective-permute-start(bf16[512,128]{1,0:T(8,128)(2,1)S(1)} %get-tuple-element.66.refs_0_), channel_id=1, source_target_pairs={{0,1},{1,0},{2,3},{3,2},{4,5},{5,4},{6,7},{7,6},{8,9},{9,8},{10,11... | collective-permute-start | bytes 393224 | tf_op jit(solution)/shard_map/ppermute | solution.py:29
  18.0 10.1 %collective-permute-start.4 = (bf16[512,128]{1,0:T(8,128)(2,1)S(1)}, bf16[512,128]{1,0:T(8,128)(2,1)S(1)}, u32[]{:S(2)}, u32[]{:S(2)}) collective-permute-start(bf16[512,128]{1,0:T(8,128)(2,1)S(1)} %get-tuple-element.71.refs_0_), channel_id=1, source_target_pairs={{0,1},{1,0},{2,3},{3,2},{4,5},{5,4},{6,7},{7,6},{8,9},{9,8},{10,11... | collective-permute-start | bytes 393224 | tf_op jit(solution)/shard_map/ppermute | solution.py:29
  24.0 9.4 %copy-start.1 = (bf16[2,512,2048]{2,1,0:T(8,128)(2,1)S(1)}, bf16[2,512,2048]{2,1,0:T(8,128)(2,1)}, u32[]{:S(2)}) copy-start(bf16[2,512,2048]{2,1,0:T(8,128)(2,1)} %rate_ref.25) | copy-start | bytes 12582916
  24.0 10.1 %collective-permute-start.8 = (bf16[512,128]{1,0:T(8,128)(2,1)S(1)}, bf16[512,128]{1,0:T(8,128)(2,1)S(1)}, u32[]{:S(2)}, u32[]{:S(2)}) collective-permute-start(bf16[512,128]{1,0:T(8,128)(2,1)S(1)} %get-tuple-element.83.refs_0_), channel_id=1, source_target_pairs={{0,1},{1,0},{2,3},{3,2},{4,5},{5,4},{6,7},{7,6},{8,9},{9,8},{10,11... | collective-permute-start | bytes 393224 | tf_op jit(solution)/shard_map/ppermute | solution.py:29
  24.1 8.2 %collective-permute-start.6 = (bf16[512,128]{1,0:T(8,128)(2,1)S(1)}, bf16[512,128]{1,0:T(8,128)(2,1)S(1)}, u32[]{:S(2)}, u32[]{:S(2)}) collective-permute-start(bf16[512,128]{1,0:T(8,128)(2,1)S(1)} %get-tuple-element.77.refs_0_), channel_id=1, source_target_pairs={{0,1},{1,0},{2,3},{3,2},{4,5},{5,4},{6,7},{7,6},{8,9},{9,8},{10,11... | collective-permute-start | bytes 393224 | tf_op jit(solution)/shard_map/ppermute | solution.py:29
  26.2 7.1 %collective-permute-start.3 = (bf16[512,128]{1,0:T(8,128)(2,1)S(1)}, bf16[512,128]{1,0:T(8,128)(2,1)S(1)}, u32[]{:S(2)}, u32[]{:S(2)}) collective-permute-start(bf16[512,128]{1,0:T(8,128)(2,1)S(1)} %get-tuple-element.67), channel_id=1, source_target_pairs={{0,2},{1,3},{2,4},{3,5},{4,6},{5,7},{6,8},{7,9},{8,10},{9,11},{10,... | collective-permute-start | bytes 393224 | tf_op jit(solution)/shard_map/ppermute | solution.py:29
  28.2 8.5 %collective-permute-start.5 = (bf16[1024,128]{1,0:T(8,128)(2,1)S(1)}, bf16[1024,128]{1,0:T(8,128)(2,1)S(1)}, u32[]{:S(2)}, u32[]{:S(2)}) collective-permute-start(bf16[1024,128]{1,0:T(8,128)(2,1)S(1)} %get-tuple-element.73), channel_id=1, source_target_pairs={{0,2},{1,3},{2,4},{3,5},{4,6},{5,7},{6,8},{7,9},{8,10},{9,11},{10,... | collective-permute-start | bytes 786440 | tf_op jit(solution)/shard_map/ppermute | solution.py:29
  32.4 8.5 %collective-permute-start.7 = (bf16[1024,128]{1,0:T(8,128)(2,1)S(1)}, bf16[1024,128]{1,0:T(8,128)(2,1)S(1)}, u32[]{:S(2)}, u32[]{:S(2)}) collective-permute-start(bf16[1024,128]{1,0:T(8,128)(2,1)S(1)} %get-tuple-element.79), channel_id=1, source_target_pairs={{0,2},{1,3},{2,4},{3,5},{4,6},{5,7},{6,8},{7,9},{8,10},{9,11},{10,... | collective-permute-start | bytes 786440 | tf_op jit(solution)/shard_map/ppermute | solution.py:29
  34.2 9.5 %collective-permute-start.9 = (bf16[1024,128]{1,0:T(8,128)(2,1)S(1)}, bf16[1024,128]{1,0:T(8,128)(2,1)S(1)}, u32[]{:S(2)}, u32[]{:S(2)}) collective-permute-start(bf16[1024,128]{1,0:T(8,128)(2,1)S(1)} %get-tuple-element.86), channel_id=1, source_target_pairs={{0,2},{1,3},{2,4},{3,5},{4,6},{5,7},{6,8},{7,9},{8,10},{9,11},{10,... | collective-permute-start | bytes 786440 | tf_op jit(solution)/shard_map/ppermute | solution.py:29
  35.0 10.3 %collective-permute-start.10 = (bf16[512,128]{1,0:T(8,128)(2,1)S(1)}, bf16[512,128]{1,0:T(8,128)(2,1)S(1)}, u32[]{:S(2)}, u32[]{:S(2)}) collective-permute-start(bf16[512,128]{1,0:T(8,128)(2,1)S(1)} %get-tuple-element.85.refs_3_.refs_0_), channel_id=1, source_target_pairs={{0,1},{1,0},{2,3},{3,2},{4,5},{5,4},{6,7},{7,6},{8,9},{9,8},{10,11... | collective-permute-start | bytes 393224 | tf_op jit(solution)/shard_map/ppermute | solution.py:29
  35.7 15.4 %collective-permute-start.14 = (bf16[512,128]{1,0:T(8,128)(2,1)S(1)}, bf16[512,128]{1,0:T(8,128)(2,1)S(1)}, u32[]{:S(2)}, u32[]{:S(2)}) collective-permute-start(bf16[512,128]{1,0:T(8,128)(2,1)S(1)} %get-tuple-element.94), channel_id=1, source_target_pairs={{0,2},{1,3},{2,4},{3,5},{4,6},{5,7},{6,8},{7,9},{8,10},{9,11},{10,... | collective-permute-start | bytes 393224 | tf_op jit(solution)/shard_map/ppermute | solution.py:29
  37.5 10.0 %collective-permute-start.11 = (bf16[512,128]{1,0:T(8,128)(2,1)S(1)}, bf16[512,128]{1,0:T(8,128)(2,1)S(1)}, u32[]{:S(2)}, u32[]{:S(2)}) collective-permute-start(bf16[512,128]{1,0:T(8,128)(2,1)S(1)} %get-tuple-element.89.refs_0_), channel_id=1, source_target_pairs={{0,1},{1,0},{2,3},{3,2},{4,5},{5,4},{6,7},{7,6},{8,9},{9,8},{10,11... | collective-permute-start | bytes 393224 | tf_op jit(solution)/shard_map/ppermute | solution.py:29
  41.6 6.6 %collective-permute-start.12 = (bf16[512,128]{1,0:T(8,128)(2,1)S(1)}, bf16[512,128]{1,0:T(8,128)(2,1)S(1)}, u32[]{:S(2)}, u32[]{:S(2)}) collective-permute-start(bf16[512,128]{1,0:T(8,128)(2,1)S(1)} %get-tuple-element.91.refs_0_), channel_id=1, source_target_pairs={{0,1},{1,0},{2,3},{3,2},{4,5},{5,4},{6,7},{7,6},{8,9},{9,8},{10,11... | collective-permute-start | bytes 393224 | tf_op jit(solution)/shard_map/ppermute | solution.py:29
  44.4 6.6 %collective-permute-start.13 = (bf16[512,128]{1,0:T(8,128)(2,1)S(1)}, bf16[512,128]{1,0:T(8,128)(2,1)S(1)}, u32[]{:S(2)}, u32[]{:S(2)}) collective-permute-start(bf16[512,128]{1,0:T(8,128)(2,1)S(1)} %get-tuple-element.93.refs_0_), channel_id=1, source_target_pairs={{0,1},{1,0},{2,3},{3,2},{4,5},{5,4},{6,7},{7,6},{8,9},{9,8},{10,11... | collective-permute-start | bytes 393224 | tf_op jit(solution)/shard_map/ppermute | solution.py:29
  46.0 7.7 %collective-permute-start.18 = (bf16[512,128]{1,0:T(8,128)(2,1)S(1)}, bf16[512,128]{1,0:T(8,128)(2,1)S(1)}, u32[]{:S(2)}, u32[]{:S(2)}) collective-permute-start(bf16[512,128]{1,0:T(8,128)(2,1)S(1)} %get-tuple-element.107.refs_0_), channel_id=1, source_target_pairs={{0,1},{1,0},{2,3},{3,2},{4,5},{5,4},{6,7},{7,6},{8,9},{9,8},{10,11... | collective-permute-start | bytes 393224 | tf_op jit(solution)/shard_map/ppermute | solution.py:29
  49.0 10.7 %collective-permute-start.16 = (bf16[512,128]{1,0:T(8,128)(2,1)S(1)}, bf16[512,128]{1,0:T(8,128)(2,1)S(1)}, u32[]{:S(2)}, u32[]{:S(2)}) collective-permute-start(bf16[512,128]{1,0:T(8,128)(2,1)S(1)} %get-tuple-element.101.refs_0_), channel_id=1, source_target_pairs={{0,1},{1,0},{2,3},{3,2},{4,5},{5,4},{6,7},{7,6},{8,9},{9,8},{10,11... | collective-permute-start | bytes 393224 | tf_op jit(solution)/shard_map/ppermute | solution.py:29
  49.7 9.2 %collective-permute-start.17 = (bf16[512,128]{1,0:T(8,128)(2,1)S(1)}, bf16[512,128]{1,0:T(8,128)(2,1)S(1)}, u32[]{:S(2)}, u32[]{:S(2)}) collective-permute-start(bf16[512,128]{1,0:T(8,128)(2,1)S(1)} %get-tuple-element.104.refs_0_), channel_id=1, source_target_pairs={{0,1},{1,0},{2,3},{3,2},{4,5},{5,4},{6,7},{7,6},{8,9},{9,8},{10,11... | collective-permute-start | bytes 393224 | tf_op jit(solution)/shard_map/ppermute | solution.py:29
  51.8 8.7 %collective-permute-start.15 = (bf16[512,128]{1,0:T(8,128)(2,1)S(1)}, bf16[512,128]{1,0:T(8,128)(2,1)S(1)}, u32[]{:S(2)}, u32[]{:S(2)}) collective-permute-start(bf16[512,128]{1,0:T(8,128)(2,1)S(1)} %get-tuple-element.98.refs_0_), channel_id=1, source_target_pairs={{0,1},{1,0},{2,3},{3,2},{4,5},{5,4},{6,7},{7,6},{8,9},{9,8},{10,11... | collective-permute-start | bytes 393224 | tf_op jit(solution)/shard_map/ppermute | solution.py:29
  (4 other events, 6.5 us)

commit v9 on v8

--- a/solution.py
+++ b/solution.py
@@ -123,11 +123,11 @@
     )(ratings, items, users)
 
 
-def chunk_kernel(n_terms, sub_epoch, column, items_at, accum_at, terms_at, rate_ref, half_ref, grad_ref, items_ref, *refs):
+def chunk_kernel(n_terms, n_after, sub_epoch, column, items_at, accum_at, terms_at, rate_ref, half_ref, grad_ref, items_ref, *refs):
     term_refs, refs = refs[:n_terms], refs[n_terms:]
     if n_terms:
         accum_ref, *refs = refs
-    term_out, grad_out, *updated = refs
+    term_out, grad_out, *updated = refs[n_after:]
     half = half_ref[...]
     half_t = half.T
     grad = grad_ref[...]
@@ -146,7 +146,7 @@
     grad_out[...] = grad
 
 
-def chunk_pass(ratings, sub_epoch, rows, half, grad, items, accum, terms, terms_at):
+def chunk_pass(ratings, sub_epoch, rows, half, grad, items, accum, terms, terms_at, after=()):
     size, rank = rows.stop - rows.start, half.shape[1]
     out_shape = [
         jax.ShapeDtypeStruct((size, rank), jnp.bfloat16),
@@ -157,13 +157,13 @@
         out_shape += [jax.ShapeDtypeStruct((size, rank), jnp.float32)] * 2
         operands += [*terms, accum[0]]
     return pl.pallas_call(
-        functools.partial(chunk_kernel, len(terms), sub_epoch, rows.start, items[1], accum[1], terms_at),
+        functools.partial(chunk_kernel, len(terms), len(after), sub_epoch, rows.start, items[1], accum[1], terms_at),
         out_shape=out_shape,
-        in_specs=[WHOLE] * len(operands),
+        in_specs=[WHOLE] * len(operands) + [pl.BlockSpec(memory_space=pl.ANY)] * len(after),
         out_specs=[WHOLE] * len(out_shape),
         compiler_params=params(),
         cost_estimate=cost(half.shape[0], size, rank),
-    )(*operands)
+    )(*operands, *after)
 
 
 def parting_kernel(n_terms, n_behind, items_ref, accum_ref, *refs):
@@ -239,14 +239,14 @@
         if c > 0:
             item_acc[c - 1] = (items[c][0], size)
         behind, terms[c] = [accum], ()
+        return [sent]
 
     for step in range(SUB * INNER):
         sub_epoch = step // INNER
         rotates = step > 0 and step % INNER == 0
         if rotates:
-            behind = []
-            for c in range(CHUNKS - 1):
-                part(c, [])
+            for c in range(1, CHUNKS - 1):
+                part(c, [term])
         if step > 0:
             user_half = users.astype(jnp.bfloat16)
             grad_user = shrink * users
@@ -254,6 +254,10 @@
             if rotates and c == 1:
                 part(CHUNKS - 1, [term])
                 item_acc[CHUNKS - 1] = (moved(behind[0], 1, 0), 0)
+            after = []
+            if c == CHUNKS - 1 and step % INNER == INNER - 1 and sub_epoch < SUB - 1:
+                behind = []
+                after = part(0, [])
             if step == 0:
                 if c % FIRST:
                     terms[c] = terms[c - 1]
@@ -266,7 +270,7 @@
             else:
                 term, grad_user, *updated = chunk_pass(
                     ratings, sub_epoch, rows[c], user_half, grad_user, items[c], item_acc[c], terms[c],
-                    c % FIRST * size if step == 1 else 0,
+                    c % FIRST * size if step == 1 else 0, after,
                 )
                 if updated:
                     items[c], item_acc[c] = ((array, 0) for array in updated)

time: 61.7 us -> 60.4 us (0.979)
  starting transfers between devices: 15.1 us -> 14.1 us
    ppermute x19, starting transfers between devices: 15.1 us -> 14.1 us  [moved(): return lax.ppermute(shard, ('loop', 'grp'), pairs)]
  transfers between devices with their start and end apart: 19 -> 19, of which waited for: 10 -> 11; matrix products, arithmetic and copies ran while one was open for 2% -> 2% of each run, Pallas kernels for 21% -> 21%
where the time goes in v9:
time: 60.4 us; the launch traced here: 60.2 us
  waiting for transfers between devices  22 us (36%)
  Pallas kernels  17.9 us (30%)
  starting transfers between devices  14.1 us (23%)
  local copies, waits for them, and re-layouts  4.07 us (7%)
  other arithmetic  1.12 us (2%)
  between operations  1.05 us (2%)
    ppermute x19, waiting for transfers between devices, moved(): return lax.ppermute(shard, ('loop', 'grp'), pairs)  22 us
    ppermute x19, starting transfers between devices, moved(): return lax.ppermute(shard, ('loop', 'grp'), pairs)  14.1 us
    pallas_call x13, Pallas kernels, chunk_pass(): pl.pallas_call(functools.partial(chunk_kernel, len(terms), len(after), su...  10.1 us
    pallas_call x1, Pallas kernels, first_pass(): pl.pallas_call(functools.partial(first_kernel, rows.start), out_shape=[ja...  4.16 us
    unnamed x18, local copies, waits for them, and re-layouts  4.07 us
    pallas_call x4, Pallas kernels, last_item_step(): pl.pallas_call(functools.partial(last_kernel, len(terms), rows.start), ou...  3.14 us
  transfers between devices with their start and end apart: 19, of which 11 were waited for; matrix products, arithmetic and copies ran while one was open for 2% of the time, Pallas kernels for 21%

profile of v9, /device:TPU:0, one launch (start us, length us, event | category | flops | bytes accessed | tf_op | source)
XLA Modules:
  0.0 60.2 jit_solution(16068130349105761417)
XLA Ops:
  0.7 4.2 %shard_map.68 = (bf16[1024,128]{1,0:T(8,128)(2,1)}, f32[512,128]{1,0:T(8,128)}, bf16[512,128]{1,0:T(8,128)(2,1)}) custom-call(bf16[2,512,2048]{2,1,0:T(8,128)(2,1)} %rate_ref.25, f32[2048,128]{1,0:T(8,128)} %items_ref.9, f32[512,128]{1,0:T(8,128)} %users_hbm.1), custom_call_target="tpu_custom_call" | custom-call | flops 402653184 | bytes 1048576 | tf_op jit(solution)/shard_map/pallas_call | solution.py:106
  4.8 3.0 %collective-permute-start = (bf16[1024,128]{1,0:T(8,128)(2,1)}, bf16[1024,128]{1,0:T(8,128)(2,1)S(1)}, u32[]{:S(2)}, u32[]{:S(2)}) collective-permute-start(bf16[1024,128]{1,0:T(8,128)(2,1)} %get-tuple-element.58.refs_0_), channel_id=1, source_target_pairs={{0,1},{1,0},{2,3},{3,2},{4,5},{5,4},{6,7},{7,6},{8,9},{9,8},{10,11... | collective-permute-start | bytes 786440 | tf_op jit(solution)/shard_map/ppermute | solution.py:29
  7.8 2.2 %copy-done = bf16[2,512,2048]{2,1,0:T(8,128)(2,1)S(1)} copy-done((bf16[2,512,2048]{2,1,0:T(8,128)(2,1)S(1)}, bf16[2,512,2048]{2,1,0:T(8,128)(2,1)}, u32[]{:S(2)}) %copy-start) | copy-done | bytes 4194328
  10.0 0.9 %copy-done.5 = f32[512,128]{1,0:T(8,128)S(1)} copy-done((f32[512,128]{1,0:T(8,128)S(1)}, f32[512,128]{1,0:T(8,128)}, u32[]{:S(2)}) %copy-start.5) | copy-done | bytes 262168
  11.0 0.9 %copy-done.6 = bf16[512,128]{1,0:T(8,128)(2,1)S(1)} copy-done((bf16[512,128]{1,0:T(8,128)(2,1)S(1)}, bf16[512,128]{1,0:T(8,128)(2,1)}, u32[]{:S(2)}) %copy-start.6) | copy-done | bytes 131096
  11.9 1.3 %shard_map.69 = (bf16[1024,128]{1,0:T(8,128)(2,1)S(1)}, f32[512,128]{1,0:T(8,128)S(1)}) custom-call(bf16[2,512,2048]{2,1,0:T(8,128)(2,1)S(1)} %copy-done, bf16[512,128]{1,0:T(8,128)(2,1)S(1)} %copy-done.6, f32[512,128]{1,0:T(8,128)S(1)} %copy-done.5, f32[2048,128]{1,0:T(8,128)S(1)} %copy-done.2), custom_call_target="tpu_custom_call" | custom-call | flops 402653184 | bytes 1048576 | tf_op jit(solution)/shard_map/pallas_call | solution.py:159
  13.4 1.0 %collective-permute-done.refs_1_ = bf16[1024,128]{1,0:T(8,128)(2,1)S(1)} collective-permute-done((bf16[1024,128]{1,0:T(8,128)(2,1)}, bf16[1024,128]{1,0:T(8,128)(2,1)S(1)}, u32[]{:S(2)}, u32[]{:S(2)}) %collective-permute-start) | collective-permute-done | bytes 262176 | tf_op jit(solution)/shard_map/ppermute | solution.py:29
  15.1 2.1 %collective-permute-start.2 = (bf16[512,128]{1,0:T(8,128)(2,1)S(1)}, bf16[512,128]{1,0:T(8,128)(2,1)S(1)}, u32[]{:S(2)}, u32[]{:S(2)}) collective-permute-start(bf16[512,128]{1,0:T(8,128)(2,1)S(1)} %get-tuple-element.65.refs_0_), channel_id=1, source_target_pairs={{0,1},{1,0},{2,3},{3,2},{4,5},{5,4},{6,7},{7,6},{8,9},{9,8},{10,11... | collective-permute-start | bytes 393224 | tf_op jit(solution)/shard_map/ppermute | solution.py:29
  18.1 4.4 %collective-permute-done.1.refs_1_ = bf16[1024,128]{1,0:T(8,128)(2,1)S(1)} collective-permute-done((bf16[1024,128]{1,0:T(8,128)(2,1)S(1)}, bf16[1024,128]{1,0:T(8,128)(2,1)S(1)}, u32[]{:S(2)}, u32[]{:S(2)}) %collective-permute-start.1) | collective-permute-done | bytes 262176 | tf_op jit(solution)/shard_map/ppermute | solution.py:29
  23.3 2.0 %collective-permute-done.2.refs_1_ = bf16[512,128]{1,0:T(8,128)(2,1)S(1)} collective-permute-done((bf16[512,128]{1,0:T(8,128)(2,1)S(1)}, bf16[512,128]{1,0:T(8,128)(2,1)S(1)}, u32[]{:S(2)}, u32[]{:S(2)}) %collective-permute-start.2) | collective-permute-done | bytes 131104 | tf_op jit(solution)/shard_map/ppermute | solution.py:29
  26.3 1.7 %collective-permute-done.4.refs_1_ = bf16[512,128]{1,0:T(8,128)(2,1)S(1)} collective-permute-done((bf16[512,128]{1,0:T(8,128)(2,1)S(1)}, bf16[512,128]{1,0:T(8,128)(2,1)S(1)}, u32[]{:S(2)}, u32[]{:S(2)}) %collective-permute-start.4) | collective-permute-done | bytes 131104 | tf_op jit(solution)/shard_map/ppermute | solution.py:29
  28.4 1.0 %collective-permute-done.6.refs_1_ = bf16[512,128]{1,0:T(8,128)(2,1)S(1)} collective-permute-done((bf16[512,128]{1,0:T(8,128)(2,1)S(1)}, bf16[512,128]{1,0:T(8,128)(2,1)S(1)}, u32[]{:S(2)}, u32[]{:S(2)}) %collective-permute-start.6) | collective-permute-done | bytes 131104 | tf_op jit(solution)/shard_map/ppermute | solution.py:29
  30.2 2.4 %collective-permute-done.3.items_ref = bf16[512,128]{1,0:T(8,128)(2,1)S(1)} collective-permute-done((bf16[512,128]{1,0:T(8,128)(2,1)S(1)}, bf16[512,128]{1,0:T(8,128)(2,1)S(1)}, u32[]{:S(2)}, u32[]{:S(2)}) %collective-permute-start.3) | collective-permute-done | bytes 131104 | tf_op jit(solution)/shard_map/ppermute | solution.py:29
  34.1 2.6 %collective-permute-done.5.items_ref.refs_2_ = bf16[1024,128]{1,0:T(8,128)(2,1)S(1)} collective-permute-done((bf16[1024,128]{1,0:T(8,128)(2,1)S(1)}, bf16[1024,128]{1,0:T(8,128)(2,1)S(1)}, u32[]{:S(2)}, u32[]{:S(2)}) %collective-permute-start.5) | collective-permute-done | bytes 262176 | tf_op jit(solution)/shard_map/ppermute | solution.py:29
  37.4 2.1 %collective-permute-done.7.items_ref.refs_2_ = bf16[1024,128]{1,0:T(8,128)(2,1)S(1)} collective-permute-done((bf16[1024,128]{1,0:T(8,128)(2,1)S(1)}, bf16[1024,128]{1,0:T(8,128)(2,1)S(1)}, u32[]{:S(2)}, u32[]{:S(2)}) %collective-permute-start.7) | collective-permute-done | bytes 262176 | tf_op jit(solution)/shard_map/ppermute | solution.py:29
  40.6 1.7 %collective-permute-start.11 = (bf16[512,128]{1,0:T(8,128)(2,1)S(1)}, bf16[512,128]{1,0:T(8,128)(2,1)S(1)}, u32[]{:S(2)}, u32[]{:S(2)}) collective-permute-start(bf16[512,128]{1,0:T(8,128)(2,1)S(1)} %get-tuple-element.89.refs_0_), channel_id=1, source_target_pairs={{0,1},{1,0},{2,3},{3,2},{4,5},{5,4},{6,7},{7,6},{8,9},{9,8},{10,11... | collective-permute-start | bytes 393224 | tf_op jit(solution)/shard_map/ppermute | solution.py:29
  44.2 1.8 %collective-permute-start.18 = (bf16[512,128]{1,0:T(8,128)(2,1)S(1)}, bf16[512,128]{1,0:T(8,128)(2,1)S(1)}, u32[]{:S(2)}, u32[]{:S(2)}) collective-permute-start(bf16[512,128]{1,0:T(8,128)(2,1)S(1)} %get-tuple-element.107.refs_0_), channel_id=1, source_target_pairs={{0,1},{1,0},{2,3},{3,2},{4,5},{5,4},{6,7},{7,6},{8,9},{9,8},{10,11... | collective-permute-start | bytes 393224 | tf_op jit(solution)/shard_map/ppermute | solution.py:29
  46.0 3.1 %collective-permute-done.11.refs_1_ = bf16[512,128]{1,0:T(8,128)(2,1)S(1)} collective-permute-done((bf16[512,128]{1,0:T(8,128)(2,1)S(1)}, bf16[512,128]{1,0:T(8,128)(2,1)S(1)}, u32[]{:S(2)}, u32[]{:S(2)}) %collective-permute-start.11) | collective-permute-done | bytes 131104 | tf_op jit(solution)/shard_map/ppermute | solution.py:29
  51.4 1.3 %collective-permute-start.17 = (bf16[512,128]{1,0:T(8,128)(2,1)S(1)}, bf16[512,128]{1,0:T(8,128)(2,1)S(1)}, u32[]{:S(2)}, u32[]{:S(2)}) collective-permute-start(bf16[512,128]{1,0:T(8,128)(2,1)S(1)} %get-tuple-element.104.refs_0_), channel_id=1, source_target_pairs={{0,1},{1,0},{2,3},{3,2},{4,5},{5,4},{6,7},{7,6},{8,9},{9,8},{10,11... | collective-permute-start | bytes 393224 | tf_op jit(solution)/shard_map/ppermute | solution.py:29
  54.8 0.8 %shard_map.86.refs_2_ = f32[2048,128]{1,0:T(8,128)} custom-call(f32[512,128]{1,0:T(8,128)S(1)} %get-tuple-element.105.items_ref, f32[512,128]{1,0:T(8,128)S(1)} %get-tuple-element.106.accum_ref, bf16[512,128]{1,0:T(8,128)(2,1)S(1)} %get-tuple-element.107.refs_0_, bf16[512,128]{1,0:T(8,128)(2,1)S(1)} %collective-permute-done.18.refs_1_), custom_call_target="tpu_custom_call" | custom-call | flops 393216 | bytes 1024 | tf_op jit(solution)/shard_map/pallas_call | solution.py:210
  55.5 0.8 %multiply_subtract_fusion = f32[512,128]{1,0:T(8,128)} fusion(f32[512,128]{1,0:T(8,128)S(1)} %get-tuple-element.95, f32[512,128]{1,0:T(8,128)S(1)} %get-tuple-element.110, f32[512,128]{1,0:T(8,128)S(1)} %get-tuple-element.87, f32[512,128]{1,0:T(8,128)S(1)} %get-tuple-element.109), kind=kLoop, calls=%fused_computation | loop fusion | flops 786432 | bytes 1310720 | tf_op jit(solution)/shard_map/sub | solution.py:34
  56.4 1.3 %collective-permute-done.17.refs_1_ = bf16[512,128]{1,0:T(8,128)(2,1)S(1)} collective-permute-done((bf16[512,128]{1,0:T(8,128)(2,1)S(1)}, bf16[512,128]{1,0:T(8,128)(2,1)S(1)}, u32[]{:S(2)}, u32[]{:S(2)}) %collective-permute-start.17) | collective-permute-done | bytes 131104 | tf_op jit(solution)/shard_map/ppermute | solution.py:29
  58.5 0.8 %shard_map.88.refs_2_ = f32[2048,128]{1,0:T(8,128)} custom-call(f32[512,128]{1,0:T(8,128)S(1)} %get-tuple-element.99.items_ref, f32[512,128]{1,0:T(8,128)S(1)} %get-tuple-element.100.accum_ref, bf16[512,128]{1,0:T(8,128)(2,1)S(1)} %get-tuple-element.101.refs_0_, ...), custom_call_target="tpu_custom_call", output_to_operand_aliasing={{}: (4, {})} | custom-call | flops 393216 | bytes 1024 | tf_op jit(solution)/shard_map/pallas_call | solution.py:210
  59.3 0.8 %shard_map.89 = f32[2048,128]{1,0:T(8,128)} custom-call(f32[512,128]{1,0:T(8,128)S(1)} %get-tuple-element.96.items_ref, f32[512,128]{1,0:T(8,128)S(1)} %get-tuple-element.97.accum_ref, bf16[512,128]{1,0:T(8,128)(2,1)S(1)} %get-tuple-element.98.refs_0_, bf16[512,128]{1,0:T(8,128)(2,1)S(1)} %collective-permute-done.15.refs_1_, ...), custom_call_target="tpu_custom_call", output_to_operand_aliasing={{}: (4, {})} | custom-call | flops 393216 | bytes 1024 | tf_op jit(solution)/shard_map/pallas_call | solution.py:210
  (60 shorter events, 15.0 us)
Async XLA Ops:
  0.6 7.2 %copy-start.2 = (f32[2048,128]{1,0:T(8,128)S(1)}, f32[2048,128]{1,0:T(8,128)}, u32[]{:S(2)}) copy-start(f32[2048,128]{1,0:T(8,128)} %items_ref.9) | copy-start | bytes 3145732
  0.6 12.6 %copy-start.7 = (f32[512,128]{1,0:T(8,128)S(1)}, f32[512,128]{1,0:T(8,128)}, u32[]{:S(2)}) copy-start(f32[512,128]{1,0:T(8,128)} %param.7) | copy-start | bytes 786436
  0.7 12.6 %copy-start.8 = (f32[512,128]{1,0:T(8,128)S(1)}, f32[512,128]{1,0:T(8,128)}, u32[]{:S(2)}) copy-start(f32[512,128]{1,0:T(8,128)} %users_hbm.1) | copy-start | bytes 786436
  4.8 9.5 %collective-permute-start = (bf16[1024,128]{1,0:T(8,128)(2,1)}, bf16[1024,128]{1,0:T(8,128)(2,1)S(1)}, u32[]{:S(2)}, u32[]{:S(2)}) collective-permute-start(bf16[1024,128]{1,0:T(8,128)(2,1)} %get-tuple-element.58.refs_0_), channel_id=1, source_target_pairs={{0,1},{1,0},{2,3},{3,2},{4,5},{5,4},{6,7},{7,6},{8,9},{9,8},{10,11... | collective-permute-start | bytes 786440 | tf_op jit(solution)/shard_map/ppermute | solution.py:29
  11.9 2.5 %copy-start.4 = (bf16[1024,128]{1,0:T(8,128)(2,1)S(1)}, bf16[1024,128]{1,0:T(8,128)(2,1)}, u32[]{:S(2)}) copy-start(bf16[1024,128]{1,0:T(8,128)(2,1)} %get-tuple-element.58.refs_0_) | copy-start | bytes 786436
  13.2 9.3 %collective-permute-start.1 = (bf16[1024,128]{1,0:T(8,128)(2,1)S(1)}, bf16[1024,128]{1,0:T(8,128)(2,1)S(1)}, u32[]{:S(2)}, u32[]{:S(2)}) collective-permute-start(bf16[1024,128]{1,0:T(8,128)(2,1)S(1)} %get-tuple-element.61.refs_0_), channel_id=1, source_target_pairs={{0,1},{1,0},{2,3},{3,2},{4,5},{5,4},{6,7},{7,6},{8,9},{9,8},{10,11... | collective-permute-start | bytes 786440 | tf_op jit(solution)/shard_map/ppermute | solution.py:29
  15.1 10.2 %collective-permute-start.2 = (bf16[512,128]{1,0:T(8,128)(2,1)S(1)}, bf16[512,128]{1,0:T(8,128)(2,1)S(1)}, u32[]{:S(2)}, u32[]{:S(2)}) collective-permute-start(bf16[512,128]{1,0:T(8,128)(2,1)S(1)} %get-tuple-element.65.refs_0_), channel_id=1, source_target_pairs={{0,1},{1,0},{2,3},{3,2},{4,5},{5,4},{6,7},{7,6},{8,9},{9,8},{10,11... | collective-permute-start | bytes 393224 | tf_op jit(solution)/shard_map/ppermute | solution.py:29
  18.0 7.5 %copy-start.1 = (bf16[2,512,2048]{2,1,0:T(8,128)(2,1)S(1)}, bf16[2,512,2048]{2,1,0:T(8,128)(2,1)}, u32[]{:S(2)}) copy-start(bf16[2,512,2048]{2,1,0:T(8,128)(2,1)} %rate_ref.25) | copy-start | bytes 12582916
  18.0 10.0 %collective-permute-start.4 = (bf16[512,128]{1,0:T(8,128)(2,1)S(1)}, bf16[512,128]{1,0:T(8,128)(2,1)S(1)}, u32[]{:S(2)}, u32[]{:S(2)}) collective-permute-start(bf16[512,128]{1,0:T(8,128)(2,1)S(1)} %get-tuple-element.71.refs_0_), channel_id=1, source_target_pairs={{0,1},{1,0},{2,3},{3,2},{4,5},{5,4},{6,7},{7,6},{8,9},{9,8},{10,11... | collective-permute-start | bytes 393224 | tf_op jit(solution)/shard_map/ppermute | solution.py:29
  23.2 6.2 %collective-permute-start.6 = (bf16[512,128]{1,0:T(8,128)(2,1)S(1)}, bf16[512,128]{1,0:T(8,128)(2,1)S(1)}, u32[]{:S(2)}, u32[]{:S(2)}) collective-permute-start(bf16[512,128]{1,0:T(8,128)(2,1)S(1)} %get-tuple-element.78.refs_0_), channel_id=1, source_target_pairs={{0,1},{1,0},{2,3},{3,2},{4,5},{5,4},{6,7},{7,6},{8,9},{9,8},{10,11... | collective-permute-start | bytes 393224 | tf_op jit(solution)/shard_map/ppermute | solution.py:29
  25.4 7.1 %collective-permute-start.3 = (bf16[512,128]{1,0:T(8,128)(2,1)S(1)}, bf16[512,128]{1,0:T(8,128)(2,1)S(1)}, u32[]{:S(2)}, u32[]{:S(2)}) collective-permute-start(bf16[512,128]{1,0:T(8,128)(2,1)S(1)} %get-tuple-element.66.refs_3_), channel_id=1, source_target_pairs={{0,2},{1,3},{2,4},{3,5},{4,6},{5,7},{6,8},{7,9},{8,10},{9,11},{10,... | collective-permute-start | bytes 393224 | tf_op jit(solution)/shard_map/ppermute | solution.py:29
  26.2 7.0 %collective-permute-start.8 = (bf16[512,128]{1,0:T(8,128)(2,1)S(1)}, bf16[512,128]{1,0:T(8,128)(2,1)S(1)}, u32[]{:S(2)}, u32[]{:S(2)}) collective-permute-start(bf16[512,128]{1,0:T(8,128)(2,1)S(1)} %get-tuple-element.73.refs_3_.refs_0_), channel_id=1, source_target_pairs={{0,1},{1,0},{2,3},{3,2},{4,5},{5,4},{6,7},{7,6},{8,9},{9,8},{10,11... | collective-permute-start | bytes 393224 | tf_op jit(solution)/shard_map/ppermute | solution.py:29
  28.2 8.5 %collective-permute-start.5 = (bf16[1024,128]{1,0:T(8,128)(2,1)S(1)}, bf16[1024,128]{1,0:T(8,128)(2,1)S(1)}, u32[]{:S(2)}, u32[]{:S(2)}) collective-permute-start(bf16[1024,128]{1,0:T(8,128)(2,1)S(1)} %get-tuple-element.74), channel_id=1, source_target_pairs={{0,2},{1,3},{2,4},{3,5},{4,6},{5,7},{6,8},{7,9},{8,10},{9,11},{10,... | collective-permute-start | bytes 786440 | tf_op jit(solution)/shard_map/ppermute | solution.py:29
  29.6 9.9 %collective-permute-start.7 = (bf16[1024,128]{1,0:T(8,128)(2,1)S(1)}, bf16[1024,128]{1,0:T(8,128)(2,1)S(1)}, u32[]{:S(2)}, u32[]{:S(2)}) collective-permute-start(bf16[1024,128]{1,0:T(8,128)(2,1)S(1)} %get-tuple-element.80), channel_id=1, source_target_pairs={{0,2},{1,3},{2,4},{3,5},{4,6},{5,7},{6,8},{7,9},{8,10},{9,11},{10,... | collective-permute-start | bytes 786440 | tf_op jit(solution)/shard_map/ppermute | solution.py:29
  33.4 8.9 %collective-permute-start.9 = (bf16[1024,128]{1,0:T(8,128)(2,1)S(1)}, bf16[1024,128]{1,0:T(8,128)(2,1)S(1)}, u32[]{:S(2)}, u32[]{:S(2)}) collective-permute-start(bf16[1024,128]{1,0:T(8,128)(2,1)S(1)} %get-tuple-element.86), channel_id=1, source_target_pairs={{0,2},{1,3},{2,4},{3,5},{4,6},{5,7},{6,8},{7,9},{8,10},{9,11},{10,... | collective-permute-start | bytes 786440 | tf_op jit(solution)/shard_map/ppermute | solution.py:29
  33.5 10.0 %collective-permute-start.10 = (bf16[512,128]{1,0:T(8,128)(2,1)S(1)}, bf16[512,128]{1,0:T(8,128)(2,1)S(1)}, u32[]{:S(2)}, u32[]{:S(2)}) collective-permute-start(bf16[512,128]{1,0:T(8,128)(2,1)S(1)} %get-tuple-element.85.refs_3_.refs_0_), channel_id=1, source_target_pairs={{0,1},{1,0},{2,3},{3,2},{4,5},{5,4},{6,7},{7,6},{8,9},{9,8},{10,11... | collective-permute-start | bytes 393224 | tf_op jit(solution)/shard_map/ppermute | solution.py:29
  33.6 19.2 %collective-permute-start.14 = (bf16[512,128]{1,0:T(8,128)(2,1)S(1)}, bf16[512,128]{1,0:T(8,128)(2,1)S(1)}, u32[]{:S(2)}, u32[]{:S(2)}) collective-permute-start(bf16[512,128]{1,0:T(8,128)(2,1)S(1)} %get-tuple-element.94), channel_id=1, source_target_pairs={{0,2},{1,3},{2,4},{3,5},{4,6},{5,7},{6,8},{7,9},{8,10},{9,11},{10,... | collective-permute-start | bytes 393224 | tf_op jit(solution)/shard_map/ppermute | solution.py:29
  40.2 9.7 %collective-permute-start.12 = (bf16[512,128]{1,0:T(8,128)(2,1)S(1)}, bf16[512,128]{1,0:T(8,128)(2,1)S(1)}, u32[]{:S(2)}, u32[]{:S(2)}) collective-permute-start(bf16[512,128]{1,0:T(8,128)(2,1)S(1)} %get-tuple-element.91.refs_0_), channel_id=1, source_target_pairs={{0,1},{1,0},{2,3},{3,2},{4,5},{5,4},{6,7},{7,6},{8,9},{9,8},{10,11... | collective-permute-start | bytes 393224 | tf_op jit(solution)/shard_map/ppermute | solution.py:29
  40.6 8.6 %collective-permute-start.11 = (bf16[512,128]{1,0:T(8,128)(2,1)S(1)}, bf16[512,128]{1,0:T(8,128)(2,1)S(1)}, u32[]{:S(2)}, u32[]{:S(2)}) collective-permute-start(bf16[512,128]{1,0:T(8,128)(2,1)S(1)} %get-tuple-element.89.refs_0_), channel_id=1, source_target_pairs={{0,1},{1,0},{2,3},{3,2},{4,5},{5,4},{6,7},{7,6},{8,9},{9,8},{10,11... | collective-permute-start | bytes 393224 | tf_op jit(solution)/shard_map/ppermute | solution.py:29
  43.0 9.7 %collective-permute-start.13 = (bf16[512,128]{1,0:T(8,128)(2,1)S(1)}, bf16[512,128]{1,0:T(8,128)(2,1)S(1)}, u32[]{:S(2)}, u32[]{:S(2)}) collective-permute-start(bf16[512,128]{1,0:T(8,128)(2,1)S(1)} %get-tuple-element.93.refs_0_), channel_id=1, source_target_pairs={{0,1},{1,0},{2,3},{3,2},{4,5},{5,4},{6,7},{7,6},{8,9},{9,8},{10,11... | collective-permute-start | bytes 393224 | tf_op jit(solution)/shard_map/ppermute | solution.py:29
  44.2 10.5 %collective-permute-start.18 = (bf16[512,128]{1,0:T(8,128)(2,1)S(1)}, bf16[512,128]{1,0:T(8,128)(2,1)S(1)}, u32[]{:S(2)}, u32[]{:S(2)}) collective-permute-start(bf16[512,128]{1,0:T(8,128)(2,1)S(1)} %get-tuple-element.107.refs_0_), channel_id=1, source_target_pairs={{0,1},{1,0},{2,3},{3,2},{4,5},{5,4},{6,7},{7,6},{8,9},{9,8},{10,11... | collective-permute-start | bytes 393224 | tf_op jit(solution)/shard_map/ppermute | solution.py:29
  50.7 7.8 %collective-permute-start.16 = (bf16[512,128]{1,0:T(8,128)(2,1)S(1)}, bf16[512,128]{1,0:T(8,128)(2,1)S(1)}, u32[]{:S(2)}, u32[]{:S(2)}) collective-permute-start(bf16[512,128]{1,0:T(8,128)(2,1)S(1)} %get-tuple-element.101.refs_0_), channel_id=1, source_target_pairs={{0,1},{1,0},{2,3},{3,2},{4,5},{5,4},{6,7},{7,6},{8,9},{9,8},{10,11... | collective-permute-start | bytes 393224 | tf_op jit(solution)/shard_map/ppermute | solution.py:29
  51.4 6.2 %collective-permute-start.17 = (bf16[512,128]{1,0:T(8,128)(2,1)S(1)}, bf16[512,128]{1,0:T(8,128)(2,1)S(1)}, u32[]{:S(2)}, u32[]{:S(2)}) collective-permute-start(bf16[512,128]{1,0:T(8,128)(2,1)S(1)} %get-tuple-element.104.refs_0_), channel_id=1, source_target_pairs={{0,1},{1,0},{2,3},{3,2},{4,5},{5,4},{6,7},{7,6},{8,9},{9,8},{10,11... | collective-permute-start | bytes 393224 | tf_op jit(solution)/shard_map/ppermute | solution.py:29
  53.5 5.7 %collective-permute-start.15 = (bf16[512,128]{1,0:T(8,128)(2,1)S(1)}, bf16[512,128]{1,0:T(8,128)(2,1)S(1)}, u32[]{:S(2)}, u32[]{:S(2)}) collective-permute-start(bf16[512,128]{1,0:T(8,128)(2,1)S(1)} %get-tuple-element.98.refs_0_), channel_id=1, source_target_pairs={{0,1},{1,0},{2,3},{3,2},{4,5},{5,4},{6,7},{7,6},{8,9},{9,8},{10,11... | collective-permute-start | bytes 393224 | tf_op jit(solution)/shard_map/ppermute | solution.py:29
  (4 other events, 6.5 us)

commit v10 on v9

--- a/solution.py
+++ b/solution.py
@@ -11,6 +11,7 @@
 INNER = 2
 CHUNKS = 4
 FIRST = 2
+LAST = 2
 TILE = 256
 
 
@@ -123,46 +124,50 @@
     )(ratings, items, users)
 
 
-def chunk_kernel(n_terms, n_after, sub_epoch, column, items_at, accum_at, terms_at, rate_ref, half_ref, grad_ref, items_ref, *refs):
-    term_refs, refs = refs[:n_terms], refs[n_terms:]
-    if n_terms:
-        accum_ref, *refs = refs
-    term_out, grad_out, *updated = refs[n_after:]
+def chunk_kernel(sub_epoch, column, size, places, rate_ref, half_ref, grad_ref, *refs):
     half = half_ref[...]
     half_t = half.T
     grad = grad_ref[...]
-    for start in range(0, term_out.shape[0], TILE):
-        at = pl.ds(start, TILE)
-        items = items_ref[pl.ds(items_at + start, TILE), :]
+    term_out, grad_out, *updated = refs[-4:] if places[0][0] else refs[-2:]
+    for piece, (n_terms, items_at, accum_at, terms_at) in enumerate(places):
+        items_ref, *refs = refs
         if n_terms:
-            accum = accum_ref[pl.ds(accum_at + start, TILE), :]
-            items, accum = item_step(items, accum, [ref[pl.ds(terms_at + start, TILE), :] for ref in term_refs])
-            updated[0][at, :] = items
-            updated[1][at, :] = accum
-        term_out[at, :], part = chunk_tile(
-            half, half_t, items, rate_ref[sub_epoch, :, pl.ds(column + start, TILE)]
-        )
-        grad = grad - part
+            accum_ref, *refs = refs
+            term_refs, refs = refs[:n_terms], refs[n_terms:]
+        for start in range(0, size, TILE):
+            at = pl.ds(piece * size + start, TILE)
+            items = items_ref[pl.ds(items_at + start, TILE), :]
+            if n_terms:
+                accum = accum_ref[pl.ds(accum_at + start, TILE), :]
+                terms = [ref[pl.ds(terms_at + start, TILE), :] for ref in term_refs]
+                items, accum = item_step(items, accum, terms)
+                updated[0][at, :] = items
+                updated[1][at, :] = accum
+            rate = rate_ref[sub_epoch, :, pl.ds(column + piece * size + start, TILE)]
+            term_out[at, :], part = chunk_tile(half, half_t, items, rate)
+            grad = grad - part
     grad_out[...] = grad
 
 
-def chunk_pass(ratings, sub_epoch, rows, half, grad, items, accum, terms, terms_at, after=()):
-    size, rank = rows.stop - rows.start, half.shape[1]
+def chunk_pass(ratings, sub_epoch, rows, half, grad, pieces, after=()):
+    total, rank = rows.stop - rows.start, half.shape[1]
     out_shape = [
-        jax.ShapeDtypeStruct((size, rank), jnp.bfloat16),
+        jax.ShapeDtypeStruct((total, rank), jnp.bfloat16),
         jax.ShapeDtypeStruct(grad.shape, jnp.float32),
     ]
-    operands = [ratings, half, grad, items[0]]
-    if terms:
-        out_shape += [jax.ShapeDtypeStruct((size, rank), jnp.float32)] * 2
-        operands += [*terms, accum[0]]
+    operands, places = [ratings, half, grad], []
+    for items, accum, terms, terms_at in pieces:
+        operands += [items[0], accum[0], *terms] if terms else [items[0]]
+        places.append((len(terms), items[1], accum[1], terms_at))
+    if places[0][0]:
+        out_shape += [jax.ShapeDtypeStruct((total, rank), jnp.float32)] * 2
     return pl.pallas_call(
-        functools.partial(chunk_kernel, len(terms), len(after), sub_epoch, rows.start, items[1], accum[1], terms_at),
+        functools.partial(chunk_kernel, sub_epoch, rows.start, total // len(pieces), places),
         out_shape=out_shape,
         in_specs=[WHOLE] * len(operands) + [pl.BlockSpec(memory_space=pl.ANY)] * len(after),
         out_specs=[WHOLE] * len(out_shape),
         compiler_params=params(),
-        cost_estimate=cost(half.shape[0], size, rank),
+        cost_estimate=cost(half.shape[0], total, rank),
     )(*operands, *after)
 
 
@@ -266,18 +271,25 @@
                 if c == 0:
                     term, grad_user, user_half = first_pass(ratings, both, users, item_factors)
                 else:
-                    term, grad_user = chunk_pass(ratings, 0, both, user_half, grad_user, items[c], item_acc[c], (), 0)
+                    piece = (items[c], item_acc[c], (), 0)
+                    term, grad_user = chunk_pass(ratings, 0, both, user_half, grad_user, [piece])
             else:
+                taken = [c]
+                if step == SUB * INNER - 1:
+                    if c % LAST:
+                        continue
+                    taken = range(c, c + LAST)
+                at = [d % FIRST * size if step == 1 else 0 for d in taken]
                 term, grad_user, *updated = chunk_pass(
-                    ratings, sub_epoch, rows[c], user_half, grad_user, items[c], item_acc[c], terms[c],
-                    c % FIRST * size if step == 1 else 0, after,
+                    ratings, sub_epoch, slice(rows[c].start, rows[taken[-1]].stop), user_half, grad_user,
+                    [(items[d], item_acc[d], terms[d], row) for d, row in zip(taken, at)], after,
                 )
                 if updated:
                     items[c], item_acc[c] = ((array, 0) for array in updated)
             terms[c] = group_terms(term)
         users, user_acc = adagrad(users, user_acc, grad_user)
     filled = []
-    for c in range(CHUNKS):
+    for c in range(0, CHUNKS, LAST):
         filled = [last_item_step(rows[c], item_factors.shape[0], items[c][0], item_acc[c][0], terms[c], filled)]
     return (users, filled[0])
 

time: 60.4 us -> 60.2 us (level)
  waiting for transfers between devices: 22 us -> 27.7 us
  starting transfers between devices: 14.1 us -> 9.87 us
  Pallas kernels: 17.9 us -> 16.3 us
    ppermute x19 -> x17, waiting for transfers between devices: 22 us -> 27.7 us  [moved(): return lax.ppermute(shard, ('loop', 'grp'), pairs)]
    ppermute x19 -> x17, starting transfers between devices: 14.1 us -> 9.87 us  [moved(): return lax.ppermute(shard, ('loop', 'grp'), pairs)]
    pallas_call x4 -> x2, Pallas kernels: 3.14 us -> 1.8 us  [last_item_step(): pl.pallas_call(functools.partial(last_kernel, len(terms), rows.start), ou...]
    pallas_call x13 -> x11, Pallas kernels: 10.1 us -> 9.82 us  [chunk_pass(): pl.pallas_call(functools.partial(chunk_kernel, sub_epoch, rows.start, tot...]
  transfers between devices with their start and end apart: 19 -> 17, of which waited for: 11 -> 13; matrix products, arithmetic and copies ran while one was open for 2% -> 2% of each run, Pallas kernels for 21% -> 19%
where the time goes in v10:
time: 60.2 us; the launch traced here: 60 us
  waiting for transfers between devices  27.7 us (46%)
  Pallas kernels  16.3 us (27%)
  starting transfers between devices  9.87 us (16%)
  local copies, waits for them, and re-layouts  4.07 us (7%)
  other arithmetic  1.11 us (2%)
  between operations  0.99 us (2%)
    ppermute x17, waiting for transfers between devices, moved(): return lax.ppermute(shard, ('loop', 'grp'), pairs)  27.7 us
    ppermute x17, starting transfers between devices, moved(): return lax.ppermute(shard, ('loop', 'grp'), pairs)  9.87 us
    pallas_call x11, Pallas kernels, chunk_pass(): pl.pallas_call(functools.partial(chunk_kernel, sub_epoch, rows.start, tot...  9.82 us
    pallas_call x1, Pallas kernels, first_pass(): pl.pallas_call(functools.partial(first_kernel, rows.start), out_shape=[ja...  4.16 us
    unnamed x18, local copies, waits for them, and re-layouts  4.07 us
    pallas_call x2, Pallas kernels, last_item_step(): pl.pallas_call(functools.partial(last_kernel, len(terms), rows.start), ou...  1.8 us
  transfers between devices with their start and end apart: 17, of which 13 were waited for; matrix products, arithmetic and copies ran while one was open for 2% of the time, Pallas kernels for 19%

profile of v10, /device:TPU:0, one launch (start us, length us, event | category | flops | bytes accessed | tf_op | source)
XLA Modules:
  0.0 60.0 jit_solution(649348800804777571)
XLA Ops:
  0.7 4.2 %shard_map.68 = (bf16[1024,128]{1,0:T(8,128)(2,1)}, f32[512,128]{1,0:T(8,128)}, bf16[512,128]{1,0:T(8,128)(2,1)}) custom-call(bf16[2,512,2048]{2,1,0:T(8,128)(2,1)} %rate_ref.21, f32[2048,128]{1,0:T(8,128)} %refs_0_.9, f32[512,128]{1,0:T(8,128)} %users_hbm.1), custom_call_target="tpu_custom_call" | custom-call | flops 402653184 | bytes 1048576 | tf_op jit(solution)/shard_map/pallas_call | solution.py:107
  4.8 3.0 %collective-permute-start = (bf16[1024,128]{1,0:T(8,128)(2,1)}, bf16[1024,128]{1,0:T(8,128)(2,1)S(1)}, u32[]{:S(2)}, u32[]{:S(2)}) collective-permute-start(bf16[1024,128]{1,0:T(8,128)(2,1)} %get-tuple-element.50.refs_2_), channel_id=1, source_target_pairs={{0,1},{1,0},{2,3},{3,2},{4,5},{5,4},{6,7},{7,6},{8,9},{9,8},{10,11... | collective-permute-start | bytes 786440 | tf_op jit(solution)/shard_map/ppermute | solution.py:30
  7.8 2.2 %copy-done = bf16[2,512,2048]{2,1,0:T(8,128)(2,1)S(1)} copy-done((bf16[2,512,2048]{2,1,0:T(8,128)(2,1)S(1)}, bf16[2,512,2048]{2,1,0:T(8,128)(2,1)}, u32[]{:S(2)}) %copy-start) | copy-done | bytes 4194328
  10.0 0.9 %copy-done.5 = f32[512,128]{1,0:T(8,128)S(1)} copy-done((f32[512,128]{1,0:T(8,128)S(1)}, f32[512,128]{1,0:T(8,128)}, u32[]{:S(2)}) %copy-start.5) | copy-done | bytes 262168
  11.0 0.9 %copy-done.6 = bf16[512,128]{1,0:T(8,128)(2,1)S(1)} copy-done((bf16[512,128]{1,0:T(8,128)(2,1)S(1)}, bf16[512,128]{1,0:T(8,128)(2,1)}, u32[]{:S(2)}) %copy-start.6) | copy-done | bytes 131096
  11.9 1.3 %shard_map.69 = (bf16[1024,128]{1,0:T(8,128)(2,1)S(1)}, f32[512,128]{1,0:T(8,128)S(1)}) custom-call(bf16[2,512,2048]{2,1,0:T(8,128)(2,1)S(1)} %copy-done, bf16[512,128]{1,0:T(8,128)(2,1)S(1)} %copy-done.6, f32[512,128]{1,0:T(8,128)S(1)} %copy-done.5, f32[2048,128]{1,0:T(8,128)S(1)} %copy-done.2), custom_call_target="tpu_custom_call" | custom-call | flops 402653184 | bytes 1048576 | tf_op jit(solution)/shard_map/pallas_call | solution.py:164
  13.4 1.0 %collective-permute-done.refs_3_ = bf16[1024,128]{1,0:T(8,128)(2,1)S(1)} collective-permute-done((bf16[1024,128]{1,0:T(8,128)(2,1)}, bf16[1024,128]{1,0:T(8,128)(2,1)S(1)}, u32[]{:S(2)}, u32[]{:S(2)}) %collective-permute-start) | collective-permute-done | bytes 262176 | tf_op jit(solution)/shard_map/ppermute | solution.py:30
  15.1 2.1 %collective-permute-start.2 = (bf16[512,128]{1,0:T(8,128)(2,1)S(1)}, bf16[512,128]{1,0:T(8,128)(2,1)S(1)}, u32[]{:S(2)}, u32[]{:S(2)}) collective-permute-start(bf16[512,128]{1,0:T(8,128)(2,1)S(1)} %get-tuple-element.57.refs_0_), channel_id=1, source_target_pairs={{0,1},{1,0},{2,3},{3,2},{4,5},{5,4},{6,7},{7,6},{8,9},{9,8},{10,11... | collective-permute-start | bytes 393224 | tf_op jit(solution)/shard_map/ppermute | solution.py:30
  18.1 4.4 %collective-permute-done.1.refs_3_ = bf16[1024,128]{1,0:T(8,128)(2,1)S(1)} collective-permute-done((bf16[1024,128]{1,0:T(8,128)(2,1)S(1)}, bf16[1024,128]{1,0:T(8,128)(2,1)S(1)}, u32[]{:S(2)}, u32[]{:S(2)}) %collective-permute-start.1) | collective-permute-done | bytes 262176 | tf_op jit(solution)/shard_map/ppermute | solution.py:30
  23.3 2.0 %collective-permute-done.2.refs_1_ = bf16[512,128]{1,0:T(8,128)(2,1)S(1)} collective-permute-done((bf16[512,128]{1,0:T(8,128)(2,1)S(1)}, bf16[512,128]{1,0:T(8,128)(2,1)S(1)}, u32[]{:S(2)}, u32[]{:S(2)}) %collective-permute-start.2) | collective-permute-done | bytes 131104 | tf_op jit(solution)/shard_map/ppermute | solution.py:30
  26.3 1.7 %collective-permute-done.4.refs_1_ = bf16[512,128]{1,0:T(8,128)(2,1)S(1)} collective-permute-done((bf16[512,128]{1,0:T(8,128)(2,1)S(1)}, bf16[512,128]{1,0:T(8,128)(2,1)S(1)}, u32[]{:S(2)}, u32[]{:S(2)}) %collective-permute-start.4) | collective-permute-done | bytes 131104 | tf_op jit(solution)/shard_map/ppermute | solution.py:30
  28.4 1.0 %collective-permute-done.6.refs_1_ = bf16[512,128]{1,0:T(8,128)(2,1)S(1)} collective-permute-done((bf16[512,128]{1,0:T(8,128)(2,1)S(1)}, bf16[512,128]{1,0:T(8,128)(2,1)S(1)}, u32[]{:S(2)}, u32[]{:S(2)}) %collective-permute-start.6) | collective-permute-done | bytes 131104 | tf_op jit(solution)/shard_map/ppermute | solution.py:30
  30.2 2.4 %collective-permute-done.3.refs_0_ = bf16[512,128]{1,0:T(8,128)(2,1)S(1)} collective-permute-done((bf16[512,128]{1,0:T(8,128)(2,1)S(1)}, bf16[512,128]{1,0:T(8,128)(2,1)S(1)}, u32[]{:S(2)}, u32[]{:S(2)}) %collective-permute-start.3) | collective-permute-done | bytes 131104 | tf_op jit(solution)/shard_map/ppermute | solution.py:30
  34.1 2.6 %collective-permute-done.5.refs_0_.refs_1_.refs_4_ = bf16[1024,128]{1,0:T(8,128)(2,1)S(1)} collective-permute-done((bf16[1024,128]{1,0:T(8,128)(2,1)S(1)}, bf16[1024,128]{1,0:T(8,128)(2,1)S(1)}, u32[]{:S(2)}, u32[]{:S(2)}) %collective-permute-start.5) | collective-permute-done | bytes 262176 | tf_op jit(solution)/shard_map/ppermute | solution.py:30
  37.8 1.7 %collective-permute-done.7.refs_0_.refs_5_ = bf16[1024,128]{1,0:T(8,128)(2,1)S(1)} collective-permute-done((bf16[1024,128]{1,0:T(8,128)(2,1)S(1)}, bf16[1024,128]{1,0:T(8,128)(2,1)S(1)}, u32[]{:S(2)}, u32[]{:S(2)}) %collective-permute-start.7) | collective-permute-done | bytes 262176 | tf_op jit(solution)/shard_map/ppermute | solution.py:30
  40.6 1.7 %collective-permute-done.9.refs_0_.refs_1_.refs_4_ = bf16[1024,128]{1,0:T(8,128)(2,1)S(1)} collective-permute-done((bf16[1024,128]{1,0:T(8,128)(2,1)S(1)}, bf16[1024,128]{1,0:T(8,128)(2,1)S(1)}, u32[]{:S(2)}, u32[]{:S(2)}) %collective-permute-start.9) | collective-permute-done | bytes 262176 | tf_op jit(solution)/shard_map/ppermute | solution.py:30
  43.9 1.4 %shard_map.82 = (bf16[1024,128]{1,0:T(8,128)(2,1)S(1)}, f32[512,128]{1,0:T(8,128)S(1)}, f32[1024,128]{1,0:T(8,128)S(1)}, f32[1024,128]{1,0:T(8,128)S(1)}) custom-call(bf16[2,512,2048]{2,1,0:T(8,128)(2,1)S(1)} %copy-done.1, bf16[512,128]{1,0:T(8,128)(2,1)S(1)} %get-tuple-element.98.half_ref, f32[512,128]{1,0:T(8,128)S(1)} %get-tuple-element.97.grad_ref, ...), custom_call_target="tpu_custom_call" | custom-call | flops 402653184 | bytes 1048576 | tf_op jit(solution)/shard_map/pallas_call | solution.py:164
  45.3 1.4 %collective-permute-start.16 = (bf16[1024,128]{1,0:T(8,128)(2,1)S(1)}, bf16[1024,128]{1,0:T(8,128)(2,1)S(1)}, u32[]{:S(2)}, u32[]{:S(2)}) collective-permute-start(bf16[1024,128]{1,0:T(8,128)(2,1)S(1)} %get-tuple-element.91.refs_0_), channel_id=1, source_target_pairs={{0,1},{1,0},{2,3},{3,2},{4,5},{5,4},{6,7},{7,6},{8,9},{9,8},{10,11... | collective-permute-start | bytes 786440 | tf_op jit(solution)/shard_map/ppermute | solution.py:30
  46.7 2.8 %collective-permute-done.14.refs_7_ = bf16[512,128]{1,0:T(8,128)(2,1)S(1)} collective-permute-done((bf16[512,128]{1,0:T(8,128)(2,1)S(1)}, bf16[512,128]{1,0:T(8,128)(2,1)S(1)}, u32[]{:S(2)}, u32[]{:S(2)}) %collective-permute-start.14) | collective-permute-done | bytes 131104 | tf_op jit(solution)/shard_map/ppermute | solution.py:30
  49.5 1.4 %shard_map.83 = (bf16[1024,128]{1,0:T(8,128)(2,1)S(1)}, f32[512,128]{1,0:T(8,128)S(1)}, f32[1024,128]{1,0:T(8,128)S(1)}, f32[1024,128]{1,0:T(8,128)S(1)}) custom-call(bf16[2,512,2048]{2,1,0:T(8,128)(2,1)S(1)} %copy-done.1, bf16[512,128]{1,0:T(8,128)(2,1)S(1)} %get-tuple-element.98.half_ref, f32[512,128]{1,0:T(8,128)S(1)} %get-tuple-element.81.grad_ref, ...), custom_call_target="tpu_custom_call" | custom-call | flops 402653184 | bytes 1048576 | tf_op jit(solution)/shard_map/pallas_call | solution.py:164
  52.1 3.1 %collective-permute-done.16.refs_1_ = bf16[1024,128]{1,0:T(8,128)(2,1)S(1)} collective-permute-done((bf16[1024,128]{1,0:T(8,128)(2,1)S(1)}, bf16[1024,128]{1,0:T(8,128)(2,1)S(1)}, u32[]{:S(2)}, u32[]{:S(2)}) %collective-permute-start.16) | collective-permute-done | bytes 262176 | tf_op jit(solution)/shard_map/ppermute | solution.py:30
  55.1 0.9 %shard_map.84.refs_2_ = f32[2048,128]{1,0:T(8,128)} custom-call(f32[1024,128]{1,0:T(8,128)S(1)} %get-tuple-element.89.items_ref, f32[1024,128]{1,0:T(8,128)S(1)} %get-tuple-element.90.accum_ref, bf16[1024,128]{1,0:T(8,128)(2,1)S(1)} %get-tuple-element.91.refs_0_, bf16[1024,128]{1,0:T(8,128)(2,1)S(1)} %collective-permute-done.16.refs_1_), custom_call_target="tpu_custom_call" | custom-call | flops 786432 | bytes 2048 | tf_op jit(solution)/shard_map/pallas_call | solution.py:215
  56.1 2.9 %collective-permute-done.15.refs_1_ = bf16[1024,128]{1,0:T(8,128)(2,1)S(1)} collective-permute-done((bf16[1024,128]{1,0:T(8,128)(2,1)S(1)}, bf16[1024,128]{1,0:T(8,128)(2,1)S(1)}, u32[]{:S(2)}, u32[]{:S(2)}) %collective-permute-start.15) | collective-permute-done | bytes 262176 | tf_op jit(solution)/shard_map/ppermute | solution.py:30
  59.0 0.9 %shard_map.85 = f32[2048,128]{1,0:T(8,128)} custom-call(f32[1024,128]{1,0:T(8,128)S(1)} %get-tuple-element.86.items_ref, f32[1024,128]{1,0:T(8,128)S(1)} %get-tuple-element.87.accum_ref, bf16[1024,128]{1,0:T(8,128)(2,1)S(1)} %get-tuple-element.88.refs_0_, bf16[1024,128]{1,0:T(8,128)(2,1)S(1)} %collective-permute-done.15.refs_1_, ...), custom_call_target="tpu_custom_call", output_to_operand_aliasing={{}: (4, {})} | custom-call | flops 786432 | bytes 2048 | tf_op jit(solution)/shard_map/pallas_call | solution.py:215
  (52 shorter events, 11.2 us)
Async XLA Ops:
  0.6 7.2 %copy-start.2 = (f32[2048,128]{1,0:T(8,128)S(1)}, f32[2048,128]{1,0:T(8,128)}, u32[]{:S(2)}) copy-start(f32[2048,128]{1,0:T(8,128)} %refs_0_.9) | copy-start | bytes 3145732
  0.6 12.6 %copy-start.7 = (f32[512,128]{1,0:T(8,128)S(1)}, f32[512,128]{1,0:T(8,128)}, u32[]{:S(2)}) copy-start(f32[512,128]{1,0:T(8,128)} %param.7) | copy-start | bytes 786436
  0.7 12.6 %copy-start.8 = (f32[512,128]{1,0:T(8,128)S(1)}, f32[512,128]{1,0:T(8,128)}, u32[]{:S(2)}) copy-start(f32[512,128]{1,0:T(8,128)} %users_hbm.1) | copy-start | bytes 786436
  4.8 9.5 %collective-permute-start = (bf16[1024,128]{1,0:T(8,128)(2,1)}, bf16[1024,128]{1,0:T(8,128)(2,1)S(1)}, u32[]{:S(2)}, u32[]{:S(2)}) collective-permute-start(bf16[1024,128]{1,0:T(8,128)(2,1)} %get-tuple-element.50.refs_2_), channel_id=1, source_target_pairs={{0,1},{1,0},{2,3},{3,2},{4,5},{5,4},{6,7},{7,6},{8,9},{9,8},{10,11... | collective-permute-start | bytes 786440 | tf_op jit(solution)/shard_map/ppermute | solution.py:30
  7.8 2.2 %copy-start = (bf16[2,512,2048]{2,1,0:T(8,128)(2,1)S(1)}, bf16[2,512,2048]{2,1,0:T(8,128)(2,1)}, u32[]{:S(2)}) copy-start(bf16[2,512,2048]{2,1,0:T(8,128)(2,1)} %rate_ref.21) | copy-start | bytes 12582916
  11.9 2.5 %copy-start.3 = (f32[2048,128]{1,0:T(8,128)S(1)}, f32[2048,128]{1,0:T(8,128)}, u32[]{:S(2)}) copy-start(f32[2048,128]{1,0:T(8,128)} %refs_1_.7) | copy-start | bytes 3145732
  11.9 2.5 %copy-start.4 = (bf16[1024,128]{1,0:T(8,128)(2,1)S(1)}, bf16[1024,128]{1,0:T(8,128)(2,1)}, u32[]{:S(2)}) copy-start(bf16[1024,128]{1,0:T(8,128)(2,1)} %get-tuple-element.50.refs_2_) | copy-start | bytes 786436
  13.2 9.3 %collective-permute-start.1 = (bf16[1024,128]{1,0:T(8,128)(2,1)S(1)}, bf16[1024,128]{1,0:T(8,128)(2,1)S(1)}, u32[]{:S(2)}, u32[]{:S(2)}) collective-permute-start(bf16[1024,128]{1,0:T(8,128)(2,1)S(1)} %get-tuple-element.53.refs_2_), channel_id=1, source_target_pairs={{0,1},{1,0},{2,3},{3,2},{4,5},{5,4},{6,7},{7,6},{8,9},{9,8},{10,11... | collective-permute-start | bytes 786440 | tf_op jit(solution)/shard_map/ppermute | solution.py:30
  15.1 10.2 %collective-permute-start.2 = (bf16[512,128]{1,0:T(8,128)(2,1)S(1)}, bf16[512,128]{1,0:T(8,128)(2,1)S(1)}, u32[]{:S(2)}, u32[]{:S(2)}) collective-permute-start(bf16[512,128]{1,0:T(8,128)(2,1)S(1)} %get-tuple-element.57.refs_0_), channel_id=1, source_target_pairs={{0,1},{1,0},{2,3},{3,2},{4,5},{5,4},{6,7},{7,6},{8,9},{9,8},{10,11... | collective-permute-start | bytes 393224 | tf_op jit(solution)/shard_map/ppermute | solution.py:30
  18.0 7.5 %copy-start.1 = (bf16[2,512,2048]{2,1,0:T(8,128)(2,1)S(1)}, bf16[2,512,2048]{2,1,0:T(8,128)(2,1)}, u32[]{:S(2)}) copy-start(bf16[2,512,2048]{2,1,0:T(8,128)(2,1)} %rate_ref.21) | copy-start | bytes 12582916
  18.0 10.0 %collective-permute-start.4 = (bf16[512,128]{1,0:T(8,128)(2,1)S(1)}, bf16[512,128]{1,0:T(8,128)(2,1)S(1)}, u32[]{:S(2)}, u32[]{:S(2)}) collective-permute-start(bf16[512,128]{1,0:T(8,128)(2,1)S(1)} %get-tuple-element.63.refs_0_), channel_id=1, source_target_pairs={{0,1},{1,0},{2,3},{3,2},{4,5},{5,4},{6,7},{7,6},{8,9},{9,8},{10,11... | collective-permute-start | bytes 393224 | tf_op jit(solution)/shard_map/ppermute | solution.py:30
  23.2 6.2 %collective-permute-start.6 = (bf16[512,128]{1,0:T(8,128)(2,1)S(1)}, bf16[512,128]{1,0:T(8,128)(2,1)S(1)}, u32[]{:S(2)}, u32[]{:S(2)}) collective-permute-start(bf16[512,128]{1,0:T(8,128)(2,1)S(1)} %get-tuple-element.70.refs_0_), channel_id=1, source_target_pairs={{0,1},{1,0},{2,3},{3,2},{4,5},{5,4},{6,7},{7,6},{8,9},{9,8},{10,11... | collective-permute-start | bytes 393224 | tf_op jit(solution)/shard_map/ppermute | solution.py:30
  25.4 7.1 %collective-permute-start.3 = (bf16[512,128]{1,0:T(8,128)(2,1)S(1)}, bf16[512,128]{1,0:T(8,128)(2,1)S(1)}, u32[]{:S(2)}, u32[]{:S(2)}) collective-permute-start(bf16[512,128]{1,0:T(8,128)(2,1)S(1)} %get-tuple-element.58.refs_4_), channel_id=1, source_target_pairs={{0,2},{1,3},{2,4},{3,5},{4,6},{5,7},{6,8},{7,9},{8,10},{9,11},{10,... | collective-permute-start | bytes 393224 | tf_op jit(solution)/shard_map/ppermute | solution.py:30
  26.2 7.0 %collective-permute-start.8 = (bf16[512,128]{1,0:T(8,128)(2,1)S(1)}, bf16[512,128]{1,0:T(8,128)(2,1)S(1)}, u32[]{:S(2)}, u32[]{:S(2)}) collective-permute-start(bf16[512,128]{1,0:T(8,128)(2,1)S(1)} %get-tuple-element.65.refs_3_.refs_0_), channel_id=1, source_target_pairs={{0,1},{1,0},{2,3},{3,2},{4,5},{5,4},{6,7},{7,6},{8,9},{9,8},{10,11... | collective-permute-start | bytes 393224 | tf_op jit(solution)/shard_map/ppermute | solution.py:30
  28.2 8.5 %collective-permute-start.5 = (bf16[1024,128]{1,0:T(8,128)(2,1)S(1)}, bf16[1024,128]{1,0:T(8,128)(2,1)S(1)}, u32[]{:S(2)}, u32[]{:S(2)}) collective-permute-start(bf16[1024,128]{1,0:T(8,128)(2,1)S(1)} %get-tuple-element.66), channel_id=1, source_target_pairs={{0,2},{1,3},{2,4},{3,5},{4,6},{5,7},{6,8},{7,9},{8,10},{9,11},{10,... | collective-permute-start | bytes 786440 | tf_op jit(solution)/shard_map/ppermute | solution.py:30
  29.6 9.9 %collective-permute-start.7 = (bf16[1024,128]{1,0:T(8,128)(2,1)S(1)}, bf16[1024,128]{1,0:T(8,128)(2,1)S(1)}, u32[]{:S(2)}, u32[]{:S(2)}) collective-permute-start(bf16[1024,128]{1,0:T(8,128)(2,1)S(1)} %get-tuple-element.72), channel_id=1, source_target_pairs={{0,2},{1,3},{2,4},{3,5},{4,6},{5,7},{6,8},{7,9},{8,10},{9,11},{10,... | collective-permute-start | bytes 786440 | tf_op jit(solution)/shard_map/ppermute | solution.py:30
  33.4 8.9 %collective-permute-start.9 = (bf16[1024,128]{1,0:T(8,128)(2,1)S(1)}, bf16[1024,128]{1,0:T(8,128)(2,1)S(1)}, u32[]{:S(2)}, u32[]{:S(2)}) collective-permute-start(bf16[1024,128]{1,0:T(8,128)(2,1)S(1)} %get-tuple-element.78), channel_id=1, source_target_pairs={{0,2},{1,3},{2,4},{3,5},{4,6},{5,7},{6,8},{7,9},{8,10},{9,11},{10,... | collective-permute-start | bytes 786440 | tf_op jit(solution)/shard_map/ppermute | solution.py:30
  33.5 10.0 %collective-permute-start.10 = (bf16[512,128]{1,0:T(8,128)(2,1)S(1)}, bf16[512,128]{1,0:T(8,128)(2,1)S(1)}, u32[]{:S(2)}, u32[]{:S(2)}) collective-permute-start(bf16[512,128]{1,0:T(8,128)(2,1)S(1)} %get-tuple-element.77.refs_3_.refs_2_), channel_id=1, source_target_pairs={{0,1},{1,0},{2,3},{3,2},{4,5},{5,4},{6,7},{7,6},{8,9},{9,8},{10,11... | collective-permute-start | bytes 393224 | tf_op jit(solution)/shard_map/ppermute | solution.py:30
  33.6 13.1 %collective-permute-start.13 = (bf16[512,128]{1,0:T(8,128)(2,1)S(1)}, bf16[512,128]{1,0:T(8,128)(2,1)S(1)}, u32[]{:S(2)}, u32[]{:S(2)}) collective-permute-start(bf16[512,128]{1,0:T(8,128)(2,1)S(1)} %get-tuple-element.83), channel_id=1, source_target_pairs={{0,2},{1,3},{2,4},{3,5},{4,6},{5,7},{6,8},{7,9},{8,10},{9,11},{10,... | collective-permute-start | bytes 393224 | tf_op jit(solution)/shard_map/ppermute | solution.py:30
  37.4 6.5 %collective-permute-start.11 = (bf16[512,128]{1,0:T(8,128)(2,1)S(1)}, bf16[512,128]{1,0:T(8,128)(2,1)S(1)}, u32[]{:S(2)}, u32[]{:S(2)}) collective-permute-start(bf16[512,128]{1,0:T(8,128)(2,1)S(1)} %get-tuple-element.80.refs_6_), channel_id=1, source_target_pairs={{0,1},{1,0},{2,3},{3,2},{4,5},{5,4},{6,7},{7,6},{8,9},{9,8},{10,11... | collective-permute-start | bytes 393224 | tf_op jit(solution)/shard_map/ppermute | solution.py:30
  40.2 6.5 %collective-permute-start.12 = (bf16[512,128]{1,0:T(8,128)(2,1)S(1)}, bf16[512,128]{1,0:T(8,128)(2,1)S(1)}, u32[]{:S(2)}, u32[]{:S(2)}) collective-permute-start(bf16[512,128]{1,0:T(8,128)(2,1)S(1)} %get-tuple-element.82.refs_2_), channel_id=1, source_target_pairs={{0,1},{1,0},{2,3},{3,2},{4,5},{5,4},{6,7},{7,6},{8,9},{9,8},{10,11... | collective-permute-start | bytes 393224 | tf_op jit(solution)/shard_map/ppermute | solution.py:30
  43.0 6.5 %collective-permute-start.14 = (bf16[512,128]{1,0:T(8,128)(2,1)S(1)}, bf16[512,128]{1,0:T(8,128)(2,1)S(1)}, u32[]{:S(2)}, u32[]{:S(2)}) collective-permute-start(bf16[512,128]{1,0:T(8,128)(2,1)S(1)} %get-tuple-element.84.refs_6_), channel_id=1, source_target_pairs={{0,1},{1,0},{2,3},{3,2},{4,5},{5,4},{6,7},{7,6},{8,9},{9,8},{10,11... | collective-permute-start | bytes 393224 | tf_op jit(solution)/shard_map/ppermute | solution.py:30
  45.3 9.9 %collective-permute-start.16 = (bf16[1024,128]{1,0:T(8,128)(2,1)S(1)}, bf16[1024,128]{1,0:T(8,128)(2,1)S(1)}, u32[]{:S(2)}, u32[]{:S(2)}) collective-permute-start(bf16[1024,128]{1,0:T(8,128)(2,1)S(1)} %get-tuple-element.91.refs_0_), channel_id=1, source_target_pairs={{0,1},{1,0},{2,3},{3,2},{4,5},{5,4},{6,7},{7,6},{8,9},{9,8},{10,11... | collective-permute-start | bytes 786440 | tf_op jit(solution)/shard_map/ppermute | solution.py:30
  50.9 8.1 %collective-permute-start.15 = (bf16[1024,128]{1,0:T(8,128)(2,1)S(1)}, bf16[1024,128]{1,0:T(8,128)(2,1)S(1)}, u32[]{:S(2)}, u32[]{:S(2)}) collective-permute-start(bf16[1024,128]{1,0:T(8,128)(2,1)S(1)} %get-tuple-element.88.refs_0_), channel_id=1, source_target_pairs={{0,1},{1,0},{2,3},{3,2},{4,5},{5,4},{6,7},{7,6},{8,9},{9,8},{10,11... | collective-permute-start | bytes 786440 | tf_op jit(solution)/shard_map/ppermute | solution.py:30
  (2 other events, 1.9 us)

commit v11 on v10

--- a/solution.py
+++ b/solution.py
@@ -171,29 +171,32 @@
     )(*operands, *after)
 
 
-def parting_kernel(n_terms, n_behind, items_ref, accum_ref, *refs):
+def parting_kernel(n_terms, n_held, items_ref, accum_ref, *refs):
     size = items_ref.shape[0]
-    items, accum = item_step(items_ref[...], accum_ref[...], [ref[...] for ref in refs[:n_terms]])
-    sent, accum_out = refs[-2:]
-    sent[pl.ds(0, size), :] = items.astype(jnp.bfloat16)
-    if n_behind:
-        sent[pl.ds(size, size), :] = refs[n_terms][...]
-    accum_out[...] = accum.astype(jnp.bfloat16)
-
-
-def parting_step(items, accum, terms, behind, after):
+    term_refs, held = refs[:n_terms], refs[n_terms : n_terms + n_held]
+    items, accum = item_step(items_ref[...], accum_ref[...], [ref[...] for ref in term_refs])
+    accum = accum.astype(jnp.bfloat16)
+    if not n_held:
+        items_out, accum_out = refs[-2:]
+        accum_out[...] = accum
+    else:
+        items_out, *accum_outs = refs[-1 - CHUNKS // LAST :]
+        for c, part in enumerate([ref[...] for ref in held] + [accum]):
+            accum_outs[c // LAST][pl.ds(c % LAST * size, size), :] = part
+    items_out[...] = items.astype(jnp.bfloat16)
+
+
+def parting_step(items, accum, terms, held, after):
     size, rank = items.shape
+    accums = [(LAST * size, rank)] * (CHUNKS // LAST) if held else [(size, rank)]
     return pl.pallas_call(
-        functools.partial(parting_kernel, len(terms), len(behind)),
-        out_shape=[
-            jax.ShapeDtypeStruct((size * (1 + len(behind)), rank), jnp.bfloat16),
-            jax.ShapeDtypeStruct((size, rank), jnp.bfloat16),
-        ],
-        in_specs=[WHOLE] * (2 + len(terms) + len(behind)) + [pl.BlockSpec(memory_space=pl.ANY)] * len(after),
-        out_specs=[WHOLE] * 2,
+        functools.partial(parting_kernel, len(terms), len(held)),
+        out_shape=[jax.ShapeDtypeStruct(shape, jnp.bfloat16) for shape in [(size, rank), *accums]],
+        in_specs=[WHOLE] * (2 + len(terms) + len(held)) + [pl.BlockSpec(memory_space=pl.ANY)] * len(after),
+        out_specs=[WHOLE] * (1 + len(accums)),
         compiler_params=params(),
         cost_estimate=cost(1, size, rank),
-    )(items, accum, *terms, *behind, *after)
+    )(items, accum, *terms, *held, *after)
 
 
 def last_kernel(n_terms, row, items_ref, accum_ref, *refs):
@@ -235,34 +238,31 @@
     items = [(item_factors, r.start) for r in rows]
     item_acc = [(item_accum, r.start) for r in rows]
     terms = [()] * CHUNKS
-    behind = []
+    held = []
 
     def part(c, after):
-        nonlocal behind
-        sent, accum = parting_step(items[c][0], item_acc[c][0], terms[c], behind, after)
-        items[c] = (moved(sent, 1, 0), 0)
-        if c > 0:
-            item_acc[c - 1] = (items[c][0], size)
-        behind, terms[c] = [accum], ()
-        return [sent]
+        whole = held if c == CHUNKS - 1 else []
+        sent, *accums = parting_step(items[c][0], item_acc[c][0], terms[c], whole, after)
+        items[c], terms[c] = (moved(sent, 1, 0), 0), ()
+        return accums
 
     for step in range(SUB * INNER):
         sub_epoch = step // INNER
         rotates = step > 0 and step % INNER == 0
         if rotates:
             for c in range(1, CHUNKS - 1):
-                part(c, [term])
+                held += part(c, [term, held[-1]])
         if step > 0:
             user_half = users.astype(jnp.bfloat16)
             grad_user = shrink * users
         for c in range(CHUNKS):
             if rotates and c == 1:
-                part(CHUNKS - 1, [term])
-                item_acc[CHUNKS - 1] = (moved(behind[0], 1, 0), 0)
+                accums = [moved(accum, 1, 0) for accum in part(CHUNKS - 1, [term])]
+                item_acc = [(accums[d // LAST], d % LAST * size) for d in range(CHUNKS)]
             after = []
             if c == CHUNKS - 1 and step % INNER == INNER - 1 and sub_epoch < SUB - 1:
-                behind = []
-                after = part(0, [])
+                held = part(0, [])
+                after = held[:]
             if step == 0:
                 if c % FIRST:
                     terms[c] = terms[c - 1]

time: 60.2 us -> 61 us (1.013)
  starting transfers between devices: 9.87 us -> 11 us
    ppermute x17 -> x18, starting transfers between devices: 9.87 us -> 11 us  [moved(): return lax.ppermute(shard, ('loop', 'grp'), pairs)]
    ppermute x17 -> x18, waiting for transfers between devices: 27.7 us -> 27.4 us  [moved(): return lax.ppermute(shard, ('loop', 'grp'), pairs)]
  transfers between devices with their start and end apart: 17 -> 18, of which waited for: 13 -> 15; matrix products, arithmetic and copies ran while one was open for 2% -> 2% of each run, Pallas kernels for 19% -> 18%
where the time goes in v11:
time: 61 us; the launch traced here: 60.8 us
  waiting for transfers between devices  27.4 us (45%)
  Pallas kernels  16.3 us (27%)
  starting transfers between devices  11 us (18%)
  local copies, waits for them, and re-layouts  4.07 us (7%)
  other arithmetic  1.11 us (2%)
  between operations  1 us (2%)
    ppermute x18, waiting for transfers between devices, moved(): return lax.ppermute(shard, ('loop', 'grp'), pairs)  27.4 us
    ppermute x18, starting transfers between devices, moved(): return lax.ppermute(shard, ('loop', 'grp'), pairs)  11 us
    pallas_call x11, Pallas kernels, chunk_pass(): pl.pallas_call(functools.partial(chunk_kernel, sub_epoch, rows.start, tot...  9.83 us
    pallas_call x1, Pallas kernels, first_pass(): pl.pallas_call(functools.partial(first_kernel, rows.start), out_shape=[ja...  4.16 us
    unnamed x18, local copies, waits for them, and re-layouts  4.07 us
    pallas_call x2, Pallas kernels, last_item_step(): pl.pallas_call(functools.partial(last_kernel, len(terms), rows.start), ou...  1.8 us
  transfers between devices with their start and end apart: 18, of which 15 were waited for; matrix products, arithmetic and copies ran while one was open for 2% of the time, Pallas kernels for 18%

profile of v11, /device:TPU:0, one launch (start us, length us, event | category | flops | bytes accessed | tf_op | source)
XLA Modules:
  0.0 60.8 jit_solution(10035471876482446594)
XLA Ops:
  0.7 4.2 %shard_map.68 = (bf16[1024,128]{1,0:T(8,128)(2,1)}, f32[512,128]{1,0:T(8,128)}, bf16[512,128]{1,0:T(8,128)(2,1)}) custom-call(bf16[2,512,2048]{2,1,0:T(8,128)(2,1)} %rate_ref.21, f32[2048,128]{1,0:T(8,128)} %refs_0_.9, f32[512,128]{1,0:T(8,128)} %users_hbm.1), custom_call_target="tpu_custom_call" | custom-call | flops 402653184 | bytes 1048576 | tf_op jit(solution)/shard_map/pallas_call | solution.py:107
  4.8 3.0 %collective-permute-start = (bf16[1024,128]{1,0:T(8,128)(2,1)}, bf16[1024,128]{1,0:T(8,128)(2,1)S(1)}, u32[]{:S(2)}, u32[]{:S(2)}) collective-permute-start(bf16[1024,128]{1,0:T(8,128)(2,1)} %get-tuple-element.51.refs_2_), channel_id=1, source_target_pairs={{0,1},{1,0},{2,3},{3,2},{4,5},{5,4},{6,7},{7,6},{8,9},{9,8},{10,11... | collective-permute-start | bytes 786440 | tf_op jit(solution)/shard_map/ppermute | solution.py:30
  7.8 2.2 %copy-done = bf16[2,512,2048]{2,1,0:T(8,128)(2,1)S(1)} copy-done((bf16[2,512,2048]{2,1,0:T(8,128)(2,1)S(1)}, bf16[2,512,2048]{2,1,0:T(8,128)(2,1)}, u32[]{:S(2)}) %copy-start) | copy-done | bytes 4194328
  10.0 0.9 %copy-done.5 = f32[512,128]{1,0:T(8,128)S(1)} copy-done((f32[512,128]{1,0:T(8,128)S(1)}, f32[512,128]{1,0:T(8,128)}, u32[]{:S(2)}) %copy-start.5) | copy-done | bytes 262168
  11.0 0.9 %copy-done.6 = bf16[512,128]{1,0:T(8,128)(2,1)S(1)} copy-done((bf16[512,128]{1,0:T(8,128)(2,1)S(1)}, bf16[512,128]{1,0:T(8,128)(2,1)}, u32[]{:S(2)}) %copy-start.6) | copy-done | bytes 131096
  11.9 1.3 %shard_map.69 = (bf16[1024,128]{1,0:T(8,128)(2,1)S(1)}, f32[512,128]{1,0:T(8,128)S(1)}) custom-call(bf16[2,512,2048]{2,1,0:T(8,128)(2,1)S(1)} %copy-done, bf16[512,128]{1,0:T(8,128)(2,1)S(1)} %copy-done.6, f32[512,128]{1,0:T(8,128)S(1)} %copy-done.5, f32[2048,128]{1,0:T(8,128)S(1)} %copy-done.2), custom_call_target="tpu_custom_call" | custom-call | flops 402653184 | bytes 1048576 | tf_op jit(solution)/shard_map/pallas_call | solution.py:164
  13.4 1.0 %collective-permute-done.refs_3_ = bf16[1024,128]{1,0:T(8,128)(2,1)S(1)} collective-permute-done((bf16[1024,128]{1,0:T(8,128)(2,1)}, bf16[1024,128]{1,0:T(8,128)(2,1)S(1)}, u32[]{:S(2)}, u32[]{:S(2)}) %collective-permute-start) | collective-permute-done | bytes 262176 | tf_op jit(solution)/shard_map/ppermute | solution.py:30
  15.1 2.1 %collective-permute-start.2 = (bf16[512,128]{1,0:T(8,128)(2,1)S(1)}, bf16[512,128]{1,0:T(8,128)(2,1)S(1)}, u32[]{:S(2)}, u32[]{:S(2)}) collective-permute-start(bf16[512,128]{1,0:T(8,128)(2,1)S(1)} %get-tuple-element.58.refs_0_), channel_id=1, source_target_pairs={{0,1},{1,0},{2,3},{3,2},{4,5},{5,4},{6,7},{7,6},{8,9},{9,8},{10,11... | collective-permute-start | bytes 393224 | tf_op jit(solution)/shard_map/ppermute | solution.py:30
  18.1 4.4 %collective-permute-done.1.refs_3_ = bf16[1024,128]{1,0:T(8,128)(2,1)S(1)} collective-permute-done((bf16[1024,128]{1,0:T(8,128)(2,1)S(1)}, bf16[1024,128]{1,0:T(8,128)(2,1)S(1)}, u32[]{:S(2)}, u32[]{:S(2)}) %collective-permute-start.1) | collective-permute-done | bytes 262176 | tf_op jit(solution)/shard_map/ppermute | solution.py:30
  23.3 2.0 %collective-permute-done.2.refs_1_ = bf16[512,128]{1,0:T(8,128)(2,1)S(1)} collective-permute-done((bf16[512,128]{1,0:T(8,128)(2,1)S(1)}, bf16[512,128]{1,0:T(8,128)(2,1)S(1)}, u32[]{:S(2)}, u32[]{:S(2)}) %collective-permute-start.2) | collective-permute-done | bytes 131104 | tf_op jit(solution)/shard_map/ppermute | solution.py:30
  26.3 1.7 %collective-permute-done.4.refs_1_ = bf16[512,128]{1,0:T(8,128)(2,1)S(1)} collective-permute-done((bf16[512,128]{1,0:T(8,128)(2,1)S(1)}, bf16[512,128]{1,0:T(8,128)(2,1)S(1)}, u32[]{:S(2)}, u32[]{:S(2)}) %collective-permute-start.4) | collective-permute-done | bytes 131104 | tf_op jit(solution)/shard_map/ppermute | solution.py:30
  28.4 1.0 %collective-permute-done.6.refs_1_ = bf16[512,128]{1,0:T(8,128)(2,1)S(1)} collective-permute-done((bf16[512,128]{1,0:T(8,128)(2,1)S(1)}, bf16[512,128]{1,0:T(8,128)(2,1)S(1)}, u32[]{:S(2)}, u32[]{:S(2)}) %collective-permute-start.6) | collective-permute-done | bytes 131104 | tf_op jit(solution)/shard_map/ppermute | solution.py:30
  30.2 2.4 %collective-permute-done.3.refs_0_ = bf16[512,128]{1,0:T(8,128)(2,1)S(1)} collective-permute-done((bf16[512,128]{1,0:T(8,128)(2,1)S(1)}, bf16[512,128]{1,0:T(8,128)(2,1)S(1)}, u32[]{:S(2)}, u32[]{:S(2)}) %collective-permute-start.3) | collective-permute-done | bytes 131104 | tf_op jit(solution)/shard_map/ppermute | solution.py:30
  33.5 1.8 %collective-permute-done.5.refs_0_.refs_4_ = bf16[512,128]{1,0:T(8,128)(2,1)S(1)} collective-permute-done((bf16[512,128]{1,0:T(8,128)(2,1)S(1)}, bf16[512,128]{1,0:T(8,128)(2,1)S(1)}, u32[]{:S(2)}, u32[]{:S(2)}) %collective-permute-start.5) | collective-permute-done | bytes 131104 | tf_op jit(solution)/shard_map/ppermute | solution.py:30
  36.4 1.7 %collective-permute-start.11 = (bf16[512,128]{1,0:T(8,128)(2,1)S(1)}, bf16[512,128]{1,0:T(8,128)(2,1)S(1)}, u32[]{:S(2)}, u32[]{:S(2)}) collective-permute-start(bf16[512,128]{1,0:T(8,128)(2,1)S(1)} %get-tuple-element.78.refs_5_.refs_2_), channel_id=1, source_target_pairs={{0,1},{1,0},{2,3},{3,2},{4,5},{5,4},{6,7},{7,6},{8,9},{9,8},{10,11... | collective-permute-start | bytes 393224 | tf_op jit(solution)/shard_map/ppermute | solution.py:30
  38.8 1.7 %collective-permute-done.9.refs_0_.refs_4_ = bf16[512,128]{1,0:T(8,128)(2,1)S(1)} collective-permute-done((bf16[512,128]{1,0:T(8,128)(2,1)S(1)}, bf16[512,128]{1,0:T(8,128)(2,1)S(1)}, u32[]{:S(2)}, u32[]{:S(2)}) %collective-permute-start.9) | collective-permute-done | bytes 131104 | tf_op jit(solution)/shard_map/ppermute | solution.py:30
  41.8 1.6 %collective-permute-start.15 = (bf16[512,128]{1,0:T(8,128)(2,1)S(1)}, bf16[512,128]{1,0:T(8,128)(2,1)S(1)}, u32[]{:S(2)}, u32[]{:S(2)}) collective-permute-start(bf16[512,128]{1,0:T(8,128)(2,1)S(1)} %get-tuple-element.86.refs_6_), channel_id=1, source_target_pairs={{0,1},{1,0},{2,3},{3,2},{4,5},{5,4},{6,7},{7,6},{8,9},{9,8},{10,11... | collective-permute-start | bytes 393224 | tf_op jit(solution)/shard_map/ppermute | solution.py:30
  43.5 1.2 %collective-permute-done.11.refs_3_ = bf16[512,128]{1,0:T(8,128)(2,1)S(1)} collective-permute-done((bf16[512,128]{1,0:T(8,128)(2,1)S(1)}, bf16[512,128]{1,0:T(8,128)(2,1)S(1)}, u32[]{:S(2)}, u32[]{:S(2)}) %collective-permute-start.11) | collective-permute-done | bytes 131104 | tf_op jit(solution)/shard_map/ppermute | solution.py:30
  44.6 2.0 %collective-permute-done.10.refs_1_.refs_5_ = bf16[1024,128]{1,0:T(8,128)(2,1)S(1)} collective-permute-done((bf16[1024,128]{1,0:T(8,128)(2,1)S(1)}, bf16[1024,128]{1,0:T(8,128)(2,1)S(1)}, u32[]{:S(2)}, u32[]{:S(2)}) %collective-permute-start.10) | collective-permute-done | bytes 262176 | tf_op jit(solution)/shard_map/ppermute | solution.py:30
  46.6 1.4 %shard_map.82 = (bf16[1024,128]{1,0:T(8,128)(2,1)S(1)}, f32[512,128]{1,0:T(8,128)S(1)}, f32[1024,128]{1,0:T(8,128)S(1)}, f32[1024,128]{1,0:T(8,128)S(1)}) custom-call(bf16[2,512,2048]{2,1,0:T(8,128)(2,1)S(1)} %copy-done.1, bf16[512,128]{1,0:T(8,128)(2,1)S(1)} %get-tuple-element.100.half_ref, f32[512,128]{1,0:T(8,128)S(1)} %get-tuple-element.99.grad_ref, ...), custom_call_target="tpu_custom_call" | custom-call | flops 402653184 | bytes 1048576 | tf_op jit(solution)/shard_map/pallas_call | solution.py:164
  48.3 1.1 %collective-permute-done.13.refs_1_.refs_5_ = bf16[1024,128]{1,0:T(8,128)(2,1)S(1)} collective-permute-done((bf16[1024,128]{1,0:T(8,128)(2,1)S(1)}, bf16[1024,128]{1,0:T(8,128)(2,1)S(1)}, u32[]{:S(2)}, u32[]{:S(2)}) %collective-permute-start.13) | collective-permute-done | bytes 262176 | tf_op jit(solution)/shard_map/ppermute | solution.py:30
  50.2 1.4 %shard_map.83 = (bf16[1024,128]{1,0:T(8,128)(2,1)S(1)}, f32[512,128]{1,0:T(8,128)S(1)}, f32[1024,128]{1,0:T(8,128)S(1)}, f32[1024,128]{1,0:T(8,128)S(1)}) custom-call(bf16[2,512,2048]{2,1,0:T(8,128)(2,1)S(1)} %copy-done.1, bf16[512,128]{1,0:T(8,128)(2,1)S(1)} %get-tuple-element.100.half_ref, f32[512,128]{1,0:T(8,128)S(1)} %get-tuple-element.83.grad_ref, ...), custom_call_target="tpu_custom_call" | custom-call | flops 402653184 | bytes 1048576 | tf_op jit(solution)/shard_map/pallas_call | solution.py:164
  53.0 4.0 %collective-permute-done.17.refs_1_ = bf16[1024,128]{1,0:T(8,128)(2,1)S(1)} collective-permute-done((bf16[1024,128]{1,0:T(8,128)(2,1)S(1)}, bf16[1024,128]{1,0:T(8,128)(2,1)S(1)}, u32[]{:S(2)}, u32[]{:S(2)}) %collective-permute-start.17) | collective-permute-done | bytes 262176 | tf_op jit(solution)/shard_map/ppermute | solution.py:30
  57.9 1.9 %collective-permute-done.16.refs_1_ = bf16[1024,128]{1,0:T(8,128)(2,1)S(1)} collective-permute-done((bf16[1024,128]{1,0:T(8,128)(2,1)S(1)}, bf16[1024,128]{1,0:T(8,128)(2,1)S(1)}, u32[]{:S(2)}, u32[]{:S(2)}) %collective-permute-start.16) | collective-permute-done | bytes 262176 | tf_op jit(solution)/shard_map/ppermute | solution.py:30
  (54 shorter events, 13.1 us)
Async XLA Ops:
  0.6 7.2 %copy-start.2 = (f32[2048,128]{1,0:T(8,128)S(1)}, f32[2048,128]{1,0:T(8,128)}, u32[]{:S(2)}) copy-start(f32[2048,128]{1,0:T(8,128)} %refs_0_.9) | copy-start | bytes 3145732
  0.6 12.6 %copy-start.7 = (f32[512,128]{1,0:T(8,128)S(1)}, f32[512,128]{1,0:T(8,128)}, u32[]{:S(2)}) copy-start(f32[512,128]{1,0:T(8,128)} %param.7) | copy-start | bytes 786436
  0.7 12.6 %copy-start.8 = (f32[512,128]{1,0:T(8,128)S(1)}, f32[512,128]{1,0:T(8,128)}, u32[]{:S(2)}) copy-start(f32[512,128]{1,0:T(8,128)} %users_hbm.1) | copy-start | bytes 786436
  4.8 9.5 %collective-permute-start = (bf16[1024,128]{1,0:T(8,128)(2,1)}, bf16[1024,128]{1,0:T(8,128)(2,1)S(1)}, u32[]{:S(2)}, u32[]{:S(2)}) collective-permute-start(bf16[1024,128]{1,0:T(8,128)(2,1)} %get-tuple-element.51.refs_2_), channel_id=1, source_target_pairs={{0,1},{1,0},{2,3},{3,2},{4,5},{5,4},{6,7},{7,6},{8,9},{9,8},{10,11... | collective-permute-start | bytes 786440 | tf_op jit(solution)/shard_map/ppermute | solution.py:30
  11.9 2.5 %copy-start.3 = (f32[2048,128]{1,0:T(8,128)S(1)}, f32[2048,128]{1,0:T(8,128)}, u32[]{:S(2)}) copy-start(f32[2048,128]{1,0:T(8,128)} %refs_1_.7) | copy-start | bytes 3145732
  11.9 2.5 %copy-start.4 = (bf16[1024,128]{1,0:T(8,128)(2,1)S(1)}, bf16[1024,128]{1,0:T(8,128)(2,1)}, u32[]{:S(2)}) copy-start(bf16[1024,128]{1,0:T(8,128)(2,1)} %get-tuple-element.51.refs_2_) | copy-start | bytes 786436
  13.2 9.3 %collective-permute-start.1 = (bf16[1024,128]{1,0:T(8,128)(2,1)S(1)}, bf16[1024,128]{1,0:T(8,128)(2,1)S(1)}, u32[]{:S(2)}, u32[]{:S(2)}) collective-permute-start(bf16[1024,128]{1,0:T(8,128)(2,1)S(1)} %get-tuple-element.54.refs_2_), channel_id=1, source_target_pairs={{0,1},{1,0},{2,3},{3,2},{4,5},{5,4},{6,7},{7,6},{8,9},{9,8},{10,11... | collective-permute-start | bytes 786440 | tf_op jit(solution)/shard_map/ppermute | solution.py:30
  15.1 10.2 %collective-permute-start.2 = (bf16[512,128]{1,0:T(8,128)(2,1)S(1)}, bf16[512,128]{1,0:T(8,128)(2,1)S(1)}, u32[]{:S(2)}, u32[]{:S(2)}) collective-permute-start(bf16[512,128]{1,0:T(8,128)(2,1)S(1)} %get-tuple-element.58.refs_0_), channel_id=1, source_target_pairs={{0,1},{1,0},{2,3},{3,2},{4,5},{5,4},{6,7},{7,6},{8,9},{9,8},{10,11... | collective-permute-start | bytes 393224 | tf_op jit(solution)/shard_map/ppermute | solution.py:30
  18.0 7.5 %copy-start.1 = (bf16[2,512,2048]{2,1,0:T(8,128)(2,1)S(1)}, bf16[2,512,2048]{2,1,0:T(8,128)(2,1)}, u32[]{:S(2)}) copy-start(bf16[2,512,2048]{2,1,0:T(8,128)(2,1)} %rate_ref.21) | copy-start | bytes 12582916
  18.0 10.0 %collective-permute-start.4 = (bf16[512,128]{1,0:T(8,128)(2,1)S(1)}, bf16[512,128]{1,0:T(8,128)(2,1)S(1)}, u32[]{:S(2)}, u32[]{:S(2)}) collective-permute-start(bf16[512,128]{1,0:T(8,128)(2,1)S(1)} %get-tuple-element.65.refs_0_), channel_id=1, source_target_pairs={{0,1},{1,0},{2,3},{3,2},{4,5},{5,4},{6,7},{7,6},{8,9},{9,8},{10,11... | collective-permute-start | bytes 393224 | tf_op jit(solution)/shard_map/ppermute | solution.py:30
  23.2 6.2 %collective-permute-start.6 = (bf16[512,128]{1,0:T(8,128)(2,1)S(1)}, bf16[512,128]{1,0:T(8,128)(2,1)S(1)}, u32[]{:S(2)}, u32[]{:S(2)}) collective-permute-start(bf16[512,128]{1,0:T(8,128)(2,1)S(1)} %get-tuple-element.71.refs_0_), channel_id=1, source_target_pairs={{0,1},{1,0},{2,3},{3,2},{4,5},{5,4},{6,7},{7,6},{8,9},{9,8},{10,11... | collective-permute-start | bytes 393224 | tf_op jit(solution)/shard_map/ppermute | solution.py:30
  25.4 7.1 %collective-permute-start.3 = (bf16[512,128]{1,0:T(8,128)(2,1)S(1)}, bf16[512,128]{1,0:T(8,128)(2,1)S(1)}, u32[]{:S(2)}, u32[]{:S(2)}) collective-permute-start(bf16[512,128]{1,0:T(8,128)(2,1)S(1)} %get-tuple-element.61), channel_id=1, source_target_pairs={{0,2},{1,3},{2,4},{3,5},{4,6},{5,7},{6,8},{7,9},{8,10},{9,11},{10,... | collective-permute-start | bytes 393224 | tf_op jit(solution)/shard_map/ppermute | solution.py:30
  26.2 7.0 %collective-permute-start.8 = (bf16[512,128]{1,0:T(8,128)(2,1)S(1)}, bf16[512,128]{1,0:T(8,128)(2,1)S(1)}, u32[]{:S(2)}, u32[]{:S(2)}) collective-permute-start(bf16[512,128]{1,0:T(8,128)(2,1)S(1)} %get-tuple-element.66.refs_2_.refs_0_), channel_id=1, source_target_pairs={{0,1},{1,0},{2,3},{3,2},{4,5},{5,4},{6,7},{7,6},{8,9},{9,8},{10,11... | collective-permute-start | bytes 393224 | tf_op jit(solution)/shard_map/ppermute | solution.py:30
  28.2 7.1 %collective-permute-start.5 = (bf16[512,128]{1,0:T(8,128)(2,1)S(1)}, bf16[512,128]{1,0:T(8,128)(2,1)S(1)}, u32[]{:S(2)}, u32[]{:S(2)}) collective-permute-start(bf16[512,128]{1,0:T(8,128)(2,1)S(1)} %get-tuple-element.67), channel_id=1, source_target_pairs={{0,2},{1,3},{2,4},{3,5},{4,6},{5,7},{6,8},{7,9},{8,10},{9,11},{10,... | collective-permute-start | bytes 393224 | tf_op jit(solution)/shard_map/ppermute | solution.py:30
  29.6 8.5 %collective-permute-start.7 = (bf16[512,128]{1,0:T(8,128)(2,1)S(1)}, bf16[512,128]{1,0:T(8,128)(2,1)S(1)}, u32[]{:S(2)}, u32[]{:S(2)}) collective-permute-start(bf16[512,128]{1,0:T(8,128)(2,1)S(1)} %get-tuple-element.73), channel_id=1, source_target_pairs={{0,2},{1,3},{2,4},{3,5},{4,6},{5,7},{6,8},{7,9},{8,10},{9,11},{10,... | collective-permute-start | bytes 393224 | tf_op jit(solution)/shard_map/ppermute | solution.py:30
  33.4 7.1 %collective-permute-start.9 = (bf16[512,128]{1,0:T(8,128)(2,1)S(1)}, bf16[512,128]{1,0:T(8,128)(2,1)S(1)}, u32[]{:S(2)}, u32[]{:S(2)}) collective-permute-start(bf16[512,128]{1,0:T(8,128)(2,1)S(1)} %get-tuple-element.79), channel_id=1, source_target_pairs={{0,2},{1,3},{2,4},{3,5},{4,6},{5,7},{6,8},{7,9},{8,10},{9,11},{10,... | collective-permute-start | bytes 393224 | tf_op jit(solution)/shard_map/ppermute | solution.py:30
  36.0 5.8 %collective-permute-start.12 = (bf16[512,128]{1,0:T(8,128)(2,1)S(1)}, bf16[512,128]{1,0:T(8,128)(2,1)S(1)}, u32[]{:S(2)}, u32[]{:S(2)}) collective-permute-start(bf16[512,128]{1,0:T(8,128)(2,1)S(1)} %get-tuple-element.82.refs_6_), channel_id=1, source_target_pairs={{0,1},{1,0},{2,3},{3,2},{4,5},{5,4},{6,7},{7,6},{8,9},{9,8},{10,11... | collective-permute-start | bytes 393224 | tf_op jit(solution)/shard_map/ppermute | solution.py:30
  36.4 8.3 %collective-permute-start.11 = (bf16[512,128]{1,0:T(8,128)(2,1)S(1)}, bf16[512,128]{1,0:T(8,128)(2,1)S(1)}, u32[]{:S(2)}, u32[]{:S(2)}) collective-permute-start(bf16[512,128]{1,0:T(8,128)(2,1)S(1)} %get-tuple-element.78.refs_5_.refs_2_), channel_id=1, source_target_pairs={{0,1},{1,0},{2,3},{3,2},{4,5},{5,4},{6,7},{7,6},{8,9},{9,8},{10,11... | collective-permute-start | bytes 393224 | tf_op jit(solution)/shard_map/ppermute | solution.py:30
  38.1 8.5 %collective-permute-start.10 = (bf16[1024,128]{1,0:T(8,128)(2,1)S(1)}, bf16[1024,128]{1,0:T(8,128)(2,1)S(1)}, u32[]{:S(2)}, u32[]{:S(2)}) collective-permute-start(bf16[1024,128]{1,0:T(8,128)(2,1)S(1)} %get-tuple-element.81), channel_id=1, source_target_pairs={{0,2},{1,3},{2,4},{3,5},{4,6},{5,7},{6,8},{7,9},{8,10},{9,11},{10,... | collective-permute-start | bytes 786440 | tf_op jit(solution)/shard_map/ppermute | solution.py:30
  38.1 11.3 %collective-permute-start.13 = (bf16[1024,128]{1,0:T(8,128)(2,1)S(1)}, bf16[1024,128]{1,0:T(8,128)(2,1)S(1)}, u32[]{:S(2)}, u32[]{:S(2)}) collective-permute-start(bf16[1024,128]{1,0:T(8,128)(2,1)S(1)} %get-tuple-element.84), channel_id=1, source_target_pairs={{0,2},{1,3},{2,4},{3,5},{4,6},{5,7},{6,8},{7,9},{8,10},{9,11},{10,... | collective-permute-start | bytes 786440 | tf_op jit(solution)/shard_map/ppermute | solution.py:30
  40.6 7.8 %collective-permute-start.14 = (bf16[512,128]{1,0:T(8,128)(2,1)S(1)}, bf16[512,128]{1,0:T(8,128)(2,1)S(1)}, u32[]{:S(2)}, u32[]{:S(2)}) collective-permute-start(bf16[512,128]{1,0:T(8,128)(2,1)S(1)} %get-tuple-element.85.refs_2_), channel_id=1, source_target_pairs={{0,1},{1,0},{2,3},{3,2},{4,5},{5,4},{6,7},{7,6},{8,9},{9,8},{10,11... | collective-permute-start | bytes 393224 | tf_op jit(solution)/shard_map/ppermute | solution.py:30
  41.8 8.4 %collective-permute-start.15 = (bf16[512,128]{1,0:T(8,128)(2,1)S(1)}, bf16[512,128]{1,0:T(8,128)(2,1)S(1)}, u32[]{:S(2)}, u32[]{:S(2)}) collective-permute-start(bf16[512,128]{1,0:T(8,128)(2,1)S(1)} %get-tuple-element.86.refs_6_), channel_id=1, source_target_pairs={{0,1},{1,0},{2,3},{3,2},{4,5},{5,4},{6,7},{7,6},{8,9},{9,8},{10,11... | collective-permute-start | bytes 393224 | tf_op jit(solution)/shard_map/ppermute | solution.py:30
  48.0 9.0 %collective-permute-start.17 = (bf16[1024,128]{1,0:T(8,128)(2,1)S(1)}, bf16[1024,128]{1,0:T(8,128)(2,1)S(1)}, u32[]{:S(2)}, u32[]{:S(2)}) collective-permute-start(bf16[1024,128]{1,0:T(8,128)(2,1)S(1)} %get-tuple-element.93.refs_0_), channel_id=1, source_target_pairs={{0,1},{1,0},{2,3},{3,2},{4,5},{5,4},{6,7},{7,6},{8,9},{9,8},{10,11... | collective-permute-start | bytes 786440 | tf_op jit(solution)/shard_map/ppermute | solution.py:30
  51.6 8.2 %collective-permute-start.16 = (bf16[1024,128]{1,0:T(8,128)(2,1)S(1)}, bf16[1024,128]{1,0:T(8,128)(2,1)S(1)}, u32[]{:S(2)}, u32[]{:S(2)}) collective-permute-start(bf16[1024,128]{1,0:T(8,128)(2,1)S(1)} %get-tuple-element.90.refs_0_), channel_id=1, source_target_pairs={{0,1},{1,0},{2,3},{3,2},{4,5},{5,4},{6,7},{7,6},{8,9},{9,8},{10,11... | collective-permute-start | bytes 786440 | tf_op jit(solution)/shard_map/ppermute | solution.py:30
  (3 other events, 4.0 us)

commit v12 on v10

--- a/solution.py
+++ b/solution.py
@@ -263,6 +263,8 @@
             if c == CHUNKS - 1 and step % INNER == INNER - 1 and sub_epoch < SUB - 1:
                 behind = []
                 after = part(0, [])
+            elif c == FIRST - 1 and step == 1:
+                after = [terms[FIRST][-1]]
             if step == 0:
                 if c % FIRST:
                     terms[c] = terms[c - 1]

time: 60.2 us -> 61 us (1.013)
  starting transfers between devices: 9.87 us -> 14.7 us
  waiting for transfers between devices: 27.7 us -> 23.7 us
    ppermute x17, starting transfers between devices: 9.87 us -> 14.7 us  [moved(): return lax.ppermute(shard, ('loop', 'grp'), pairs)]
    ppermute x17, waiting for transfers between devices: 27.7 us -> 23.7 us  [moved(): return lax.ppermute(shard, ('loop', 'grp'), pairs)]
  transfers between devices with their start and end apart: 17 -> 17, of which waited for: 13 -> 11; matrix products, arithmetic and copies ran while one was open for 2% -> 2% of each run, Pallas kernels for 19% -> 18%
where the time goes in v12:
time: 61 us; the launch traced here: 60.8 us
  waiting for transfers between devices  23.7 us (39%)
  Pallas kernels  16.3 us (27%)
  starting transfers between devices  14.7 us (24%)
  local copies, waits for them, and re-layouts  4.07 us (7%)
  other arithmetic  1.11 us (2%)
  between operations  0.99 us (2%)
    ppermute x17, waiting for transfers between devices, moved(): return lax.ppermute(shard, ('loop', 'grp'), pairs)  23.7 us
    ppermute x17, starting transfers between devices, moved(): return lax.ppermute(shard, ('loop', 'grp'), pairs)  14.7 us
    pallas_call x11, Pallas kernels, chunk_pass(): pl.pallas_call(functools.partial(chunk_kernel, sub_epoch, rows.start, tot...  9.83 us
    pallas_call x1, Pallas kernels, first_pass(): pl.pallas_call(functools.partial(first_kernel, rows.start), out_shape=[ja...  4.16 us
    unnamed x18, local copies, waits for them, and re-layouts  4.07 us
    pallas_call x2, Pallas kernels, last_item_step(): pl.pallas_call(functools.partial(last_kernel, len(terms), rows.start), ou...  1.8 us
  transfers between devices with their start and end apart: 17, of which 11 were waited for; matrix products, arithmetic and copies ran while one was open for 2% of the time, Pallas kernels for 18%

profile of v12, /device:TPU:0, one launch (start us, length us, event | category | flops | bytes accessed | tf_op | source)
XLA Modules:
  0.0 60.8 jit_solution(1974027860078237858)
XLA Ops:
  0.7 4.2 %shard_map.68 = (bf16[1024,128]{1,0:T(8,128)(2,1)}, f32[512,128]{1,0:T(8,128)}, bf16[512,128]{1,0:T(8,128)(2,1)}) custom-call(bf16[2,512,2048]{2,1,0:T(8,128)(2,1)} %rate_ref.21, f32[2048,128]{1,0:T(8,128)} %refs_0_.9, f32[512,128]{1,0:T(8,128)} %users_hbm.1), custom_call_target="tpu_custom_call" | custom-call | flops 402653184 | bytes 1048576 | tf_op jit(solution)/shard_map/pallas_call | solution.py:107
  4.8 3.0 %collective-permute-start = (bf16[1024,128]{1,0:T(8,128)(2,1)}, bf16[1024,128]{1,0:T(8,128)(2,1)S(1)}, u32[]{:S(2)}, u32[]{:S(2)}) collective-permute-start(bf16[1024,128]{1,0:T(8,128)(2,1)} %get-tuple-element.50.refs_2_), channel_id=1, source_target_pairs={{0,1},{1,0},{2,3},{3,2},{4,5},{5,4},{6,7},{7,6},{8,9},{9,8},{10,11... | collective-permute-start | bytes 786440 | tf_op jit(solution)/shard_map/ppermute | solution.py:30
  7.8 2.2 %copy-done = bf16[2,512,2048]{2,1,0:T(8,128)(2,1)S(1)} copy-done((bf16[2,512,2048]{2,1,0:T(8,128)(2,1)S(1)}, bf16[2,512,2048]{2,1,0:T(8,128)(2,1)}, u32[]{:S(2)}) %copy-start) | copy-done | bytes 4194328
  10.0 0.9 %copy-done.5 = f32[512,128]{1,0:T(8,128)S(1)} copy-done((f32[512,128]{1,0:T(8,128)S(1)}, f32[512,128]{1,0:T(8,128)}, u32[]{:S(2)}) %copy-start.5) | copy-done | bytes 262168
  11.0 0.9 %copy-done.6 = bf16[512,128]{1,0:T(8,128)(2,1)S(1)} copy-done((bf16[512,128]{1,0:T(8,128)(2,1)S(1)}, bf16[512,128]{1,0:T(8,128)(2,1)}, u32[]{:S(2)}) %copy-start.6) | copy-done | bytes 131096
  11.9 1.3 %shard_map.69 = (bf16[1024,128]{1,0:T(8,128)(2,1)S(1)}, f32[512,128]{1,0:T(8,128)S(1)}) custom-call(bf16[2,512,2048]{2,1,0:T(8,128)(2,1)S(1)} %copy-done, bf16[512,128]{1,0:T(8,128)(2,1)S(1)} %copy-done.6, f32[512,128]{1,0:T(8,128)S(1)} %copy-done.5, f32[2048,128]{1,0:T(8,128)S(1)} %copy-done.2), custom_call_target="tpu_custom_call" | custom-call | flops 402653184 | bytes 1048576 | tf_op jit(solution)/shard_map/pallas_call | solution.py:164
  13.4 1.0 %collective-permute-done.refs_3_ = bf16[1024,128]{1,0:T(8,128)(2,1)S(1)} collective-permute-done((bf16[1024,128]{1,0:T(8,128)(2,1)}, bf16[1024,128]{1,0:T(8,128)(2,1)S(1)}, u32[]{:S(2)}, u32[]{:S(2)}) %collective-permute-start) | collective-permute-done | bytes 262176 | tf_op jit(solution)/shard_map/ppermute | solution.py:30
  15.1 2.1 %collective-permute-start.2 = (bf16[512,128]{1,0:T(8,128)(2,1)S(1)}, bf16[512,128]{1,0:T(8,128)(2,1)S(1)}, u32[]{:S(2)}, u32[]{:S(2)}) collective-permute-start(bf16[512,128]{1,0:T(8,128)(2,1)S(1)} %get-tuple-element.57.refs_0_), channel_id=1, source_target_pairs={{0,1},{1,0},{2,3},{3,2},{4,5},{5,4},{6,7},{7,6},{8,9},{9,8},{10,11... | collective-permute-start | bytes 393224 | tf_op jit(solution)/shard_map/ppermute | solution.py:30
  17.2 5.2 %collective-permute-done.1.refs_4_.refs_3_ = bf16[1024,128]{1,0:T(8,128)(2,1)S(1)} collective-permute-done((bf16[1024,128]{1,0:T(8,128)(2,1)S(1)}, bf16[1024,128]{1,0:T(8,128)(2,1)S(1)}, u32[]{:S(2)}, u32[]{:S(2)}) %collective-permute-start.1) | collective-permute-done | bytes 262176 | tf_op jit(solution)/shard_map/ppermute | solution.py:30
  24.0 2.0 %collective-permute-start.6 = (bf16[512,128]{1,0:T(8,128)(2,1)S(1)}, bf16[512,128]{1,0:T(8,128)(2,1)S(1)}, u32[]{:S(2)}, u32[]{:S(2)}) collective-permute-start(bf16[512,128]{1,0:T(8,128)(2,1)S(1)} %get-tuple-element.70.refs_0_), channel_id=1, source_target_pairs={{0,1},{1,0},{2,3},{3,2},{4,5},{5,4},{6,7},{7,6},{8,9},{9,8},{10,11... | collective-permute-start | bytes 393224 | tf_op jit(solution)/shard_map/ppermute | solution.py:30
  27.2 1.1 %collective-permute-done.4.refs_1_ = bf16[512,128]{1,0:T(8,128)(2,1)S(1)} collective-permute-done((bf16[512,128]{1,0:T(8,128)(2,1)S(1)}, bf16[512,128]{1,0:T(8,128)(2,1)S(1)}, u32[]{:S(2)}, u32[]{:S(2)}) %collective-permute-start.4) | collective-permute-done | bytes 131104 | tf_op jit(solution)/shard_map/ppermute | solution.py:30
  30.3 3.0 %collective-permute-done.3.refs_0_ = bf16[512,128]{1,0:T(8,128)(2,1)S(1)} collective-permute-done((bf16[512,128]{1,0:T(8,128)(2,1)S(1)}, bf16[512,128]{1,0:T(8,128)(2,1)S(1)}, u32[]{:S(2)}, u32[]{:S(2)}) %collective-permute-start.3) | collective-permute-done | bytes 131104 | tf_op jit(solution)/shard_map/ppermute | solution.py:30
  35.0 1.9 %collective-permute-done.5.refs_0_.refs_1_.refs_4_ = bf16[1024,128]{1,0:T(8,128)(2,1)S(1)} collective-permute-done((bf16[1024,128]{1,0:T(8,128)(2,1)S(1)}, bf16[1024,128]{1,0:T(8,128)(2,1)S(1)}, u32[]{:S(2)}, u32[]{:S(2)}) %collective-permute-start.5) | collective-permute-done | bytes 262176 | tf_op jit(solution)/shard_map/ppermute | solution.py:30
  37.6 1.0 %collective-permute-start.11 = (bf16[512,128]{1,0:T(8,128)(2,1)S(1)}, bf16[512,128]{1,0:T(8,128)(2,1)S(1)}, u32[]{:S(2)}, u32[]{:S(2)}) collective-permute-start(bf16[512,128]{1,0:T(8,128)(2,1)S(1)} %get-tuple-element.80.refs_6_), channel_id=1, source_target_pairs={{0,1},{1,0},{2,3},{3,2},{4,5},{5,4},{6,7},{7,6},{8,9},{9,8},{10,11... | collective-permute-start | bytes 393224 | tf_op jit(solution)/shard_map/ppermute | solution.py:30
  38.6 1.1 %collective-permute-done.7.refs_0_.refs_5_ = bf16[1024,128]{1,0:T(8,128)(2,1)S(1)} collective-permute-done((bf16[1024,128]{1,0:T(8,128)(2,1)S(1)}, bf16[1024,128]{1,0:T(8,128)(2,1)S(1)}, u32[]{:S(2)}, u32[]{:S(2)}) %collective-permute-start.7) | collective-permute-done | bytes 262176 | tf_op jit(solution)/shard_map/ppermute | solution.py:30
  40.4 1.0 %collective-permute-start.12 = (bf16[512,128]{1,0:T(8,128)(2,1)S(1)}, bf16[512,128]{1,0:T(8,128)(2,1)S(1)}, u32[]{:S(2)}, u32[]{:S(2)}) collective-permute-start(bf16[512,128]{1,0:T(8,128)(2,1)S(1)} %get-tuple-element.82.refs_2_), channel_id=1, source_target_pairs={{0,1},{1,0},{2,3},{3,2},{4,5},{5,4},{6,7},{7,6},{8,9},{9,8},{10,11... | collective-permute-start | bytes 393224 | tf_op jit(solution)/shard_map/ppermute | solution.py:30
  41.4 1.4 %collective-permute-done.9.refs_0_.refs_1_.refs_4_ = bf16[1024,128]{1,0:T(8,128)(2,1)S(1)} collective-permute-done((bf16[1024,128]{1,0:T(8,128)(2,1)S(1)}, bf16[1024,128]{1,0:T(8,128)(2,1)S(1)}, u32[]{:S(2)}, u32[]{:S(2)}) %collective-permute-start.9) | collective-permute-done | bytes 262176 | tf_op jit(solution)/shard_map/ppermute | solution.py:30
  44.3 1.4 %shard_map.82 = (bf16[1024,128]{1,0:T(8,128)(2,1)S(1)}, f32[512,128]{1,0:T(8,128)S(1)}, f32[1024,128]{1,0:T(8,128)S(1)}, f32[1024,128]{1,0:T(8,128)S(1)}) custom-call(bf16[2,512,2048]{2,1,0:T(8,128)(2,1)S(1)} %copy-done.1, bf16[512,128]{1,0:T(8,128)(2,1)S(1)} %get-tuple-element.98.half_ref, f32[512,128]{1,0:T(8,128)S(1)} %get-tuple-element.97.grad_ref, ...), custom_call_target="tpu_custom_call" | custom-call | flops 402653184 | bytes 1048576 | tf_op jit(solution)/shard_map/pallas_call | solution.py:164
  45.7 1.4 %collective-permute-start.16 = (bf16[1024,128]{1,0:T(8,128)(2,1)S(1)}, bf16[1024,128]{1,0:T(8,128)(2,1)S(1)}, u32[]{:S(2)}, u32[]{:S(2)}) collective-permute-start(bf16[1024,128]{1,0:T(8,128)(2,1)S(1)} %get-tuple-element.91.refs_0_), channel_id=1, source_target_pairs={{0,1},{1,0},{2,3},{3,2},{4,5},{5,4},{6,7},{7,6},{8,9},{9,8},{10,11... | collective-permute-start | bytes 786440 | tf_op jit(solution)/shard_map/ppermute | solution.py:30
  47.1 2.9 %collective-permute-done.14.refs_7_ = bf16[512,128]{1,0:T(8,128)(2,1)S(1)} collective-permute-done((bf16[512,128]{1,0:T(8,128)(2,1)S(1)}, bf16[512,128]{1,0:T(8,128)(2,1)S(1)}, u32[]{:S(2)}, u32[]{:S(2)}) %collective-permute-start.14) | collective-permute-done | bytes 131104 | tf_op jit(solution)/shard_map/ppermute | solution.py:30
  49.9 1.4 %shard_map.83 = (bf16[1024,128]{1,0:T(8,128)(2,1)S(1)}, f32[512,128]{1,0:T(8,128)S(1)}, f32[1024,128]{1,0:T(8,128)S(1)}, f32[1024,128]{1,0:T(8,128)S(1)}) custom-call(bf16[2,512,2048]{2,1,0:T(8,128)(2,1)S(1)} %copy-done.1, bf16[512,128]{1,0:T(8,128)(2,1)S(1)} %get-tuple-element.98.half_ref, f32[512,128]{1,0:T(8,128)S(1)} %get-tuple-element.81.grad_ref, ...), custom_call_target="tpu_custom_call" | custom-call | flops 402653184 | bytes 1048576 | tf_op jit(solution)/shard_map/pallas_call | solution.py:164
  52.9 2.7 %collective-permute-done.16.refs_1_ = bf16[1024,128]{1,0:T(8,128)(2,1)S(1)} collective-permute-done((bf16[1024,128]{1,0:T(8,128)(2,1)S(1)}, bf16[1024,128]{1,0:T(8,128)(2,1)S(1)}, u32[]{:S(2)}, u32[]{:S(2)}) %collective-permute-start.16) | collective-permute-done | bytes 262176 | tf_op jit(solution)/shard_map/ppermute | solution.py:30
  55.6 0.9 %shard_map.84.refs_2_ = f32[2048,128]{1,0:T(8,128)} custom-call(f32[1024,128]{1,0:T(8,128)S(1)} %get-tuple-element.89.items_ref, f32[1024,128]{1,0:T(8,128)S(1)} %get-tuple-element.90.accum_ref, bf16[1024,128]{1,0:T(8,128)(2,1)S(1)} %get-tuple-element.91.refs_0_, bf16[1024,128]{1,0:T(8,128)(2,1)S(1)} %collective-permute-done.16.refs_1_), custom_call_target="tpu_custom_call" | custom-call | flops 786432 | bytes 2048 | tf_op jit(solution)/shard_map/pallas_call | solution.py:215
  56.5 3.3 %collective-permute-done.15.refs_1_ = bf16[1024,128]{1,0:T(8,128)(2,1)S(1)} collective-permute-done((bf16[1024,128]{1,0:T(8,128)(2,1)S(1)}, bf16[1024,128]{1,0:T(8,128)(2,1)S(1)}, u32[]{:S(2)}, u32[]{:S(2)}) %collective-permute-start.15) | collective-permute-done | bytes 262176 | tf_op jit(solution)/shard_map/ppermute | solution.py:30
  (52 shorter events, 12.7 us)
Async XLA Ops:
  0.6 7.2 %copy-start.2 = (f32[2048,128]{1,0:T(8,128)S(1)}, f32[2048,128]{1,0:T(8,128)}, u32[]{:S(2)}) copy-start(f32[2048,128]{1,0:T(8,128)} %refs_0_.9) | copy-start | bytes 3145732
  0.6 12.6 %copy-start.7 = (f32[512,128]{1,0:T(8,128)S(1)}, f32[512,128]{1,0:T(8,128)}, u32[]{:S(2)}) copy-start(f32[512,128]{1,0:T(8,128)} %param.7) | copy-start | bytes 786436
  0.7 12.6 %copy-start.8 = (f32[512,128]{1,0:T(8,128)S(1)}, f32[512,128]{1,0:T(8,128)}, u32[]{:S(2)}) copy-start(f32[512,128]{1,0:T(8,128)} %users_hbm.1) | copy-start | bytes 786436
  4.8 9.5 %collective-permute-start = (bf16[1024,128]{1,0:T(8,128)(2,1)}, bf16[1024,128]{1,0:T(8,128)(2,1)S(1)}, u32[]{:S(2)}, u32[]{:S(2)}) collective-permute-start(bf16[1024,128]{1,0:T(8,128)(2,1)} %get-tuple-element.50.refs_2_), channel_id=1, source_target_pairs={{0,1},{1,0},{2,3},{3,2},{4,5},{5,4},{6,7},{7,6},{8,9},{9,8},{10,11... | collective-permute-start | bytes 786440 | tf_op jit(solution)/shard_map/ppermute | solution.py:30
  7.8 2.2 %copy-start = (bf16[2,512,2048]{2,1,0:T(8,128)(2,1)S(1)}, bf16[2,512,2048]{2,1,0:T(8,128)(2,1)}, u32[]{:S(2)}) copy-start(bf16[2,512,2048]{2,1,0:T(8,128)(2,1)} %rate_ref.21) | copy-start | bytes 12582916
  11.9 2.5 %copy-start.3 = (f32[2048,128]{1,0:T(8,128)S(1)}, f32[2048,128]{1,0:T(8,128)}, u32[]{:S(2)}) copy-start(f32[2048,128]{1,0:T(8,128)} %refs_1_.7) | copy-start | bytes 3145732
  11.9 2.5 %copy-start.4 = (bf16[1024,128]{1,0:T(8,128)(2,1)S(1)}, bf16[1024,128]{1,0:T(8,128)(2,1)}, u32[]{:S(2)}) copy-start(bf16[1024,128]{1,0:T(8,128)(2,1)} %get-tuple-element.50.refs_2_) | copy-start | bytes 786436
  13.2 9.2 %collective-permute-start.1 = (bf16[1024,128]{1,0:T(8,128)(2,1)S(1)}, bf16[1024,128]{1,0:T(8,128)(2,1)S(1)}, u32[]{:S(2)}, u32[]{:S(2)}) collective-permute-start(bf16[1024,128]{1,0:T(8,128)(2,1)S(1)} %get-tuple-element.52.refs_2_), channel_id=1, source_target_pairs={{0,1},{1,0},{2,3},{3,2},{4,5},{5,4},{6,7},{7,6},{8,9},{9,8},{10,11... | collective-permute-start | bytes 786440 | tf_op jit(solution)/shard_map/ppermute | solution.py:30
  15.1 11.0 %collective-permute-start.2 = (bf16[512,128]{1,0:T(8,128)(2,1)S(1)}, bf16[512,128]{1,0:T(8,128)(2,1)S(1)}, u32[]{:S(2)}, u32[]{:S(2)}) collective-permute-start(bf16[512,128]{1,0:T(8,128)(2,1)S(1)} %get-tuple-element.57.refs_0_), channel_id=1, source_target_pairs={{0,1},{1,0},{2,3},{3,2},{4,5},{5,4},{6,7},{7,6},{8,9},{9,8},{10,11... | collective-permute-start | bytes 393224 | tf_op jit(solution)/shard_map/ppermute | solution.py:30
  23.2 3.1 %copy-start.1 = (bf16[2,512,2048]{2,1,0:T(8,128)(2,1)S(1)}, bf16[2,512,2048]{2,1,0:T(8,128)(2,1)}, u32[]{:S(2)}) copy-start(bf16[2,512,2048]{2,1,0:T(8,128)(2,1)} %rate_ref.21) | copy-start | bytes 12582916
  23.2 5.0 %collective-permute-start.4 = (bf16[512,128]{1,0:T(8,128)(2,1)S(1)}, bf16[512,128]{1,0:T(8,128)(2,1)S(1)}, u32[]{:S(2)}, u32[]{:S(2)}) collective-permute-start(bf16[512,128]{1,0:T(8,128)(2,1)S(1)} %get-tuple-element.63.refs_0_), channel_id=1, source_target_pairs={{0,1},{1,0},{2,3},{3,2},{4,5},{5,4},{6,7},{7,6},{8,9},{9,8},{10,11... | collective-permute-start | bytes 393224 | tf_op jit(solution)/shard_map/ppermute | solution.py:30
  24.0 5.6 %collective-permute-start.6 = (bf16[512,128]{1,0:T(8,128)(2,1)S(1)}, bf16[512,128]{1,0:T(8,128)(2,1)S(1)}, u32[]{:S(2)}, u32[]{:S(2)}) collective-permute-start(bf16[512,128]{1,0:T(8,128)(2,1)S(1)} %get-tuple-element.70.refs_0_), channel_id=1, source_target_pairs={{0,1},{1,0},{2,3},{3,2},{4,5},{5,4},{6,7},{7,6},{8,9},{9,8},{10,11... | collective-permute-start | bytes 393224 | tf_op jit(solution)/shard_map/ppermute | solution.py:30
  26.2 7.1 %collective-permute-start.3 = (bf16[512,128]{1,0:T(8,128)(2,1)S(1)}, bf16[512,128]{1,0:T(8,128)(2,1)S(1)}, u32[]{:S(2)}, u32[]{:S(2)}) collective-permute-start(bf16[512,128]{1,0:T(8,128)(2,1)S(1)} %get-tuple-element.58.refs_4_), channel_id=1, source_target_pairs={{0,2},{1,3},{2,4},{3,5},{4,6},{5,7},{6,8},{7,9},{8,10},{9,11},{10,... | collective-permute-start | bytes 393224 | tf_op jit(solution)/shard_map/ppermute | solution.py:30
  27.0 7.0 %collective-permute-start.8 = (bf16[512,128]{1,0:T(8,128)(2,1)S(1)}, bf16[512,128]{1,0:T(8,128)(2,1)S(1)}, u32[]{:S(2)}, u32[]{:S(2)}) collective-permute-start(bf16[512,128]{1,0:T(8,128)(2,1)S(1)} %get-tuple-element.65.refs_3_.refs_0_), channel_id=1, source_target_pairs={{0,1},{1,0},{2,3},{3,2},{4,5},{5,4},{6,7},{7,6},{8,9},{9,8},{10,11... | collective-permute-start | bytes 393224 | tf_op jit(solution)/shard_map/ppermute | solution.py:30
  28.3 8.5 %collective-permute-start.5 = (bf16[1024,128]{1,0:T(8,128)(2,1)S(1)}, bf16[1024,128]{1,0:T(8,128)(2,1)S(1)}, u32[]{:S(2)}, u32[]{:S(2)}) collective-permute-start(bf16[1024,128]{1,0:T(8,128)(2,1)S(1)} %get-tuple-element.66), channel_id=1, source_target_pairs={{0,2},{1,3},{2,4},{3,5},{4,6},{5,7},{6,8},{7,9},{8,10},{9,11},{10,... | collective-permute-start | bytes 786440 | tf_op jit(solution)/shard_map/ppermute | solution.py:30
  29.8 9.9 %collective-permute-start.7 = (bf16[1024,128]{1,0:T(8,128)(2,1)S(1)}, bf16[1024,128]{1,0:T(8,128)(2,1)S(1)}, u32[]{:S(2)}, u32[]{:S(2)}) collective-permute-start(bf16[1024,128]{1,0:T(8,128)(2,1)S(1)} %get-tuple-element.72), channel_id=1, source_target_pairs={{0,2},{1,3},{2,4},{3,5},{4,6},{5,7},{6,8},{7,9},{8,10},{9,11},{10,... | collective-permute-start | bytes 786440 | tf_op jit(solution)/shard_map/ppermute | solution.py:30
  34.2 8.5 %collective-permute-start.9 = (bf16[1024,128]{1,0:T(8,128)(2,1)S(1)}, bf16[1024,128]{1,0:T(8,128)(2,1)S(1)}, u32[]{:S(2)}, u32[]{:S(2)}) collective-permute-start(bf16[1024,128]{1,0:T(8,128)(2,1)S(1)} %get-tuple-element.78), channel_id=1, source_target_pairs={{0,2},{1,3},{2,4},{3,5},{4,6},{5,7},{6,8},{7,9},{8,10},{9,11},{10,... | collective-permute-start | bytes 786440 | tf_op jit(solution)/shard_map/ppermute | solution.py:30
  34.3 10.0 %collective-permute-start.10 = (bf16[512,128]{1,0:T(8,128)(2,1)S(1)}, bf16[512,128]{1,0:T(8,128)(2,1)S(1)}, u32[]{:S(2)}, u32[]{:S(2)}) collective-permute-start(bf16[512,128]{1,0:T(8,128)(2,1)S(1)} %get-tuple-element.77.refs_3_.refs_2_), channel_id=1, source_target_pairs={{0,1},{1,0},{2,3},{3,2},{4,5},{5,4},{6,7},{7,6},{8,9},{9,8},{10,11... | collective-permute-start | bytes 393224 | tf_op jit(solution)/shard_map/ppermute | solution.py:30
  34.4 12.7 %collective-permute-start.13 = (bf16[512,128]{1,0:T(8,128)(2,1)S(1)}, bf16[512,128]{1,0:T(8,128)(2,1)S(1)}, u32[]{:S(2)}, u32[]{:S(2)}) collective-permute-start(bf16[512,128]{1,0:T(8,128)(2,1)S(1)} %get-tuple-element.83), channel_id=1, source_target_pairs={{0,2},{1,3},{2,4},{3,5},{4,6},{5,7},{6,8},{7,9},{8,10},{9,11},{10,... | collective-permute-start | bytes 393224 | tf_op jit(solution)/shard_map/ppermute | solution.py:30
  37.6 6.7 %collective-permute-start.11 = (bf16[512,128]{1,0:T(8,128)(2,1)S(1)}, bf16[512,128]{1,0:T(8,128)(2,1)S(1)}, u32[]{:S(2)}, u32[]{:S(2)}) collective-permute-start(bf16[512,128]{1,0:T(8,128)(2,1)S(1)} %get-tuple-element.80.refs_6_), channel_id=1, source_target_pairs={{0,1},{1,0},{2,3},{3,2},{4,5},{5,4},{6,7},{7,6},{8,9},{9,8},{10,11... | collective-permute-start | bytes 393224 | tf_op jit(solution)/shard_map/ppermute | solution.py:30
  40.4 6.7 %collective-permute-start.12 = (bf16[512,128]{1,0:T(8,128)(2,1)S(1)}, bf16[512,128]{1,0:T(8,128)(2,1)S(1)}, u32[]{:S(2)}, u32[]{:S(2)}) collective-permute-start(bf16[512,128]{1,0:T(8,128)(2,1)S(1)} %get-tuple-element.82.refs_2_), channel_id=1, source_target_pairs={{0,1},{1,0},{2,3},{3,2},{4,5},{5,4},{6,7},{7,6},{8,9},{9,8},{10,11... | collective-permute-start | bytes 393224 | tf_op jit(solution)/shard_map/ppermute | solution.py:30
  43.4 6.5 %collective-permute-start.14 = (bf16[512,128]{1,0:T(8,128)(2,1)S(1)}, bf16[512,128]{1,0:T(8,128)(2,1)S(1)}, u32[]{:S(2)}, u32[]{:S(2)}) collective-permute-start(bf16[512,128]{1,0:T(8,128)(2,1)S(1)} %get-tuple-element.84.refs_6_), channel_id=1, source_target_pairs={{0,1},{1,0},{2,3},{3,2},{4,5},{5,4},{6,7},{7,6},{8,9},{9,8},{10,11... | collective-permute-start | bytes 393224 | tf_op jit(solution)/shard_map/ppermute | solution.py:30
  45.7 9.9 %collective-permute-start.16 = (bf16[1024,128]{1,0:T(8,128)(2,1)S(1)}, bf16[1024,128]{1,0:T(8,128)(2,1)S(1)}, u32[]{:S(2)}, u32[]{:S(2)}) collective-permute-start(bf16[1024,128]{1,0:T(8,128)(2,1)S(1)} %get-tuple-element.91.refs_0_), channel_id=1, source_target_pairs={{0,1},{1,0},{2,3},{3,2},{4,5},{5,4},{6,7},{7,6},{8,9},{9,8},{10,11... | collective-permute-start | bytes 786440 | tf_op jit(solution)/shard_map/ppermute | solution.py:30
  51.3 8.4 %collective-permute-start.15 = (bf16[1024,128]{1,0:T(8,128)(2,1)S(1)}, bf16[1024,128]{1,0:T(8,128)(2,1)S(1)}, u32[]{:S(2)}, u32[]{:S(2)}) collective-permute-start(bf16[1024,128]{1,0:T(8,128)(2,1)S(1)} %get-tuple-element.88.refs_0_), channel_id=1, source_target_pairs={{0,1},{1,0},{2,3},{3,2},{4,5},{5,4},{6,7},{7,6},{8,9},{9,8},{10,11... | collective-permute-start | bytes 786440 | tf_op jit(solution)/shard_map/ppermute | solution.py:30
  (2 other events, 1.9 us)

commit v13 on v12

--- a/solution.py
+++ b/solution.py
@@ -260,7 +260,7 @@
                 part(CHUNKS - 1, [term])
                 item_acc[CHUNKS - 1] = (moved(behind[0], 1, 0), 0)
             after = []
-            if c == CHUNKS - 1 and step % INNER == INNER - 1 and sub_epoch < SUB - 1:
+            if c == CHUNKS - 2 and step % INNER == INNER - 1 and sub_epoch < SUB - 1:
                 behind = []
                 after = part(0, [])
             elif c == FIRST - 1 and step == 1:

time: 61 us -> 62.4 us (1.023)
  starting transfers between devices: 14.7 us -> 16.7 us
    ppermute x17, starting transfers between devices: 14.7 us -> 16.7 us  [moved(): return lax.ppermute(shard, ('loop', 'grp'), pairs)]
    ppermute x17, waiting for transfers between devices: 23.7 us -> 23.1 us  [moved(): return lax.ppermute(shard, ('loop', 'grp'), pairs)]
  transfers between devices with their start and end apart: 17 -> 17, of which waited for: 11 -> 12; matrix products, arithmetic and copies ran while one was open for 2% -> 2% of each run, Pallas kernels for 18% -> 18%
where the time goes in v13:
time: 62.4 us; the launch traced here: 62.2 us
  waiting for transfers between devices  23.1 us (37%)
  starting transfers between devices  16.7 us (27%)
  Pallas kernels  16.3 us (26%)
  local copies, waits for them, and re-layouts  4.07 us (7%)
  other arithmetic  1.11 us (2%)
  between operations  0.98 us (2%)
    ppermute x17, waiting for transfers between devices, moved(): return lax.ppermute(shard, ('loop', 'grp'), pairs)  23.1 us
    ppermute x17, starting transfers between devices, moved(): return lax.ppermute(shard, ('loop', 'grp'), pairs)  16.7 us
    pallas_call x11, Pallas kernels, chunk_pass(): pl.pallas_call(functools.partial(chunk_kernel, sub_epoch, rows.start, tot...  9.83 us
    pallas_call x1, Pallas kernels, first_pass(): pl.pallas_call(functools.partial(first_kernel, rows.start), out_shape=[ja...  4.16 us
    unnamed x18, local copies, waits for them, and re-layouts  4.07 us
    pallas_call x2, Pallas kernels, last_item_step(): pl.pallas_call(functools.partial(last_kernel, len(terms), rows.start), ou...  1.8 us
  transfers between devices with their start and end apart: 17, of which 12 were waited for; matrix products, arithmetic and copies ran while one was open for 2% of the time, Pallas kernels for 18%

profile of v13, /device:TPU:0, one launch (start us, length us, event | category | flops | bytes accessed | tf_op | source)
XLA Modules:
  0.0 62.2 jit_solution(13125029530067267143)
XLA Ops:
  0.7 4.2 %shard_map.68 = (bf16[1024,128]{1,0:T(8,128)(2,1)}, f32[512,128]{1,0:T(8,128)}, bf16[512,128]{1,0:T(8,128)(2,1)}) custom-call(bf16[2,512,2048]{2,1,0:T(8,128)(2,1)} %rate_ref.21, f32[2048,128]{1,0:T(8,128)} %refs_0_.9, f32[512,128]{1,0:T(8,128)} %users_hbm.1), custom_call_target="tpu_custom_call" | custom-call | flops 402653184 | bytes 1048576 | tf_op jit(solution)/shard_map/pallas_call | solution.py:107
  4.8 3.0 %collective-permute-start = (bf16[1024,128]{1,0:T(8,128)(2,1)}, bf16[1024,128]{1,0:T(8,128)(2,1)S(1)}, u32[]{:S(2)}, u32[]{:S(2)}) collective-permute-start(bf16[1024,128]{1,0:T(8,128)(2,1)} %get-tuple-element.50.refs_2_), channel_id=1, source_target_pairs={{0,1},{1,0},{2,3},{3,2},{4,5},{5,4},{6,7},{7,6},{8,9},{9,8},{10,11... | collective-permute-start | bytes 786440 | tf_op jit(solution)/shard_map/ppermute | solution.py:30
  7.8 2.2 %copy-done = bf16[2,512,2048]{2,1,0:T(8,128)(2,1)S(1)} copy-done((bf16[2,512,2048]{2,1,0:T(8,128)(2,1)S(1)}, bf16[2,512,2048]{2,1,0:T(8,128)(2,1)}, u32[]{:S(2)}) %copy-start) | copy-done | bytes 4194328
  10.0 0.9 %copy-done.5 = f32[512,128]{1,0:T(8,128)S(1)} copy-done((f32[512,128]{1,0:T(8,128)S(1)}, f32[512,128]{1,0:T(8,128)}, u32[]{:S(2)}) %copy-start.5) | copy-done | bytes 262168
  11.0 0.9 %copy-done.6 = bf16[512,128]{1,0:T(8,128)(2,1)S(1)} copy-done((bf16[512,128]{1,0:T(8,128)(2,1)S(1)}, bf16[512,128]{1,0:T(8,128)(2,1)}, u32[]{:S(2)}) %copy-start.6) | copy-done | bytes 131096
  11.9 1.3 %shard_map.69 = (bf16[1024,128]{1,0:T(8,128)(2,1)S(1)}, f32[512,128]{1,0:T(8,128)S(1)}) custom-call(bf16[2,512,2048]{2,1,0:T(8,128)(2,1)S(1)} %copy-done, bf16[512,128]{1,0:T(8,128)(2,1)S(1)} %copy-done.6, f32[512,128]{1,0:T(8,128)S(1)} %copy-done.5, f32[2048,128]{1,0:T(8,128)S(1)} %copy-done.2), custom_call_target="tpu_custom_call" | custom-call | flops 402653184 | bytes 1048576 | tf_op jit(solution)/shard_map/pallas_call | solution.py:164
  13.4 1.0 %collective-permute-done.refs_3_ = bf16[1024,128]{1,0:T(8,128)(2,1)S(1)} collective-permute-done((bf16[1024,128]{1,0:T(8,128)(2,1)}, bf16[1024,128]{1,0:T(8,128)(2,1)S(1)}, u32[]{:S(2)}, u32[]{:S(2)}) %collective-permute-start) | collective-permute-done | bytes 262176 | tf_op jit(solution)/shard_map/ppermute | solution.py:30
  15.1 2.1 %collective-permute-start.2 = (bf16[512,128]{1,0:T(8,128)(2,1)S(1)}, bf16[512,128]{1,0:T(8,128)(2,1)S(1)}, u32[]{:S(2)}, u32[]{:S(2)}) collective-permute-start(bf16[512,128]{1,0:T(8,128)(2,1)S(1)} %get-tuple-element.56.refs_0_), channel_id=1, source_target_pairs={{0,1},{1,0},{2,3},{3,2},{4,5},{5,4},{6,7},{7,6},{8,9},{9,8},{10,11... | collective-permute-start | bytes 393224 | tf_op jit(solution)/shard_map/ppermute | solution.py:30
  17.2 5.2 %collective-permute-done.1.refs_4_.refs_3_ = bf16[1024,128]{1,0:T(8,128)(2,1)S(1)} collective-permute-done((bf16[1024,128]{1,0:T(8,128)(2,1)S(1)}, bf16[1024,128]{1,0:T(8,128)(2,1)S(1)}, u32[]{:S(2)}, u32[]{:S(2)}) %collective-permute-start.1) | collective-permute-done | bytes 262176 | tf_op jit(solution)/shard_map/ppermute | solution.py:30
  23.3 1.2 %collective-permute-done.2.refs_1_ = bf16[512,128]{1,0:T(8,128)(2,1)S(1)} collective-permute-done((bf16[512,128]{1,0:T(8,128)(2,1)S(1)}, bf16[512,128]{1,0:T(8,128)(2,1)S(1)}, u32[]{:S(2)}, u32[]{:S(2)}) %collective-permute-start.2) | collective-permute-done | bytes 131104 | tf_op jit(solution)/shard_map/ppermute | solution.py:30
  27.0 1.3 %collective-permute-start.8 = (bf16[512,128]{1,0:T(8,128)(2,1)S(1)}, bf16[512,128]{1,0:T(8,128)(2,1)S(1)}, u32[]{:S(2)}, u32[]{:S(2)}) collective-permute-start(bf16[512,128]{1,0:T(8,128)(2,1)S(1)} %get-tuple-element.65.refs_3_.refs_0_), channel_id=1, source_target_pairs={{0,1},{1,0},{2,3},{3,2},{4,5},{5,4},{6,7},{7,6},{8,9},{9,8},{10,11... | collective-permute-start | bytes 393224 | tf_op jit(solution)/shard_map/ppermute | solution.py:30
  28.5 1.1 %collective-permute-start.5 = (bf16[1024,128]{1,0:T(8,128)(2,1)S(1)}, bf16[1024,128]{1,0:T(8,128)(2,1)S(1)}, u32[]{:S(2)}, u32[]{:S(2)}) collective-permute-start(bf16[1024,128]{1,0:T(8,128)(2,1)S(1)} %get-tuple-element.66), channel_id=1, source_target_pairs={{0,2},{1,3},{2,4},{3,5},{4,6},{5,7},{6,8},{7,9},{8,10},{9,11},{10,... | collective-permute-start | bytes 786440 | tf_op jit(solution)/shard_map/ppermute | solution.py:30
  29.7 1.6 %collective-permute-done.6.refs_1_ = bf16[512,128]{1,0:T(8,128)(2,1)S(1)} collective-permute-done((bf16[512,128]{1,0:T(8,128)(2,1)S(1)}, bf16[512,128]{1,0:T(8,128)(2,1)S(1)}, u32[]{:S(2)}, u32[]{:S(2)}) %collective-permute-start.6) | collective-permute-done | bytes 131104 | tf_op jit(solution)/shard_map/ppermute | solution.py:30
  31.4 1.3 %collective-permute-start.7 = (bf16[1024,128]{1,0:T(8,128)(2,1)S(1)}, bf16[1024,128]{1,0:T(8,128)(2,1)S(1)}, u32[]{:S(2)}, u32[]{:S(2)}) collective-permute-start(bf16[1024,128]{1,0:T(8,128)(2,1)S(1)} %get-tuple-element.72), channel_id=1, source_target_pairs={{0,2},{1,3},{2,4},{3,5},{4,6},{5,7},{6,8},{7,9},{8,10},{9,11},{10,... | collective-permute-start | bytes 786440 | tf_op jit(solution)/shard_map/ppermute | solution.py:30
  38.6 1.4 %collective-permute-done.7.refs_0_.refs_5_ = bf16[1024,128]{1,0:T(8,128)(2,1)S(1)} collective-permute-done((bf16[1024,128]{1,0:T(8,128)(2,1)S(1)}, bf16[1024,128]{1,0:T(8,128)(2,1)S(1)}, u32[]{:S(2)}, u32[]{:S(2)}) %collective-permute-start.7) | collective-permute-done | bytes 262176 | tf_op jit(solution)/shard_map/ppermute | solution.py:30
  40.7 2.1 %collective-permute-done.9.refs_0_.refs_1_.refs_4_ = bf16[1024,128]{1,0:T(8,128)(2,1)S(1)} collective-permute-done((bf16[1024,128]{1,0:T(8,128)(2,1)S(1)}, bf16[1024,128]{1,0:T(8,128)(2,1)S(1)}, u32[]{:S(2)}, u32[]{:S(2)}) %collective-permute-start.9) | collective-permute-done | bytes 262176 | tf_op jit(solution)/shard_map/ppermute | solution.py:30
  44.3 1.3 %collective-permute-start.12 = (bf16[512,128]{1,0:T(8,128)(2,1)S(1)}, bf16[512,128]{1,0:T(8,128)(2,1)S(1)}, u32[]{:S(2)}, u32[]{:S(2)}) collective-permute-start(bf16[512,128]{1,0:T(8,128)(2,1)S(1)} %get-tuple-element.82.refs_2_), channel_id=1, source_target_pairs={{0,1},{1,0},{2,3},{3,2},{4,5},{5,4},{6,7},{7,6},{8,9},{9,8},{10,11... | collective-permute-start | bytes 393224 | tf_op jit(solution)/shard_map/ppermute | solution.py:30
  45.7 1.4 %shard_map.82 = (bf16[1024,128]{1,0:T(8,128)(2,1)S(1)}, f32[512,128]{1,0:T(8,128)S(1)}, f32[1024,128]{1,0:T(8,128)S(1)}, f32[1024,128]{1,0:T(8,128)S(1)}) custom-call(bf16[2,512,2048]{2,1,0:T(8,128)(2,1)S(1)} %copy-done.1, bf16[512,128]{1,0:T(8,128)(2,1)S(1)} %get-tuple-element.98.half_ref, f32[512,128]{1,0:T(8,128)S(1)} %get-tuple-element.97.grad_ref, ...), custom_call_target="tpu_custom_call" | custom-call | flops 402653184 | bytes 1048576 | tf_op jit(solution)/shard_map/pallas_call | solution.py:164
  47.9 0.9 %collective-permute-done.14.refs_7_ = bf16[512,128]{1,0:T(8,128)(2,1)S(1)} collective-permute-done((bf16[512,128]{1,0:T(8,128)(2,1)S(1)}, bf16[512,128]{1,0:T(8,128)(2,1)S(1)}, u32[]{:S(2)}, u32[]{:S(2)}) %collective-permute-start.14) | collective-permute-done | bytes 131104 | tf_op jit(solution)/shard_map/ppermute | solution.py:30
  48.8 2.8 %collective-permute-done.12.refs_3_ = bf16[512,128]{1,0:T(8,128)(2,1)S(1)} collective-permute-done((bf16[512,128]{1,0:T(8,128)(2,1)S(1)}, bf16[512,128]{1,0:T(8,128)(2,1)S(1)}, u32[]{:S(2)}, u32[]{:S(2)}) %collective-permute-start.12) | collective-permute-done | bytes 131104 | tf_op jit(solution)/shard_map/ppermute | solution.py:30
  51.6 1.4 %shard_map.83 = (bf16[1024,128]{1,0:T(8,128)(2,1)S(1)}, f32[512,128]{1,0:T(8,128)S(1)}, f32[1024,128]{1,0:T(8,128)S(1)}, f32[1024,128]{1,0:T(8,128)S(1)}) custom-call(bf16[2,512,2048]{2,1,0:T(8,128)(2,1)S(1)} %copy-done.1, bf16[512,128]{1,0:T(8,128)(2,1)S(1)} %get-tuple-element.98.half_ref, f32[512,128]{1,0:T(8,128)S(1)} %get-tuple-element.81.grad_ref, ...), custom_call_target="tpu_custom_call" | custom-call | flops 402653184 | bytes 1048576 | tf_op jit(solution)/shard_map/pallas_call | solution.py:164
  54.7 2.6 %collective-permute-done.16.refs_1_ = bf16[1024,128]{1,0:T(8,128)(2,1)S(1)} collective-permute-done((bf16[1024,128]{1,0:T(8,128)(2,1)S(1)}, bf16[1024,128]{1,0:T(8,128)(2,1)S(1)}, u32[]{:S(2)}, u32[]{:S(2)}) %collective-permute-start.16) | collective-permute-done | bytes 262176 | tf_op jit(solution)/shard_map/ppermute | solution.py:30
  57.2 0.9 %shard_map.84.refs_2_ = f32[2048,128]{1,0:T(8,128)} custom-call(f32[1024,128]{1,0:T(8,128)S(1)} %get-tuple-element.89.items_ref, f32[1024,128]{1,0:T(8,128)S(1)} %get-tuple-element.90.accum_ref, bf16[1024,128]{1,0:T(8,128)(2,1)S(1)} %get-tuple-element.91.refs_0_, bf16[1024,128]{1,0:T(8,128)(2,1)S(1)} %collective-permute-done.16.refs_1_), custom_call_target="tpu_custom_call" | custom-call | flops 786432 | bytes 2048 | tf_op jit(solution)/shard_map/pallas_call | solution.py:215
  58.2 3.0 %collective-permute-done.15.refs_1_ = bf16[1024,128]{1,0:T(8,128)(2,1)S(1)} collective-permute-done((bf16[1024,128]{1,0:T(8,128)(2,1)S(1)}, bf16[1024,128]{1,0:T(8,128)(2,1)S(1)}, u32[]{:S(2)}, u32[]{:S(2)}) %collective-permute-start.15) | collective-permute-done | bytes 262176 | tf_op jit(solution)/shard_map/ppermute | solution.py:30
  (52 shorter events, 16.1 us)
Async XLA Ops:
  0.6 7.2 %copy-start.2 = (f32[2048,128]{1,0:T(8,128)S(1)}, f32[2048,128]{1,0:T(8,128)}, u32[]{:S(2)}) copy-start(f32[2048,128]{1,0:T(8,128)} %refs_0_.9) | copy-start | bytes 3145732
  0.6 12.6 %copy-start.7 = (f32[512,128]{1,0:T(8,128)S(1)}, f32[512,128]{1,0:T(8,128)}, u32[]{:S(2)}) copy-start(f32[512,128]{1,0:T(8,128)} %param.7) | copy-start | bytes 786436
  0.7 12.6 %copy-start.8 = (f32[512,128]{1,0:T(8,128)S(1)}, f32[512,128]{1,0:T(8,128)}, u32[]{:S(2)}) copy-start(f32[512,128]{1,0:T(8,128)} %users_hbm.1) | copy-start | bytes 786436
  4.8 9.5 %collective-permute-start = (bf16[1024,128]{1,0:T(8,128)(2,1)}, bf16[1024,128]{1,0:T(8,128)(2,1)S(1)}, u32[]{:S(2)}, u32[]{:S(2)}) collective-permute-start(bf16[1024,128]{1,0:T(8,128)(2,1)} %get-tuple-element.50.refs_2_), channel_id=1, source_target_pairs={{0,1},{1,0},{2,3},{3,2},{4,5},{5,4},{6,7},{7,6},{8,9},{9,8},{10,11... | collective-permute-start | bytes 786440 | tf_op jit(solution)/shard_map/ppermute | solution.py:30
  7.8 2.2 %copy-start = (bf16[2,512,2048]{2,1,0:T(8,128)(2,1)S(1)}, bf16[2,512,2048]{2,1,0:T(8,128)(2,1)}, u32[]{:S(2)}) copy-start(bf16[2,512,2048]{2,1,0:T(8,128)(2,1)} %rate_ref.21) | copy-start | bytes 12582916
  11.9 2.5 %copy-start.3 = (f32[2048,128]{1,0:T(8,128)S(1)}, f32[2048,128]{1,0:T(8,128)}, u32[]{:S(2)}) copy-start(f32[2048,128]{1,0:T(8,128)} %refs_1_.7) | copy-start | bytes 3145732
  11.9 2.5 %copy-start.4 = (bf16[1024,128]{1,0:T(8,128)(2,1)S(1)}, bf16[1024,128]{1,0:T(8,128)(2,1)}, u32[]{:S(2)}) copy-start(bf16[1024,128]{1,0:T(8,128)(2,1)} %get-tuple-element.50.refs_2_) | copy-start | bytes 786436
  13.2 9.2 %collective-permute-start.1 = (bf16[1024,128]{1,0:T(8,128)(2,1)S(1)}, bf16[1024,128]{1,0:T(8,128)(2,1)S(1)}, u32[]{:S(2)}, u32[]{:S(2)}) collective-permute-start(bf16[1024,128]{1,0:T(8,128)(2,1)S(1)} %get-tuple-element.52.refs_2_), channel_id=1, source_target_pairs={{0,1},{1,0},{2,3},{3,2},{4,5},{5,4},{6,7},{7,6},{8,9},{9,8},{10,11... | collective-permute-start | bytes 786440 | tf_op jit(solution)/shard_map/ppermute | solution.py:30
  15.1 9.6 %copy-start.1 = (bf16[2,512,2048]{2,1,0:T(8,128)(2,1)S(1)}, bf16[2,512,2048]{2,1,0:T(8,128)(2,1)}, u32[]{:S(2)}) copy-start(bf16[2,512,2048]{2,1,0:T(8,128)(2,1)} %rate_ref.21) | copy-start | bytes 12582916
  15.1 9.4 %collective-permute-start.2 = (bf16[512,128]{1,0:T(8,128)(2,1)S(1)}, bf16[512,128]{1,0:T(8,128)(2,1)S(1)}, u32[]{:S(2)}, u32[]{:S(2)}) collective-permute-start(bf16[512,128]{1,0:T(8,128)(2,1)S(1)} %get-tuple-element.56.refs_0_), channel_id=1, source_target_pairs={{0,1},{1,0},{2,3},{3,2},{4,5},{5,4},{6,7},{7,6},{8,9},{9,8},{10,11... | collective-permute-start | bytes 393224 | tf_op jit(solution)/shard_map/ppermute | solution.py:30
  23.2 5.2 %collective-permute-start.4 = (bf16[512,128]{1,0:T(8,128)(2,1)S(1)}, bf16[512,128]{1,0:T(8,128)(2,1)S(1)}, u32[]{:S(2)}, u32[]{:S(2)}) collective-permute-start(bf16[512,128]{1,0:T(8,128)(2,1)S(1)} %get-tuple-element.63.refs_0_), channel_id=1, source_target_pairs={{0,1},{1,0},{2,3},{3,2},{4,5},{5,4},{6,7},{7,6},{8,9},{9,8},{10,11... | collective-permute-start | bytes 393224 | tf_op jit(solution)/shard_map/ppermute | solution.py:30
  24.6 8.1 %collective-permute-start.3 = (bf16[512,128]{1,0:T(8,128)(2,1)S(1)}, bf16[512,128]{1,0:T(8,128)(2,1)S(1)}, u32[]{:S(2)}, u32[]{:S(2)}) collective-permute-start(bf16[512,128]{1,0:T(8,128)(2,1)S(1)} %get-tuple-element.57.refs_4_), channel_id=1, source_target_pairs={{0,2},{1,3},{2,4},{3,5},{4,6},{5,7},{6,8},{7,9},{8,10},{9,11},{10,... | collective-permute-start | bytes 393224 | tf_op jit(solution)/shard_map/ppermute | solution.py:30
  25.5 5.8 %collective-permute-start.6 = (bf16[512,128]{1,0:T(8,128)(2,1)S(1)}, bf16[512,128]{1,0:T(8,128)(2,1)S(1)}, u32[]{:S(2)}, u32[]{:S(2)}) collective-permute-start(bf16[512,128]{1,0:T(8,128)(2,1)S(1)} %get-tuple-element.70.refs_0_), channel_id=1, source_target_pairs={{0,1},{1,0},{2,3},{3,2},{4,5},{5,4},{6,7},{7,6},{8,9},{9,8},{10,11... | collective-permute-start | bytes 393224 | tf_op jit(solution)/shard_map/ppermute | solution.py:30
  27.0 7.1 %collective-permute-start.8 = (bf16[512,128]{1,0:T(8,128)(2,1)S(1)}, bf16[512,128]{1,0:T(8,128)(2,1)S(1)}, u32[]{:S(2)}, u32[]{:S(2)}) collective-permute-start(bf16[512,128]{1,0:T(8,128)(2,1)S(1)} %get-tuple-element.65.refs_3_.refs_0_), channel_id=1, source_target_pairs={{0,1},{1,0},{2,3},{3,2},{4,5},{5,4},{6,7},{7,6},{8,9},{9,8},{10,11... | collective-permute-start | bytes 393224 | tf_op jit(solution)/shard_map/ppermute | solution.py:30
  28.5 8.5 %collective-permute-start.5 = (bf16[1024,128]{1,0:T(8,128)(2,1)S(1)}, bf16[1024,128]{1,0:T(8,128)(2,1)S(1)}, u32[]{:S(2)}, u32[]{:S(2)}) collective-permute-start(bf16[1024,128]{1,0:T(8,128)(2,1)S(1)} %get-tuple-element.66), channel_id=1, source_target_pairs={{0,2},{1,3},{2,4},{3,5},{4,6},{5,7},{6,8},{7,9},{8,10},{9,11},{10,... | collective-permute-start | bytes 786440 | tf_op jit(solution)/shard_map/ppermute | solution.py:30
  31.4 8.5 %collective-permute-start.7 = (bf16[1024,128]{1,0:T(8,128)(2,1)S(1)}, bf16[1024,128]{1,0:T(8,128)(2,1)S(1)}, u32[]{:S(2)}, u32[]{:S(2)}) collective-permute-start(bf16[1024,128]{1,0:T(8,128)(2,1)S(1)} %get-tuple-element.72), channel_id=1, source_target_pairs={{0,2},{1,3},{2,4},{3,5},{4,6},{5,7},{6,8},{7,9},{8,10},{9,11},{10,... | collective-permute-start | bytes 786440 | tf_op jit(solution)/shard_map/ppermute | solution.py:30
  34.2 8.5 %collective-permute-start.9 = (bf16[1024,128]{1,0:T(8,128)(2,1)S(1)}, bf16[1024,128]{1,0:T(8,128)(2,1)S(1)}, u32[]{:S(2)}, u32[]{:S(2)}) collective-permute-start(bf16[1024,128]{1,0:T(8,128)(2,1)S(1)} %get-tuple-element.78), channel_id=1, source_target_pairs={{0,2},{1,3},{2,4},{3,5},{4,6},{5,7},{6,8},{7,9},{8,10},{9,11},{10,... | collective-permute-start | bytes 786440 | tf_op jit(solution)/shard_map/ppermute | solution.py:30
  35.0 10.7 %collective-permute-start.10 = (bf16[512,128]{1,0:T(8,128)(2,1)S(1)}, bf16[512,128]{1,0:T(8,128)(2,1)S(1)}, u32[]{:S(2)}, u32[]{:S(2)}) collective-permute-start(bf16[512,128]{1,0:T(8,128)(2,1)S(1)} %get-tuple-element.77.refs_3_.refs_2_), channel_id=1, source_target_pairs={{0,1},{1,0},{2,3},{3,2},{4,5},{5,4},{6,7},{7,6},{8,9},{9,8},{10,11... | collective-permute-start | bytes 393224 | tf_op jit(solution)/shard_map/ppermute | solution.py:30
  35.7 12.1 %collective-permute-start.13 = (bf16[512,128]{1,0:T(8,128)(2,1)S(1)}, bf16[512,128]{1,0:T(8,128)(2,1)S(1)}, u32[]{:S(2)}, u32[]{:S(2)}) collective-permute-start(bf16[512,128]{1,0:T(8,128)(2,1)S(1)} %get-tuple-element.83), channel_id=1, source_target_pairs={{0,2},{1,3},{2,4},{3,5},{4,6},{5,7},{6,8},{7,9},{8,10},{9,11},{10,... | collective-permute-start | bytes 393224 | tf_op jit(solution)/shard_map/ppermute | solution.py:30
  37.7 7.9 %collective-permute-start.11 = (bf16[512,128]{1,0:T(8,128)(2,1)S(1)}, bf16[512,128]{1,0:T(8,128)(2,1)S(1)}, u32[]{:S(2)}, u32[]{:S(2)}) collective-permute-start(bf16[512,128]{1,0:T(8,128)(2,1)S(1)} %get-tuple-element.80.refs_6_), channel_id=1, source_target_pairs={{0,1},{1,0},{2,3},{3,2},{4,5},{5,4},{6,7},{7,6},{8,9},{9,8},{10,11... | collective-permute-start | bytes 393224 | tf_op jit(solution)/shard_map/ppermute | solution.py:30
  43.5 5.3 %collective-permute-start.14 = (bf16[512,128]{1,0:T(8,128)(2,1)S(1)}, bf16[512,128]{1,0:T(8,128)(2,1)S(1)}, u32[]{:S(2)}, u32[]{:S(2)}) collective-permute-start(bf16[512,128]{1,0:T(8,128)(2,1)S(1)} %get-tuple-element.84.refs_6_), channel_id=1, source_target_pairs={{0,1},{1,0},{2,3},{3,2},{4,5},{5,4},{6,7},{7,6},{8,9},{9,8},{10,11... | collective-permute-start | bytes 393224 | tf_op jit(solution)/shard_map/ppermute | solution.py:30
  44.3 7.3 %collective-permute-start.12 = (bf16[512,128]{1,0:T(8,128)(2,1)S(1)}, bf16[512,128]{1,0:T(8,128)(2,1)S(1)}, u32[]{:S(2)}, u32[]{:S(2)}) collective-permute-start(bf16[512,128]{1,0:T(8,128)(2,1)S(1)} %get-tuple-element.82.refs_2_), channel_id=1, source_target_pairs={{0,1},{1,0},{2,3},{3,2},{4,5},{5,4},{6,7},{7,6},{8,9},{9,8},{10,11... | collective-permute-start | bytes 393224 | tf_op jit(solution)/shard_map/ppermute | solution.py:30
  47.1 10.2 %collective-permute-start.16 = (bf16[1024,128]{1,0:T(8,128)(2,1)S(1)}, bf16[1024,128]{1,0:T(8,128)(2,1)S(1)}, u32[]{:S(2)}, u32[]{:S(2)}) collective-permute-start(bf16[1024,128]{1,0:T(8,128)(2,1)S(1)} %get-tuple-element.91.refs_0_), channel_id=1, source_target_pairs={{0,1},{1,0},{2,3},{3,2},{4,5},{5,4},{6,7},{7,6},{8,9},{9,8},{10,11... | collective-permute-start | bytes 786440 | tf_op jit(solution)/shard_map/ppermute | solution.py:30
  53.0 8.2 %collective-permute-start.15 = (bf16[1024,128]{1,0:T(8,128)(2,1)S(1)}, bf16[1024,128]{1,0:T(8,128)(2,1)S(1)}, u32[]{:S(2)}, u32[]{:S(2)}) collective-permute-start(bf16[1024,128]{1,0:T(8,128)(2,1)S(1)} %get-tuple-element.88.refs_0_), channel_id=1, source_target_pairs={{0,1},{1,0},{2,3},{3,2},{4,5},{5,4},{6,7},{7,6},{8,9},{9,8},{10,11... | collective-permute-start | bytes 786440 | tf_op jit(solution)/shard_map/ppermute | solution.py:30
  (2 other events, 1.9 us)

commit v14 on v10

--- a/solution.py
+++ b/solution.py
@@ -72,7 +72,7 @@
 AWAY = pl.BlockSpec(memory_space=pltpu.HBM)
 
 
-def first_kernel(column, rate_hbm, items_hbm, users_hbm, term_out, grad_out, half_out, *scratch):
+def first_kernel(column, rate_hbm, items_hbm, users_hbm, term_out, grad_out, *scratch):
     users_ref, rate_ref, items_ref, sems = scratch
     load_users = pltpu.make_async_copy(users_hbm, users_ref, sems.at[2, 0])
     load_users.start()
@@ -92,7 +92,6 @@
     grad = shrink * users_ref[...]
     half = users_ref[...].astype(jnp.bfloat16)
     half_t = half.T
-    half_out[...] = half
     for t in tiles:
         for load in loads[t]:
             load.wait()
@@ -109,10 +108,9 @@
         out_shape=[
             jax.ShapeDtypeStruct((size, rank), jnp.bfloat16),
             jax.ShapeDtypeStruct(users.shape, jnp.float32),
-            jax.ShapeDtypeStruct(users.shape, jnp.bfloat16),
         ],
         in_specs=[AWAY] * 3,
-        out_specs=[WHOLE] * 3,
+        out_specs=[WHOLE] * 2,
         scratch_shapes=[
             pltpu.VMEM(users.shape, jnp.float32),
             pltpu.VMEM((size // TILE, n_users, TILE), jnp.bfloat16),
@@ -125,7 +123,7 @@
 
 
 def chunk_kernel(sub_epoch, column, size, places, rate_ref, half_ref, grad_ref, *refs):
-    half = half_ref[...]
+    half = half_ref[...].astype(jnp.bfloat16)
     half_t = half.T
     grad = grad_ref[...]
     term_out, grad_out, *updated = refs[-4:] if places[0][0] else refs[-2:]
@@ -269,10 +267,10 @@
                     continue
                 both = slice(rows[c].start, rows[c + FIRST - 1].stop)
                 if c == 0:
-                    term, grad_user, user_half = first_pass(ratings, both, users, item_factors)
+                    term, grad_user = first_pass(ratings, both, users, item_factors)
                 else:
                     piece = (items[c], item_acc[c], (), 0)
-                    term, grad_user = chunk_pass(ratings, 0, both, user_half, grad_user, [piece])
+                    term, grad_user = chunk_pass(ratings, 0, both, users, grad_user, [piece])
             else:
                 taken = [c]
                 if step == SUB * INNER - 1:

time: 60.2 us -> 59.3 us (0.985)
  starting transfers between devices: 9.87 us -> 17.6 us
  waiting for transfers between devices: 27.7 us -> 20 us
  local copies, waits for them, and re-layouts: 4.07 us -> 3.16 us
    ppermute x17, starting transfers between devices: 9.87 us -> 17.6 us  [moved(): return lax.ppermute(shard, ('loop', 'grp'), pairs)]
    ppermute x17, waiting for transfers between devices: 27.7 us -> 20 us  [moved(): return lax.ppermute(shard, ('loop', 'grp'), pairs)]
    unnamed x18 -> x16, local copies, waits for them, and re-layouts: 4.07 us -> 3.16 us
  transfers between devices with their start and end apart: 17 -> 17, of which waited for: 13 -> 12; matrix products, arithmetic and copies ran while one was open for 2% -> 2% of each run, Pallas kernels for 19% -> 19%
where the time goes in v14:
time: 59.3 us; the launch traced here: 59.1 us
  waiting for transfers between devices  20 us (34%)
  starting transfers between devices  17.6 us (30%)
  Pallas kernels  16.2 us (27%)
  local copies, waits for them, and re-layouts  3.16 us (5%)
  other arithmetic  1.11 us (2%)
  between operations  0.99 us (2%)
    ppermute x17, waiting for transfers between devices, moved(): return lax.ppermute(shard, ('loop', 'grp'), pairs)  20 us
    ppermute x17, starting transfers between devices, moved(): return lax.ppermute(shard, ('loop', 'grp'), pairs)  17.6 us
    pallas_call x11, Pallas kernels, chunk_pass(): pl.pallas_call(functools.partial(chunk_kernel, sub_epoch, rows.start, tot...  9.83 us
    pallas_call x1, Pallas kernels, first_pass(): pl.pallas_call(functools.partial(first_kernel, rows.start), out_shape=[ja...  4.12 us
    unnamed x16, local copies, waits for them, and re-layouts  3.16 us
    pallas_call x2, Pallas kernels, last_item_step(): pl.pallas_call(functools.partial(last_kernel, len(terms), rows.start), ou...  1.8 us
  transfers between devices with their start and end apart: 17, of which 12 were waited for; matrix products, arithmetic and copies ran while one was open for 2% of the time, Pallas kernels for 19%

profile of v14, /device:TPU:0, one launch (start us, length us, event | category | flops | bytes accessed | tf_op | source)
XLA Modules:
  0.0 59.1 jit_solution(18131090380796196952)
XLA Ops:
  0.7 4.1 %shard_map.68 = (bf16[1024,128]{1,0:T(8,128)(2,1)}, f32[512,128]{1,0:T(8,128)}) custom-call(bf16[2,512,2048]{2,1,0:T(8,128)(2,1)} %rate_ref.21, f32[2048,128]{1,0:T(8,128)} %refs_0_.9, f32[512,128]{1,0:T(8,128)} %half_ref.1), custom_call_target="tpu_custom_call" | custom-call | flops 402653184 | bytes 1048576 | tf_op jit(solution)/shard_map/pallas_call | solution.py:106
  4.8 3.0 %collective-permute-start = (bf16[1024,128]{1,0:T(8,128)(2,1)}, bf16[1024,128]{1,0:T(8,128)(2,1)S(1)}, u32[]{:S(2)}, u32[]{:S(2)}) collective-permute-start(bf16[1024,128]{1,0:T(8,128)(2,1)} %get-tuple-element.48.refs_2_), channel_id=1, source_target_pairs={{0,1},{1,0},{2,3},{3,2},{4,5},{5,4},{6,7},{7,6},{8,9},{9,8},{10,11... | collective-permute-start | bytes 786440 | tf_op jit(solution)/shard_map/ppermute | solution.py:30
  7.8 2.2 %copy-done = bf16[2,512,2048]{2,1,0:T(8,128)(2,1)S(1)} copy-done((bf16[2,512,2048]{2,1,0:T(8,128)(2,1)S(1)}, bf16[2,512,2048]{2,1,0:T(8,128)(2,1)}, u32[]{:S(2)}) %copy-start) | copy-done | bytes 4194328
  10.0 0.9 %copy-done.6 = f32[512,128]{1,0:T(8,128)S(1)} copy-done((f32[512,128]{1,0:T(8,128)S(1)}, f32[512,128]{1,0:T(8,128)}, u32[]{:S(2)}) %copy-start.6) | copy-done | bytes 262168
  10.9 1.3 %shard_map.69 = (bf16[1024,128]{1,0:T(8,128)(2,1)S(1)}, f32[512,128]{1,0:T(8,128)S(1)}) custom-call(bf16[2,512,2048]{2,1,0:T(8,128)(2,1)S(1)} %copy-done, f32[512,128]{1,0:T(8,128)S(1)} %copy-done.4, f32[512,128]{1,0:T(8,128)S(1)} %copy-done.6, f32[2048,128]{1,0:T(8,128)S(1)} %copy-done.2), custom_call_target="tpu_custom_call" | custom-call | flops 402653184 | bytes 1048576 | tf_op jit(solution)/shard_map/pallas_call | solution.py:162
  12.4 2.4 %collective-permute-done.refs_3_ = bf16[1024,128]{1,0:T(8,128)(2,1)S(1)} collective-permute-done((bf16[1024,128]{1,0:T(8,128)(2,1)}, bf16[1024,128]{1,0:T(8,128)(2,1)S(1)}, u32[]{:S(2)}, u32[]{:S(2)}) %collective-permute-start) | collective-permute-done | bytes 262176 | tf_op jit(solution)/shard_map/ppermute | solution.py:30
  15.6 2.4 %collective-permute-start.2 = (bf16[512,128]{1,0:T(8,128)(2,1)S(1)}, bf16[512,128]{1,0:T(8,128)(2,1)S(1)}, u32[]{:S(2)}, u32[]{:S(2)}) collective-permute-start(bf16[512,128]{1,0:T(8,128)(2,1)S(1)} %get-tuple-element.55.refs_0_), channel_id=1, source_target_pairs={{0,1},{1,0},{2,3},{3,2},{4,5},{5,4},{6,7},{7,6},{8,9},{9,8},{10,11... | collective-permute-start | bytes 393224 | tf_op jit(solution)/shard_map/ppermute | solution.py:30
  18.9 2.7 %collective-permute-done.1.refs_3_ = bf16[1024,128]{1,0:T(8,128)(2,1)S(1)} collective-permute-done((bf16[1024,128]{1,0:T(8,128)(2,1)S(1)}, bf16[1024,128]{1,0:T(8,128)(2,1)S(1)}, u32[]{:S(2)}, u32[]{:S(2)}) %collective-permute-start.1) | collective-permute-done | bytes 262176 | tf_op jit(solution)/shard_map/ppermute | solution.py:30
  22.3 1.3 %collective-permute-start.6 = (bf16[512,128]{1,0:T(8,128)(2,1)S(1)}, bf16[512,128]{1,0:T(8,128)(2,1)S(1)}, u32[]{:S(2)}, u32[]{:S(2)}) collective-permute-start(bf16[512,128]{1,0:T(8,128)(2,1)S(1)} %get-tuple-element.68.refs_0_), channel_id=1, source_target_pairs={{0,1},{1,0},{2,3},{3,2},{4,5},{5,4},{6,7},{7,6},{8,9},{9,8},{10,11... | collective-permute-start | bytes 393224 | tf_op jit(solution)/shard_map/ppermute | solution.py:30
  25.3 1.3 %collective-permute-start.8 = (bf16[512,128]{1,0:T(8,128)(2,1)S(1)}, bf16[512,128]{1,0:T(8,128)(2,1)S(1)}, u32[]{:S(2)}, u32[]{:S(2)}) collective-permute-start(bf16[512,128]{1,0:T(8,128)(2,1)S(1)} %get-tuple-element.63.refs_3_.refs_0_), channel_id=1, source_target_pairs={{0,1},{1,0},{2,3},{3,2},{4,5},{5,4},{6,7},{7,6},{8,9},{9,8},{10,11... | collective-permute-start | bytes 393224 | tf_op jit(solution)/shard_map/ppermute | solution.py:30
  29.3 2.3 %collective-permute-done.3.refs_0_ = bf16[512,128]{1,0:T(8,128)(2,1)S(1)} collective-permute-done((bf16[512,128]{1,0:T(8,128)(2,1)S(1)}, bf16[512,128]{1,0:T(8,128)(2,1)S(1)}, u32[]{:S(2)}, u32[]{:S(2)}) %collective-permute-start.3) | collective-permute-done | bytes 131104 | tf_op jit(solution)/shard_map/ppermute | solution.py:30
  32.5 1.3 %collective-permute-start.10 = (bf16[512,128]{1,0:T(8,128)(2,1)S(1)}, bf16[512,128]{1,0:T(8,128)(2,1)S(1)}, u32[]{:S(2)}, u32[]{:S(2)}) collective-permute-start(bf16[512,128]{1,0:T(8,128)(2,1)S(1)} %get-tuple-element.75.refs_3_.refs_2_), channel_id=1, source_target_pairs={{0,1},{1,0},{2,3},{3,2},{4,5},{5,4},{6,7},{7,6},{8,9},{9,8},{10,11... | collective-permute-start | bytes 393224 | tf_op jit(solution)/shard_map/ppermute | solution.py:30
  33.9 1.9 %collective-permute-done.5.refs_0_.refs_1_.refs_4_ = bf16[1024,128]{1,0:T(8,128)(2,1)S(1)} collective-permute-done((bf16[1024,128]{1,0:T(8,128)(2,1)S(1)}, bf16[1024,128]{1,0:T(8,128)(2,1)S(1)}, u32[]{:S(2)}, u32[]{:S(2)}) %collective-permute-start.5) | collective-permute-done | bytes 262176 | tf_op jit(solution)/shard_map/ppermute | solution.py:30
  36.5 1.4 %collective-permute-start.11 = (bf16[512,128]{1,0:T(8,128)(2,1)S(1)}, bf16[512,128]{1,0:T(8,128)(2,1)S(1)}, u32[]{:S(2)}, u32[]{:S(2)}) collective-permute-start(bf16[512,128]{1,0:T(8,128)(2,1)S(1)} %get-tuple-element.78.refs_6_), channel_id=1, source_target_pairs={{0,1},{1,0},{2,3},{3,2},{4,5},{5,4},{6,7},{7,6},{8,9},{9,8},{10,11... | collective-permute-start | bytes 393224 | tf_op jit(solution)/shard_map/ppermute | solution.py:30
  39.3 1.4 %collective-permute-start.12 = (bf16[512,128]{1,0:T(8,128)(2,1)S(1)}, bf16[512,128]{1,0:T(8,128)(2,1)S(1)}, u32[]{:S(2)}, u32[]{:S(2)}) collective-permute-start(bf16[512,128]{1,0:T(8,128)(2,1)S(1)} %get-tuple-element.80.refs_2_), channel_id=1, source_target_pairs={{0,1},{1,0},{2,3},{3,2},{4,5},{5,4},{6,7},{7,6},{8,9},{9,8},{10,11... | collective-permute-start | bytes 393224 | tf_op jit(solution)/shard_map/ppermute | solution.py:30
  42.1 1.4 %collective-permute-start.14 = (bf16[512,128]{1,0:T(8,128)(2,1)S(1)}, bf16[512,128]{1,0:T(8,128)(2,1)S(1)}, u32[]{:S(2)}, u32[]{:S(2)}) collective-permute-start(bf16[512,128]{1,0:T(8,128)(2,1)S(1)} %get-tuple-element.82.refs_6_), channel_id=1, source_target_pairs={{0,1},{1,0},{2,3},{3,2},{4,5},{5,4},{6,7},{7,6},{8,9},{9,8},{10,11... | collective-permute-start | bytes 393224 | tf_op jit(solution)/shard_map/ppermute | solution.py:30
  43.6 1.4 %shard_map.82 = (bf16[1024,128]{1,0:T(8,128)(2,1)S(1)}, f32[512,128]{1,0:T(8,128)S(1)}, f32[1024,128]{1,0:T(8,128)S(1)}, f32[1024,128]{1,0:T(8,128)S(1)}) custom-call(bf16[2,512,2048]{2,1,0:T(8,128)(2,1)S(1)} %copy-done.1, bf16[512,128]{1,0:T(8,128)(2,1)S(1)} %get-tuple-element.96.half_ref, f32[512,128]{1,0:T(8,128)S(1)} %get-tuple-element.95.grad_ref, ...), custom_call_target="tpu_custom_call" | custom-call | flops 402653184 | bytes 1048576 | tf_op jit(solution)/shard_map/pallas_call | solution.py:162
  45.8 2.8 %collective-permute-done.14.refs_7_ = bf16[512,128]{1,0:T(8,128)(2,1)S(1)} collective-permute-done((bf16[512,128]{1,0:T(8,128)(2,1)S(1)}, bf16[512,128]{1,0:T(8,128)(2,1)S(1)}, u32[]{:S(2)}, u32[]{:S(2)}) %collective-permute-start.14) | collective-permute-done | bytes 131104 | tf_op jit(solution)/shard_map/ppermute | solution.py:30
  48.6 1.4 %shard_map.83 = (bf16[1024,128]{1,0:T(8,128)(2,1)S(1)}, f32[512,128]{1,0:T(8,128)S(1)}, f32[1024,128]{1,0:T(8,128)S(1)}, f32[1024,128]{1,0:T(8,128)S(1)}) custom-call(bf16[2,512,2048]{2,1,0:T(8,128)(2,1)S(1)} %copy-done.1, bf16[512,128]{1,0:T(8,128)(2,1)S(1)} %get-tuple-element.96.half_ref, f32[512,128]{1,0:T(8,128)S(1)} %get-tuple-element.79.grad_ref, ...), custom_call_target="tpu_custom_call" | custom-call | flops 402653184 | bytes 1048576 | tf_op jit(solution)/shard_map/pallas_call | solution.py:162
  50.0 1.4 %collective-permute-start.15 = (bf16[1024,128]{1,0:T(8,128)(2,1)S(1)}, bf16[1024,128]{1,0:T(8,128)(2,1)S(1)}, u32[]{:S(2)}, u32[]{:S(2)}) collective-permute-start(bf16[1024,128]{1,0:T(8,128)(2,1)S(1)} %get-tuple-element.86.refs_0_), channel_id=1, source_target_pairs={{0,1},{1,0},{2,3},{3,2},{4,5},{5,4},{6,7},{7,6},{8,9},{9,8},{10,11... | collective-permute-start | bytes 786440 | tf_op jit(solution)/shard_map/ppermute | solution.py:30
  52.2 2.1 %collective-permute-done.16.refs_1_ = bf16[1024,128]{1,0:T(8,128)(2,1)S(1)} collective-permute-done((bf16[1024,128]{1,0:T(8,128)(2,1)S(1)}, bf16[1024,128]{1,0:T(8,128)(2,1)S(1)}, u32[]{:S(2)}, u32[]{:S(2)}) %collective-permute-start.16) | collective-permute-done | bytes 262176 | tf_op jit(solution)/shard_map/ppermute | solution.py:30
  54.3 0.9 %shard_map.84.refs_2_ = f32[2048,128]{1,0:T(8,128)} custom-call(f32[1024,128]{1,0:T(8,128)S(1)} %get-tuple-element.87.items_ref, f32[1024,128]{1,0:T(8,128)S(1)} %get-tuple-element.88.accum_ref, bf16[1024,128]{1,0:T(8,128)(2,1)S(1)} %get-tuple-element.89.refs_0_, bf16[1024,128]{1,0:T(8,128)(2,1)S(1)} %collective-permute-done.16.refs_1_), custom_call_target="tpu_custom_call" | custom-call | flops 786432 | bytes 2048 | tf_op jit(solution)/shard_map/pallas_call | solution.py:213
  55.2 2.8 %collective-permute-done.15.refs_1_ = bf16[1024,128]{1,0:T(8,128)(2,1)S(1)} collective-permute-done((bf16[1024,128]{1,0:T(8,128)(2,1)S(1)}, bf16[1024,128]{1,0:T(8,128)(2,1)S(1)}, u32[]{:S(2)}, u32[]{:S(2)}) %collective-permute-start.15) | collective-permute-done | bytes 262176 | tf_op jit(solution)/shard_map/ppermute | solution.py:30
  58.0 0.9 %shard_map.85 = f32[2048,128]{1,0:T(8,128)} custom-call(f32[1024,128]{1,0:T(8,128)S(1)} %get-tuple-element.84.items_ref, f32[1024,128]{1,0:T(8,128)S(1)} %get-tuple-element.85.accum_ref, bf16[1024,128]{1,0:T(8,128)(2,1)S(1)} %get-tuple-element.86.refs_0_, bf16[1024,128]{1,0:T(8,128)(2,1)S(1)} %collective-permute-done.15.refs_1_, ...), custom_call_target="tpu_custom_call", output_to_operand_aliasing={{}: (4, {})} | custom-call | flops 786432 | bytes 2048 | tf_op jit(solution)/shard_map/pallas_call | solution.py:213
  (50 shorter events, 12.9 us)
Async XLA Ops:
  0.6 7.2 %copy-start.4 = (f32[512,128]{1,0:T(8,128)S(1)}, f32[512,128]{1,0:T(8,128)}, u32[]{:S(2)}) copy-start(f32[512,128]{1,0:T(8,128)} %half_ref.1) | copy-start | bytes 786436
  0.6 7.2 %copy-start.2 = (f32[2048,128]{1,0:T(8,128)S(1)}, f32[2048,128]{1,0:T(8,128)}, u32[]{:S(2)}) copy-start(f32[2048,128]{1,0:T(8,128)} %refs_0_.9) | copy-start | bytes 3145732
  0.7 11.7 %copy-start.7 = (f32[512,128]{1,0:T(8,128)S(1)}, f32[512,128]{1,0:T(8,128)}, u32[]{:S(2)}) copy-start(f32[512,128]{1,0:T(8,128)} %param.7) | copy-start | bytes 786436
  4.8 10.0 %collective-permute-start = (bf16[1024,128]{1,0:T(8,128)(2,1)}, bf16[1024,128]{1,0:T(8,128)(2,1)S(1)}, u32[]{:S(2)}, u32[]{:S(2)}) collective-permute-start(bf16[1024,128]{1,0:T(8,128)(2,1)} %get-tuple-element.48.refs_2_), channel_id=1, source_target_pairs={{0,1},{1,0},{2,3},{3,2},{4,5},{5,4},{6,7},{7,6},{8,9},{9,8},{10,11... | collective-permute-start | bytes 786440 | tf_op jit(solution)/shard_map/ppermute | solution.py:30
  7.8 2.2 %copy-start = (bf16[2,512,2048]{2,1,0:T(8,128)(2,1)S(1)}, bf16[2,512,2048]{2,1,0:T(8,128)(2,1)}, u32[]{:S(2)}) copy-start(bf16[2,512,2048]{2,1,0:T(8,128)(2,1)} %rate_ref.21) | copy-start | bytes 12582916
  10.9 3.9 %copy-start.3 = (f32[2048,128]{1,0:T(8,128)S(1)}, f32[2048,128]{1,0:T(8,128)}, u32[]{:S(2)}) copy-start(f32[2048,128]{1,0:T(8,128)} %refs_1_.7) | copy-start | bytes 3145732
  10.9 3.9 %copy-start.5 = (bf16[1024,128]{1,0:T(8,128)(2,1)S(1)}, bf16[1024,128]{1,0:T(8,128)(2,1)}, u32[]{:S(2)}) copy-start(bf16[1024,128]{1,0:T(8,128)(2,1)} %get-tuple-element.48.refs_2_) | copy-start | bytes 786436
  12.2 9.3 %collective-permute-start.1 = (bf16[1024,128]{1,0:T(8,128)(2,1)S(1)}, bf16[1024,128]{1,0:T(8,128)(2,1)S(1)}, u32[]{:S(2)}, u32[]{:S(2)}) collective-permute-start(bf16[1024,128]{1,0:T(8,128)(2,1)S(1)} %get-tuple-element.51.refs_2_), channel_id=1, source_target_pairs={{0,1},{1,0},{2,3},{3,2},{4,5},{5,4},{6,7},{7,6},{8,9},{9,8},{10,11... | collective-permute-start | bytes 786440 | tf_op jit(solution)/shard_map/ppermute | solution.py:30
  15.6 8.8 %collective-permute-start.2 = (bf16[512,128]{1,0:T(8,128)(2,1)S(1)}, bf16[512,128]{1,0:T(8,128)(2,1)S(1)}, u32[]{:S(2)}, u32[]{:S(2)}) collective-permute-start(bf16[512,128]{1,0:T(8,128)(2,1)S(1)} %get-tuple-element.55.refs_0_), channel_id=1, source_target_pairs={{0,1},{1,0},{2,3},{3,2},{4,5},{5,4},{6,7},{7,6},{8,9},{9,8},{10,11... | collective-permute-start | bytes 393224 | tf_op jit(solution)/shard_map/ppermute | solution.py:30
  18.8 5.8 %copy-start.1 = (bf16[2,512,2048]{2,1,0:T(8,128)(2,1)S(1)}, bf16[2,512,2048]{2,1,0:T(8,128)(2,1)}, u32[]{:S(2)}) copy-start(bf16[2,512,2048]{2,1,0:T(8,128)(2,1)} %rate_ref.21) | copy-start | bytes 12582916
  18.8 8.3 %collective-permute-start.4 = (bf16[512,128]{1,0:T(8,128)(2,1)S(1)}, bf16[512,128]{1,0:T(8,128)(2,1)S(1)}, u32[]{:S(2)}, u32[]{:S(2)}) collective-permute-start(bf16[512,128]{1,0:T(8,128)(2,1)S(1)} %get-tuple-element.61.refs_0_), channel_id=1, source_target_pairs={{0,1},{1,0},{2,3},{3,2},{4,5},{5,4},{6,7},{7,6},{8,9},{9,8},{10,11... | collective-permute-start | bytes 393224 | tf_op jit(solution)/shard_map/ppermute | solution.py:30
  22.3 6.2 %collective-permute-start.6 = (bf16[512,128]{1,0:T(8,128)(2,1)S(1)}, bf16[512,128]{1,0:T(8,128)(2,1)S(1)}, u32[]{:S(2)}, u32[]{:S(2)}) collective-permute-start(bf16[512,128]{1,0:T(8,128)(2,1)S(1)} %get-tuple-element.68.refs_0_), channel_id=1, source_target_pairs={{0,1},{1,0},{2,3},{3,2},{4,5},{5,4},{6,7},{7,6},{8,9},{9,8},{10,11... | collective-permute-start | bytes 393224 | tf_op jit(solution)/shard_map/ppermute | solution.py:30
  24.5 7.1 %collective-permute-start.3 = (bf16[512,128]{1,0:T(8,128)(2,1)S(1)}, bf16[512,128]{1,0:T(8,128)(2,1)S(1)}, u32[]{:S(2)}, u32[]{:S(2)}) collective-permute-start(bf16[512,128]{1,0:T(8,128)(2,1)S(1)} %get-tuple-element.56.refs_4_), channel_id=1, source_target_pairs={{0,2},{1,3},{2,4},{3,5},{4,6},{5,7},{6,8},{7,9},{8,10},{9,11},{10,... | collective-permute-start | bytes 393224 | tf_op jit(solution)/shard_map/ppermute | solution.py:30
  25.3 7.0 %collective-permute-start.8 = (bf16[512,128]{1,0:T(8,128)(2,1)S(1)}, bf16[512,128]{1,0:T(8,128)(2,1)S(1)}, u32[]{:S(2)}, u32[]{:S(2)}) collective-permute-start(bf16[512,128]{1,0:T(8,128)(2,1)S(1)} %get-tuple-element.63.refs_3_.refs_0_), channel_id=1, source_target_pairs={{0,1},{1,0},{2,3},{3,2},{4,5},{5,4},{6,7},{7,6},{8,9},{9,8},{10,11... | collective-permute-start | bytes 393224 | tf_op jit(solution)/shard_map/ppermute | solution.py:30
  27.2 8.5 %collective-permute-start.5 = (bf16[1024,128]{1,0:T(8,128)(2,1)S(1)}, bf16[1024,128]{1,0:T(8,128)(2,1)S(1)}, u32[]{:S(2)}, u32[]{:S(2)}) collective-permute-start(bf16[1024,128]{1,0:T(8,128)(2,1)S(1)} %get-tuple-element.64), channel_id=1, source_target_pairs={{0,2},{1,3},{2,4},{3,5},{4,6},{5,7},{6,8},{7,9},{8,10},{9,11},{10,... | collective-permute-start | bytes 786440 | tf_op jit(solution)/shard_map/ppermute | solution.py:30
  28.6 9.9 %collective-permute-start.7 = (bf16[1024,128]{1,0:T(8,128)(2,1)S(1)}, bf16[1024,128]{1,0:T(8,128)(2,1)S(1)}, u32[]{:S(2)}, u32[]{:S(2)}) collective-permute-start(bf16[1024,128]{1,0:T(8,128)(2,1)S(1)} %get-tuple-element.70), channel_id=1, source_target_pairs={{0,2},{1,3},{2,4},{3,5},{4,6},{5,7},{6,8},{7,9},{8,10},{9,11},{10,... | collective-permute-start | bytes 786440 | tf_op jit(solution)/shard_map/ppermute | solution.py:30
  32.5 8.9 %collective-permute-start.9 = (bf16[1024,128]{1,0:T(8,128)(2,1)S(1)}, bf16[1024,128]{1,0:T(8,128)(2,1)S(1)}, u32[]{:S(2)}, u32[]{:S(2)}) collective-permute-start(bf16[1024,128]{1,0:T(8,128)(2,1)S(1)} %get-tuple-element.76), channel_id=1, source_target_pairs={{0,2},{1,3},{2,4},{3,5},{4,6},{5,7},{6,8},{7,9},{8,10},{9,11},{10,... | collective-permute-start | bytes 786440 | tf_op jit(solution)/shard_map/ppermute | solution.py:30
  32.5 11.1 %collective-permute-start.10 = (bf16[512,128]{1,0:T(8,128)(2,1)S(1)}, bf16[512,128]{1,0:T(8,128)(2,1)S(1)}, u32[]{:S(2)}, u32[]{:S(2)}) collective-permute-start(bf16[512,128]{1,0:T(8,128)(2,1)S(1)} %get-tuple-element.75.refs_3_.refs_2_), channel_id=1, source_target_pairs={{0,1},{1,0},{2,3},{3,2},{4,5},{5,4},{6,7},{7,6},{8,9},{9,8},{10,11... | collective-permute-start | bytes 393224 | tf_op jit(solution)/shard_map/ppermute | solution.py:30
  33.9 11.9 %collective-permute-start.13 = (bf16[512,128]{1,0:T(8,128)(2,1)S(1)}, bf16[512,128]{1,0:T(8,128)(2,1)S(1)}, u32[]{:S(2)}, u32[]{:S(2)}) collective-permute-start(bf16[512,128]{1,0:T(8,128)(2,1)S(1)} %get-tuple-element.81), channel_id=1, source_target_pairs={{0,2},{1,3},{2,4},{3,5},{4,6},{5,7},{6,8},{7,9},{8,10},{9,11},{10,... | collective-permute-start | bytes 393224 | tf_op jit(solution)/shard_map/ppermute | solution.py:30
  36.5 7.1 %collective-permute-start.11 = (bf16[512,128]{1,0:T(8,128)(2,1)S(1)}, bf16[512,128]{1,0:T(8,128)(2,1)S(1)}, u32[]{:S(2)}, u32[]{:S(2)}) collective-permute-start(bf16[512,128]{1,0:T(8,128)(2,1)S(1)} %get-tuple-element.78.refs_6_), channel_id=1, source_target_pairs={{0,1},{1,0},{2,3},{3,2},{4,5},{5,4},{6,7},{7,6},{8,9},{9,8},{10,11... | collective-permute-start | bytes 393224 | tf_op jit(solution)/shard_map/ppermute | solution.py:30
  39.3 6.5 %collective-permute-start.12 = (bf16[512,128]{1,0:T(8,128)(2,1)S(1)}, bf16[512,128]{1,0:T(8,128)(2,1)S(1)}, u32[]{:S(2)}, u32[]{:S(2)}) collective-permute-start(bf16[512,128]{1,0:T(8,128)(2,1)S(1)} %get-tuple-element.80.refs_2_), channel_id=1, source_target_pairs={{0,1},{1,0},{2,3},{3,2},{4,5},{5,4},{6,7},{7,6},{8,9},{9,8},{10,11... | collective-permute-start | bytes 393224 | tf_op jit(solution)/shard_map/ppermute | solution.py:30
  42.1 6.5 %collective-permute-start.14 = (bf16[512,128]{1,0:T(8,128)(2,1)S(1)}, bf16[512,128]{1,0:T(8,128)(2,1)S(1)}, u32[]{:S(2)}, u32[]{:S(2)}) collective-permute-start(bf16[512,128]{1,0:T(8,128)(2,1)S(1)} %get-tuple-element.82.refs_6_), channel_id=1, source_target_pairs={{0,1},{1,0},{2,3},{3,2},{4,5},{5,4},{6,7},{7,6},{8,9},{9,8},{10,11... | collective-permute-start | bytes 393224 | tf_op jit(solution)/shard_map/ppermute | solution.py:30
  45.0 9.3 %collective-permute-start.16 = (bf16[1024,128]{1,0:T(8,128)(2,1)S(1)}, bf16[1024,128]{1,0:T(8,128)(2,1)S(1)}, u32[]{:S(2)}, u32[]{:S(2)}) collective-permute-start(bf16[1024,128]{1,0:T(8,128)(2,1)S(1)} %get-tuple-element.89.refs_0_), channel_id=1, source_target_pairs={{0,1},{1,0},{2,3},{3,2},{4,5},{5,4},{6,7},{7,6},{8,9},{9,8},{10,11... | collective-permute-start | bytes 786440 | tf_op jit(solution)/shard_map/ppermute | solution.py:30
  50.0 8.1 %collective-permute-start.15 = (bf16[1024,128]{1,0:T(8,128)(2,1)S(1)}, bf16[1024,128]{1,0:T(8,128)(2,1)S(1)}, u32[]{:S(2)}, u32[]{:S(2)}) collective-permute-start(bf16[1024,128]{1,0:T(8,128)(2,1)S(1)} %get-tuple-element.86.refs_0_), channel_id=1, source_target_pairs={{0,1},{1,0},{2,3},{3,2},{4,5},{5,4},{6,7},{7,6},{8,9},{9,8},{10,11... | collective-permute-start | bytes 786440 | tf_op jit(solution)/shard_map/ppermute | solution.py:30
  (1 other events, 0.9 us)

commit v15 on v14

--- a/solution.py
+++ b/solution.py
@@ -72,8 +72,9 @@
 AWAY = pl.BlockSpec(memory_space=pltpu.HBM)
 
 
-def first_kernel(column, rate_hbm, items_hbm, users_hbm, term_out, grad_out, *scratch):
+def first_kernel(column, rate_hbm, items_hbm, users_hbm, term_out, grad_out, done_out, *scratch):
     users_ref, rate_ref, items_ref, sems = scratch
+    done_out[...] = jnp.zeros(done_out.shape, done_out.dtype)
     load_users = pltpu.make_async_copy(users_hbm, users_ref, sems.at[2, 0])
     load_users.start()
     tiles = range(term_out.shape[0] // TILE)
@@ -108,9 +109,10 @@
         out_shape=[
             jax.ShapeDtypeStruct((size, rank), jnp.bfloat16),
             jax.ShapeDtypeStruct(users.shape, jnp.float32),
+            jax.ShapeDtypeStruct((8, 128), jnp.float32),
         ],
         in_specs=[AWAY] * 3,
-        out_specs=[WHOLE] * 2,
+        out_specs=[WHOLE] * 3,
         scratch_shapes=[
             pltpu.VMEM(users.shape, jnp.float32),
             pltpu.VMEM((size // TILE, n_users, TILE), jnp.bfloat16),
@@ -122,10 +124,12 @@
     )(ratings, items, users)
 
 
-def chunk_kernel(sub_epoch, column, size, places, rate_ref, half_ref, grad_ref, *refs):
+def chunk_kernel(sub_epoch, column, size, places, adds, rate_ref, half_ref, *refs):
+    if adds:
+        grad_ref, *refs = refs
     half = half_ref[...].astype(jnp.bfloat16)
     half_t = half.T
-    grad = grad_ref[...]
+    grad = grad_ref[...] if adds else jnp.zeros(half.shape, jnp.float32)
     term_out, grad_out, *updated = refs[-4:] if places[0][0] else refs[-2:]
     for piece, (n_terms, items_at, accum_at, terms_at) in enumerate(places):
         items_ref, *refs = refs
@@ -151,16 +155,16 @@
     total, rank = rows.stop - rows.start, half.shape[1]
     out_shape = [
         jax.ShapeDtypeStruct((total, rank), jnp.bfloat16),
-        jax.ShapeDtypeStruct(grad.shape, jnp.float32),
+        jax.ShapeDtypeStruct(half.shape, jnp.float32),
     ]
-    operands, places = [ratings, half, grad], []
+    operands, places = [ratings, half] + ([] if grad is None else [grad]), []
     for items, accum, terms, terms_at in pieces:
         operands += [items[0], accum[0], *terms] if terms else [items[0]]
         places.append((len(terms), items[1], accum[1], terms_at))
     if places[0][0]:
         out_shape += [jax.ShapeDtypeStruct((total, rank), jnp.float32)] * 2
     return pl.pallas_call(
-        functools.partial(chunk_kernel, sub_epoch, rows.start, total // len(pieces), places),
+        functools.partial(chunk_kernel, sub_epoch, rows.start, total // len(pieces), places, grad is not None),
         out_shape=out_shape,
         in_specs=[WHOLE] * len(operands) + [pl.BlockSpec(memory_space=pl.ANY)] * len(after),
         out_specs=[WHOLE] * len(out_shape),
@@ -267,10 +271,11 @@
                     continue
                 both = slice(rows[c].start, rows[c + FIRST - 1].stop)
                 if c == 0:
-                    term, grad_user = first_pass(ratings, both, users, item_factors)
+                    term, grad_user, done = first_pass(ratings, both, users, item_factors)
                 else:
                     piece = (items[c], item_acc[c], (), 0)
-                    term, grad_user = chunk_pass(ratings, 0, both, users, grad_user, [piece])
+                    term, more = chunk_pass(ratings, 0, both, users, None, [piece], [done])
+                    grad_user = grad_user + more
             else:
                 taken = [c]
                 if step == SUB * INNER - 1:

time: 59.3 us -> 59.2 us (level)
  starting transfers between devices: 17.6 us -> 19.6 us
  waiting for transfers between devices: 20 us -> 18.2 us
    ppermute x17, starting transfers between devices: 17.6 us -> 19.6 us  [moved(): return lax.ppermute(shard, ('loop', 'grp'), pairs)]
    ppermute x17, waiting for transfers between devices: 20 us -> 18.2 us  [moved(): return lax.ppermute(shard, ('loop', 'grp'), pairs)]
    unnamed x16 -> x18, local copies, waits for them, and re-layouts: 3.16 us -> 2.9 us
where the time goes in v15:
time: 59.2 us; the launch traced here: 59 us
  starting transfers between devices  19.6 us (33%)
  waiting for transfers between devices  18.2 us (31%)
  Pallas kernels  16.3 us (28%)
  local copies, waits for them, and re-layouts  2.9 us (5%)
  other arithmetic  1.13 us (2%)
  between operations  0.99 us (2%)
    ppermute x17, starting transfers between devices, moved(): return lax.ppermute(shard, ('loop', 'grp'), pairs)  19.6 us
    ppermute x17, waiting for transfers between devices, moved(): return lax.ppermute(shard, ('loop', 'grp'), pairs)  18.2 us
    pallas_call x11, Pallas kernels, chunk_pass(): pl.pallas_call(functools.partial(chunk_kernel, sub_epoch, rows.start, tot...  9.85 us
    pallas_call x1, Pallas kernels, first_pass(): pl.pallas_call(functools.partial(first_kernel, rows.start), out_shape=[ja...  4.12 us
    unnamed x18, local copies, waits for them, and re-layouts  2.9 us
    pallas_call x2, Pallas kernels, last_item_step(): pl.pallas_call(functools.partial(last_kernel, len(terms), rows.start), ou...  1.8 us
  transfers between devices with their start and end apart: 17, of which 12 were waited for; matrix products, arithmetic and copies ran while one was open for 2% of the time, Pallas kernels for 19%

profile of v15, /device:TPU:0, one launch (start us, length us, event | category | flops | bytes accessed | tf_op | source)
XLA Modules:
  0.0 59.0 jit_solution(18072730055154679056)
XLA Ops:
  0.7 4.1 %shard_map.68 = (bf16[1024,128]{1,0:T(8,128)(2,1)}, f32[512,128]{1,0:T(8,128)}, f32[8,128]{1,0:T(8,128)}) custom-call(bf16[2,512,2048]{2,1,0:T(8,128)(2,1)} %rate_ref.21, f32[2048,128]{1,0:T(8,128)} %refs_1_.7, f32[512,128]{1,0:T(8,128)} %half_ref.1), custom_call_target="tpu_custom_call" | custom-call | flops 402653184 | bytes 1048576 | tf_op jit(solution)/shard_map/pallas_call | solution.py:107
  4.8 3.0 %collective-permute-start = (bf16[1024,128]{1,0:T(8,128)(2,1)}, bf16[1024,128]{1,0:T(8,128)(2,1)S(1)}, u32[]{:S(2)}, u32[]{:S(2)}) collective-permute-start(bf16[1024,128]{1,0:T(8,128)(2,1)} %get-tuple-element.50.refs_3_), channel_id=1, source_target_pairs={{0,1},{1,0},{2,3},{3,2},{4,5},{5,4},{6,7},{7,6},{8,9},{9,8},{10,11... | collective-permute-start | bytes 786440 | tf_op jit(solution)/shard_map/ppermute | solution.py:30
  7.8 2.2 %copy-done = bf16[2,512,2048]{2,1,0:T(8,128)(2,1)S(1)} copy-done((bf16[2,512,2048]{2,1,0:T(8,128)(2,1)S(1)}, bf16[2,512,2048]{2,1,0:T(8,128)(2,1)}, u32[]{:S(2)}) %copy-start) | copy-done | bytes 4194328
  10.7 1.3 %shard_map.69 = (bf16[1024,128]{1,0:T(8,128)(2,1)S(1)}, f32[512,128]{1,0:T(8,128)S(1)}) custom-call(bf16[2,512,2048]{2,1,0:T(8,128)(2,1)S(1)} %copy-done, f32[512,128]{1,0:T(8,128)S(1)} %copy-done.4, f32[2048,128]{1,0:T(8,128)S(1)} %copy-done.2, f32[8,128]{1,0:T(8,128)S(1)} %copy-done.6), custom_call_target="tpu_custom_call" | custom-call | flops 402653184 | bytes 1048576 | tf_op jit(solution)/shard_map/pallas_call | solution.py:166
  12.2 2.6 %collective-permute-done.refs_4_ = bf16[1024,128]{1,0:T(8,128)(2,1)S(1)} collective-permute-done((bf16[1024,128]{1,0:T(8,128)(2,1)}, bf16[1024,128]{1,0:T(8,128)(2,1)S(1)}, u32[]{:S(2)}, u32[]{:S(2)}) %collective-permute-start) | collective-permute-done | bytes 262176 | tf_op jit(solution)/shard_map/ppermute | solution.py:30
  15.6 2.4 %collective-permute-start.2 = (bf16[512,128]{1,0:T(8,128)(2,1)S(1)}, bf16[512,128]{1,0:T(8,128)(2,1)S(1)}, u32[]{:S(2)}, u32[]{:S(2)}) collective-permute-start(bf16[512,128]{1,0:T(8,128)(2,1)S(1)} %get-tuple-element.57.refs_0_), channel_id=1, source_target_pairs={{0,1},{1,0},{2,3},{3,2},{4,5},{5,4},{6,7},{7,6},{8,9},{9,8},{10,11... | collective-permute-start | bytes 393224 | tf_op jit(solution)/shard_map/ppermute | solution.py:30
  18.9 2.4 %collective-permute-done.1.refs_4_ = bf16[1024,128]{1,0:T(8,128)(2,1)S(1)} collective-permute-done((bf16[1024,128]{1,0:T(8,128)(2,1)S(1)}, bf16[1024,128]{1,0:T(8,128)(2,1)S(1)}, u32[]{:S(2)}, u32[]{:S(2)}) %collective-permute-start.1) | collective-permute-done | bytes 262176 | tf_op jit(solution)/shard_map/ppermute | solution.py:30
  22.0 1.6 %collective-permute-start.6 = (bf16[512,128]{1,0:T(8,128)(2,1)S(1)}, bf16[512,128]{1,0:T(8,128)(2,1)S(1)}, u32[]{:S(2)}, u32[]{:S(2)}) collective-permute-start(bf16[512,128]{1,0:T(8,128)(2,1)S(1)} %get-tuple-element.70.refs_0_), channel_id=1, source_target_pairs={{0,1},{1,0},{2,3},{3,2},{4,5},{5,4},{6,7},{7,6},{8,9},{9,8},{10,11... | collective-permute-start | bytes 393224 | tf_op jit(solution)/shard_map/ppermute | solution.py:30
  25.0 1.6 %collective-permute-start.8 = (bf16[512,128]{1,0:T(8,128)(2,1)S(1)}, bf16[512,128]{1,0:T(8,128)(2,1)S(1)}, u32[]{:S(2)}, u32[]{:S(2)}) collective-permute-start(bf16[512,128]{1,0:T(8,128)(2,1)S(1)} %get-tuple-element.65.refs_3_.refs_0_), channel_id=1, source_target_pairs={{0,1},{1,0},{2,3},{3,2},{4,5},{5,4},{6,7},{7,6},{8,9},{9,8},{10,11... | collective-permute-start | bytes 393224 | tf_op jit(solution)/shard_map/ppermute | solution.py:30
  27.0 1.1 %collective-permute-start.5 = (bf16[1024,128]{1,0:T(8,128)(2,1)S(1)}, bf16[1024,128]{1,0:T(8,128)(2,1)S(1)}, u32[]{:S(2)}, u32[]{:S(2)}) collective-permute-start(bf16[1024,128]{1,0:T(8,128)(2,1)S(1)} %get-tuple-element.66), channel_id=1, source_target_pairs={{0,2},{1,3},{2,4},{3,5},{4,6},{5,7},{6,8},{7,9},{8,10},{9,11},{10,... | collective-permute-start | bytes 786440 | tf_op jit(solution)/shard_map/ppermute | solution.py:30
  29.0 2.3 %collective-permute-done.3.refs_1_ = bf16[512,128]{1,0:T(8,128)(2,1)S(1)} collective-permute-done((bf16[512,128]{1,0:T(8,128)(2,1)S(1)}, bf16[512,128]{1,0:T(8,128)(2,1)S(1)}, u32[]{:S(2)}, u32[]{:S(2)}) %collective-permute-start.3) | collective-permute-done | bytes 131104 | tf_op jit(solution)/shard_map/ppermute | solution.py:30
  32.3 1.6 %collective-permute-start.10 = (bf16[512,128]{1,0:T(8,128)(2,1)S(1)}, bf16[512,128]{1,0:T(8,128)(2,1)S(1)}, u32[]{:S(2)}, u32[]{:S(2)}) collective-permute-start(bf16[512,128]{1,0:T(8,128)(2,1)S(1)} %get-tuple-element.77.refs_3_), channel_id=1, source_target_pairs={{0,1},{1,0},{2,3},{3,2},{4,5},{5,4},{6,7},{7,6},{8,9},{9,8},{10,11... | collective-permute-start | bytes 393224 | tf_op jit(solution)/shard_map/ppermute | solution.py:30
  34.0 1.6 %collective-permute-done.5.refs_1_.refs_2_.refs_5_ = bf16[1024,128]{1,0:T(8,128)(2,1)S(1)} collective-permute-done((bf16[1024,128]{1,0:T(8,128)(2,1)S(1)}, bf16[1024,128]{1,0:T(8,128)(2,1)S(1)}, u32[]{:S(2)}, u32[]{:S(2)}) %collective-permute-start.5) | collective-permute-done | bytes 262176 | tf_op jit(solution)/shard_map/ppermute | solution.py:30
  36.3 1.6 %collective-permute-start.11 = (bf16[512,128]{1,0:T(8,128)(2,1)S(1)}, bf16[512,128]{1,0:T(8,128)(2,1)S(1)}, u32[]{:S(2)}, u32[]{:S(2)}) collective-permute-start(bf16[512,128]{1,0:T(8,128)(2,1)S(1)} %get-tuple-element.80.refs_7_), channel_id=1, source_target_pairs={{0,1},{1,0},{2,3},{3,2},{4,5},{5,4},{6,7},{7,6},{8,9},{9,8},{10,11... | collective-permute-start | bytes 393224 | tf_op jit(solution)/shard_map/ppermute | solution.py:30
  39.1 1.6 %collective-permute-start.12 = (bf16[512,128]{1,0:T(8,128)(2,1)S(1)}, bf16[512,128]{1,0:T(8,128)(2,1)S(1)}, u32[]{:S(2)}, u32[]{:S(2)}) collective-permute-start(bf16[512,128]{1,0:T(8,128)(2,1)S(1)} %get-tuple-element.82.refs_3_), channel_id=1, source_target_pairs={{0,1},{1,0},{2,3},{3,2},{4,5},{5,4},{6,7},{7,6},{8,9},{9,8},{10,11... | collective-permute-start | bytes 393224 | tf_op jit(solution)/shard_map/ppermute | solution.py:30
  41.9 1.6 %collective-permute-start.14 = (bf16[512,128]{1,0:T(8,128)(2,1)S(1)}, bf16[512,128]{1,0:T(8,128)(2,1)S(1)}, u32[]{:S(2)}, u32[]{:S(2)}) collective-permute-start(bf16[512,128]{1,0:T(8,128)(2,1)S(1)} %get-tuple-element.84.refs_7_), channel_id=1, source_target_pairs={{0,1},{1,0},{2,3},{3,2},{4,5},{5,4},{6,7},{7,6},{8,9},{9,8},{10,11... | collective-permute-start | bytes 393224 | tf_op jit(solution)/shard_map/ppermute | solution.py:30
  43.6 1.4 %shard_map.82 = (bf16[1024,128]{1,0:T(8,128)(2,1)S(1)}, f32[512,128]{1,0:T(8,128)S(1)}, f32[1024,128]{1,0:T(8,128)S(1)}, f32[1024,128]{1,0:T(8,128)S(1)}) custom-call(bf16[2,512,2048]{2,1,0:T(8,128)(2,1)S(1)} %copy-done.1, bf16[512,128]{1,0:T(8,128)(2,1)S(1)} %get-tuple-element.98.half_ref, f32[512,128]{1,0:T(8,128)S(1)} %get-tuple-element.97.refs_0_, ...), custom_call_target="tpu_custom_call" | custom-call | flops 402653184 | bytes 1048576 | tf_op jit(solution)/shard_map/pallas_call | solution.py:166
  45.8 2.6 %collective-permute-done.14.refs_8_ = bf16[512,128]{1,0:T(8,128)(2,1)S(1)} collective-permute-done((bf16[512,128]{1,0:T(8,128)(2,1)S(1)}, bf16[512,128]{1,0:T(8,128)(2,1)S(1)}, u32[]{:S(2)}, u32[]{:S(2)}) %collective-permute-start.14) | collective-permute-done | bytes 131104 | tf_op jit(solution)/shard_map/ppermute | solution.py:30
  48.4 1.4 %shard_map.83 = (bf16[1024,128]{1,0:T(8,128)(2,1)S(1)}, f32[512,128]{1,0:T(8,128)S(1)}, f32[1024,128]{1,0:T(8,128)S(1)}, f32[1024,128]{1,0:T(8,128)S(1)}) custom-call(bf16[2,512,2048]{2,1,0:T(8,128)(2,1)S(1)} %copy-done.1, bf16[512,128]{1,0:T(8,128)(2,1)S(1)} %get-tuple-element.98.half_ref, f32[512,128]{1,0:T(8,128)S(1)} %get-tuple-element.81.refs_0_, ...), custom_call_target="tpu_custom_call" | custom-call | flops 402653184 | bytes 1048576 | tf_op jit(solution)/shard_map/pallas_call | solution.py:166
  49.8 1.6 %collective-permute-start.15 = (bf16[1024,128]{1,0:T(8,128)(2,1)S(1)}, bf16[1024,128]{1,0:T(8,128)(2,1)S(1)}, u32[]{:S(2)}, u32[]{:S(2)}) collective-permute-start(bf16[1024,128]{1,0:T(8,128)(2,1)S(1)} %get-tuple-element.88.refs_0_), channel_id=1, source_target_pairs={{0,1},{1,0},{2,3},{3,2},{4,5},{5,4},{6,7},{7,6},{8,9},{9,8},{10,11... | collective-permute-start | bytes 786440 | tf_op jit(solution)/shard_map/ppermute | solution.py:30
  52.2 2.1 %collective-permute-done.16.refs_1_ = bf16[1024,128]{1,0:T(8,128)(2,1)S(1)} collective-permute-done((bf16[1024,128]{1,0:T(8,128)(2,1)S(1)}, bf16[1024,128]{1,0:T(8,128)(2,1)S(1)}, u32[]{:S(2)}, u32[]{:S(2)}) %collective-permute-start.16) | collective-permute-done | bytes 262176 | tf_op jit(solution)/shard_map/ppermute | solution.py:30
  54.3 0.9 %shard_map.84.refs_2_ = f32[2048,128]{1,0:T(8,128)} custom-call(f32[1024,128]{1,0:T(8,128)S(1)} %get-tuple-element.89.items_ref, f32[1024,128]{1,0:T(8,128)S(1)} %get-tuple-element.90.accum_ref, bf16[1024,128]{1,0:T(8,128)(2,1)S(1)} %get-tuple-element.91.refs_0_, bf16[1024,128]{1,0:T(8,128)(2,1)S(1)} %collective-permute-done.16.refs_1_), custom_call_target="tpu_custom_call" | custom-call | flops 786432 | bytes 2048 | tf_op jit(solution)/shard_map/pallas_call | solution.py:217
  55.2 2.8 %collective-permute-done.15.refs_1_ = bf16[1024,128]{1,0:T(8,128)(2,1)S(1)} collective-permute-done((bf16[1024,128]{1,0:T(8,128)(2,1)S(1)}, bf16[1024,128]{1,0:T(8,128)(2,1)S(1)}, u32[]{:S(2)}, u32[]{:S(2)}) %collective-permute-start.15) | collective-permute-done | bytes 262176 | tf_op jit(solution)/shard_map/ppermute | solution.py:30
  58.0 0.9 %shard_map.85 = f32[2048,128]{1,0:T(8,128)} custom-call(f32[1024,128]{1,0:T(8,128)S(1)} %get-tuple-element.86.items_ref, f32[1024,128]{1,0:T(8,128)S(1)} %get-tuple-element.87.accum_ref, bf16[1024,128]{1,0:T(8,128)(2,1)S(1)} %get-tuple-element.88.refs_0_, bf16[1024,128]{1,0:T(8,128)(2,1)S(1)} %collective-permute-done.15.refs_1_, ...), custom_call_target="tpu_custom_call", output_to_operand_aliasing={{}: (4, {})} | custom-call | flops 786432 | bytes 2048 | tf_op jit(solution)/shard_map/pallas_call | solution.py:217
  (52 shorter events, 11.6 us)
Async XLA Ops:
  0.6 7.2 %copy-start.4 = (f32[512,128]{1,0:T(8,128)S(1)}, f32[512,128]{1,0:T(8,128)}, u32[]{:S(2)}) copy-start(f32[512,128]{1,0:T(8,128)} %half_ref.1) | copy-start | bytes 786436
  0.6 7.2 %copy-start.2 = (f32[2048,128]{1,0:T(8,128)S(1)}, f32[2048,128]{1,0:T(8,128)}, u32[]{:S(2)}) copy-start(f32[2048,128]{1,0:T(8,128)} %refs_1_.7) | copy-start | bytes 3145732
  0.7 11.4 %copy-start.7 = (f32[512,128]{1,0:T(8,128)S(1)}, f32[512,128]{1,0:T(8,128)}, u32[]{:S(2)}) copy-start(f32[512,128]{1,0:T(8,128)} %param.7) | copy-start | bytes 786436
  4.8 10.0 %collective-permute-start = (bf16[1024,128]{1,0:T(8,128)(2,1)}, bf16[1024,128]{1,0:T(8,128)(2,1)S(1)}, u32[]{:S(2)}, u32[]{:S(2)}) collective-permute-start(bf16[1024,128]{1,0:T(8,128)(2,1)} %get-tuple-element.50.refs_3_), channel_id=1, source_target_pairs={{0,1},{1,0},{2,3},{3,2},{4,5},{5,4},{6,7},{7,6},{8,9},{9,8},{10,11... | collective-permute-start | bytes 786440 | tf_op jit(solution)/shard_map/ppermute | solution.py:30
  7.8 2.2 %copy-start = (bf16[2,512,2048]{2,1,0:T(8,128)(2,1)S(1)}, bf16[2,512,2048]{2,1,0:T(8,128)(2,1)}, u32[]{:S(2)}) copy-start(bf16[2,512,2048]{2,1,0:T(8,128)(2,1)} %rate_ref.21) | copy-start | bytes 12582916
  10.7 4.1 %copy-start.3 = (f32[2048,128]{1,0:T(8,128)S(1)}, f32[2048,128]{1,0:T(8,128)}, u32[]{:S(2)}) copy-start(f32[2048,128]{1,0:T(8,128)} %refs_2_.7) | copy-start | bytes 3145732
  10.7 4.1 %copy-start.5 = (bf16[1024,128]{1,0:T(8,128)(2,1)S(1)}, bf16[1024,128]{1,0:T(8,128)(2,1)}, u32[]{:S(2)}) copy-start(bf16[1024,128]{1,0:T(8,128)(2,1)} %get-tuple-element.50.refs_3_) | copy-start | bytes 786436
  12.0 9.3 %collective-permute-start.1 = (bf16[1024,128]{1,0:T(8,128)(2,1)S(1)}, bf16[1024,128]{1,0:T(8,128)(2,1)S(1)}, u32[]{:S(2)}, u32[]{:S(2)}) collective-permute-start(bf16[1024,128]{1,0:T(8,128)(2,1)S(1)} %get-tuple-element.53.refs_3_), channel_id=1, source_target_pairs={{0,1},{1,0},{2,3},{3,2},{4,5},{5,4},{6,7},{7,6},{8,9},{9,8},{10,11... | collective-permute-start | bytes 786440 | tf_op jit(solution)/shard_map/ppermute | solution.py:30
  15.6 8.5 %collective-permute-start.2 = (bf16[512,128]{1,0:T(8,128)(2,1)S(1)}, bf16[512,128]{1,0:T(8,128)(2,1)S(1)}, u32[]{:S(2)}, u32[]{:S(2)}) collective-permute-start(bf16[512,128]{1,0:T(8,128)(2,1)S(1)} %get-tuple-element.57.refs_0_), channel_id=1, source_target_pairs={{0,1},{1,0},{2,3},{3,2},{4,5},{5,4},{6,7},{7,6},{8,9},{9,8},{10,11... | collective-permute-start | bytes 393224 | tf_op jit(solution)/shard_map/ppermute | solution.py:30
  18.8 5.5 %copy-start.1 = (bf16[2,512,2048]{2,1,0:T(8,128)(2,1)S(1)}, bf16[2,512,2048]{2,1,0:T(8,128)(2,1)}, u32[]{:S(2)}) copy-start(bf16[2,512,2048]{2,1,0:T(8,128)(2,1)} %rate_ref.21) | copy-start | bytes 12582916
  18.8 8.1 %collective-permute-start.4 = (bf16[512,128]{1,0:T(8,128)(2,1)S(1)}, bf16[512,128]{1,0:T(8,128)(2,1)S(1)}, u32[]{:S(2)}, u32[]{:S(2)}) collective-permute-start(bf16[512,128]{1,0:T(8,128)(2,1)S(1)} %get-tuple-element.63.refs_0_), channel_id=1, source_target_pairs={{0,1},{1,0},{2,3},{3,2},{4,5},{5,4},{6,7},{7,6},{8,9},{9,8},{10,11... | collective-permute-start | bytes 393224 | tf_op jit(solution)/shard_map/ppermute | solution.py:30
  22.0 6.3 %collective-permute-start.6 = (bf16[512,128]{1,0:T(8,128)(2,1)S(1)}, bf16[512,128]{1,0:T(8,128)(2,1)S(1)}, u32[]{:S(2)}, u32[]{:S(2)}) collective-permute-start(bf16[512,128]{1,0:T(8,128)(2,1)S(1)} %get-tuple-element.70.refs_0_), channel_id=1, source_target_pairs={{0,1},{1,0},{2,3},{3,2},{4,5},{5,4},{6,7},{7,6},{8,9},{9,8},{10,11... | collective-permute-start | bytes 393224 | tf_op jit(solution)/shard_map/ppermute | solution.py:30
  24.2 7.1 %collective-permute-start.3 = (bf16[512,128]{1,0:T(8,128)(2,1)S(1)}, bf16[512,128]{1,0:T(8,128)(2,1)S(1)}, u32[]{:S(2)}, u32[]{:S(2)}) collective-permute-start(bf16[512,128]{1,0:T(8,128)(2,1)S(1)} %get-tuple-element.58.refs_5_), channel_id=1, source_target_pairs={{0,2},{1,3},{2,4},{3,5},{4,6},{5,7},{6,8},{7,9},{8,10},{9,11},{10,... | collective-permute-start | bytes 393224 | tf_op jit(solution)/shard_map/ppermute | solution.py:30
  25.0 7.0 %collective-permute-start.8 = (bf16[512,128]{1,0:T(8,128)(2,1)S(1)}, bf16[512,128]{1,0:T(8,128)(2,1)S(1)}, u32[]{:S(2)}, u32[]{:S(2)}) collective-permute-start(bf16[512,128]{1,0:T(8,128)(2,1)S(1)} %get-tuple-element.65.refs_3_.refs_0_), channel_id=1, source_target_pairs={{0,1},{1,0},{2,3},{3,2},{4,5},{5,4},{6,7},{7,6},{8,9},{9,8},{10,11... | collective-permute-start | bytes 393224 | tf_op jit(solution)/shard_map/ppermute | solution.py:30
  27.0 8.5 %collective-permute-start.5 = (bf16[1024,128]{1,0:T(8,128)(2,1)S(1)}, bf16[1024,128]{1,0:T(8,128)(2,1)S(1)}, u32[]{:S(2)}, u32[]{:S(2)}) collective-permute-start(bf16[1024,128]{1,0:T(8,128)(2,1)S(1)} %get-tuple-element.66), channel_id=1, source_target_pairs={{0,2},{1,3},{2,4},{3,5},{4,6},{5,7},{6,8},{7,9},{8,10},{9,11},{10,... | collective-permute-start | bytes 786440 | tf_op jit(solution)/shard_map/ppermute | solution.py:30
  28.5 9.9 %collective-permute-start.7 = (bf16[1024,128]{1,0:T(8,128)(2,1)S(1)}, bf16[1024,128]{1,0:T(8,128)(2,1)S(1)}, u32[]{:S(2)}, u32[]{:S(2)}) collective-permute-start(bf16[1024,128]{1,0:T(8,128)(2,1)S(1)} %get-tuple-element.72), channel_id=1, source_target_pairs={{0,2},{1,3},{2,4},{3,5},{4,6},{5,7},{6,8},{7,9},{8,10},{9,11},{10,... | collective-permute-start | bytes 786440 | tf_op jit(solution)/shard_map/ppermute | solution.py:30
  32.2 9.0 %collective-permute-start.9 = (bf16[1024,128]{1,0:T(8,128)(2,1)S(1)}, bf16[1024,128]{1,0:T(8,128)(2,1)S(1)}, u32[]{:S(2)}, u32[]{:S(2)}) collective-permute-start(bf16[1024,128]{1,0:T(8,128)(2,1)S(1)} %get-tuple-element.78), channel_id=1, source_target_pairs={{0,2},{1,3},{2,4},{3,5},{4,6},{5,7},{6,8},{7,9},{8,10},{9,11},{10,... | collective-permute-start | bytes 786440 | tf_op jit(solution)/shard_map/ppermute | solution.py:30
  32.3 11.3 %collective-permute-start.10 = (bf16[512,128]{1,0:T(8,128)(2,1)S(1)}, bf16[512,128]{1,0:T(8,128)(2,1)S(1)}, u32[]{:S(2)}, u32[]{:S(2)}) collective-permute-start(bf16[512,128]{1,0:T(8,128)(2,1)S(1)} %get-tuple-element.77.refs_3_), channel_id=1, source_target_pairs={{0,1},{1,0},{2,3},{3,2},{4,5},{5,4},{6,7},{7,6},{8,9},{9,8},{10,11... | collective-permute-start | bytes 393224 | tf_op jit(solution)/shard_map/ppermute | solution.py:30
  33.9 11.9 %collective-permute-start.13 = (bf16[512,128]{1,0:T(8,128)(2,1)S(1)}, bf16[512,128]{1,0:T(8,128)(2,1)S(1)}, u32[]{:S(2)}, u32[]{:S(2)}) collective-permute-start(bf16[512,128]{1,0:T(8,128)(2,1)S(1)} %get-tuple-element.83), channel_id=1, source_target_pairs={{0,2},{1,3},{2,4},{3,5},{4,6},{5,7},{6,8},{7,9},{8,10},{9,11},{10,... | collective-permute-start | bytes 393224 | tf_op jit(solution)/shard_map/ppermute | solution.py:30
  36.3 7.3 %collective-permute-start.11 = (bf16[512,128]{1,0:T(8,128)(2,1)S(1)}, bf16[512,128]{1,0:T(8,128)(2,1)S(1)}, u32[]{:S(2)}, u32[]{:S(2)}) collective-permute-start(bf16[512,128]{1,0:T(8,128)(2,1)S(1)} %get-tuple-element.80.refs_7_), channel_id=1, source_target_pairs={{0,1},{1,0},{2,3},{3,2},{4,5},{5,4},{6,7},{7,6},{8,9},{9,8},{10,11... | collective-permute-start | bytes 393224 | tf_op jit(solution)/shard_map/ppermute | solution.py:30
  39.1 6.7 %collective-permute-start.12 = (bf16[512,128]{1,0:T(8,128)(2,1)S(1)}, bf16[512,128]{1,0:T(8,128)(2,1)S(1)}, u32[]{:S(2)}, u32[]{:S(2)}) collective-permute-start(bf16[512,128]{1,0:T(8,128)(2,1)S(1)} %get-tuple-element.82.refs_3_), channel_id=1, source_target_pairs={{0,1},{1,0},{2,3},{3,2},{4,5},{5,4},{6,7},{7,6},{8,9},{9,8},{10,11... | collective-permute-start | bytes 393224 | tf_op jit(solution)/shard_map/ppermute | solution.py:30
  41.9 6.5 %collective-permute-start.14 = (bf16[512,128]{1,0:T(8,128)(2,1)S(1)}, bf16[512,128]{1,0:T(8,128)(2,1)S(1)}, u32[]{:S(2)}, u32[]{:S(2)}) collective-permute-start(bf16[512,128]{1,0:T(8,128)(2,1)S(1)} %get-tuple-element.84.refs_7_), channel_id=1, source_target_pairs={{0,1},{1,0},{2,3},{3,2},{4,5},{5,4},{6,7},{7,6},{8,9},{9,8},{10,11... | collective-permute-start | bytes 393224 | tf_op jit(solution)/shard_map/ppermute | solution.py:30
  45.0 9.3 %collective-permute-start.16 = (bf16[1024,128]{1,0:T(8,128)(2,1)S(1)}, bf16[1024,128]{1,0:T(8,128)(2,1)S(1)}, u32[]{:S(2)}, u32[]{:S(2)}) collective-permute-start(bf16[1024,128]{1,0:T(8,128)(2,1)S(1)} %get-tuple-element.91.refs_0_), channel_id=1, source_target_pairs={{0,1},{1,0},{2,3},{3,2},{4,5},{5,4},{6,7},{7,6},{8,9},{9,8},{10,11... | collective-permute-start | bytes 786440 | tf_op jit(solution)/shard_map/ppermute | solution.py:30
  49.8 8.2 %collective-permute-start.15 = (bf16[1024,128]{1,0:T(8,128)(2,1)S(1)}, bf16[1024,128]{1,0:T(8,128)(2,1)S(1)}, u32[]{:S(2)}, u32[]{:S(2)}) collective-permute-start(bf16[1024,128]{1,0:T(8,128)(2,1)S(1)} %get-tuple-element.88.refs_0_), channel_id=1, source_target_pairs={{0,1},{1,0},{2,3},{3,2},{4,5},{5,4},{6,7},{7,6},{8,9},{9,8},{10,11... | collective-permute-start | bytes 786440 | tf_op jit(solution)/shard_map/ppermute | solution.py:30
  (2 other events, 2.1 us)

commit v16 on v15

--- a/solution.py
+++ b/solution.py
@@ -119,7 +119,7 @@
             pltpu.VMEM((size // TILE, TILE, rank), jnp.float32),
             pltpu.SemaphoreType.DMA((3, size // TILE)),
         ],
-        compiler_params=params(62),
+        compiler_params=params(57),
         cost_estimate=cost(n_users, size, rank),
     )(ratings, items, users)
 

time: 59.2 us -> 59.3 us (level)
  starting transfers between devices: 19.6 us -> 22 us
  local copies, waits for them, and re-layouts: 2.9 us -> 0.71 us
    ppermute x17, starting transfers between devices: 19.6 us -> 22 us  [moved(): return lax.ppermute(shard, ('loop', 'grp'), pairs)]
    unnamed x18 -> x16, local copies, waits for them, and re-layouts: 2.9 us -> 0.71 us
  transfers between devices with their start and end apart: 17 -> 17, of which waited for: 12 -> 10; matrix products, arithmetic and copies ran while one was open for 2% -> 2% of each run, Pallas kernels for 19% -> 19%
where the time goes in v16:
time: 59.3 us; the launch traced here: 59.1 us
  starting transfers between devices  22 us (37%)
  waiting for transfers between devices  17.9 us (30%)
  Pallas kernels  16.3 us (27%)
  other arithmetic  1.13 us (2%)
  between operations  0.99 us (2%)
  local copies, waits for them, and re-layouts  0.71 us (1%)
    ppermute x17, starting transfers between devices, moved(): return lax.ppermute(shard, ('loop', 'grp'), pairs)  22 us
    ppermute x17, waiting for transfers between devices, moved(): return lax.ppermute(shard, ('loop', 'grp'), pairs)  17.9 us
    pallas_call x11, Pallas kernels, chunk_pass(): pl.pallas_call(functools.partial(chunk_kernel, sub_epoch, rows.start, tot...  9.86 us
    pallas_call x1, Pallas kernels, first_pass(): pl.pallas_call(functools.partial(first_kernel, rows.start), out_shape=[ja...  4.16 us
    pallas_call x2, Pallas kernels, last_item_step(): pl.pallas_call(functools.partial(last_kernel, len(terms), rows.start), ou...  1.8 us
  transfers between devices with their start and end apart: 17, of which 10 were waited for; matrix products, arithmetic and copies ran while one was open for 2% of the time, Pallas kernels for 19%

profile of v16, /device:TPU:0, one launch (start us, length us, event | category | flops | bytes accessed | tf_op | source)
XLA Modules:
  0.0 59.1 jit_solution(4046804287911863725)
XLA Ops:
  0.7 4.2 %shard_map.68 = (bf16[1024,128]{1,0:T(8,128)(2,1)}, f32[512,128]{1,0:T(8,128)}, f32[8,128]{1,0:T(8,128)}) custom-call(bf16[2,512,2048]{2,1,0:T(8,128)(2,1)} %rate_ref.21, f32[2048,128]{1,0:T(8,128)} %refs_1_.7, f32[512,128]{1,0:T(8,128)} %half_ref.1), custom_call_target="tpu_custom_call" | custom-call | flops 402653184 | bytes 1048576 | tf_op jit(solution)/shard_map/pallas_call | solution.py:107
  4.9 3.0 %collective-permute-start = (bf16[1024,128]{1,0:T(8,128)(2,1)}, bf16[1024,128]{1,0:T(8,128)(2,1)S(1)}, u32[]{:S(2)}, u32[]{:S(2)}) collective-permute-start(bf16[1024,128]{1,0:T(8,128)(2,1)} %get-tuple-element.50.refs_3_), channel_id=1, source_target_pairs={{0,1},{1,0},{2,3},{3,2},{4,5},{5,4},{6,7},{7,6},{8,9},{9,8},{10,11... | collective-permute-start | bytes 786440 | tf_op jit(solution)/shard_map/ppermute | solution.py:30
  8.6 1.3 %shard_map.69 = (bf16[1024,128]{1,0:T(8,128)(2,1)S(1)}, f32[512,128]{1,0:T(8,128)S(1)}) custom-call(bf16[2,512,2048]{2,1,0:T(8,128)(2,1)S(1)} %copy-done, f32[512,128]{1,0:T(8,128)S(1)} %copy-done.3, f32[2048,128]{1,0:T(8,128)S(1)} %copy-done.1, f32[8,128]{1,0:T(8,128)S(1)} %copy-done.5), custom_call_target="tpu_custom_call" | custom-call | flops 402653184 | bytes 1048576 | tf_op jit(solution)/shard_map/pallas_call | solution.py:166
  10.1 5.1 %collective-permute-done.refs_4_ = bf16[1024,128]{1,0:T(8,128)(2,1)S(1)} collective-permute-done((bf16[1024,128]{1,0:T(8,128)(2,1)}, bf16[1024,128]{1,0:T(8,128)(2,1)S(1)}, u32[]{:S(2)}, u32[]{:S(2)}) %collective-permute-start) | collective-permute-done | bytes 262176 | tf_op jit(solution)/shard_map/ppermute | solution.py:30
  16.0 2.1 %collective-permute-start.2 = (bf16[512,128]{1,0:T(8,128)(2,1)S(1)}, bf16[512,128]{1,0:T(8,128)(2,1)S(1)}, u32[]{:S(2)}, u32[]{:S(2)}) collective-permute-start(bf16[512,128]{1,0:T(8,128)(2,1)S(1)} %get-tuple-element.57.refs_0_), channel_id=1, source_target_pairs={{0,1},{1,0},{2,3},{3,2},{4,5},{5,4},{6,7},{7,6},{8,9},{9,8},{10,11... | collective-permute-start | bytes 393224 | tf_op jit(solution)/shard_map/ppermute | solution.py:30
  18.9 1.9 %collective-permute-done.1.refs_4_ = bf16[1024,128]{1,0:T(8,128)(2,1)S(1)} collective-permute-done((bf16[1024,128]{1,0:T(8,128)(2,1)S(1)}, bf16[1024,128]{1,0:T(8,128)(2,1)S(1)}, u32[]{:S(2)}, u32[]{:S(2)}) %collective-permute-start.1) | collective-permute-done | bytes 262176 | tf_op jit(solution)/shard_map/ppermute | solution.py:30
  21.6 2.1 %collective-permute-start.6 = (bf16[512,128]{1,0:T(8,128)(2,1)S(1)}, bf16[512,128]{1,0:T(8,128)(2,1)S(1)}, u32[]{:S(2)}, u32[]{:S(2)}) collective-permute-start(bf16[512,128]{1,0:T(8,128)(2,1)S(1)} %get-tuple-element.70.refs_0_), channel_id=1, source_target_pairs={{0,1},{1,0},{2,3},{3,2},{4,5},{5,4},{6,7},{7,6},{8,9},{9,8},{10,11... | collective-permute-start | bytes 393224 | tf_op jit(solution)/shard_map/ppermute | solution.py:30
  24.6 2.1 %collective-permute-start.8 = (bf16[512,128]{1,0:T(8,128)(2,1)S(1)}, bf16[512,128]{1,0:T(8,128)(2,1)S(1)}, u32[]{:S(2)}, u32[]{:S(2)}) collective-permute-start(bf16[512,128]{1,0:T(8,128)(2,1)S(1)} %get-tuple-element.65.refs_3_.refs_0_), channel_id=1, source_target_pairs={{0,1},{1,0},{2,3},{3,2},{4,5},{5,4},{6,7},{7,6},{8,9},{9,8},{10,11... | collective-permute-start | bytes 393224 | tf_op jit(solution)/shard_map/ppermute | solution.py:30
  26.8 1.4 %collective-permute-start.5 = (bf16[1024,128]{1,0:T(8,128)(2,1)S(1)}, bf16[1024,128]{1,0:T(8,128)(2,1)S(1)}, u32[]{:S(2)}, u32[]{:S(2)}) collective-permute-start(bf16[1024,128]{1,0:T(8,128)(2,1)S(1)} %get-tuple-element.66), channel_id=1, source_target_pairs={{0,2},{1,3},{2,4},{3,5},{4,6},{5,7},{6,8},{7,9},{8,10},{9,11},{10,... | collective-permute-start | bytes 786440 | tf_op jit(solution)/shard_map/ppermute | solution.py:30
  29.1 1.8 %collective-permute-done.3.refs_1_ = bf16[512,128]{1,0:T(8,128)(2,1)S(1)} collective-permute-done((bf16[512,128]{1,0:T(8,128)(2,1)S(1)}, bf16[512,128]{1,0:T(8,128)(2,1)S(1)}, u32[]{:S(2)}, u32[]{:S(2)}) %collective-permute-start.3) | collective-permute-done | bytes 131104 | tf_op jit(solution)/shard_map/ppermute | solution.py:30
  31.9 2.1 %collective-permute-start.10 = (bf16[512,128]{1,0:T(8,128)(2,1)S(1)}, bf16[512,128]{1,0:T(8,128)(2,1)S(1)}, u32[]{:S(2)}, u32[]{:S(2)}) collective-permute-start(bf16[512,128]{1,0:T(8,128)(2,1)S(1)} %get-tuple-element.77.refs_3_), channel_id=1, source_target_pairs={{0,1},{1,0},{2,3},{3,2},{4,5},{5,4},{6,7},{7,6},{8,9},{9,8},{10,11... | collective-permute-start | bytes 393224 | tf_op jit(solution)/shard_map/ppermute | solution.py:30
  34.0 1.4 %collective-permute-done.5.refs_1_.refs_2_.refs_5_ = bf16[1024,128]{1,0:T(8,128)(2,1)S(1)} collective-permute-done((bf16[1024,128]{1,0:T(8,128)(2,1)S(1)}, bf16[1024,128]{1,0:T(8,128)(2,1)S(1)}, u32[]{:S(2)}, u32[]{:S(2)}) %collective-permute-start.5) | collective-permute-done | bytes 262176 | tf_op jit(solution)/shard_map/ppermute | solution.py:30
  36.1 1.9 %collective-permute-start.11 = (bf16[512,128]{1,0:T(8,128)(2,1)S(1)}, bf16[512,128]{1,0:T(8,128)(2,1)S(1)}, u32[]{:S(2)}, u32[]{:S(2)}) collective-permute-start(bf16[512,128]{1,0:T(8,128)(2,1)S(1)} %get-tuple-element.80.refs_7_), channel_id=1, source_target_pairs={{0,1},{1,0},{2,3},{3,2},{4,5},{5,4},{6,7},{7,6},{8,9},{9,8},{10,11... | collective-permute-start | bytes 393224 | tf_op jit(solution)/shard_map/ppermute | solution.py:30
  38.9 1.9 %collective-permute-start.12 = (bf16[512,128]{1,0:T(8,128)(2,1)S(1)}, bf16[512,128]{1,0:T(8,128)(2,1)S(1)}, u32[]{:S(2)}, u32[]{:S(2)}) collective-permute-start(bf16[512,128]{1,0:T(8,128)(2,1)S(1)} %get-tuple-element.82.refs_3_), channel_id=1, source_target_pairs={{0,1},{1,0},{2,3},{3,2},{4,5},{5,4},{6,7},{7,6},{8,9},{9,8},{10,11... | collective-permute-start | bytes 393224 | tf_op jit(solution)/shard_map/ppermute | solution.py:30
  41.7 1.9 %collective-permute-start.14 = (bf16[512,128]{1,0:T(8,128)(2,1)S(1)}, bf16[512,128]{1,0:T(8,128)(2,1)S(1)}, u32[]{:S(2)}, u32[]{:S(2)}) collective-permute-start(bf16[512,128]{1,0:T(8,128)(2,1)S(1)} %get-tuple-element.84.refs_7_), channel_id=1, source_target_pairs={{0,1},{1,0},{2,3},{3,2},{4,5},{5,4},{6,7},{7,6},{8,9},{9,8},{10,11... | collective-permute-start | bytes 393224 | tf_op jit(solution)/shard_map/ppermute | solution.py:30
  43.7 1.4 %shard_map.82 = (bf16[1024,128]{1,0:T(8,128)(2,1)S(1)}, f32[512,128]{1,0:T(8,128)S(1)}, f32[1024,128]{1,0:T(8,128)S(1)}, f32[1024,128]{1,0:T(8,128)S(1)}) custom-call(bf16[2,512,2048]{2,1,0:T(8,128)(2,1)S(1)} %copy-done, bf16[512,128]{1,0:T(8,128)(2,1)S(1)} %get-tuple-element.98.half_ref, f32[512,128]{1,0:T(8,128)S(1)} %get-tuple-element.97.refs_0_, ...), custom_call_target="tpu_custom_call" | custom-call | flops 402653184 | bytes 1048576 | tf_op jit(solution)/shard_map/pallas_call | solution.py:166
  45.8 2.3 %collective-permute-done.14.refs_8_ = bf16[512,128]{1,0:T(8,128)(2,1)S(1)} collective-permute-done((bf16[512,128]{1,0:T(8,128)(2,1)S(1)}, bf16[512,128]{1,0:T(8,128)(2,1)S(1)}, u32[]{:S(2)}, u32[]{:S(2)}) %collective-permute-start.14) | collective-permute-done | bytes 131104 | tf_op jit(solution)/shard_map/ppermute | solution.py:30
  48.2 1.4 %shard_map.83 = (bf16[1024,128]{1,0:T(8,128)(2,1)S(1)}, f32[512,128]{1,0:T(8,128)S(1)}, f32[1024,128]{1,0:T(8,128)S(1)}, f32[1024,128]{1,0:T(8,128)S(1)}) custom-call(bf16[2,512,2048]{2,1,0:T(8,128)(2,1)S(1)} %copy-done, bf16[512,128]{1,0:T(8,128)(2,1)S(1)} %get-tuple-element.98.half_ref, f32[512,128]{1,0:T(8,128)S(1)} %get-tuple-element.81.refs_0_, ...), custom_call_target="tpu_custom_call" | custom-call | flops 402653184 | bytes 1048576 | tf_op jit(solution)/shard_map/pallas_call | solution.py:166
  49.6 1.9 %collective-permute-start.15 = (bf16[1024,128]{1,0:T(8,128)(2,1)S(1)}, bf16[1024,128]{1,0:T(8,128)(2,1)S(1)}, u32[]{:S(2)}, u32[]{:S(2)}) collective-permute-start(bf16[1024,128]{1,0:T(8,128)(2,1)S(1)} %get-tuple-element.88.refs_0_), channel_id=1, source_target_pairs={{0,1},{1,0},{2,3},{3,2},{4,5},{5,4},{6,7},{7,6},{8,9},{9,8},{10,11... | collective-permute-start | bytes 786440 | tf_op jit(solution)/shard_map/ppermute | solution.py:30
  51.4 0.8 %multiply_subtract_fusion = f32[512,128]{1,0:T(8,128)} fusion(f32[512,128]{1,0:T(8,128)S(1)} %get-tuple-element.85, f32[512,128]{1,0:T(8,128)S(1)} %get-tuple-element.94, f32[512,128]{1,0:T(8,128)S(1)} %get-tuple-element.79, f32[512,128]{1,0:T(8,128)S(1)} %get-tuple-element.93), kind=kLoop, calls=%fused_computation | loop fusion | flops 786432 | bytes 1310720 | tf_op jit(solution)/shard_map/sub | solution.py:35
  52.3 2.1 %collective-permute-done.16.refs_1_ = bf16[1024,128]{1,0:T(8,128)(2,1)S(1)} collective-permute-done((bf16[1024,128]{1,0:T(8,128)(2,1)S(1)}, bf16[1024,128]{1,0:T(8,128)(2,1)S(1)}, u32[]{:S(2)}, u32[]{:S(2)}) %collective-permute-start.16) | collective-permute-done | bytes 262176 | tf_op jit(solution)/shard_map/ppermute | solution.py:30
  54.4 0.9 %shard_map.84.refs_2_ = f32[2048,128]{1,0:T(8,128)} custom-call(f32[1024,128]{1,0:T(8,128)S(1)} %get-tuple-element.89.items_ref, f32[1024,128]{1,0:T(8,128)S(1)} %get-tuple-element.90.accum_ref, bf16[1024,128]{1,0:T(8,128)(2,1)S(1)} %get-tuple-element.91.refs_0_, bf16[1024,128]{1,0:T(8,128)(2,1)S(1)} %collective-permute-done.16.refs_1_), custom_call_target="tpu_custom_call" | custom-call | flops 786432 | bytes 2048 | tf_op jit(solution)/shard_map/pallas_call | solution.py:217
  55.3 2.8 %collective-permute-done.15.refs_1_ = bf16[1024,128]{1,0:T(8,128)(2,1)S(1)} collective-permute-done((bf16[1024,128]{1,0:T(8,128)(2,1)S(1)}, bf16[1024,128]{1,0:T(8,128)(2,1)S(1)}, u32[]{:S(2)}, u32[]{:S(2)}) %collective-permute-start.15) | collective-permute-done | bytes 262176 | tf_op jit(solution)/shard_map/ppermute | solution.py:30
  58.0 0.9 %shard_map.85 = f32[2048,128]{1,0:T(8,128)} custom-call(f32[1024,128]{1,0:T(8,128)S(1)} %get-tuple-element.86.items_ref, f32[1024,128]{1,0:T(8,128)S(1)} %get-tuple-element.87.accum_ref, bf16[1024,128]{1,0:T(8,128)(2,1)S(1)} %get-tuple-element.88.refs_0_, bf16[1024,128]{1,0:T(8,128)(2,1)S(1)} %collective-permute-done.15.refs_1_, ...), custom_call_target="tpu_custom_call", output_to_operand_aliasing={{}: (4, {})} | custom-call | flops 786432 | bytes 2048 | tf_op jit(solution)/shard_map/pallas_call | solution.py:217
  (50 shorter events, 9.7 us)
Async XLA Ops:
  0.6 7.2 %copy-start = (bf16[2,512,2048]{2,1,0:T(8,128)(2,1)S(1)}, bf16[2,512,2048]{2,1,0:T(8,128)(2,1)}, u32[]{:S(2)}) copy-start(bf16[2,512,2048]{2,1,0:T(8,128)(2,1)} %rate_ref.21) | copy-start | bytes 12582916
  0.6 7.2 %copy-start.3 = (f32[512,128]{1,0:T(8,128)S(1)}, f32[512,128]{1,0:T(8,128)}, u32[]{:S(2)}) copy-start(f32[512,128]{1,0:T(8,128)} %half_ref.1) | copy-start | bytes 786436
  0.6 7.2 %copy-start.1 = (f32[2048,128]{1,0:T(8,128)S(1)}, f32[2048,128]{1,0:T(8,128)}, u32[]{:S(2)}) copy-start(f32[2048,128]{1,0:T(8,128)} %refs_1_.7) | copy-start | bytes 3145732
  4.8 10.4 %copy-start.2 = (f32[2048,128]{1,0:T(8,128)S(1)}, f32[2048,128]{1,0:T(8,128)}, u32[]{:S(2)}) copy-start(f32[2048,128]{1,0:T(8,128)} %refs_2_.7) | copy-start | bytes 3145732
  4.8 10.4 %copy-start.4 = (bf16[1024,128]{1,0:T(8,128)(2,1)S(1)}, bf16[1024,128]{1,0:T(8,128)(2,1)}, u32[]{:S(2)}) copy-start(bf16[1024,128]{1,0:T(8,128)(2,1)} %get-tuple-element.50.refs_3_) | copy-start | bytes 786436
  4.9 10.4 %collective-permute-start = (bf16[1024,128]{1,0:T(8,128)(2,1)}, bf16[1024,128]{1,0:T(8,128)(2,1)S(1)}, u32[]{:S(2)}, u32[]{:S(2)}) collective-permute-start(bf16[1024,128]{1,0:T(8,128)(2,1)} %get-tuple-element.50.refs_3_), channel_id=1, source_target_pairs={{0,1},{1,0},{2,3},{3,2},{4,5},{5,4},{6,7},{7,6},{8,9},{9,8},{10,11... | collective-permute-start | bytes 786440 | tf_op jit(solution)/shard_map/ppermute | solution.py:30
  8.6 1.5 %copy-start.6 = (f32[512,128]{1,0:T(8,128)S(1)}, f32[512,128]{1,0:T(8,128)}, u32[]{:S(2)}) copy-start(f32[512,128]{1,0:T(8,128)} %param.7) | copy-start | bytes 786436
  8.6 1.5 %copy-start.7 = (f32[512,128]{1,0:T(8,128)S(1)}, f32[512,128]{1,0:T(8,128)}, u32[]{:S(2)}) copy-start(f32[512,128]{1,0:T(8,128)} %get-tuple-element.47) | copy-start | bytes 786436
  9.9 11.0 %collective-permute-start.1 = (bf16[1024,128]{1,0:T(8,128)(2,1)S(1)}, bf16[1024,128]{1,0:T(8,128)(2,1)S(1)}, u32[]{:S(2)}, u32[]{:S(2)}) collective-permute-start(bf16[1024,128]{1,0:T(8,128)(2,1)S(1)} %get-tuple-element.53.refs_3_), channel_id=1, source_target_pairs={{0,1},{1,0},{2,3},{3,2},{4,5},{5,4},{6,7},{7,6},{8,9},{9,8},{10,11... | collective-permute-start | bytes 786440 | tf_op jit(solution)/shard_map/ppermute | solution.py:30
  16.0 7.7 %collective-permute-start.2 = (bf16[512,128]{1,0:T(8,128)(2,1)S(1)}, bf16[512,128]{1,0:T(8,128)(2,1)S(1)}, u32[]{:S(2)}, u32[]{:S(2)}) collective-permute-start(bf16[512,128]{1,0:T(8,128)(2,1)S(1)} %get-tuple-element.57.refs_0_), channel_id=1, source_target_pairs={{0,1},{1,0},{2,3},{3,2},{4,5},{5,4},{6,7},{7,6},{8,9},{9,8},{10,11... | collective-permute-start | bytes 393224 | tf_op jit(solution)/shard_map/ppermute | solution.py:30
  18.9 7.8 %collective-permute-start.4 = (bf16[512,128]{1,0:T(8,128)(2,1)S(1)}, bf16[512,128]{1,0:T(8,128)(2,1)S(1)}, u32[]{:S(2)}, u32[]{:S(2)}) collective-permute-start(bf16[512,128]{1,0:T(8,128)(2,1)S(1)} %get-tuple-element.63.refs_0_), channel_id=1, source_target_pairs={{0,1},{1,0},{2,3},{3,2},{4,5},{5,4},{6,7},{7,6},{8,9},{9,8},{10,11... | collective-permute-start | bytes 393224 | tf_op jit(solution)/shard_map/ppermute | solution.py:30
  21.6 6.8 %collective-permute-start.6 = (bf16[512,128]{1,0:T(8,128)(2,1)S(1)}, bf16[512,128]{1,0:T(8,128)(2,1)S(1)}, u32[]{:S(2)}, u32[]{:S(2)}) collective-permute-start(bf16[512,128]{1,0:T(8,128)(2,1)S(1)} %get-tuple-element.70.refs_0_), channel_id=1, source_target_pairs={{0,1},{1,0},{2,3},{3,2},{4,5},{5,4},{6,7},{7,6},{8,9},{9,8},{10,11... | collective-permute-start | bytes 393224 | tf_op jit(solution)/shard_map/ppermute | solution.py:30
  23.8 7.1 %collective-permute-start.3 = (bf16[512,128]{1,0:T(8,128)(2,1)S(1)}, bf16[512,128]{1,0:T(8,128)(2,1)S(1)}, u32[]{:S(2)}, u32[]{:S(2)}) collective-permute-start(bf16[512,128]{1,0:T(8,128)(2,1)S(1)} %get-tuple-element.58.refs_5_), channel_id=1, source_target_pairs={{0,2},{1,3},{2,4},{3,5},{4,6},{5,7},{6,8},{7,9},{8,10},{9,11},{10,... | collective-permute-start | bytes 393224 | tf_op jit(solution)/shard_map/ppermute | solution.py:30
  24.6 7.0 %collective-permute-start.8 = (bf16[512,128]{1,0:T(8,128)(2,1)S(1)}, bf16[512,128]{1,0:T(8,128)(2,1)S(1)}, u32[]{:S(2)}, u32[]{:S(2)}) collective-permute-start(bf16[512,128]{1,0:T(8,128)(2,1)S(1)} %get-tuple-element.65.refs_3_.refs_0_), channel_id=1, source_target_pairs={{0,1},{1,0},{2,3},{3,2},{4,5},{5,4},{6,7},{7,6},{8,9},{9,8},{10,11... | collective-permute-start | bytes 393224 | tf_op jit(solution)/shard_map/ppermute | solution.py:30
  26.8 8.5 %collective-permute-start.5 = (bf16[1024,128]{1,0:T(8,128)(2,1)S(1)}, bf16[1024,128]{1,0:T(8,128)(2,1)S(1)}, u32[]{:S(2)}, u32[]{:S(2)}) collective-permute-start(bf16[1024,128]{1,0:T(8,128)(2,1)S(1)} %get-tuple-element.66), channel_id=1, source_target_pairs={{0,2},{1,3},{2,4},{3,5},{4,6},{5,7},{6,8},{7,9},{8,10},{9,11},{10,... | collective-permute-start | bytes 786440 | tf_op jit(solution)/shard_map/ppermute | solution.py:30
  28.6 9.6 %collective-permute-start.7 = (bf16[1024,128]{1,0:T(8,128)(2,1)S(1)}, bf16[1024,128]{1,0:T(8,128)(2,1)S(1)}, u32[]{:S(2)}, u32[]{:S(2)}) collective-permute-start(bf16[1024,128]{1,0:T(8,128)(2,1)S(1)} %get-tuple-element.72), channel_id=1, source_target_pairs={{0,2},{1,3},{2,4},{3,5},{4,6},{5,7},{6,8},{7,9},{8,10},{9,11},{10,... | collective-permute-start | bytes 786440 | tf_op jit(solution)/shard_map/ppermute | solution.py:30
  31.8 9.2 %collective-permute-start.9 = (bf16[1024,128]{1,0:T(8,128)(2,1)S(1)}, bf16[1024,128]{1,0:T(8,128)(2,1)S(1)}, u32[]{:S(2)}, u32[]{:S(2)}) collective-permute-start(bf16[1024,128]{1,0:T(8,128)(2,1)S(1)} %get-tuple-element.78), channel_id=1, source_target_pairs={{0,2},{1,3},{2,4},{3,5},{4,6},{5,7},{6,8},{7,9},{8,10},{9,11},{10,... | collective-permute-start | bytes 786440 | tf_op jit(solution)/shard_map/ppermute | solution.py:30
  31.9 11.8 %collective-permute-start.10 = (bf16[512,128]{1,0:T(8,128)(2,1)S(1)}, bf16[512,128]{1,0:T(8,128)(2,1)S(1)}, u32[]{:S(2)}, u32[]{:S(2)}) collective-permute-start(bf16[512,128]{1,0:T(8,128)(2,1)S(1)} %get-tuple-element.77.refs_3_), channel_id=1, source_target_pairs={{0,1},{1,0},{2,3},{3,2},{4,5},{5,4},{6,7},{7,6},{8,9},{9,8},{10,11... | collective-permute-start | bytes 393224 | tf_op jit(solution)/shard_map/ppermute | solution.py:30
  33.9 11.9 %collective-permute-start.13 = (bf16[512,128]{1,0:T(8,128)(2,1)S(1)}, bf16[512,128]{1,0:T(8,128)(2,1)S(1)}, u32[]{:S(2)}, u32[]{:S(2)}) collective-permute-start(bf16[512,128]{1,0:T(8,128)(2,1)S(1)} %get-tuple-element.83), channel_id=1, source_target_pairs={{0,2},{1,3},{2,4},{3,5},{4,6},{5,7},{6,8},{7,9},{8,10},{9,11},{10,... | collective-permute-start | bytes 393224 | tf_op jit(solution)/shard_map/ppermute | solution.py:30
  36.1 7.6 %collective-permute-start.11 = (bf16[512,128]{1,0:T(8,128)(2,1)S(1)}, bf16[512,128]{1,0:T(8,128)(2,1)S(1)}, u32[]{:S(2)}, u32[]{:S(2)}) collective-permute-start(bf16[512,128]{1,0:T(8,128)(2,1)S(1)} %get-tuple-element.80.refs_7_), channel_id=1, source_target_pairs={{0,1},{1,0},{2,3},{3,2},{4,5},{5,4},{6,7},{7,6},{8,9},{9,8},{10,11... | collective-permute-start | bytes 393224 | tf_op jit(solution)/shard_map/ppermute | solution.py:30
  38.9 6.9 %collective-permute-start.12 = (bf16[512,128]{1,0:T(8,128)(2,1)S(1)}, bf16[512,128]{1,0:T(8,128)(2,1)S(1)}, u32[]{:S(2)}, u32[]{:S(2)}) collective-permute-start(bf16[512,128]{1,0:T(8,128)(2,1)S(1)} %get-tuple-element.82.refs_3_), channel_id=1, source_target_pairs={{0,1},{1,0},{2,3},{3,2},{4,5},{5,4},{6,7},{7,6},{8,9},{9,8},{10,11... | collective-permute-start | bytes 393224 | tf_op jit(solution)/shard_map/ppermute | solution.py:30
  41.7 6.5 %collective-permute-start.14 = (bf16[512,128]{1,0:T(8,128)(2,1)S(1)}, bf16[512,128]{1,0:T(8,128)(2,1)S(1)}, u32[]{:S(2)}, u32[]{:S(2)}) collective-permute-start(bf16[512,128]{1,0:T(8,128)(2,1)S(1)} %get-tuple-element.84.refs_7_), channel_id=1, source_target_pairs={{0,1},{1,0},{2,3},{3,2},{4,5},{5,4},{6,7},{7,6},{8,9},{9,8},{10,11... | collective-permute-start | bytes 393224 | tf_op jit(solution)/shard_map/ppermute | solution.py:30
  45.0 9.3 %collective-permute-start.16 = (bf16[1024,128]{1,0:T(8,128)(2,1)S(1)}, bf16[1024,128]{1,0:T(8,128)(2,1)S(1)}, u32[]{:S(2)}, u32[]{:S(2)}) collective-permute-start(bf16[1024,128]{1,0:T(8,128)(2,1)S(1)} %get-tuple-element.91.refs_0_), channel_id=1, source_target_pairs={{0,1},{1,0},{2,3},{3,2},{4,5},{5,4},{6,7},{7,6},{8,9},{9,8},{10,11... | collective-permute-start | bytes 786440 | tf_op jit(solution)/shard_map/ppermute | solution.py:30
  49.6 8.5 %collective-permute-start.15 = (bf16[1024,128]{1,0:T(8,128)(2,1)S(1)}, bf16[1024,128]{1,0:T(8,128)(2,1)S(1)}, u32[]{:S(2)}, u32[]{:S(2)}) collective-permute-start(bf16[1024,128]{1,0:T(8,128)(2,1)S(1)} %get-tuple-element.88.refs_0_), channel_id=1, source_target_pairs={{0,1},{1,0},{2,3},{3,2},{4,5},{5,4},{6,7},{7,6},{8,9},{9,8},{10,11... | collective-permute-start | bytes 786440 | tf_op jit(solution)/shard_map/ppermute | solution.py:30
  (1 other events, 0.7 us)
